TPU v7x, 32 devices: a whole 2x2x4 slice. The times are simulated.
32 devices in a mesh: grp: 2 (over y), pre: 4 (over z), row: 4 (over x, core).
Axes of the slice: x: 2, y: 2, z: 4, core: 2. Of those that a mesh axis runs over, the one named last changes fastest.
Arguments:
- queries: bfloat16 [32, 2, 8192], P(('grp', 'row')), parts along dimension 0, may hold values from -200 to 200
- prefix_keys: bfloat16 [1024, 1024], P(('grp', 'pre')), parts along dimension 0, may hold values from -7 to 7
- prefix_values: bfloat16 [1024, 1024], P(('grp', 'pre')), parts along dimension 0, may hold values from -6 to 6
- suffix_keys: bfloat16 [32, 64, 1024], P(('grp', 'row'), 'pre'), parts along dimension 0, may hold values from -6 to 6
- suffix_values: bfloat16 [32, 64, 1024], P(('grp', 'row'), 'pre'), parts along dimension 0, may hold values from -6 to 6
- new_keys: bfloat16 [32, 2, 1024], P(('grp', 'row')), parts along dimension 0, may hold values from -6 to 6
- new_values: bfloat16 [32, 2, 1024], P(('grp', 'row')), parts along dimension 0, may hold values from -6 to 6
- hidden: bfloat16 [32, 2, 8192], P(('grp', 'pre'), None, 'row'), parts along dimension 0, may hold values from -6 to 6
- adapter_ids: int32 [32], P(('grp', 'row')), parts along dimension 0, may hold values from 0 to 127
- suffix_lengths: int32 [32], P(('grp', 'row')), parts along dimension 0, may hold values from 1 to 64
- kv_scales: bfloat16 [128, 2, 1024], replicated, may hold values from 0.25 to 1.75
- ffn_scales: bfloat16 [128, 14336], P(None, 'pre'), may hold values from 0.25 to 1.75
- out_weight: bfloat16 [8192, 8192], P('pre', 'row'), may hold values from -0.0625 to 0.0625
- norm_gain: bfloat16 [8192], P('row'), may hold values from 0.25 to 1.75
- gate_up: bfloat16 [8192, 2, 14336], P('row', None, 'pre'), may hold values from -0.0625 to 0.0625
Outputs:
- residual: bfloat16 [32, 2, 8192], P(('grp', 'pre'), None, 'row'), parts along dimension 0
- activation: bfloat16 [32, 2, 14336], P(('grp', 'row'), None, 'pre'), parts along dimension 0
There are 2 independent parts, one for each index of `grp`. A program takes and returns all parts, laid end to end along the dimension named above; an argument that names none is the same for every part. Nothing has to cross between parts.
All inputs are finite; a program needn't handle non-finite values.
Results may differ from a plain program's by a relative error of at most 0.015.
Values may be sent and summed in bfloat16 or wider, within the bound.
No kernel may reach another device: no remote copies, remote signals or barrier semaphores. Data moves between devices by JAX's collectives and lax.ppermute only.
A program may use at most 128 MiB of HBM per device.

v0:
```python
import jax
import jax.numpy as jnp
from jax import lax
from jax.sharding import PartitionSpec as P

D = 8192
HEADS = 64
KV_HEADS = 8
HD = 128
STEPS = 2


masked_score = -1e30


def joined(value, axis, combine):
    everything = jax.tree.map(lambda part: lax.all_gather(part, axis), value)
    first = jax.tree.map(lambda part: part[0], everything)

    def lap(k, so_far):
        return combine(so_far, jax.tree.map(lambda part: part[k], everything))

    return lax.fori_loop(1, lax.axis_size(axis), lap, first)


def combine_partials(first, second):
    highest = jnp.maximum(first[0], second[0])
    left_factor = jnp.exp(first[0] - highest)
    right_factor = jnp.exp(second[0] - highest)
    return (
        highest,
        first[1] * left_factor + second[1] * right_factor,
        first[2] * left_factor[..., None] + second[2] * right_factor[..., None],
    )


def per_device(
    queries,
    prefix_keys,
    prefix_values,
    suffix_keys,
    suffix_values,
    new_keys,
    new_values,
    hidden,
    adapter_ids,
    suffix_lengths,
    kv_scales,
    ffn_scales,
    out_weight,
    norm_gain,
    gate_up,
):
    row_local = queries.shape[0]
    prefix_local = prefix_keys.shape[0]
    suffix_local = suffix_keys.shape[1]
    kv_width = prefix_keys.shape[1]
    adapters = kv_scales.shape[0]
    group_size = HEADS // KV_HEADS
    score_scale = HD ** (-0.5)
    pre_count = lax.axis_size("pre")
    pre_index = lax.axis_index("pre")
    block_width = HEADS * HD // pre_count
    onehot = (adapter_ids[:, None] == jnp.arange(adapters, dtype=jnp.int32)[None, :]).astype(
        jnp.bfloat16
    )
    scale_rows = jnp.dot(
        onehot, kv_scales.reshape(adapters, 2 * kv_width), preferred_element_type=jnp.float32
    )
    scale_rows = scale_rows.reshape(row_local, 2, KV_HEADS, HD)
    key_scale = scale_rows[:, 0]
    value_scale = scale_rows[:, 1]
    ffn_rows = jnp.dot(onehot, ffn_scales, preferred_element_type=jnp.float32)
    cached_key = prefix_keys.reshape(prefix_local, KV_HEADS, HD)
    cached_value = prefix_values.reshape(prefix_local, KV_HEADS, HD)
    recent_key = suffix_keys.reshape(row_local, suffix_local, KV_HEADS, HD)
    recent_value = suffix_values.reshape(row_local, suffix_local, KV_HEADS, HD)
    fresh_key = (
        new_keys.astype(jnp.float32).reshape(row_local, STEPS, KV_HEADS, HD) * key_scale[:, None]
    ).astype(jnp.bfloat16)
    fresh_value = (
        new_values.astype(jnp.float32).reshape(row_local, STEPS, KV_HEADS, HD)
        * value_scale[:, None]
    ).astype(jnp.bfloat16)
    positions = pre_index * suffix_local + jnp.arange(suffix_local, dtype=jnp.int32)
    in_suffix = (positions[None, :] < suffix_lengths[:, None])[:, None, None, None, :]
    owner = pre_index == 0

    def attend(start_step, step_count):
        finish = start_step + step_count
        query_heads = queries.reshape(row_local, step_count, KV_HEADS, group_size, HD)
        scaled_query = (query_heads.astype(jnp.float32) * key_scale[:, None, :, None, :]).astype(
            jnp.bfloat16
        )
        prefix_scores = (
            jnp.einsum(
                "rskgd,tkd->rskgt", scaled_query, cached_key, preferred_element_type=jnp.float32
            )
            * score_scale
        )
        suffix_scores = (
            jnp.einsum(
                "rskgd,rtkd->rskgt", query_heads, recent_key, preferred_element_type=jnp.float32
            )
            * score_scale
        )
        suffix_scores = jnp.where(in_suffix, suffix_scores, masked_score)
        in_order = (
            jnp.arange(finish, dtype=jnp.int32)[None, :]
            <= (start_step + jnp.arange(step_count, dtype=jnp.int32))[:, None]
        )
        new_mask = (in_order & owner)[None, :, None, None, :]
        new_scores = (
            jnp.einsum(
                "rskgd,rnkd->rskgn", query_heads, fresh_key, preferred_element_type=jnp.float32
            )
            * score_scale
        )
        new_scores = jnp.where(new_mask, new_scores, masked_score)
        peak_score = jnp.maximum(
            jnp.maximum(jnp.max(prefix_scores, axis=-1), jnp.max(suffix_scores, axis=-1)),
            jnp.max(new_scores, axis=-1),
        )
        prefix_weight = jnp.exp(prefix_scores - peak_score[..., None]).astype(jnp.bfloat16)
        suffix_weight = jnp.where(
            in_suffix, jnp.exp(suffix_scores - peak_score[..., None]), 0.0
        ).astype(jnp.bfloat16)
        new_weight = jnp.where(new_mask, jnp.exp(new_scores - peak_score[..., None]), 0.0).astype(
            jnp.bfloat16
        )
        weight_sum = (
            jnp.sum(prefix_weight.astype(jnp.float32), axis=-1)
            + jnp.sum(suffix_weight.astype(jnp.float32), axis=-1)
            + jnp.sum(new_weight.astype(jnp.float32), axis=-1)
        )
        numerator = jnp.einsum(
            "rskgt,tkd->rskgd", prefix_weight, cached_value, preferred_element_type=jnp.float32
        )
        numerator = numerator * value_scale[:, None, :, None, :]
        numerator = numerator + jnp.einsum(
            "rskgt,rtkd->rskgd", suffix_weight, recent_value, preferred_element_type=jnp.float32
        )
        numerator = numerator + jnp.einsum(
            "rskgn,rnkd->rskgd", new_weight, fresh_value, preferred_element_type=jnp.float32
        )
        return (peak_score, weight_sum, numerator)

    def layer(start_step, step_count):
        finish = start_step + step_count
        peak_score, weight_sum, numerator = attend(start_step, step_count)
        peak_score, weight_sum, numerator = joined(
            (peak_score, weight_sum, numerator), "pre", combine_partials
        )
        mixed_all = (
            (numerator / weight_sum[..., None])
            .astype(jnp.bfloat16)
            .reshape(row_local, step_count, HEADS * HD)
        )
        mixed_block = lax.dynamic_slice_in_dim(mixed_all, pre_index * block_width, block_width, 2)
        gathered = lax.all_gather(mixed_block, "row", axis=0, tiled=True)
        out_cols = out_weight.shape[1]
        amount = gathered.shape[0] // pre_count * lax.axis_size("pre")
        product = jnp.dot(
            gathered.reshape(amount * step_count, block_width),
            out_weight,
            preferred_element_type=jnp.float32,
        )
        projected = lax.psum_scatter(
            product.reshape(amount, step_count, out_cols), "pre", scatter_dimension=0, tiled=True
        )
        residual = (hidden.astype(jnp.float32) + projected).astype(jnp.bfloat16)
        stacked = lax.all_gather(residual, "pre", axis=0, tiled=True)
        rows_all = stacked.shape[0]
        feature_local = stacked.shape[2]
        ff_local = gate_up.shape[2]
        widened = stacked.astype(jnp.float32)
        squares = jnp.sum(widened * widened, axis=2)
        normed = (widened * norm_gain.astype(jnp.float32)).astype(jnp.bfloat16)
        products = jnp.dot(
            normed.reshape(rows_all * step_count, feature_local),
            gate_up.reshape(feature_local, 2 * ff_local),
            preferred_element_type=jnp.float32,
        )
        products = products.reshape(rows_all, step_count, 2 * ff_local)
        summed, square_sums = (
            lax.psum_scatter(products, "row", scatter_dimension=0, tiled=True),
            lax.psum_scatter(squares, "row", scatter_dimension=0, tiled=True),
        )
        inverse = lax.rsqrt(square_sums / D + 1e-05)[..., None]
        gate_part = summed[..., :ff_local] * inverse
        up_part = summed[..., ff_local:] * inverse
        activation = (jax.nn.silu(gate_part) * up_part * ffn_rows[:, None, :]).astype(jnp.bfloat16)
        return (residual, activation)

    step_spans = [(0, STEPS)]
    results = [layer(start_step, step_count) for start_step, step_count in step_spans]
    residual_all = jnp.concatenate([entry[0] for entry in results], axis=1)
    activation_all = jnp.concatenate([entry[1] for entry in results], axis=1)
    return (residual_all, activation_all)


def solution(mesh):
    placed = (
        P(("grp", "row"), None, None),
        P(("grp", "pre"), None),
        P(("grp", "pre"), None),
        P(("grp", "row"), "pre", None),
        P(("grp", "row"), "pre", None),
        P(("grp", "row"), None, None),
        P(("grp", "row"), None, None),
        P(("grp", "pre"), None, "row"),
        P(("grp", "row")),
        P(("grp", "row")),
        P(),
        P(None, "pre"),
        P("pre", "row"),
        P("row"),
        P("row", None, "pre"),
    )
    return jax.shard_map(
        per_device,
        mesh=mesh,
        in_specs=placed,
        out_specs=(P(("grp", "pre"), None, "row"), P(("grp", "row"), None, "pre")),
        check_vma=False,
    )
```

profile of v0, /device:TPU:0, one launch (start us, length us, event | category | flops | bytes accessed | tf_op | source)
XLA Modules:
  0.0 205.3 jit_solution(3568298268383382114)
XLA Ops:
  7.2 0.0 all-gather.5.cloned.1.call-start
  7.2 1.2 copy.156
  8.5 0.3 copy.102
  8.8 0.9 fusion.44
  9.7 1.0 reshape.147
  10.7 0.9 copy.158
  11.7 1.0 copy.157
  12.7 0.7 broadcast_compare_fusion
  13.4 0.4 fusion.53
  13.8 0.3 fusion.52
  14.1 1.4 fusion.51
  15.6 0.2 convert_reduce_fusion.2
  15.8 0.3 convert_reduce_fusion
  16.1 0.9 copy.160
  17.1 1.0 copy.159
  18.1 0.2 convolution_bitcast_fusion.1
  18.2 0.9 convolution_bitcast_fusion.2
  19.2 1.0 fusion.11
  20.2 0.0 all-reduce.6.cloned.1.call-start
  20.2 0.3 convert_reduce_fusion.1
  20.6 15.3 %all-gather.1 = f32[16,2,8,8]{3,2,1,0:T(8,128)S(1)} all-gather(f32[4,2,8,8]{3,2,1,0:T(8,128)S(1)} %copy_add_fusion), channel_id=3, replica_groups=mesh['grp'=2,'pre'=4,'row'=4] {'pre'}, dimensions={0}, use_global_device_ids=true | all-gather | bytes 10240 | tf_op jit(solution)/shard_map/all_gather | solution.py:17
  35.9 14.7 %all-gather = f32[16,2,8,8]{3,2,1,0:T(8,128)S(1)} all-gather(f32[4,2,8,8]{3,2,1,0:T(8,128)S(1)} %copy_maximum_fusion), channel_id=2, replica_groups=mesh['grp'=2,'pre'=4,'row'=4] {'pre'}, dimensions={0}, use_global_device_ids=true | all-gather | bytes 10240 | tf_op jit(solution)/shard_map/all_gather | solution.py:17
  50.5 2.8 %all-gather.5.cloned.1.call-done = f32[16,2,8,8,128]{4,3,1,0,2:T(8,128)} async-done(((f32[4,2,8,8,128]{4,3,1,0,2:T(8,128)}), f32[16,2,8,8,128]{4,3,1,0,2:T(8,128)}) %all-gather.5.cloned.1.call-update) | async-done | bytes 1048592 | tf_op jit(solution)/shard_map/all_gather | solution.py:17
  53.3 1.0 slice.35
  54.3 3.8 %while.19 = (s32[]{:T(128)}, f32[4,2,8,8]{3,2,1,0:T(8,128)S(1)}, f32[4,2,8,8]{3,2,1,0:T(8,128)S(1)}, f32[4,2,8,8,128]{4,3,2,1,0:T(8,128)S(1)}, f32[4,4,2,8,8]{4,...) while((s32[]{:T(128)}, f32[4,2,8,8]{3,2,1,0:T(8,128)S(1)}, ...), condition=%wide.region_7.8_spmd, body=%wide.region_6.7_spmd.sunk | while | flops 199685 | bytes 807063 | solution.py:23
  54.3 1.2 fusion.60
  55.6 1.2 fusion.60
  56.9 1.2 fusion.60
  58.1 0.1 divide_convert_fusion
  58.4 5.4 %all_gather.24 = bf16[16,2,2048]{2,1,0:T(2,128)(2,1)S(1)} all-gather(bf16[4,2,2048]{2,1,0:T(2,128)(2,1)S(1)} %constant_dynamic-slice_fusion.1), channel_id=1, replica_groups=mesh['grp'=2,'pre'=4,'row'=4] {'row'}, dimensions={0}, use_global_device_ids=true | all-gather | bytes 163840 | tf_op jit(solution)/shard_map/all_gather | solution.py:160
  63.8 5.6 %fusion.4 = f32[16,2,2048]{2,0,1:T(8,128)} fusion(bf16[2048,2048]{1,0:T(8,128)(2,1)} %param.29, bf16[16,2,2048]{2,1,0:T(2,128)(2,1)S(1)} %all_gather.24), kind=kOutput, calls=%fused_computation.10 | convolution fusion | flops 268435456 | bytes 8781824 | tf_op jit(solution)/shard_map/dot_general | solution.py:163
  69.4 0.0 all-reduce.6.cloned.1.call-update
  69.5 0.0 all-reduce.8.cloned.1.call-start
  69.6 62.1 %reshape.180 = bf16[2048,7168,1]{1,0,2:T(8,128)(2,1)} reshape(bf16[2048,2,3584]{2,1,0:T(2,128)(2,1)} %param.31) | data formatting | bytes 58720256 | tf_op jit(solution)/shard_map/reshape | solution.py:181
  131.7 0.6 dynamic-slice
  132.3 0.6 dynamic-slice.2
  134.1 0.0 all-reduce.6.cloned.1.call-done
  134.2 0.9 fusion.31
  135.2 13.4 %all_gather.25 = bf16[16,2,2048]{2,1,0:T(2,128)(2,1)S(1)} all-gather(bf16[4,2,2048]{2,1,0:T(2,128)(2,1)S(1)} %copy.130), channel_id=1, replica_groups=mesh['grp'=2,'pre'=4,'row'=4] {'pre'}, dimensions={0}, use_global_device_ids=true | all-gather | bytes 163840 | tf_op jit(solution)/shard_map/all_gather | solution.py:172
  148.6 13.0 %fusion.18 = f32[16,2,7168]{2,0,1:T(8,128)} fusion(bf16[2048,7168,1]{1,0,2:T(8,128)(2,1)} %reshape.180, f32[2048]{0:T(1024)S(1)} %convert_element_type.68, bf16[16,2,2048]{2,1,0:T(2,128)(2,1)S(1)} %all_gather.25), kind=kOutput, calls=%fused_computation.38 | convolution fusion | flops 939720704 | bytes 30416896 | tf_op jit(solution)/shard_map/dot_general | solution.py:179
  161.5 0.0 all-reduce.8.cloned.1.call-update
  161.6 0.3 fusion.42
  161.9 0.1 fusion.15
  162.0 5.7 %all-reduce.2 = f32[16,2]{0,1:T(2,128)S(1)} all-reduce(f32[16,2]{0,1:T(2,128)S(1)} %fusion.15), channel_id=7, replica_groups=mesh['grp'=2,'pre'=4,'row'=4] {'row'}, use_global_device_ids=true, to_apply=%region_11.12.clone | all-reduce | flops 32 | bytes 256
  167.6 0.1 fusion.47
  167.7 29.2 %all-reduce.8.cloned.1.call-done = f32[16,2,7168]{2,0,1:T(8,128)} async-done(((f32[16,2,7168]{2,0,1:T(8,128)}), f32[16,2,7168]{2,0,1:T(8,128)}) %all-reduce.8.cloned.1.call-update) | async-done | bytes 917520
  196.9 1.2 multiply_convert_fusion.2
  198.1 0.7 copy.131
  (35 shorter events, 0.4 us)
Async XLA Ops:
  7.2 154.4 %copy-start = (bf16[128,3584]{1,0:T(8,128)(2,1)S(1)}, bf16[128,3584]{1,0:T(8,128)(2,1)}, u32[]{:S(2)}) copy-start(bf16[128,3584]{1,0:T(8,128)(2,1)} %param.28) | copy-start | bytes 2752516
  7.2 46.1 %all-gather.5.cloned.1.call-start = ((), (), s32[]{:S(2)}) async-start(), calls=%async_computation | async-start | bytes 1310720 | tf_op jit(solution)/shard_map/all_gather | solution.py:17
  20.2 114.0 %all-reduce.6.cloned.1.call-start = ((), (), s32[]{:S(2)}) async-start(), calls=%async_computation.1 | async-start | bytes 524288
  69.5 127.4 %all-reduce.8.cloned.1.call-start = ((), (), s32[]{:S(2)}) async-start(), calls=%async_computation.2 | async-start | bytes 1835008
  69.5 62.1 %copy-start.3 = (bf16[2048]{0:T(1024)(128)(2,1)S(1)}, bf16[2048]{0:T(1024)(128)(2,1)}, u32[]{:S(2)}) copy-start(bf16[2048]{0:T(1024)(128)(2,1)} %param.30) | copy-start | bytes 12292
  69.5 62.1 %copy-start.6 = (u32[32]{0:T(128)S(1)}, u32[32]{0:T(128)}, u32[]{:S(2)}) copy-start(u32[32]{0:T(128)} %constant.77) | copy-start | bytes 388
  69.5 62.7 %copy-start.5 = (u32[32]{0:T(128)S(1)}, u32[32]{0:T(128)}, u32[]{:S(2)}) copy-start(u32[32]{0:T(128)} %constant.81) | copy-start | bytes 388
  69.6 64.6 %copy-start.2 = (bf16[4,2,2048]{2,1,0:T(2,128)(2,1)S(1)}, bf16[4,2,2048]{2,1,0:T(2,128)(2,1)}, u32[]{:S(2)}) copy-start(bf16[4,2,2048]{2,1,0:T(2,128)(2,1)} %param.24) | copy-start | bytes 98308
  131.6 29.9 %copy-start.4 = (s32[4]{0:T(128)S(1)}, s32[4]{0:T(128)}, u32[]{:S(2)}) copy-start(s32[4]{0:T(128)} %param.25) | copy-start | bytes 52
  135.2 63.6 %copy-start.1 = (bf16[4,2,2048]{2,1,0:T(2,128)(2,1)}, bf16[4,2,2048]{2,1,0:T(2,128)(2,1)S(1)}, u32[]{:S(2)}) copy-start(bf16[4,2,2048]{2,1,0:T(2,128)(2,1)S(1)} %copy.130) | copy-start | bytes 98308
Sparse Core Ops, SparseCore 0:
  20.3 32.9 all-gather.4
  69.6 35.1 all-reduce.5
  161.7 35.1 all-reduce.7
where the time goes:
time: 207 us; the launch traced here: 205 us
  local copies, waits for them, and re-layouts  71.5 us (35%)
  blocking collectives  54.4 us (26%)
  waiting for transfers between devices  32 us (15%)
  matrix products  24 us (12%)
  between operations  15.4 us (7%)
  other arithmetic  7.79 us (4%)
    reshape x1, local copies, waits for them, and re-layouts, layer(): gate_up.reshape(feature_local, 2 * ff_local)  62.1 us
    all_gather x2, blocking collectives, joined(): everything = jax.tree.map(lambda part: lax.all_gather(part, axis), value)  30 us
    unnamed x5, waiting for transfers between devices  29.3 us
    all_gather x1, blocking collectives, layer(): stacked = lax.all_gather(residual, 'pre', axis=0, tiled=True)  13.4 us
    dot_general x1, matrix products, layer(): jnp.dot(normed.reshape(rows_all * step_count, feature_local), gate_up.res...  13 us
    unnamed x23, local copies, waits for them, and re-layouts  6.98 us
    unnamed x1, blocking collectives  5.65 us
    dot_general x1, matrix products, layer(): jnp.dot(gathered.reshape(amount * step_count, block_width), out_weight, p...  5.64 us
  transfers between devices with their start and end apart: 3, of which 2 were waited for; matrix products, arithmetic and copies ran while one was open for 31% of the time, Pallas kernels for 0%

commit v1 on v0

v1 whole, which is shorter than its diff:
```python
import functools

import jax
import jax.numpy as jnp
from jax import lax
from jax.experimental import pallas as pl
from jax.experimental.pallas import tpu as pltpu
from jax.sharding import PartitionSpec as P

D = 8192
HEADS = 64
KV_HEADS = 8
HD = 128
STEPS = 2
LANES = 128

masked_score = -1e30
f32 = jnp.float32
bf16 = jnp.bfloat16
VMEM = pl.BlockSpec(memory_space=pltpu.VMEM)
SMEM = pl.BlockSpec(memory_space=pltpu.SMEM)
ANY = pl.BlockSpec(memory_space=pl.ANY)


def wrapped(index, count):
    return lax.rem(index + count, count)


def dot(left, right):
    return jnp.dot(left, right, preferred_element_type=f32)


def dot_t(left, right):
    return lax.dot_general(left, right, (((1,), (1,)), ((), ())), preferred_element_type=f32)


def pick(index, scalars):
    value = jnp.full(index.shape, scalars[0], jnp.int32)
    for at in range(1, len(scalars)):
        value = jnp.where(index == at, scalars[at], value)
    return value


def three_parts(value):
    high = value.astype(bf16).astype(f32)
    rest = value - high
    middle = rest.astype(bf16).astype(f32)
    return high, middle, rest - middle


def attend_kernel(
    pre_count,
    ids,
    lengths,
    where,
    queries,
    prefix_keys,
    prefix_values,
    suffix_keys,
    suffix_values,
    new_keys,
    new_values,
    kv_scales,
    *rest,
):
    outs, (scales, stage, sem) = rest[:pre_count], rest[pre_count:]
    rows = queries.shape[0]
    tokens = rows * STEPS
    suffix_local = suffix_keys.shape[1]
    width = suffix_keys.shape[2]
    suffix_all = rows * suffix_local
    group = HEADS // KV_HEADS
    block = HEADS * HD // pre_count
    block_heads = block // HD
    me = where[0]
    copies = [
        pltpu.make_async_copy(kv_scales.at[ids[r]], scales.at[r], sem.at[r]) for r in range(rows)
    ]
    for copy in copies:
        copy.start()

    count = group * tokens
    row_at = lax.broadcasted_iota(jnp.int32, (count, LANES), 0)
    column = lax.broadcasted_iota(jnp.int32, (count, LANES), 1)
    token = lax.rem(row_at, tokens)
    row_of = token // STEPS
    step = lax.rem(token, STEPS)
    limit = pick(row_of, [lengths[r] for r in range(rows)])
    in_suffix = (
        (column < suffix_all)
        & (column // suffix_local == row_of)
        & (me * suffix_local + lax.rem(column, suffix_local) < limit)
    )
    fresh = column - suffix_all
    in_new = (
        (fresh >= 0)
        & (fresh < tokens)
        & (fresh // STEPS == row_of)
        & (lax.rem(fresh + LANES * STEPS, STEPS) <= step)
        & (me == 0)
    )
    allowed = in_suffix | in_new

    query = queries[...].reshape(tokens, HEADS * HD).astype(f32)
    fill = jnp.zeros((LANES - suffix_all - tokens, width), f32)
    for copy in copies:
        copy.wait()
    scale = scales[...].reshape(tokens, width).astype(f32)
    odd = lax.rem(lax.broadcasted_iota(jnp.int32, scale.shape, 0), 2) == 1
    key_scale = jnp.where(odd, pltpu.roll(scale, 1, 0), scale)
    value_scale = jnp.where(odd, scale, pltpu.roll(scale, tokens - 1, 0))
    fresh_key = new_keys[...].reshape(tokens, width).astype(f32) * key_scale
    fresh_value = new_values[...].reshape(tokens, width).astype(f32) * value_scale
    own_keys = jnp.concatenate(
        [
            suffix_keys[...].reshape(suffix_all, width),
            jnp.concatenate([fresh_key, fill], axis=0).astype(bf16),
        ],
        axis=0,
    )
    own_values = jnp.concatenate(
        [
            suffix_values[...].reshape(suffix_all, width),
            jnp.concatenate([fresh_value, fill], axis=0).astype(bf16),
        ],
        axis=0,
    )
    lane = lax.broadcasted_iota(jnp.int32, (tokens, LANES), 1)
    peaks = [jnp.zeros((tokens, LANES), f32) for _ in range(pre_count)]
    sums = [jnp.zeros((tokens, LANES), f32) for _ in range(pre_count)]
    for k in range(KV_HEADS):
        span = slice(k * HD, (k + 1) * HD)
        heads = [query[:, h * HD : (h + 1) * HD] for h in range(k * group, (k + 1) * group)]
        plain = jnp.concatenate(heads, axis=0).astype(bf16)
        scaled = jnp.concatenate([head * key_scale[:, span] for head in heads], axis=0).astype(bf16)
        prefix_scores = dot_t(scaled, prefix_keys[:, span]) * (HD**-0.5)
        own_scores = jnp.where(allowed, dot_t(plain, own_keys[:, span]) * (HD**-0.5), masked_score)
        peak = jnp.max(jnp.maximum(prefix_scores, own_scores), axis=1, keepdims=True)
        prefix_weight = jnp.exp(prefix_scores - peak).astype(bf16)
        own_weight = jnp.where(allowed, jnp.exp(own_scores - peak), 0.0).astype(bf16)
        total = jnp.sum(prefix_weight.astype(f32) + own_weight.astype(f32), axis=1, keepdims=True)
        from_prefix = dot(prefix_weight, prefix_values[:, span])
        from_own = dot(own_weight, own_values[:, span])
        for g in range(group):
            h = k * group + g
            at, j = h // block_heads, h % block_heads
            part = slice(g * tokens, (g + 1) * tokens)
            value = from_prefix[part] * value_scale[:, span] + from_own[part]
            stage[at, :, j * HD : (j + 1) * HD] = value.astype(bf16)
            peaks[at] = jnp.where(lane == j, peak[part], peaks[at])
            sums[at] = jnp.where(lane == j, total[part], sums[at])
    for at in range(pre_count):
        packed = jnp.zeros((tokens, LANES), f32)
        for place, piece in enumerate(three_parts(peaks[at]) + three_parts(sums[at])):
            packed = packed + (pltpu.roll(piece, place * block_heads, 1) if place else piece)
        stage[at, :, block:] = packed.astype(bf16)
    for s in range(pre_count):
        outs[s][...] = stage[wrapped(me + s, pre_count)]


def merge_kernel(parts, *rest):
    blocks, out = rest[:parts], rest[parts]
    block = out.shape[1]
    block_heads = block // HD
    peaks, sums = [], []
    for ref in blocks:
        packed = ref[:, block:].astype(f32)
        pieces = [
            pltpu.roll(packed, LANES - place * block_heads, 1) if place else packed
            for place in range(6)
        ]
        peaks.append(pieces[0] + pieces[1] + pieces[2])
        sums.append(pieces[3] + pieces[4] + pieces[5])
    lane = lax.broadcasted_iota(jnp.int32, peaks[0].shape, 1)
    real = lane < block_heads
    highest = functools.reduce(jnp.maximum, peaks)
    factors = [jnp.where(real, jnp.exp(jnp.where(real, peak - highest, 0.0)), 0.0) for peak in peaks]
    total = sum(factor * amount for factor, amount in zip(factors, sums))
    total = jnp.where(real, total, 1.0)
    factors = [factor / total for factor in factors]
    for j in range(block_heads):
        span = slice(j * HD, (j + 1) * HD)
        value = sum(
            ref[:, span].astype(f32) * factor[:, j : j + 1] for ref, factor in zip(blocks, factors)
        )
        out[:, span] = value.astype(bf16)


def project_kernel(row_count, pre_count, where, *rest):
    blocks, weight = rest[:row_count], rest[row_count]
    outs = rest[row_count + 1 : row_count + 1 + pre_count]
    stacked, product = rest[row_count + 1 + pre_count :]
    tokens = blocks[0].shape[0]
    amount = outs[0].shape[0]
    pre_at, row_at = where[0], where[1]
    for s, ref in enumerate(blocks):
        start = pl.multiple_of(wrapped(row_at - s, row_count) * tokens, tokens)
        stacked[pl.ds(start, tokens), :] = ref[...].astype(f32)
    product[...] = dot(stacked[...].astype(bf16), weight[...])
    for s, out in enumerate(outs):
        start = pl.multiple_of(wrapped(pre_at + s, pre_count) * amount, amount)
        out[...] = product[pl.ds(start, amount), :].astype(out.dtype)


def residual_kernel(parts, hidden, *rest):
    blocks, (out, sent) = rest[:parts], rest[parts:]
    amount, width = sent.shape
    value = sum(ref[...].astype(f32) for ref in blocks)
    value = hidden[...].reshape(amount, width).astype(f32) + value
    sent[...] = value.astype(bf16)
    out[...] = value.astype(bf16).reshape(out.shape)


def feed_kernel(pre_count, row_count, where, gain, *rest):
    blocks, weight = rest[:pre_count], rest[pre_count]
    outs = rest[pre_count + 1 : pre_count + 1 + row_count]
    stacked, spread, product = rest[pre_count + 1 + row_count :]
    amount, depth = blocks[0].shape
    rows = pre_count * amount
    tokens = rows // row_count
    wide = weight.shape[2]
    pre_at, row_at = where[0], where[1]
    for s, ref in enumerate(blocks):
        start = pl.multiple_of(wrapped(pre_at - s, pre_count) * amount, amount)
        stacked[pl.ds(start, amount), :] = ref[...].astype(f32)
    value = stacked[...]
    squares = jnp.sum(value * value, axis=1, keepdims=True)
    normed = (value * gain[...].astype(f32)).astype(bf16)
    source = lax.broadcasted_iota(jnp.int32, (HD, 2 * HD), 0)
    target = lax.broadcasted_iota(jnp.int32, (HD, 2 * HD), 1)
    for b in range(depth // HD):
        piece = normed[:, b * HD : (b + 1) * HD]
        for half in range(2):
            selector = (target == 2 * source + half).astype(bf16)
            spread[half * rows : (half + 1) * rows, 2 * b * HD : 2 * (b + 1) * HD] = dot(
                piece, selector
            ).astype(bf16)
    left = spread[...]
    flat = weight.reshape(2 * depth, wide)
    tile = next(size for size in (512, 448, 256, 128) if wide % size == 0)
    for j in range(wide // tile):
        product[:, j * tile : (j + 1) * tile] = dot(left, flat[:, j * tile : (j + 1) * tile])
    lane = lax.broadcasted_iota(jnp.int32, (rows, LANES), 1)
    pieces = three_parts(squares)
    packed = sum(jnp.where(lane == place, piece, 0.0) for place, piece in enumerate(pieces))
    product[0:rows, wide:] = packed
    for s, out in enumerate(outs):
        start = pl.multiple_of(wrapped(row_at + s, row_count) * tokens, tokens)
        out[:, :wide] = product[pl.ds(start, tokens), :wide].astype(out.dtype)
        out[:, wide : 2 * wide] = product[pl.ds(rows + start, tokens), :wide].astype(out.dtype)
        out[:, 2 * wide :] = product[pl.ds(start, tokens), wide:].astype(out.dtype)


def scale_kernel(ids, table, out):
    tokens = out.shape[0]
    adapters = table.shape[0]
    row_of = lax.broadcasted_iota(jnp.int32, (tokens, adapters), 0) // STEPS
    column = lax.broadcasted_iota(jnp.int32, (tokens, adapters), 1)
    chosen = pick(row_of, [ids[r] for r in range(tokens // STEPS)])
    out[...] = dot((chosen == column).astype(bf16), table[...])


def activate_kernel(parts, scales, *rest):
    blocks, out = rest[:parts], rest[parts]
    tokens, wide = scales.shape
    squares = sum(ref[:, 2 * wide :].astype(f32) for ref in blocks)
    squares = jnp.sum(squares, axis=1, keepdims=True)
    inverse = lax.rsqrt(squares / D + 1e-05)
    gate = sum(ref[:, :wide].astype(f32) for ref in blocks) * inverse
    up = sum(ref[:, wide : 2 * wide].astype(f32) for ref in blocks) * inverse
    value = gate / (1.0 + jnp.exp(-gate)) * up * scales[...]
    out[...] = value.astype(bf16).reshape(out.shape)


def shifted(parts, axis):
    count = lax.axis_size(axis)
    return [parts[0]] + [
        lax.ppermute(parts[s], axis, [(i, (i + s) % count) for i in range(count)])
        for s in range(1, count)
    ]


def shape_of(dims, dtype=bf16):
    return jax.ShapeDtypeStruct(dims, dtype)


def params(mib):
    return pltpu.CompilerParams(vmem_limit_bytes=mib << 20)


def per_device(
    queries,
    prefix_keys,
    prefix_values,
    suffix_keys,
    suffix_values,
    new_keys,
    new_values,
    hidden,
    adapter_ids,
    suffix_lengths,
    kv_scales,
    ffn_scales,
    out_weight,
    norm_gain,
    gate_up,
):
    rows = queries.shape[0]
    tokens = rows * STEPS
    kv_width = prefix_keys.shape[1]
    pre_count = lax.axis_size("pre")
    row_count = lax.axis_size("row")
    where = jnp.stack([lax.axis_index("pre"), lax.axis_index("row")]).astype(jnp.int32)
    block = HEADS * HD // pre_count
    amount = hidden.shape[0] * STEPS
    out_cols = out_weight.shape[1]
    depth, _, wide = gate_up.shape

    ffn_rows = pl.pallas_call(
        scale_kernel,
        in_specs=[SMEM, VMEM],
        out_specs=VMEM,
        out_shape=shape_of((tokens, wide), f32),
        compiler_params=params(4),
    )(adapter_ids, ffn_scales)

    partials = pl.pallas_call(
        functools.partial(attend_kernel, pre_count),
        in_specs=[SMEM] * 3 + [VMEM] * 7 + [ANY],
        out_specs=[VMEM] * pre_count,
        out_shape=[shape_of((tokens, block + LANES))] * pre_count,
        scratch_shapes=[
            pltpu.VMEM((rows, 2, kv_width), bf16),
            pltpu.VMEM((pre_count, tokens, block + LANES), bf16),
            pltpu.SemaphoreType.DMA((rows,)),
        ],
        compiler_params=params(8),
    )(
        adapter_ids,
        suffix_lengths,
        where,
        queries,
        prefix_keys,
        prefix_values,
        suffix_keys,
        suffix_values,
        new_keys,
        new_values,
        kv_scales,
    )
    mixed = pl.pallas_call(
        functools.partial(merge_kernel, pre_count),
        in_specs=[VMEM] * pre_count,
        out_specs=VMEM,
        out_shape=shape_of((tokens, block)),
        compiler_params=params(4),
    )(*shifted(partials, "pre"))
    gathered = shifted([mixed] * row_count, "row")
    products = pl.pallas_call(
        functools.partial(project_kernel, row_count, pre_count),
        in_specs=[SMEM] + [VMEM] * (row_count + 1),
        out_specs=[VMEM] * pre_count,
        out_shape=[
            shape_of((amount, out_cols), bf16 if s else f32) for s in range(pre_count)
        ],
        scratch_shapes=[
            pltpu.VMEM((row_count * tokens, block), f32),
            pltpu.VMEM((row_count * tokens, out_cols), f32),
        ],
        compiler_params=params(12),
    )(where, *gathered, out_weight)
    residual, sent = pl.pallas_call(
        functools.partial(residual_kernel, pre_count),
        in_specs=[VMEM] * (pre_count + 1),
        out_specs=[VMEM] * 2,
        out_shape=[shape_of(hidden.shape), shape_of((amount, out_cols))],
        compiler_params=params(4),
    )(hidden, *shifted(products, "pre"))
    stacked = shifted([sent] * pre_count, "pre")
    total_rows = pre_count * amount
    fed = pl.pallas_call(
        functools.partial(feed_kernel, pre_count, row_count),
        in_specs=[SMEM] + [VMEM] * (pre_count + 2),
        out_specs=[VMEM] * row_count,
        out_shape=[
            shape_of((tokens, 2 * wide + LANES), bf16 if s else f32) for s in range(row_count)
        ],
        scratch_shapes=[
            pltpu.VMEM((total_rows, depth), f32),
            pltpu.VMEM((2 * total_rows, 2 * depth), bf16),
            pltpu.VMEM((2 * total_rows, wide + LANES), f32),
        ],
        compiler_params=params(40),
    )(where, norm_gain.reshape(1, depth), *stacked, gate_up)
    activation = pl.pallas_call(
        functools.partial(activate_kernel, row_count),
        in_specs=[VMEM] * (row_count + 1),
        out_specs=VMEM,
        out_shape=shape_of((rows, STEPS, wide)),
        compiler_params=params(4),
    )(ffn_rows, *shifted(fed, "row"))
    return (residual, activation)


def solution(mesh):
    placed = (
        P(("grp", "row"), None, None),
        P(("grp", "pre"), None),
        P(("grp", "pre"), None),
        P(("grp", "row"), "pre", None),
        P(("grp", "row"), "pre", None),
        P(("grp", "row"), None, None),
        P(("grp", "row"), None, None),
        P(("grp", "pre"), None, "row"),
        P(("grp", "row")),
        P(("grp", "row")),
        P(),
        P(None, "pre"),
        P("pre", "row"),
        P("row"),
        P("row", None, "pre"),
    )
    return jax.shard_map(
        per_device,
        mesh=mesh,
        in_specs=placed,
        out_specs=(P(("grp", "pre"), None, "row"), P(("grp", "row"), None, "pre")),
        check_vma=False,
    )
```

time: 207 us -> 74.1 us (0.36)
  local copies, waits for them, and re-layouts: 71.5 us -> 13.3 us
  blocking collectives: 54.4 us -> 0 us
  matrix products: 24 us -> 0 us
  Pallas kernels: 0 us -> 22.9 us
  starting transfers between devices: 0.12 us -> 19.9 us
  waiting for transfers between devices: 32 us -> 16.2 us
  between operations: 15.4 us -> 0.72 us
  other arithmetic: 7.79 us -> 0.08 us
    reshape x5 -> x1, local copies, waits for them, and re-layouts: 63.2 us -> 0.69 us  [per_device(): norm_gain.reshape(1, depth)]
    all_gather x4 -> x0, blocking collectives: 48.8 us -> none  [the longest x2 30 us: joined(): everything = jax.tree.map(lambda part: lax.all_gather(part, axis), value)]
    unnamed x5 -> x0, waiting for transfers between devices: 29.3 us -> none
    dot_general x10 -> x0, matrix products: 24 us -> none  [the longest x1 13 us: layer(): jnp.dot(normed.reshape(rows_all * step_count, feature_local), gate_up.res...]
    pallas_call x0 -> x7, Pallas kernels: none -> 22.9 us  [the longest x1 15.5 us: per_device(): pl.pallas_call(functools.partial(feed_kernel, pre_count, row_count), in_s...]
    ppermute x0 -> x15, starting transfers between devices: none -> 19.9 us  [shifted(): lax.ppermute(parts[s], axis, [(i, (i + s) % count) for i in range(count)])]
    ppermute x0 -> x15, waiting for transfers between devices: none -> 16.2 us  [shifted(): lax.ppermute(parts[s], axis, [(i, (i + s) % count) for i in range(count)])]
    unnamed x1 -> x0, blocking collectives: 5.65 us -> none
  transfers between devices with their start and end apart: 3 -> 15, of which waited for: 2 -> 13; matrix products, arithmetic and copies ran while one was open for 31% -> 1% of each run, Pallas kernels for 0% -> 1%
where the time goes in v1:
time: 74.1 us; the launch traced here: 73 us
  Pallas kernels  22.9 us (31%)
  starting transfers between devices  19.9 us (27%)
  waiting for transfers between devices  16.2 us (22%)
  local copies, waits for them, and re-layouts  13.3 us (18%)
    ppermute x15, starting transfers between devices, shifted(): lax.ppermute(parts[s], axis, [(i, (i + s) % count) for i in range(count)])  19.9 us
    ppermute x15, waiting for transfers between devices, shifted(): lax.ppermute(parts[s], axis, [(i, (i + s) % count) for i in range(count)])  16.2 us
    pallas_call x1, Pallas kernels, per_device(): pl.pallas_call(functools.partial(feed_kernel, pre_count, row_count), in_s...  15.5 us
    unnamed x28, local copies, waits for them, and re-layouts  12.6 us
    pallas_call x1, Pallas kernels, per_device(): pl.pallas_call(functools.partial(attend_kernel, pre_count), in_specs=[SME...  2.84 us
    pallas_call x1, Pallas kernels, per_device(): pl.pallas_call(functools.partial(project_kernel, row_count, pre_count), i...  2.1 us
  transfers between devices with their start and end apart: 15, of which 13 were waited for; matrix products, arithmetic and copies ran while one was open for 1% of the time, Pallas kernels for 1%

profile of v1, /device:TPU:0, one launch (start us, length us, event | category | flops | bytes accessed | tf_op | source)
XLA Modules:
  0.0 73.0 jit_solution(18187768931576680047)
XLA Ops:
  0.6 0.1 pad_add_fusion.where
  0.7 1.1 %copy-done.2 = bf16[128,2,1024]{2,1,0:T(2,128)(2,1)S(1)} copy-done((bf16[128,2,1024]{2,1,0:T(2,128)(2,1)S(1)}, bf16[128,2,1024]{2,1,0:T(2,128)(2,1)}, u32[]{:S(2)}) %copy-start.2) | copy-done | bytes 524312
  1.8 0.9 %copy-done.3 = bf16[128,1024]{1,0:T(8,128)(2,1)S(1)} copy-done((bf16[128,1024]{1,0:T(8,128)(2,1)S(1)}, bf16[128,1024]{1,0:T(8,128)(2,1)}, u32[]{:S(2)}) %copy-start.3) | copy-done | bytes 262168
  2.8 0.9 %copy-done.4 = bf16[128,1024]{1,0:T(8,128)(2,1)S(1)} copy-done((bf16[128,1024]{1,0:T(8,128)(2,1)S(1)}, bf16[128,1024]{1,0:T(8,128)(2,1)}, u32[]{:S(2)}) %copy-start.4) | copy-done | bytes 262168
  3.7 0.9 %copy-done.5 = bf16[4,2,8192]{2,1,0:T(2,128)(2,1)S(1)} copy-done((bf16[4,2,8192]{2,1,0:T(2,128)(2,1)S(1)}, bf16[4,2,8192]{2,1,0:T(2,128)(2,1)}, u32[]{:S(2)}) %copy-start.5) | copy-done | bytes 131096
  4.6 0.9 %copy-done.6 = bf16[4,16,1024]{2,1,0:T(8,128)(2,1)S(1)} copy-done((bf16[4,16,1024]{2,1,0:T(8,128)(2,1)S(1)}, bf16[4,16,1024]{2,1,0:T(8,128)(2,1)}, u32[]{:S(2)}) %copy-start.6) | copy-done | bytes 131096
  5.5 0.9 %copy-done.7 = bf16[4,16,1024]{2,1,0:T(8,128)(2,1)S(1)} copy-done((bf16[4,16,1024]{2,1,0:T(8,128)(2,1)S(1)}, bf16[4,16,1024]{2,1,0:T(8,128)(2,1)}, u32[]{:S(2)}) %copy-start.7) | copy-done | bytes 131096
  6.4 0.7 copy-done.9
  7.2 0.7 copy-done.10
  7.9 0.7 copy-done.11
  8.5 0.7 copy-done.13
  9.2 2.8 %shard_map.158 = (bf16[8,2176]{1,0:T(8,128)(2,1)S(1)}, bf16[8,2176]{1,0:T(8,128)(2,1)S(1)}, bf16[8,2176]{1,0:T(8,128)(2,1)S(1)}, bf16[8,2176]{1,0:T(8,128)(2,1)S(1)}) custom-call(s32[4]{0:T(128)S(1)} %copy-done.11, s32[4]{0:T(128)S(1)} %copy-done.13, s32[2]{0:T(128)S(1)} %pad_add_fusion.where, bf16[4,2,8192]{2,1,0:T(2,128)(2,1)S(1)} %copy-done.5, ...), custom_call_target="tpu_custom_call" | custom-call | tf_op jit(solution)/shard_map/pallas_call | solution.py:327
  12.0 3.1 %collective-permute-start = (bf16[8,2176]{1,0:T(8,128)(2,1)S(1)}, bf16[8,2176]{1,0:T(8,128)(2,1)S(1)}, u32[]{:S(2)}, u32[]{:S(2)}) collective-permute-start(bf16[8,2176]{1,0:T(8,128)(2,1)S(1)} %get-tuple-element.17), channel_id=1, source_target_pairs={{0,4},{4,8},{8,12},{12,0},{1,5},{5,9},{9,13},{13,1},{2,6},{6,10},{... | collective-permute-start | bytes 104456 | tf_op jit(solution)/shard_map/ppermute | solution.py:278
  15.1 2.6 %collective-permute-start.1 = (bf16[8,2176]{1,0:T(8,128)(2,1)S(1)}, bf16[8,2176]{1,0:T(8,128)(2,1)S(1)}, u32[]{:S(2)}, u32[]{:S(2)}) collective-permute-start(bf16[8,2176]{1,0:T(8,128)(2,1)S(1)} %get-tuple-element.18), channel_id=1, source_target_pairs={{0,8},{4,12},{8,0},{12,4},{1,9},{5,13},{9,1},{13,5},{2,10},{6,14},... | collective-permute-start | bytes 104456 | tf_op jit(solution)/shard_map/ppermute | solution.py:278
  17.7 1.3 %collective-permute-start.2 = (bf16[8,2176]{1,0:T(8,128)(2,1)S(1)}, bf16[8,2176]{1,0:T(8,128)(2,1)S(1)}, u32[]{:S(2)}, u32[]{:S(2)}) collective-permute-start(bf16[8,2176]{1,0:T(8,128)(2,1)S(1)} %get-tuple-element.19), channel_id=1, source_target_pairs={{0,12},{4,0},{8,4},{12,8},{1,13},{5,1},{9,5},{13,9},{2,14},{6,2},{... | collective-permute-start | bytes 104456 | tf_op jit(solution)/shard_map/ppermute | solution.py:278
  19.1 1.3 %collective-permute-done.1.rest_2_ = bf16[8,2176]{1,0:T(8,128)(2,1)S(1)} collective-permute-done((bf16[8,2176]{1,0:T(8,128)(2,1)S(1)}, bf16[8,2176]{1,0:T(8,128)(2,1)S(1)}, u32[]{:S(2)}, u32[]{:S(2)}) %collective-permute-start.1) | collective-permute-done | bytes 34848 | tf_op jit(solution)/shard_map/ppermute | solution.py:278
  20.3 1.3 %collective-permute-done.2.rest_3_ = bf16[8,2176]{1,0:T(8,128)(2,1)S(1)} collective-permute-done((bf16[8,2176]{1,0:T(8,128)(2,1)S(1)}, bf16[8,2176]{1,0:T(8,128)(2,1)S(1)}, u32[]{:S(2)}, u32[]{:S(2)}) %collective-permute-start.2) | collective-permute-done | bytes 34848 | tf_op jit(solution)/shard_map/ppermute | solution.py:278
  21.6 0.3 shard_map.159.rest_0_
  21.9 0.1 collective-permute-start.3
  22.0 1.6 %collective-permute-start.4 = (bf16[8,2048]{1,0:T(8,128)(2,1)S(1)}, bf16[8,2048]{1,0:T(8,128)(2,1)S(1)}, u32[]{:S(2)}, u32[]{:S(2)}) collective-permute-start(bf16[8,2048]{1,0:T(8,128)(2,1)S(1)} %shard_map.159.rest_0_), channel_id=1, source_target_pairs={{0,2},{1,3},{2,0},{3,1},{4,6},{5,7},{6,4},{7,5},{8,10},{9,11},{10,... | collective-permute-start | bytes 98312 | tf_op jit(solution)/shard_map/ppermute | solution.py:278
  23.5 1.4 %collective-permute-start.5 = (bf16[8,2048]{1,0:T(8,128)(2,1)S(1)}, bf16[8,2048]{1,0:T(8,128)(2,1)S(1)}, u32[]{:S(2)}, u32[]{:S(2)}) collective-permute-start(bf16[8,2048]{1,0:T(8,128)(2,1)S(1)} %shard_map.159.rest_0_), channel_id=1, source_target_pairs={{0,3},{1,0},{2,1},{3,2},{4,7},{5,4},{6,5},{7,6},{8,11},{9,8},{10,9... | collective-permute-start | bytes 98312 | tf_op jit(solution)/shard_map/ppermute | solution.py:278
  24.9 0.4 collective-permute-done.3.rest_1_
  25.3 0.7 collective-permute-done.4.rest_2_
  26.0 0.6 collective-permute-done.5.rest_3_
  26.5 3.4 %copy-done = bf16[2048,2048]{1,0:T(8,128)(2,1)S(1)} copy-done((bf16[2048,2048]{1,0:T(8,128)(2,1)S(1)}, bf16[2048,2048]{1,0:T(8,128)(2,1)}, u32[]{:S(2)}) %copy-start) | copy-done | bytes 8388632
  29.9 2.1 %shard_map.160 = (f32[8,2048]{1,0:T(8,128)S(1)}, bf16[8,2048]{1,0:T(8,128)(2,1)S(1)}, bf16[8,2048]{1,0:T(8,128)(2,1)S(1)}, bf16[8,2048]{1,0:T(8,128)(2,1)S(1)}) custom-call(s32[2]{0:T(128)S(1)} %pad_add_fusion.where, bf16[8,2048]{1,0:T(8,128)(2,1)S(1)} %shard_map.159.rest_0_, bf16[8,2048]{1,0:T(8,128)(2,1)S(1)} %collective-permute-done.3.rest_1_, ...), custom_call_target="tpu_custom_call" | custom-call | tf_op jit(solution)/shard_map/pallas_call | solution.py:359
  32.0 0.3 collective-permute-start.6
  32.3 3.5 %collective-permute-start.7 = (bf16[8,2048]{1,0:T(8,128)(2,1)S(1)}, bf16[8,2048]{1,0:T(8,128)(2,1)S(1)}, u32[]{:S(2)}, u32[]{:S(2)}) collective-permute-start(bf16[8,2048]{1,0:T(8,128)(2,1)S(1)} %get-tuple-element.22), channel_id=1, source_target_pairs={{0,8},{4,12},{8,0},{12,4},{1,9},{5,13},{9,1},{13,5},{2,10},{6,14},... | collective-permute-start | bytes 98312 | tf_op jit(solution)/shard_map/ppermute | solution.py:278
  35.8 0.1 collective-permute-start.8
  35.9 2.3 %collective-permute-done.6.rest_1_ = bf16[8,2048]{1,0:T(8,128)(2,1)S(1)} collective-permute-done((bf16[8,2048]{1,0:T(8,128)(2,1)S(1)}, bf16[8,2048]{1,0:T(8,128)(2,1)S(1)}, u32[]{:S(2)}, u32[]{:S(2)}) %collective-permute-start.6) | collective-permute-done | bytes 32800 | tf_op jit(solution)/shard_map/ppermute | solution.py:278
  38.2 1.1 %collective-permute-done.7.rest_2_ = bf16[8,2048]{1,0:T(8,128)(2,1)S(1)} collective-permute-done((bf16[8,2048]{1,0:T(8,128)(2,1)S(1)}, bf16[8,2048]{1,0:T(8,128)(2,1)S(1)}, u32[]{:S(2)}, u32[]{:S(2)}) %collective-permute-start.7) | collective-permute-done | bytes 32800 | tf_op jit(solution)/shard_map/ppermute | solution.py:278
  39.3 0.4 collective-permute-done.8.rest_3_
  39.7 0.8 %copy-done.8 = bf16[4,2,2048]{2,1,0:T(2,128)(2,1)S(1)} copy-done((bf16[4,2,2048]{2,1,0:T(2,128)(2,1)S(1)}, bf16[4,2,2048]{2,1,0:T(2,128)(2,1)}, u32[]{:S(2)}) %copy-start.8) | copy-done | bytes 32792
  40.5 0.7 shard_map.161
  41.1 1.1 %collective-permute-start.10 = (bf16[8,2048]{1,0:T(8,128)(2,1)S(1)}, bf16[8,2048]{1,0:T(8,128)(2,1)S(1)}, u32[]{:S(2)}, u32[]{:S(2)}) collective-permute-start(bf16[8,2048]{1,0:T(8,128)(2,1)S(1)} %get-tuple-element.25.rest_0_), channel_id=1, source_target_pairs={{0,8},{4,12},{8,0},{12,4},{1,9},{5,13},{9,1},{13,5},{2,10},{6,14},... | collective-permute-start | bytes 98312 | tf_op jit(solution)/shard_map/ppermute | solution.py:278
  42.2 1.9 %collective-permute-start.11 = (bf16[8,2048]{1,0:T(8,128)(2,1)S(1)}, bf16[8,2048]{1,0:T(8,128)(2,1)S(1)}, u32[]{:S(2)}, u32[]{:S(2)}) collective-permute-start(bf16[8,2048]{1,0:T(8,128)(2,1)S(1)} %get-tuple-element.25.rest_0_), channel_id=1, source_target_pairs={{0,12},{4,0},{8,4},{12,8},{1,13},{5,1},{9,5},{13,9},{2,14},{6,2},{... | collective-permute-start | bytes 98312 | tf_op jit(solution)/shard_map/ppermute | solution.py:278
  44.2 0.1 collective-permute-start.9
  44.2 0.7 reshape.7.gain
  44.9 1.4 %collective-permute-done.10.rest_2_ = bf16[8,2048]{1,0:T(8,128)(2,1)S(1)} collective-permute-done((bf16[8,2048]{1,0:T(8,128)(2,1)S(1)}, bf16[8,2048]{1,0:T(8,128)(2,1)S(1)}, u32[]{:S(2)}, u32[]{:S(2)}) %collective-permute-start.10) | collective-permute-done | bytes 32800 | tf_op jit(solution)/shard_map/ppermute | solution.py:278
  46.3 3.5 %collective-permute-done.9.rest_1_ = bf16[8,2048]{1,0:T(8,128)(2,1)S(1)} collective-permute-done((bf16[8,2048]{1,0:T(8,128)(2,1)S(1)}, bf16[8,2048]{1,0:T(8,128)(2,1)S(1)}, u32[]{:S(2)}, u32[]{:S(2)}) %collective-permute-start.9) | collective-permute-done | bytes 32800 | tf_op jit(solution)/shard_map/ppermute | solution.py:278
  49.9 15.5 %shard_map.163 = (f32[8,7296]{1,0:T(8,128)S(1)}, bf16[8,7296]{1,0:T(8,128)(2,1)S(1)}, bf16[8,7296]{1,0:T(8,128)(2,1)S(1)}, bf16[8,7296]{1,0:T(8,128)(2,1)S(1)}) custom-call(s32[2]{0:T(128)S(1)} %pad_add_fusion.where, bf16[1,2048]{1,0:T(2,128)(2,1)S(1)} %reshape.7.gain, bf16[8,2048]{1,0:T(8,128)(2,1)S(1)} %get-tuple-element.25.rest_0_, ...), custom_call_target="tpu_custom_call" | custom-call | tf_op jit(solution)/shard_map/pallas_call | solution.py:381
  65.4 1.4 %collective-permute-start.13 = (bf16[8,7296]{1,0:T(8,128)(2,1)S(1)}, bf16[8,7296]{1,0:T(8,128)(2,1)S(1)}, u32[]{:S(2)}, u32[]{:S(2)}) collective-permute-start(bf16[8,7296]{1,0:T(8,128)(2,1)S(1)} %get-tuple-element.28), channel_id=1, source_target_pairs={{0,2},{1,3},{2,0},{3,1},{4,6},{5,7},{6,4},{7,5},{8,10},{9,11},{10,... | collective-permute-start | bytes 350216 | tf_op jit(solution)/shard_map/ppermute | solution.py:278
  66.8 1.4 %collective-permute-start.14 = (bf16[8,7296]{1,0:T(8,128)(2,1)S(1)}, bf16[8,7296]{1,0:T(8,128)(2,1)S(1)}, u32[]{:S(2)}, u32[]{:S(2)}) collective-permute-start(bf16[8,7296]{1,0:T(8,128)(2,1)S(1)} %get-tuple-element.29), channel_id=1, source_target_pairs={{0,3},{1,0},{2,1},{3,2},{4,7},{5,4},{6,5},{7,6},{8,11},{9,8},{10,9... | collective-permute-start | bytes 350216 | tf_op jit(solution)/shard_map/ppermute | solution.py:278
  68.2 0.8 %shard_map.162.scales = f32[8,3584]{1,0:T(8,128)S(1)} custom-call(s32[4]{0:T(128)S(1)} %copy-done.12, bf16[128,3584]{1,0:T(8,128)(2,1)S(1)} %copy-done.1), custom_call_target="tpu_custom_call" | custom-call | tf_op jit(solution)/shard_map/pallas_call | solution.py:319
  68.9 1.4 %collective-permute-done.12.rest_1_ = bf16[8,7296]{1,0:T(8,128)(2,1)S(1)} collective-permute-done((bf16[8,7296]{1,0:T(8,128)(2,1)S(1)}, bf16[8,7296]{1,0:T(8,128)(2,1)S(1)}, u32[]{:S(2)}, u32[]{:S(2)}) %collective-permute-start.12) | collective-permute-done | bytes 116768 | tf_op jit(solution)/shard_map/ppermute | solution.py:278
  70.3 1.2 %collective-permute-done.13.rest_2_ = bf16[8,7296]{1,0:T(8,128)(2,1)S(1)} collective-permute-done((bf16[8,7296]{1,0:T(8,128)(2,1)S(1)}, bf16[8,7296]{1,0:T(8,128)(2,1)S(1)}, u32[]{:S(2)}, u32[]{:S(2)}) %collective-permute-start.13) | collective-permute-done | bytes 116768 | tf_op jit(solution)/shard_map/ppermute | solution.py:278
  71.5 0.7 collective-permute-done.14.rest_3_
  72.2 0.8 %shard_map.164 = bf16[4,2,3584]{2,1,0:T(2,128)(2,1)} custom-call(f32[8,3584]{1,0:T(8,128)S(1)} %shard_map.162.scales, f32[8,7296]{1,0:T(8,128)S(1)} %get-tuple-element.26.rest_0_, bf16[8,7296]{1,0:T(8,128)(2,1)S(1)} %collective-permute-done.12.rest_1_, bf16[8,7296]{1,0:T(8,128)(2,1)S(1)} %collective-permute-done.13.rest_2_, ...), custom_call_target="tpu_custom_call" | custom-call | tf_op jit(solution)/shard_map/pallas_call | solution.py:395
  (19 shorter events, 0.1 us)
Async XLA Ops:
  0.6 67.5 %copy-start.1 = (bf16[128,3584]{1,0:T(8,128)(2,1)S(1)}, bf16[128,3584]{1,0:T(8,128)(2,1)}, u32[]{:S(2)}) copy-start(bf16[128,3584]{1,0:T(8,128)(2,1)} %table.1) | copy-start | bytes 2752516
  0.7 1.1 %copy-start.2 = (bf16[128,2,1024]{2,1,0:T(2,128)(2,1)S(1)}, bf16[128,2,1024]{2,1,0:T(2,128)(2,1)}, u32[]{:S(2)}) copy-start(bf16[128,2,1024]{2,1,0:T(2,128)(2,1)} %kv_scales.1) | copy-start | bytes 1572868
  1.8 0.9 %copy-start.3 = (bf16[128,1024]{1,0:T(8,128)(2,1)S(1)}, bf16[128,1024]{1,0:T(8,128)(2,1)}, u32[]{:S(2)}) copy-start(bf16[128,1024]{1,0:T(8,128)(2,1)} %prefix_keys.1) | copy-start | bytes 786436
  2.8 0.9 %copy-start.4 = (bf16[128,1024]{1,0:T(8,128)(2,1)S(1)}, bf16[128,1024]{1,0:T(8,128)(2,1)}, u32[]{:S(2)}) copy-start(bf16[128,1024]{1,0:T(8,128)(2,1)} %prefix_values.1) | copy-start | bytes 786436
  3.7 0.9 %copy-start.5 = (bf16[4,2,8192]{2,1,0:T(2,128)(2,1)S(1)}, bf16[4,2,8192]{2,1,0:T(2,128)(2,1)}, u32[]{:S(2)}) copy-start(bf16[4,2,8192]{2,1,0:T(2,128)(2,1)} %queries.1) | copy-start | bytes 393220
  4.6 0.9 %copy-start.6 = (bf16[4,16,1024]{2,1,0:T(8,128)(2,1)S(1)}, bf16[4,16,1024]{2,1,0:T(8,128)(2,1)}, u32[]{:S(2)}) copy-start(bf16[4,16,1024]{2,1,0:T(8,128)(2,1)} %suffix_keys.1) | copy-start | bytes 393220
  5.5 0.9 %copy-start.7 = (bf16[4,16,1024]{2,1,0:T(8,128)(2,1)S(1)}, bf16[4,16,1024]{2,1,0:T(8,128)(2,1)}, u32[]{:S(2)}) copy-start(bf16[4,16,1024]{2,1,0:T(8,128)(2,1)} %suffix_values.1) | copy-start | bytes 393220
  6.4 0.7 copy-start.9
  7.2 0.7 copy-start.10
  7.9 0.7 copy-start.11
  8.5 0.7 copy-start.13
  9.2 59.0 %copy-start.12 = (s32[4]{0:T(128)S(1)}, s32[4]{0:T(128)}, u32[]{:S(2)}) copy-start(s32[4]{0:T(128)} %ids.3) | copy-start | bytes 52
  12.0 7.0 %collective-permute-start = (bf16[8,2176]{1,0:T(8,128)(2,1)S(1)}, bf16[8,2176]{1,0:T(8,128)(2,1)S(1)}, u32[]{:S(2)}, u32[]{:S(2)}) collective-permute-start(bf16[8,2176]{1,0:T(8,128)(2,1)S(1)} %get-tuple-element.17), channel_id=1, source_target_pairs={{0,4},{4,8},{8,12},{12,0},{1,5},{5,9},{9,13},{13,1},{2,6},{6,10},{... | collective-permute-start | bytes 104456 | tf_op jit(solution)/shard_map/ppermute | solution.py:278
  15.1 5.2 %collective-permute-start.1 = (bf16[8,2176]{1,0:T(8,128)(2,1)S(1)}, bf16[8,2176]{1,0:T(8,128)(2,1)S(1)}, u32[]{:S(2)}, u32[]{:S(2)}) collective-permute-start(bf16[8,2176]{1,0:T(8,128)(2,1)S(1)} %get-tuple-element.18), channel_id=1, source_target_pairs={{0,8},{4,12},{8,0},{12,4},{1,9},{5,13},{9,1},{13,5},{2,10},{6,14},... | collective-permute-start | bytes 104456 | tf_op jit(solution)/shard_map/ppermute | solution.py:278
  17.7 3.9 %collective-permute-start.2 = (bf16[8,2176]{1,0:T(8,128)(2,1)S(1)}, bf16[8,2176]{1,0:T(8,128)(2,1)S(1)}, u32[]{:S(2)}, u32[]{:S(2)}) collective-permute-start(bf16[8,2176]{1,0:T(8,128)(2,1)S(1)} %get-tuple-element.19), channel_id=1, source_target_pairs={{0,12},{4,0},{8,4},{12,8},{1,13},{5,1},{9,5},{13,9},{2,14},{6,2},{... | collective-permute-start | bytes 104456 | tf_op jit(solution)/shard_map/ppermute | solution.py:278
  21.9 3.4 %collective-permute-start.3 = (bf16[8,2048]{1,0:T(8,128)(2,1)S(1)}, bf16[8,2048]{1,0:T(8,128)(2,1)S(1)}, u32[]{:S(2)}, u32[]{:S(2)}) collective-permute-start(bf16[8,2048]{1,0:T(8,128)(2,1)S(1)} %shard_map.159.rest_0_), channel_id=1, source_target_pairs={{0,1},{1,2},{2,3},{3,0},{4,5},{5,6},{6,7},{7,4},{8,9},{9,10},{10,1... | collective-permute-start | bytes 98312 | tf_op jit(solution)/shard_map/ppermute | solution.py:278
  22.0 4.0 %collective-permute-start.4 = (bf16[8,2048]{1,0:T(8,128)(2,1)S(1)}, bf16[8,2048]{1,0:T(8,128)(2,1)S(1)}, u32[]{:S(2)}, u32[]{:S(2)}) collective-permute-start(bf16[8,2048]{1,0:T(8,128)(2,1)S(1)} %shard_map.159.rest_0_), channel_id=1, source_target_pairs={{0,2},{1,3},{2,0},{3,1},{4,6},{5,7},{6,4},{7,5},{8,10},{9,11},{10,... | collective-permute-start | bytes 98312 | tf_op jit(solution)/shard_map/ppermute | solution.py:278
  23.5 3.0 %collective-permute-start.5 = (bf16[8,2048]{1,0:T(8,128)(2,1)S(1)}, bf16[8,2048]{1,0:T(8,128)(2,1)S(1)}, u32[]{:S(2)}, u32[]{:S(2)}) collective-permute-start(bf16[8,2048]{1,0:T(8,128)(2,1)S(1)} %shard_map.159.rest_0_), channel_id=1, source_target_pairs={{0,3},{1,0},{2,1},{3,2},{4,7},{5,4},{6,5},{7,6},{8,11},{9,8},{10,9... | collective-permute-start | bytes 98312 | tf_op jit(solution)/shard_map/ppermute | solution.py:278
  26.5 3.4 %copy-start = (bf16[2048,2048]{1,0:T(8,128)(2,1)S(1)}, bf16[2048,2048]{1,0:T(8,128)(2,1)}, u32[]{:S(2)}) copy-start(bf16[2048,2048]{1,0:T(8,128)(2,1)} %rest_4_.2) | copy-start | bytes 25165828
  32.0 6.2 %collective-permute-start.6 = (bf16[8,2048]{1,0:T(8,128)(2,1)S(1)}, bf16[8,2048]{1,0:T(8,128)(2,1)S(1)}, u32[]{:S(2)}, u32[]{:S(2)}) collective-permute-start(bf16[8,2048]{1,0:T(8,128)(2,1)S(1)} %get-tuple-element.21), channel_id=1, source_target_pairs={{0,4},{4,8},{8,12},{12,0},{1,5},{5,9},{9,13},{13,1},{2,6},{6,10},{... | collective-permute-start | bytes 98312 | tf_op jit(solution)/shard_map/ppermute | solution.py:278
  32.3 7.0 %collective-permute-start.7 = (bf16[8,2048]{1,0:T(8,128)(2,1)S(1)}, bf16[8,2048]{1,0:T(8,128)(2,1)S(1)}, u32[]{:S(2)}, u32[]{:S(2)}) collective-permute-start(bf16[8,2048]{1,0:T(8,128)(2,1)S(1)} %get-tuple-element.22), channel_id=1, source_target_pairs={{0,8},{4,12},{8,0},{12,4},{1,9},{5,13},{9,1},{13,5},{2,10},{6,14},... | collective-permute-start | bytes 98312 | tf_op jit(solution)/shard_map/ppermute | solution.py:278
  35.8 3.9 %collective-permute-start.8 = (bf16[8,2048]{1,0:T(8,128)(2,1)S(1)}, bf16[8,2048]{1,0:T(8,128)(2,1)S(1)}, u32[]{:S(2)}, u32[]{:S(2)}) collective-permute-start(bf16[8,2048]{1,0:T(8,128)(2,1)S(1)} %get-tuple-element.23), channel_id=1, source_target_pairs={{0,12},{4,0},{8,4},{12,8},{1,13},{5,1},{9,5},{13,9},{2,14},{6,2},{... | collective-permute-start | bytes 98312 | tf_op jit(solution)/shard_map/ppermute | solution.py:278
  39.7 0.8 %copy-start.8 = (bf16[4,2,2048]{2,1,0:T(2,128)(2,1)S(1)}, bf16[4,2,2048]{2,1,0:T(2,128)(2,1)}, u32[]{:S(2)}) copy-start(bf16[4,2,2048]{2,1,0:T(2,128)(2,1)} %hidden.1) | copy-start | bytes 98308
  41.1 5.2 %collective-permute-start.10 = (bf16[8,2048]{1,0:T(8,128)(2,1)S(1)}, bf16[8,2048]{1,0:T(8,128)(2,1)S(1)}, u32[]{:S(2)}, u32[]{:S(2)}) collective-permute-start(bf16[8,2048]{1,0:T(8,128)(2,1)S(1)} %get-tuple-element.25.rest_0_), channel_id=1, source_target_pairs={{0,8},{4,12},{8,0},{12,4},{1,9},{5,13},{9,1},{13,5},{2,10},{6,14},... | collective-permute-start | bytes 98312 | tf_op jit(solution)/shard_map/ppermute | solution.py:278
  42.2 4.1 %collective-permute-start.11 = (bf16[8,2048]{1,0:T(8,128)(2,1)S(1)}, bf16[8,2048]{1,0:T(8,128)(2,1)S(1)}, u32[]{:S(2)}, u32[]{:S(2)}) collective-permute-start(bf16[8,2048]{1,0:T(8,128)(2,1)S(1)} %get-tuple-element.25.rest_0_), channel_id=1, source_target_pairs={{0,12},{4,0},{8,4},{12,8},{1,13},{5,1},{9,5},{13,9},{2,14},{6,2},{... | collective-permute-start | bytes 98312 | tf_op jit(solution)/shard_map/ppermute | solution.py:278
  44.2 5.7 %collective-permute-start.9 = (bf16[8,2048]{1,0:T(8,128)(2,1)S(1)}, bf16[8,2048]{1,0:T(8,128)(2,1)S(1)}, u32[]{:S(2)}, u32[]{:S(2)}) collective-permute-start(bf16[8,2048]{1,0:T(8,128)(2,1)S(1)} %get-tuple-element.25.rest_0_), channel_id=1, source_target_pairs={{0,4},{4,8},{8,12},{12,0},{1,5},{5,9},{9,13},{13,1},{2,6},{6,10},{... | collective-permute-start | bytes 98312 | tf_op jit(solution)/shard_map/ppermute | solution.py:278
  65.4 4.9 %collective-permute-start.12 = (bf16[8,7296]{1,0:T(8,128)(2,1)S(1)}, bf16[8,7296]{1,0:T(8,128)(2,1)S(1)}, u32[]{:S(2)}, u32[]{:S(2)}) collective-permute-start(bf16[8,7296]{1,0:T(8,128)(2,1)S(1)} %get-tuple-element.27), channel_id=1, source_target_pairs={{0,1},{1,2},{2,3},{3,0},{4,5},{5,6},{6,7},{7,4},{8,9},{9,10},{10,1... | collective-permute-start | bytes 350216 | tf_op jit(solution)/shard_map/ppermute | solution.py:278
  65.4 6.1 %collective-permute-start.13 = (bf16[8,7296]{1,0:T(8,128)(2,1)S(1)}, bf16[8,7296]{1,0:T(8,128)(2,1)S(1)}, u32[]{:S(2)}, u32[]{:S(2)}) collective-permute-start(bf16[8,7296]{1,0:T(8,128)(2,1)S(1)} %get-tuple-element.28), channel_id=1, source_target_pairs={{0,2},{1,3},{2,0},{3,1},{4,6},{5,7},{6,4},{7,5},{8,10},{9,11},{10,... | collective-permute-start | bytes 350216 | tf_op jit(solution)/shard_map/ppermute | solution.py:278
  66.8 5.4 %collective-permute-start.14 = (bf16[8,7296]{1,0:T(8,128)(2,1)S(1)}, bf16[8,7296]{1,0:T(8,128)(2,1)S(1)}, u32[]{:S(2)}, u32[]{:S(2)}) collective-permute-start(bf16[8,7296]{1,0:T(8,128)(2,1)S(1)} %get-tuple-element.29), channel_id=1, source_target_pairs={{0,3},{1,0},{2,1},{3,2},{4,7},{5,4},{6,5},{7,6},{8,11},{9,8},{10,9... | collective-permute-start | bytes 350216 | tf_op jit(solution)/shard_map/ppermute | solution.py:278

commit v2 on v1

--- a/solution.py
+++ b/solution.py
@@ -19,7 +19,7 @@
 bf16 = jnp.bfloat16
 VMEM = pl.BlockSpec(memory_space=pltpu.VMEM)
 SMEM = pl.BlockSpec(memory_space=pltpu.SMEM)
-ANY = pl.BlockSpec(memory_space=pl.ANY)
+HBM = pl.BlockSpec(memory_space=pltpu.HBM)
 
 
 def wrapped(index, count):
@@ -63,7 +63,24 @@
     kv_scales,
     *rest,
 ):
-    outs, (scales, stage, sem) = rest[:pre_count], rest[pre_count:]
+    outs, (scales, stage, sem) = rest[:pre_count], rest[pre_count : pre_count + 3]
+    held, held_sem = rest[pre_count + 3 : -1], rest[-1]
+    sources = (
+        queries,
+        prefix_keys,
+        suffix_keys,
+        new_keys,
+        new_values,
+        suffix_values,
+        prefix_values,
+    )
+    loads = [
+        pltpu.make_async_copy(source, target, held_sem.at[at])
+        for at, (source, target) in enumerate(zip(sources, held))
+    ]
+    for copy in loads:
+        copy.start()
+    queries, prefix_keys, suffix_keys, new_keys, new_values, suffix_values, prefix_values = held
     rows = queries.shape[0]
     tokens = rows * STEPS
     suffix_local = suffix_keys.shape[1]
@@ -101,6 +118,8 @@
     )
     allowed = in_suffix | in_new
 
+    for copy in loads:
+        copy.wait()
     query = queries[...].reshape(tokens, HEADS * HD).astype(f32)
     fill = jnp.zeros((LANES - suffix_all - tokens, width), f32)
     for copy in copies:
@@ -225,7 +244,7 @@
         stacked[pl.ds(start, amount), :] = ref[...].astype(f32)
     value = stacked[...]
     squares = jnp.sum(value * value, axis=1, keepdims=True)
-    normed = (value * gain[...].astype(f32)).astype(bf16)
+    normed = (value * gain[...].astype(f32).reshape(1, depth)).astype(bf16)
     source = lax.broadcasted_iota(jnp.int32, (HD, 2 * HD), 0)
     target = lax.broadcasted_iota(jnp.int32, (HD, 2 * HD), 1)
     for b in range(depth // HD):
@@ -286,6 +305,10 @@
 
 def params(mib):
     return pltpu.CompilerParams(vmem_limit_bytes=mib << 20)
+
+
+def cost(micros):
+    return pl.CostEstimate(flops=micros * 10**9, bytes_accessed=0, transcendentals=0)
 
 
 def per_device(
@@ -326,15 +349,29 @@
 
     partials = pl.pallas_call(
         functools.partial(attend_kernel, pre_count),
-        in_specs=[SMEM] * 3 + [VMEM] * 7 + [ANY],
+        in_specs=[SMEM] * 3 + [HBM] * 8,
         out_specs=[VMEM] * pre_count,
         out_shape=[shape_of((tokens, block + LANES))] * pre_count,
         scratch_shapes=[
             pltpu.VMEM((rows, 2, kv_width), bf16),
             pltpu.VMEM((pre_count, tokens, block + LANES), bf16),
             pltpu.SemaphoreType.DMA((rows,)),
-        ],
-        compiler_params=params(8),
+        ]
+        + [
+            pltpu.VMEM(source.shape, source.dtype)
+            for source in (
+                queries,
+                prefix_keys,
+                suffix_keys,
+                new_keys,
+                new_values,
+                suffix_values,
+                prefix_values,
+            )
+        ]
+        + [pltpu.SemaphoreType.DMA((7,))],
+        compiler_params=params(60),
+        cost_estimate=cost(20),
     )(
         adapter_ids,
         suffix_lengths,
@@ -354,6 +391,7 @@
         out_specs=VMEM,
         out_shape=shape_of((tokens, block)),
         compiler_params=params(4),
+        cost_estimate=cost(40),
     )(*shifted(partials, "pre"))
     gathered = shifted([mixed] * row_count, "row")
     products = pl.pallas_call(
@@ -367,7 +405,8 @@
             pltpu.VMEM((row_count * tokens, block), f32),
             pltpu.VMEM((row_count * tokens, out_cols), f32),
         ],
-        compiler_params=params(12),
+        compiler_params=params(8),
+        cost_estimate=cost(40),
     )(where, *gathered, out_weight)
     residual, sent = pl.pallas_call(
         functools.partial(residual_kernel, pre_count),
@@ -375,6 +414,7 @@
         out_specs=[VMEM] * 2,
         out_shape=[shape_of(hidden.shape), shape_of((amount, out_cols))],
         compiler_params=params(4),
+        cost_estimate=cost(40),
     )(hidden, *shifted(products, "pre"))
     stacked = shifted([sent] * pre_count, "pre")
     total_rows = pre_count * amount
@@ -390,8 +430,9 @@
             pltpu.VMEM((2 * total_rows, 2 * depth), bf16),
             pltpu.VMEM((2 * total_rows, wide + LANES), f32),
         ],
-        compiler_params=params(40),
-    )(where, norm_gain.reshape(1, depth), *stacked, gate_up)
+        compiler_params=params(8),
+        cost_estimate=cost(16),
+    )(where, norm_gain, *stacked, gate_up)
     activation = pl.pallas_call(
         functools.partial(activate_kernel, row_count),
         in_specs=[VMEM] * (row_count + 1),

time: 74.1 us -> 56.1 us (0.76)
  local copies, waits for them, and re-layouts: 13.3 us -> 0.82 us
  Pallas kernels: 22.9 us -> 16.2 us
  waiting for transfers between devices: 16.2 us -> 17.1 us
    unnamed x28, local copies, waits for them, and re-layouts: 12.6 us -> 0.82 us
    pallas_call x1, Pallas kernels: 15.5 us -> 6.79 us  [per_device(): pl.pallas_call(functools.partial(feed_kernel, pre_count, row_count), in_s...]
    pallas_call x1, Pallas kernels: 2.84 us -> 4.87 us  [per_device(): pl.pallas_call(functools.partial(attend_kernel, pre_count), in_specs=[SME...]
    ppermute x15, waiting for transfers between devices: 16.2 us -> 17.1 us  [shifted(): lax.ppermute(parts[s], axis, [(i, (i + s) % count) for i in range(count)])]
  transfers between devices with their start and end apart: 15 -> 15, of which waited for: 13 -> 14; matrix products, arithmetic and copies ran while one was open for 1% -> 0% of each run, Pallas kernels for 1% -> 1%
where the time goes in v2:
time: 56.1 us; the launch traced here: 55.3 us
  starting transfers between devices  19.9 us (35%)
  waiting for transfers between devices  17.1 us (30%)
  Pallas kernels  16.2 us (29%)
  local copies, waits for them, and re-layouts  0.82 us (1%)
  between operations  0.79 us (1%)
    ppermute x15, starting transfers between devices, shifted(): lax.ppermute(parts[s], axis, [(i, (i + s) % count) for i in range(count)])  19.9 us
    ppermute x15, waiting for transfers between devices, shifted(): lax.ppermute(parts[s], axis, [(i, (i + s) % count) for i in range(count)])  17.1 us
    pallas_call x1, Pallas kernels, per_device(): pl.pallas_call(functools.partial(feed_kernel, pre_count, row_count), in_s...  6.79 us
    pallas_call x1, Pallas kernels, per_device(): pl.pallas_call(functools.partial(attend_kernel, pre_count), in_specs=[SME...  4.87 us
    pallas_call x1, Pallas kernels, per_device(): pl.pallas_call(functools.partial(project_kernel, row_count, pre_count), i...  2.11 us
  transfers between devices with their start and end apart: 15, of which 14 were waited for; matrix products, arithmetic and copies ran while one was open for 0% of the time, Pallas kernels for 1%

profile of v2, /device:TPU:0, one launch (start us, length us, event | category | flops | bytes accessed | tf_op | source)
XLA Modules:
  0.0 55.3 jit_solution(5470464269573849201)
XLA Ops:
  0.6 0.6 %pad_add_fusion.where = s32[2]{0:T(128)} fusion(s32[1]{0:T(128)} %bitcast.1, s32[1]{0:T(128)} %bitcast), kind=kLoop, calls=%fused_computation | loop fusion | flops 2 | bytes 16 | tf_op jit(solution)/shard_map/stack | solution.py:336
  1.2 4.9 %shard_map.158 = (bf16[8,2176]{1,0:T(8,128)(2,1)}, bf16[8,2176]{1,0:T(8,128)(2,1)}, bf16[8,2176]{1,0:T(8,128)(2,1)}, bf16[8,2176]{1,0:T(8,128)(2,1)}) custom-call(s32[4]{0:T(128)} %ids.3, s32[4]{0:T(128)} %lengths.1, s32[2]{0:T(128)} %pad_add_fusion.where, bf16[4,2,8192]{2,1,0:T(2,128)(2,1)} %queries.1, bf16[128,1024]{1,0:T(8,128)(2,1)} %prefix_keys.1, ...), custom_call_target="tpu_custom_call" | custom-call | flops 20000000000 | tf_op jit(solution)/shard_map/pallas_call | solution.py:350
  6.1 3.1 %collective-permute-start = (bf16[8,2176]{1,0:T(8,128)(2,1)}, bf16[8,2176]{1,0:T(8,128)(2,1)S(1)}, u32[]{:S(2)}, u32[]{:S(2)}) collective-permute-start(bf16[8,2176]{1,0:T(8,128)(2,1)} %get-tuple-element.17), channel_id=1, source_target_pairs={{0,4},{4,8},{8,12},{12,0},{1,5},{5,9},{9,13},{13,1},{2,6},{6,10},{... | collective-permute-start | bytes 104456 | tf_op jit(solution)/shard_map/ppermute | solution.py:297
  9.1 2.6 %collective-permute-start.1 = (bf16[8,2176]{1,0:T(8,128)(2,1)}, bf16[8,2176]{1,0:T(8,128)(2,1)S(1)}, u32[]{:S(2)}, u32[]{:S(2)}) collective-permute-start(bf16[8,2176]{1,0:T(8,128)(2,1)} %get-tuple-element.18), channel_id=1, source_target_pairs={{0,8},{4,12},{8,0},{12,4},{1,9},{5,13},{9,1},{13,5},{2,10},{6,14},... | collective-permute-start | bytes 104456 | tf_op jit(solution)/shard_map/ppermute | solution.py:297
  11.7 1.3 %collective-permute-start.2 = (bf16[8,2176]{1,0:T(8,128)(2,1)}, bf16[8,2176]{1,0:T(8,128)(2,1)S(1)}, u32[]{:S(2)}, u32[]{:S(2)}) collective-permute-start(bf16[8,2176]{1,0:T(8,128)(2,1)} %get-tuple-element.19), channel_id=1, source_target_pairs={{0,12},{4,0},{8,4},{12,8},{1,13},{5,1},{9,5},{13,9},{2,14},{6,2},{... | collective-permute-start | bytes 104456 | tf_op jit(solution)/shard_map/ppermute | solution.py:297
  13.1 0.2 collective-permute-done.rest_1_
  13.3 1.3 %collective-permute-done.1.rest_2_ = bf16[8,2176]{1,0:T(8,128)(2,1)S(1)} collective-permute-done((bf16[8,2176]{1,0:T(8,128)(2,1)}, bf16[8,2176]{1,0:T(8,128)(2,1)S(1)}, u32[]{:S(2)}, u32[]{:S(2)}) %collective-permute-start.1) | collective-permute-done | bytes 34848 | tf_op jit(solution)/shard_map/ppermute | solution.py:297
  14.6 1.3 %collective-permute-done.2.rest_3_ = bf16[8,2176]{1,0:T(8,128)(2,1)S(1)} collective-permute-done((bf16[8,2176]{1,0:T(8,128)(2,1)}, bf16[8,2176]{1,0:T(8,128)(2,1)S(1)}, u32[]{:S(2)}, u32[]{:S(2)}) %collective-permute-start.2) | collective-permute-done | bytes 34848 | tf_op jit(solution)/shard_map/ppermute | solution.py:297
  15.9 0.8 %copy-done.6 = bf16[8,2176]{1,0:T(8,128)(2,1)S(1)} copy-done((bf16[8,2176]{1,0:T(8,128)(2,1)S(1)}, bf16[8,2176]{1,0:T(8,128)(2,1)}, u32[]{:S(2)}) %copy-start.6) | copy-done | bytes 34840
  16.6 0.3 shard_map.159.rest_0_
  16.9 0.0 copy-start.3
  16.9 0.1 collective-permute-start.3
  17.0 1.6 %collective-permute-start.4 = (bf16[8,2048]{1,0:T(8,128)(2,1)S(1)}, bf16[8,2048]{1,0:T(8,128)(2,1)S(1)}, u32[]{:S(2)}, u32[]{:S(2)}) collective-permute-start(bf16[8,2048]{1,0:T(8,128)(2,1)S(1)} %shard_map.159.rest_0_), channel_id=1, source_target_pairs={{0,2},{1,3},{2,0},{3,1},{4,6},{5,7},{6,4},{7,5},{8,10},{9,11},{10,... | collective-permute-start | bytes 98312 | tf_op jit(solution)/shard_map/ppermute | solution.py:297
  18.6 1.4 %collective-permute-start.5 = (bf16[8,2048]{1,0:T(8,128)(2,1)S(1)}, bf16[8,2048]{1,0:T(8,128)(2,1)S(1)}, u32[]{:S(2)}, u32[]{:S(2)}) collective-permute-start(bf16[8,2048]{1,0:T(8,128)(2,1)S(1)} %shard_map.159.rest_0_), channel_id=1, source_target_pairs={{0,3},{1,0},{2,1},{3,2},{4,7},{5,4},{6,5},{7,6},{8,11},{9,8},{10,9... | collective-permute-start | bytes 98312 | tf_op jit(solution)/shard_map/ppermute | solution.py:297
  19.9 0.4 collective-permute-done.3.rest_1_
  20.3 0.7 %collective-permute-done.4.rest_2_ = bf16[8,2048]{1,0:T(8,128)(2,1)S(1)} collective-permute-done((bf16[8,2048]{1,0:T(8,128)(2,1)S(1)}, bf16[8,2048]{1,0:T(8,128)(2,1)S(1)}, u32[]{:S(2)}, u32[]{:S(2)}) %collective-permute-start.4) | collective-permute-done | bytes 32800 | tf_op jit(solution)/shard_map/ppermute | solution.py:297
  21.0 0.6 %collective-permute-done.5.rest_3_ = bf16[8,2048]{1,0:T(8,128)(2,1)S(1)} collective-permute-done((bf16[8,2048]{1,0:T(8,128)(2,1)S(1)}, bf16[8,2048]{1,0:T(8,128)(2,1)S(1)}, u32[]{:S(2)}, u32[]{:S(2)}) %collective-permute-start.5) | collective-permute-done | bytes 32800 | tf_op jit(solution)/shard_map/ppermute | solution.py:297
  21.5 0.0 copy-done.2
  21.5 0.0 copy-done.5
  21.5 0.0 slice-start.2
  21.6 0.0 slice-start.3
  21.6 2.1 %shard_map.160 = (f32[8,2048]{1,0:T(8,128)S(1)}, bf16[8,2048]{1,0:T(8,128)(2,1)S(1)}, bf16[8,2048]{1,0:T(8,128)(2,1)S(1)}, bf16[8,2048]{1,0:T(8,128)(2,1)S(1)}) custom-call(s32[2]{0:T(128)S(1)} %copy-done.5, bf16[8,2048]{1,0:T(8,128)(2,1)S(1)} %shard_map.159.rest_0_, bf16[8,2048]{1,0:T(8,128)(2,1)S(1)} %collective-permute-done.3.rest_1_, ...), custom_call_target="tpu_custom_call" | custom-call | flops 40000000000 | tf_op jit(solution)/shard_map/pallas_call | solution.py:397
  23.7 0.3 collective-permute-start.6
  24.0 3.5 %collective-permute-start.7 = (bf16[8,2048]{1,0:T(8,128)(2,1)S(1)}, bf16[8,2048]{1,0:T(8,128)(2,1)S(1)}, u32[]{:S(2)}, u32[]{:S(2)}) collective-permute-start(bf16[8,2048]{1,0:T(8,128)(2,1)S(1)} %get-tuple-element.22), channel_id=1, source_target_pairs={{0,8},{4,12},{8,0},{12,4},{1,9},{5,13},{9,1},{13,5},{2,10},{6,14},... | collective-permute-start | bytes 98312 | tf_op jit(solution)/shard_map/ppermute | solution.py:297
  27.5 0.1 collective-permute-start.8
  27.6 2.3 %collective-permute-done.6.rest_1_ = bf16[8,2048]{1,0:T(8,128)(2,1)S(1)} collective-permute-done((bf16[8,2048]{1,0:T(8,128)(2,1)S(1)}, bf16[8,2048]{1,0:T(8,128)(2,1)S(1)}, u32[]{:S(2)}, u32[]{:S(2)}) %collective-permute-start.6) | collective-permute-done | bytes 32800 | tf_op jit(solution)/shard_map/ppermute | solution.py:297
  29.9 1.1 %collective-permute-done.7.rest_2_ = bf16[8,2048]{1,0:T(8,128)(2,1)S(1)} collective-permute-done((bf16[8,2048]{1,0:T(8,128)(2,1)S(1)}, bf16[8,2048]{1,0:T(8,128)(2,1)S(1)}, u32[]{:S(2)}, u32[]{:S(2)}) %collective-permute-start.7) | collective-permute-done | bytes 32800 | tf_op jit(solution)/shard_map/ppermute | solution.py:297
  31.0 0.4 collective-permute-done.8.rest_3_
  31.4 0.0 copy-done.3
  31.4 0.0 copy-start.4
  31.4 0.7 %shard_map.161 = (bf16[4,2,2048]{2,1,0:T(2,128)(2,1)}, bf16[8,2048]{1,0:T(8,128)(2,1)S(1)}) custom-call(bf16[4,2,2048]{2,1,0:T(2,128)(2,1)S(1)} %copy-done.3, f32[8,2048]{1,0:T(8,128)S(1)} %get-tuple-element.20.rest_0_, bf16[8,2048]{1,0:T(8,128)(2,1)S(1)} %collective-permute-done.6.rest_1_, bf16[8,2048]{1,0:T(8,128)(2,1)S(1)} %collective-permute-done.7.rest_2_, ...), custom_call_target="tpu_custom_call" | custom-call | flops 40000000000 | tf_op jit(solution)/shard_map/pallas_call | solution.py:411
  32.1 1.1 %collective-permute-start.10 = (bf16[8,2048]{1,0:T(8,128)(2,1)S(1)}, bf16[8,2048]{1,0:T(8,128)(2,1)S(1)}, u32[]{:S(2)}, u32[]{:S(2)}) collective-permute-start(bf16[8,2048]{1,0:T(8,128)(2,1)S(1)} %get-tuple-element.25.rest_0_), channel_id=1, source_target_pairs={{0,8},{4,12},{8,0},{12,4},{1,9},{5,13},{9,1},{13,5},{2,10},{6,14},... | collective-permute-start | bytes 98312 | tf_op jit(solution)/shard_map/ppermute | solution.py:297
  33.2 1.9 %collective-permute-start.11 = (bf16[8,2048]{1,0:T(8,128)(2,1)S(1)}, bf16[8,2048]{1,0:T(8,128)(2,1)S(1)}, u32[]{:S(2)}, u32[]{:S(2)}) collective-permute-start(bf16[8,2048]{1,0:T(8,128)(2,1)S(1)} %get-tuple-element.25.rest_0_), channel_id=1, source_target_pairs={{0,12},{4,0},{8,4},{12,8},{1,13},{5,1},{9,5},{13,9},{2,14},{6,2},{... | collective-permute-start | bytes 98312 | tf_op jit(solution)/shard_map/ppermute | solution.py:297
  35.1 0.1 collective-permute-start.9
  35.2 2.0 %collective-permute-done.10.rest_2_ = bf16[8,2048]{1,0:T(8,128)(2,1)S(1)} collective-permute-done((bf16[8,2048]{1,0:T(8,128)(2,1)S(1)}, bf16[8,2048]{1,0:T(8,128)(2,1)S(1)}, u32[]{:S(2)}, u32[]{:S(2)}) %collective-permute-start.10) | collective-permute-done | bytes 32800 | tf_op jit(solution)/shard_map/ppermute | solution.py:297
  37.2 0.0 collective-permute-done.11.rest_3_
  37.3 3.5 %collective-permute-done.9.rest_1_ = bf16[8,2048]{1,0:T(8,128)(2,1)S(1)} collective-permute-done((bf16[8,2048]{1,0:T(8,128)(2,1)S(1)}, bf16[8,2048]{1,0:T(8,128)(2,1)S(1)}, u32[]{:S(2)}, u32[]{:S(2)}) %collective-permute-start.9) | collective-permute-done | bytes 32800 | tf_op jit(solution)/shard_map/ppermute | solution.py:297
  40.8 0.0 slice-done
  40.9 6.8 %shard_map.163 = (f32[8,7296]{1,0:T(8,128)S(1)}, bf16[8,7296]{1,0:T(8,128)(2,1)S(1)}, bf16[8,7296]{1,0:T(8,128)(2,1)S(1)}, bf16[8,7296]{1,0:T(8,128)(2,1)S(1)}) custom-call(s32[2]{0:T(128)S(1)} %copy-done.5, bf16[2048]{0:T(1024)(128)(2,1)S(1)} %copy-done.4, bf16[8,2048]{1,0:T(8,128)(2,1)S(1)} %get-tuple-element.25.rest_0_, ...), custom_call_target="tpu_custom_call" | custom-call | flops 16000000000 | tf_op jit(solution)/shard_map/pallas_call | solution.py:421
  47.7 0.1 collective-permute-start.12
  47.7 1.4 %collective-permute-start.13 = (bf16[8,7296]{1,0:T(8,128)(2,1)S(1)}, bf16[8,7296]{1,0:T(8,128)(2,1)S(1)}, u32[]{:S(2)}, u32[]{:S(2)}) collective-permute-start(bf16[8,7296]{1,0:T(8,128)(2,1)S(1)} %get-tuple-element.28), channel_id=1, source_target_pairs={{0,2},{1,3},{2,0},{3,1},{4,6},{5,7},{6,4},{7,5},{8,10},{9,11},{10,... | collective-permute-start | bytes 350216 | tf_op jit(solution)/shard_map/ppermute | solution.py:297
  49.1 1.4 %collective-permute-start.14 = (bf16[8,7296]{1,0:T(8,128)(2,1)S(1)}, bf16[8,7296]{1,0:T(8,128)(2,1)S(1)}, u32[]{:S(2)}, u32[]{:S(2)}) collective-permute-start(bf16[8,7296]{1,0:T(8,128)(2,1)S(1)} %get-tuple-element.29), channel_id=1, source_target_pairs={{0,3},{1,0},{2,1},{3,2},{4,7},{5,4},{6,5},{7,6},{8,11},{9,8},{10,9... | collective-permute-start | bytes 350216 | tf_op jit(solution)/shard_map/ppermute | solution.py:297
  50.5 0.0 copy-done
  50.5 0.8 %shard_map.162.scales = f32[8,3584]{1,0:T(8,128)S(1)} custom-call(s32[4]{0:T(128)S(1)} %copy-done.1, bf16[128,3584]{1,0:T(8,128)(2,1)S(1)} %copy-done), custom_call_target="tpu_custom_call" | custom-call | tf_op jit(solution)/shard_map/pallas_call | solution.py:342
  51.3 1.3 %collective-permute-done.12.rest_1_ = bf16[8,7296]{1,0:T(8,128)(2,1)S(1)} collective-permute-done((bf16[8,7296]{1,0:T(8,128)(2,1)S(1)}, bf16[8,7296]{1,0:T(8,128)(2,1)S(1)}, u32[]{:S(2)}, u32[]{:S(2)}) %collective-permute-start.12) | collective-permute-done | bytes 116768 | tf_op jit(solution)/shard_map/ppermute | solution.py:297
  52.6 1.2 %collective-permute-done.13.rest_2_ = bf16[8,7296]{1,0:T(8,128)(2,1)S(1)} collective-permute-done((bf16[8,7296]{1,0:T(8,128)(2,1)S(1)}, bf16[8,7296]{1,0:T(8,128)(2,1)S(1)}, u32[]{:S(2)}, u32[]{:S(2)}) %collective-permute-start.13) | collective-permute-done | bytes 116768 | tf_op jit(solution)/shard_map/ppermute | solution.py:297
  53.8 0.7 %collective-permute-done.14.rest_3_ = bf16[8,7296]{1,0:T(8,128)(2,1)S(1)} collective-permute-done((bf16[8,7296]{1,0:T(8,128)(2,1)S(1)}, bf16[8,7296]{1,0:T(8,128)(2,1)S(1)}, u32[]{:S(2)}, u32[]{:S(2)}) %collective-permute-start.14) | collective-permute-done | bytes 116768 | tf_op jit(solution)/shard_map/ppermute | solution.py:297
  54.6 0.8 %shard_map.164 = bf16[4,2,3584]{2,1,0:T(2,128)(2,1)} custom-call(f32[8,3584]{1,0:T(8,128)S(1)} %shard_map.162.scales, f32[8,7296]{1,0:T(8,128)S(1)} %get-tuple-element.26.rest_0_, bf16[8,7296]{1,0:T(8,128)(2,1)S(1)} %collective-permute-done.12.rest_1_, bf16[8,7296]{1,0:T(8,128)(2,1)S(1)} %collective-permute-done.13.rest_2_, ...), custom_call_target="tpu_custom_call" | custom-call | tf_op jit(solution)/shard_map/pallas_call | solution.py:436
  (19 shorter events, 0.0 us)
Async XLA Ops:
  6.1 7.2 %collective-permute-start = (bf16[8,2176]{1,0:T(8,128)(2,1)}, bf16[8,2176]{1,0:T(8,128)(2,1)S(1)}, u32[]{:S(2)}, u32[]{:S(2)}) collective-permute-start(bf16[8,2176]{1,0:T(8,128)(2,1)} %get-tuple-element.17), channel_id=1, source_target_pairs={{0,4},{4,8},{8,12},{12,0},{1,5},{5,9},{9,13},{13,1},{2,6},{6,10},{... | collective-permute-start | bytes 104456 | tf_op jit(solution)/shard_map/ppermute | solution.py:297
  9.1 5.4 %collective-permute-start.1 = (bf16[8,2176]{1,0:T(8,128)(2,1)}, bf16[8,2176]{1,0:T(8,128)(2,1)S(1)}, u32[]{:S(2)}, u32[]{:S(2)}) collective-permute-start(bf16[8,2176]{1,0:T(8,128)(2,1)} %get-tuple-element.18), channel_id=1, source_target_pairs={{0,8},{4,12},{8,0},{12,4},{1,9},{5,13},{9,1},{13,5},{2,10},{6,14},... | collective-permute-start | bytes 104456 | tf_op jit(solution)/shard_map/ppermute | solution.py:297
  11.7 4.1 %collective-permute-start.2 = (bf16[8,2176]{1,0:T(8,128)(2,1)}, bf16[8,2176]{1,0:T(8,128)(2,1)S(1)}, u32[]{:S(2)}, u32[]{:S(2)}) collective-permute-start(bf16[8,2176]{1,0:T(8,128)(2,1)} %get-tuple-element.19), channel_id=1, source_target_pairs={{0,12},{4,0},{8,4},{12,8},{1,13},{5,1},{9,5},{13,9},{2,14},{6,2},{... | collective-permute-start | bytes 104456 | tf_op jit(solution)/shard_map/ppermute | solution.py:297
  15.9 0.8 %copy-start.6 = (bf16[8,2176]{1,0:T(8,128)(2,1)S(1)}, bf16[8,2176]{1,0:T(8,128)(2,1)}, u32[]{:S(2)}) copy-start(bf16[8,2176]{1,0:T(8,128)(2,1)} %get-tuple-element.16.rest_0_) | copy-start | bytes 104452
  16.6 4.9 %copy-start.2 = (bf16[2048,2048]{1,0:T(8,128)(2,1)S(1)}, bf16[2048,2048]{1,0:T(8,128)(2,1)}, u32[]{:S(2)}) copy-start(bf16[2048,2048]{1,0:T(8,128)(2,1)} %rest_4_.2) | copy-start | bytes 25165828
  16.6 4.9 %copy-start.5 = (s32[2]{0:T(128)S(1)}, s32[2]{0:T(128)}, u32[]{:S(2)}) copy-start(s32[2]{0:T(128)} %pad_add_fusion.where) | copy-start | bytes 28
  16.9 14.5 %copy-start.3 = (bf16[4,2,2048]{2,1,0:T(2,128)(2,1)S(1)}, bf16[4,2,2048]{2,1,0:T(2,128)(2,1)}, u32[]{:S(2)}) copy-start(bf16[4,2,2048]{2,1,0:T(2,128)(2,1)} %hidden.1) | copy-start | bytes 98308
  16.9 3.4 %collective-permute-start.3 = (bf16[8,2048]{1,0:T(8,128)(2,1)S(1)}, bf16[8,2048]{1,0:T(8,128)(2,1)S(1)}, u32[]{:S(2)}, u32[]{:S(2)}) collective-permute-start(bf16[8,2048]{1,0:T(8,128)(2,1)S(1)} %shard_map.159.rest_0_), channel_id=1, source_target_pairs={{0,1},{1,2},{2,3},{3,0},{4,5},{5,6},{6,7},{7,4},{8,9},{9,10},{10,1... | collective-permute-start | bytes 98312 | tf_op jit(solution)/shard_map/ppermute | solution.py:297
  17.0 4.0 %collective-permute-start.4 = (bf16[8,2048]{1,0:T(8,128)(2,1)S(1)}, bf16[8,2048]{1,0:T(8,128)(2,1)S(1)}, u32[]{:S(2)}, u32[]{:S(2)}) collective-permute-start(bf16[8,2048]{1,0:T(8,128)(2,1)S(1)} %shard_map.159.rest_0_), channel_id=1, source_target_pairs={{0,2},{1,3},{2,0},{3,1},{4,6},{5,7},{6,4},{7,5},{8,10},{9,11},{10,... | collective-permute-start | bytes 98312 | tf_op jit(solution)/shard_map/ppermute | solution.py:297
  18.6 3.0 %collective-permute-start.5 = (bf16[8,2048]{1,0:T(8,128)(2,1)S(1)}, bf16[8,2048]{1,0:T(8,128)(2,1)S(1)}, u32[]{:S(2)}, u32[]{:S(2)}) collective-permute-start(bf16[8,2048]{1,0:T(8,128)(2,1)S(1)} %shard_map.159.rest_0_), channel_id=1, source_target_pairs={{0,3},{1,0},{2,1},{3,2},{4,7},{5,4},{6,5},{7,6},{8,11},{9,8},{10,9... | collective-permute-start | bytes 98312 | tf_op jit(solution)/shard_map/ppermute | solution.py:297
  21.5 19.3 %slice-start = ((s8[29360128]{0:T(1024)(128)(4,1)}), s8[4194304]{0:T(1024)(128)(4,1)S(1)}, s32[]{:S(2)}) async-start(s8[29360128]{0:T(1024)(128)(4,1)} %bitcast.2), calls=%async_computation | async-start | bytes 8388608
  21.5 19.3 %slice-start.1 = ((s8[29360128]{0:T(1024)(128)(4,1)}), s8[4194304]{0:T(1024)(128)(4,1)S(1)}, s32[]{:S(2)}) async-start(s8[29360128]{0:T(1024)(128)(4,1)} %bitcast.2), calls=%async_computation.1 | async-start | bytes 8388608
  21.5 19.3 %slice-start.2 = ((s8[29360128]{0:T(1024)(128)(4,1)}), s8[4194304]{0:T(1024)(128)(4,1)S(1)}, s32[]{:S(2)}) async-start(s8[29360128]{0:T(1024)(128)(4,1)} %bitcast.2), calls=%async_computation.2 | async-start | bytes 8388608
  21.6 19.3 %slice-start.3 = ((s8[29360128]{0:T(1024)(128)(4,1)}), s8[4194304]{0:T(1024)(128)(4,1)S(1)}, s32[]{:S(2)}) async-start(s8[29360128]{0:T(1024)(128)(4,1)} %bitcast.2), calls=%async_computation.3 | async-start | bytes 8388608
  23.7 6.2 %collective-permute-start.6 = (bf16[8,2048]{1,0:T(8,128)(2,1)S(1)}, bf16[8,2048]{1,0:T(8,128)(2,1)S(1)}, u32[]{:S(2)}, u32[]{:S(2)}) collective-permute-start(bf16[8,2048]{1,0:T(8,128)(2,1)S(1)} %get-tuple-element.21), channel_id=1, source_target_pairs={{0,4},{4,8},{8,12},{12,0},{1,5},{5,9},{9,13},{13,1},{2,6},{6,10},{... | collective-permute-start | bytes 98312 | tf_op jit(solution)/shard_map/ppermute | solution.py:297
  24.0 7.0 %collective-permute-start.7 = (bf16[8,2048]{1,0:T(8,128)(2,1)S(1)}, bf16[8,2048]{1,0:T(8,128)(2,1)S(1)}, u32[]{:S(2)}, u32[]{:S(2)}) collective-permute-start(bf16[8,2048]{1,0:T(8,128)(2,1)S(1)} %get-tuple-element.22), channel_id=1, source_target_pairs={{0,8},{4,12},{8,0},{12,4},{1,9},{5,13},{9,1},{13,5},{2,10},{6,14},... | collective-permute-start | bytes 98312 | tf_op jit(solution)/shard_map/ppermute | solution.py:297
  27.5 3.9 %collective-permute-start.8 = (bf16[8,2048]{1,0:T(8,128)(2,1)S(1)}, bf16[8,2048]{1,0:T(8,128)(2,1)S(1)}, u32[]{:S(2)}, u32[]{:S(2)}) collective-permute-start(bf16[8,2048]{1,0:T(8,128)(2,1)S(1)} %get-tuple-element.23), channel_id=1, source_target_pairs={{0,12},{4,0},{8,4},{12,8},{1,13},{5,1},{9,5},{13,9},{2,14},{6,2},{... | collective-permute-start | bytes 98312 | tf_op jit(solution)/shard_map/ppermute | solution.py:297
  31.4 9.5 %slice-start.4 = ((s8[29360128]{0:T(1024)(128)(4,1)}), s8[4194304]{0:T(1024)(128)(4,1)S(1)}, s32[]{:S(2)}) async-start(s8[29360128]{0:T(1024)(128)(4,1)} %bitcast.2), calls=%async_computation.4 | async-start | bytes 8388608
  31.4 9.5 %slice-start.5 = ((s8[29360128]{0:T(1024)(128)(4,1)}), s8[4194304]{0:T(1024)(128)(4,1)S(1)}, s32[]{:S(2)}) async-start(s8[29360128]{0:T(1024)(128)(4,1)} %bitcast.2), calls=%async_computation.5 | async-start | bytes 8388608
  31.4 9.5 %slice-start.6 = ((s8[29360128]{0:T(1024)(128)(4,1)}), s8[4194304]{0:T(1024)(128)(4,1)S(1)}, s32[]{:S(2)}) async-start(s8[29360128]{0:T(1024)(128)(4,1)} %bitcast.2), calls=%async_computation.6 | async-start | bytes 8388608
  31.4 9.5 %copy-start.4 = (bf16[2048]{0:T(1024)(128)(2,1)S(1)}, bf16[2048]{0:T(1024)(128)(2,1)}, u32[]{:S(2)}) copy-start(bf16[2048]{0:T(1024)(128)(2,1)} %gain.1) | copy-start | bytes 12292
  32.1 18.4 %copy-start = (bf16[128,3584]{1,0:T(8,128)(2,1)S(1)}, bf16[128,3584]{1,0:T(8,128)(2,1)}, u32[]{:S(2)}) copy-start(bf16[128,3584]{1,0:T(8,128)(2,1)} %table.1) | copy-start | bytes 2752516
  32.1 18.4 %copy-start.1 = (s32[4]{0:T(128)S(1)}, s32[4]{0:T(128)}, u32[]{:S(2)}) copy-start(s32[4]{0:T(128)} %ids.3) | copy-start | bytes 52
  32.1 5.2 %collective-permute-start.10 = (bf16[8,2048]{1,0:T(8,128)(2,1)S(1)}, bf16[8,2048]{1,0:T(8,128)(2,1)S(1)}, u32[]{:S(2)}, u32[]{:S(2)}) collective-permute-start(bf16[8,2048]{1,0:T(8,128)(2,1)S(1)} %get-tuple-element.25.rest_0_), channel_id=1, source_target_pairs={{0,8},{4,12},{8,0},{12,4},{1,9},{5,13},{9,1},{13,5},{2,10},{6,14},... | collective-permute-start | bytes 98312 | tf_op jit(solution)/shard_map/ppermute | solution.py:297
  33.2 4.1 %collective-permute-start.11 = (bf16[8,2048]{1,0:T(8,128)(2,1)S(1)}, bf16[8,2048]{1,0:T(8,128)(2,1)S(1)}, u32[]{:S(2)}, u32[]{:S(2)}) collective-permute-start(bf16[8,2048]{1,0:T(8,128)(2,1)S(1)} %get-tuple-element.25.rest_0_), channel_id=1, source_target_pairs={{0,12},{4,0},{8,4},{12,8},{1,13},{5,1},{9,5},{13,9},{2,14},{6,2},{... | collective-permute-start | bytes 98312 | tf_op jit(solution)/shard_map/ppermute | solution.py:297
  35.1 5.7 %collective-permute-start.9 = (bf16[8,2048]{1,0:T(8,128)(2,1)S(1)}, bf16[8,2048]{1,0:T(8,128)(2,1)S(1)}, u32[]{:S(2)}, u32[]{:S(2)}) collective-permute-start(bf16[8,2048]{1,0:T(8,128)(2,1)S(1)} %get-tuple-element.25.rest_0_), channel_id=1, source_target_pairs={{0,4},{4,8},{8,12},{12,0},{1,5},{5,9},{9,13},{13,1},{2,6},{6,10},{... | collective-permute-start | bytes 98312 | tf_op jit(solution)/shard_map/ppermute | solution.py:297
  47.7 4.9 %collective-permute-start.12 = (bf16[8,7296]{1,0:T(8,128)(2,1)S(1)}, bf16[8,7296]{1,0:T(8,128)(2,1)S(1)}, u32[]{:S(2)}, u32[]{:S(2)}) collective-permute-start(bf16[8,7296]{1,0:T(8,128)(2,1)S(1)} %get-tuple-element.27), channel_id=1, source_target_pairs={{0,1},{1,2},{2,3},{3,0},{4,5},{5,6},{6,7},{7,4},{8,9},{9,10},{10,1... | collective-permute-start | bytes 350216 | tf_op jit(solution)/shard_map/ppermute | solution.py:297
  47.7 6.1 %collective-permute-start.13 = (bf16[8,7296]{1,0:T(8,128)(2,1)S(1)}, bf16[8,7296]{1,0:T(8,128)(2,1)S(1)}, u32[]{:S(2)}, u32[]{:S(2)}) collective-permute-start(bf16[8,7296]{1,0:T(8,128)(2,1)S(1)} %get-tuple-element.28), channel_id=1, source_target_pairs={{0,2},{1,3},{2,0},{3,1},{4,6},{5,7},{6,4},{7,5},{8,10},{9,11},{10,... | collective-permute-start | bytes 350216 | tf_op jit(solution)/shard_map/ppermute | solution.py:297
  49.1 5.4 %collective-permute-start.14 = (bf16[8,7296]{1,0:T(8,128)(2,1)S(1)}, bf16[8,7296]{1,0:T(8,128)(2,1)S(1)}, u32[]{:S(2)}, u32[]{:S(2)}) collective-permute-start(bf16[8,7296]{1,0:T(8,128)(2,1)S(1)} %get-tuple-element.29), channel_id=1, source_target_pairs={{0,3},{1,0},{2,1},{3,2},{4,7},{5,4},{6,5},{7,6},{8,11},{9,8},{10,9... | collective-permute-start | bytes 350216 | tf_op jit(solution)/shard_map/ppermute | solution.py:297

commit v3 on v2

--- a/solution.py
+++ b/solution.py
@@ -22,8 +22,16 @@
 HBM = pl.BlockSpec(memory_space=pltpu.HBM)
 
 
-def wrapped(index, count):
-    return lax.rem(index + count, count)
+def target_of(index, step, count):
+    if count & (count - 1) == 0:
+        return index ^ step
+    return (index + step) % count
+
+
+def source_of(index, step, count):
+    if count & (count - 1) == 0:
+        return index ^ step
+    return lax.rem(index + count - step, count)
 
 
 def dot(left, right):
@@ -52,7 +60,6 @@
     pre_count,
     ids,
     lengths,
-    where,
     queries,
     prefix_keys,
     prefix_values,
@@ -64,7 +71,11 @@
     *rest,
 ):
     outs, (scales, stage, sem) = rest[:pre_count], rest[pre_count : pre_count + 3]
-    held, held_sem = rest[pre_count + 3 : -1], rest[-1]
+    held, (id_mem, length_mem, small_sem, held_sem) = rest[pre_count + 3 : -4], rest[-4:]
+    id_copy = pltpu.make_async_copy(ids, id_mem, small_sem.at[0])
+    length_copy = pltpu.make_async_copy(lengths, length_mem, small_sem.at[1])
+    id_copy.start()
+    length_copy.start()
     sources = (
         queries,
         prefix_keys,
@@ -89,20 +100,23 @@
     group = HEADS // KV_HEADS
     block = HEADS * HD // pre_count
     block_heads = block // HD
-    me = where[0]
+    me = lax.axis_index("pre")
+    id_copy.wait()
     copies = [
-        pltpu.make_async_copy(kv_scales.at[ids[r]], scales.at[r], sem.at[r]) for r in range(rows)
+        pltpu.make_async_copy(kv_scales.at[id_mem[r]], scales.at[r], sem.at[r])
+        for r in range(rows)
     ]
     for copy in copies:
         copy.start()
 
+    length_copy.wait()
     count = group * tokens
     row_at = lax.broadcasted_iota(jnp.int32, (count, LANES), 0)
     column = lax.broadcasted_iota(jnp.int32, (count, LANES), 1)
     token = lax.rem(row_at, tokens)
     row_of = token // STEPS
     step = lax.rem(token, STEPS)
-    limit = pick(row_of, [lengths[r] for r in range(rows)])
+    limit = pick(row_of, [length_mem[r] for r in range(rows)])
     in_suffix = (
         (column < suffix_all)
         & (column // suffix_local == row_of)
@@ -174,7 +188,7 @@
             packed = packed + (pltpu.roll(piece, place * block_heads, 1) if place else piece)
         stage[at, :, block:] = packed.astype(bf16)
     for s in range(pre_count):
-        outs[s][...] = stage[wrapped(me + s, pre_count)]
+        outs[s][...] = stage[target_of(me, s, pre_count)]
 
 
 def merge_kernel(parts, *rest):
@@ -205,19 +219,19 @@
         out[:, span] = value.astype(bf16)
 
 
-def project_kernel(row_count, pre_count, where, *rest):
+def project_kernel(row_count, pre_count, *rest):
     blocks, weight = rest[:row_count], rest[row_count]
     outs = rest[row_count + 1 : row_count + 1 + pre_count]
     stacked, product = rest[row_count + 1 + pre_count :]
     tokens = blocks[0].shape[0]
     amount = outs[0].shape[0]
-    pre_at, row_at = where[0], where[1]
+    pre_at, row_at = lax.axis_index("pre"), lax.axis_index("row")
     for s, ref in enumerate(blocks):
-        start = pl.multiple_of(wrapped(row_at - s, row_count) * tokens, tokens)
+        start = pl.multiple_of(source_of(row_at, s, row_count) * tokens, tokens)
         stacked[pl.ds(start, tokens), :] = ref[...].astype(f32)
     product[...] = dot(stacked[...].astype(bf16), weight[...])
     for s, out in enumerate(outs):
-        start = pl.multiple_of(wrapped(pre_at + s, pre_count) * amount, amount)
+        start = pl.multiple_of(target_of(pre_at, s, pre_count) * amount, amount)
         out[...] = product[pl.ds(start, amount), :].astype(out.dtype)
 
 
@@ -230,7 +244,7 @@
     out[...] = value.astype(bf16).reshape(out.shape)
 
 
-def feed_kernel(pre_count, row_count, where, gain, *rest):
+def feed_kernel(pre_count, row_count, gain, *rest):
     blocks, weight = rest[:pre_count], rest[pre_count]
     outs = rest[pre_count + 1 : pre_count + 1 + row_count]
     stacked, spread, product = rest[pre_count + 1 + row_count :]
@@ -238,9 +252,9 @@
     rows = pre_count * amount
     tokens = rows // row_count
     wide = weight.shape[2]
-    pre_at, row_at = where[0], where[1]
+    pre_at, row_at = lax.axis_index("pre"), lax.axis_index("row")
     for s, ref in enumerate(blocks):
-        start = pl.multiple_of(wrapped(pre_at - s, pre_count) * amount, amount)
+        start = pl.multiple_of(source_of(pre_at, s, pre_count) * amount, amount)
         stacked[pl.ds(start, amount), :] = ref[...].astype(f32)
     value = stacked[...]
     squares = jnp.sum(value * value, axis=1, keepdims=True)
@@ -264,7 +278,7 @@
     packed = sum(jnp.where(lane == place, piece, 0.0) for place, piece in enumerate(pieces))
     product[0:rows, wide:] = packed
     for s, out in enumerate(outs):
-        start = pl.multiple_of(wrapped(row_at + s, row_count) * tokens, tokens)
+        start = pl.multiple_of(target_of(row_at, s, row_count) * tokens, tokens)
         out[:, :wide] = product[pl.ds(start, tokens), :wide].astype(out.dtype)
         out[:, wide : 2 * wide] = product[pl.ds(rows + start, tokens), :wide].astype(out.dtype)
         out[:, 2 * wide :] = product[pl.ds(start, tokens), wide:].astype(out.dtype)
@@ -294,7 +308,7 @@
 def shifted(parts, axis):
     count = lax.axis_size(axis)
     return [parts[0]] + [
-        lax.ppermute(parts[s], axis, [(i, (i + s) % count) for i in range(count)])
+        lax.ppermute(parts[s], axis, [(i, target_of(i, s, count)) for i in range(count)])
         for s in range(1, count)
     ]
 
@@ -333,7 +347,6 @@
     kv_width = prefix_keys.shape[1]
     pre_count = lax.axis_size("pre")
     row_count = lax.axis_size("row")
-    where = jnp.stack([lax.axis_index("pre"), lax.axis_index("row")]).astype(jnp.int32)
     block = HEADS * HD // pre_count
     amount = hidden.shape[0] * STEPS
     out_cols = out_weight.shape[1]
@@ -349,7 +362,7 @@
 
     partials = pl.pallas_call(
         functools.partial(attend_kernel, pre_count),
-        in_specs=[SMEM] * 3 + [HBM] * 8,
+        in_specs=[HBM] * 10,
         out_specs=[VMEM] * pre_count,
         out_shape=[shape_of((tokens, block + LANES))] * pre_count,
         scratch_shapes=[
@@ -369,13 +382,17 @@
                 prefix_values,
             )
         ]
-        + [pltpu.SemaphoreType.DMA((7,))],
+        + [
+            pltpu.SMEM((rows,), jnp.int32),
+            pltpu.SMEM((rows,), jnp.int32),
+            pltpu.SemaphoreType.DMA((2,)),
+            pltpu.SemaphoreType.DMA((7,)),
+        ],
         compiler_params=params(60),
         cost_estimate=cost(20),
     )(
         adapter_ids,
         suffix_lengths,
-        where,
         queries,
         prefix_keys,
         prefix_values,
@@ -396,7 +413,7 @@
     gathered = shifted([mixed] * row_count, "row")
     products = pl.pallas_call(
         functools.partial(project_kernel, row_count, pre_count),
-        in_specs=[SMEM] + [VMEM] * (row_count + 1),
+        in_specs=[VMEM] * (row_count + 1),
         out_specs=[VMEM] * pre_count,
         out_shape=[
             shape_of((amount, out_cols), bf16 if s else f32) for s in range(pre_count)
@@ -407,7 +424,7 @@
         ],
         compiler_params=params(8),
         cost_estimate=cost(40),
-    )(where, *gathered, out_weight)
+    )(*gathered, out_weight)
     residual, sent = pl.pallas_call(
         functools.partial(residual_kernel, pre_count),
         in_specs=[VMEM] * (pre_count + 1),
@@ -420,7 +437,7 @@
     total_rows = pre_count * amount
     fed = pl.pallas_call(
         functools.partial(feed_kernel, pre_count, row_count),
-        in_specs=[SMEM] + [VMEM] * (pre_count + 2),
+        in_specs=[VMEM] * (pre_count + 2),
         out_specs=[VMEM] * row_count,
         out_shape=[
             shape_of((tokens, 2 * wide + LANES), bf16 if s else f32) for s in range(row_count)
@@ -432,7 +449,7 @@
         ],
         compiler_params=params(8),
         cost_estimate=cost(16),
-    )(where, norm_gain, *stacked, gate_up)
+    )(norm_gain, *stacked, gate_up)
     activation = pl.pallas_call(
         functools.partial(activate_kernel, row_count),
         in_specs=[VMEM] * (row_count + 1),

time: 56.1 us -> 54.2 us (0.966)
  waiting for transfers between devices: 17.1 us -> 19.7 us
  starting transfers between devices: 19.9 us -> 17.9 us
  Pallas kernels: 16.2 us -> 14.7 us
    ppermute x15, waiting for transfers between devices: 17.1 us -> 19.7 us  [shifted(): lax.ppermute(parts[s], axis, [(i, target_of(i, s, count)) for i in range(...]
    ppermute x15, starting transfers between devices: 19.9 us -> 17.9 us  [shifted(): lax.ppermute(parts[s], axis, [(i, target_of(i, s, count)) for i in range(...]
    pallas_call x1, Pallas kernels: 6.79 us -> 6.17 us  [per_device(): pl.pallas_call(functools.partial(feed_kernel, pre_count, row_count), in_s...]
  transfers between devices with their start and end apart: 15 -> 15, of which waited for: 14 -> 11; matrix products, arithmetic and copies ran while one was open for 0% -> 0% of each run, Pallas kernels for 1% -> 1%
where the time goes in v3:
time: 54.2 us; the launch traced here: 53.9 us
  waiting for transfers between devices  19.7 us (36%)
  starting transfers between devices  17.9 us (33%)
  Pallas kernels  14.7 us (27%)
  local copies, waits for them, and re-layouts  0.81 us (1%)
  between operations  0.79 us (1%)
    ppermute x15, waiting for transfers between devices, shifted(): lax.ppermute(parts[s], axis, [(i, target_of(i, s, count)) for i in range(...  19.7 us
    ppermute x15, starting transfers between devices, shifted(): lax.ppermute(parts[s], axis, [(i, target_of(i, s, count)) for i in range(...  17.9 us
    pallas_call x1, Pallas kernels, per_device(): pl.pallas_call(functools.partial(feed_kernel, pre_count, row_count), in_s...  6.17 us
    pallas_call x1, Pallas kernels, per_device(): pl.pallas_call(functools.partial(attend_kernel, pre_count), in_specs=[HBM...  4.54 us
    pallas_call x1, Pallas kernels, per_device(): pl.pallas_call(functools.partial(project_kernel, row_count, pre_count), i...  1.56 us
  transfers between devices with their start and end apart: 15, of which 11 were waited for; matrix products, arithmetic and copies ran while one was open for 0% of the time, Pallas kernels for 1%

profile of v3, /device:TPU:0, one launch (start us, length us, event | category | flops | bytes accessed | tf_op | source)
XLA Modules:
  0.0 53.9 jit_solution(17379251205050332008)
XLA Ops:
  0.6 4.5 %shard_map.158 = (bf16[8,2176]{1,0:T(8,128)(2,1)}, bf16[8,2176]{1,0:T(8,128)(2,1)}, bf16[8,2176]{1,0:T(8,128)(2,1)}, bf16[8,2176]{1,0:T(8,128)(2,1)}) custom-call(s32[4]{0:T(128)} %ids.3, s32[4]{0:T(128)} %lengths.1, bf16[4,2,8192]{2,1,0:T(2,128)(2,1)} %queries.1, bf16[128,1024]{1,0:T(8,128)(2,1)} %prefix_keys.1, bf16[128,1024]{1,0:T(8,128)(2,1)} %prefix_values.1, ...), custom_call_target="tpu_custom_call" | custom-call | flops 20000000000 | tf_op jit(solution)/shard_map/pallas_call | solution.py:363
  5.2 3.1 %collective-permute-start = (bf16[8,2176]{1,0:T(8,128)(2,1)}, bf16[8,2176]{1,0:T(8,128)(2,1)S(1)}, u32[]{:S(2)}, u32[]{:S(2)}) collective-permute-start(bf16[8,2176]{1,0:T(8,128)(2,1)} %get-tuple-element.17), channel_id=1, source_target_pairs={{0,4},{4,0},{8,12},{12,8},{1,5},{5,1},{9,13},{13,9},{2,6},{6,2},{1... | collective-permute-start | bytes 104456 | tf_op jit(solution)/shard_map/ppermute | solution.py:311
  8.3 2.6 %collective-permute-start.1 = (bf16[8,2176]{1,0:T(8,128)(2,1)}, bf16[8,2176]{1,0:T(8,128)(2,1)S(1)}, u32[]{:S(2)}, u32[]{:S(2)}) collective-permute-start(bf16[8,2176]{1,0:T(8,128)(2,1)} %get-tuple-element.18), channel_id=1, source_target_pairs={{0,8},{4,12},{8,0},{12,4},{1,9},{5,13},{9,1},{13,5},{2,10},{6,14},... | collective-permute-start | bytes 104456 | tf_op jit(solution)/shard_map/ppermute | solution.py:311
  10.9 0.0 collective-permute-start.2
  10.9 0.0 collective-permute-done.rest_1_
  10.9 3.1 %collective-permute-done.1.rest_2_ = bf16[8,2176]{1,0:T(8,128)(2,1)S(1)} collective-permute-done((bf16[8,2176]{1,0:T(8,128)(2,1)}, bf16[8,2176]{1,0:T(8,128)(2,1)S(1)}, u32[]{:S(2)}, u32[]{:S(2)}) %collective-permute-start.1) | collective-permute-done | bytes 34848 | tf_op jit(solution)/shard_map/ppermute | solution.py:311
  13.9 2.9 %collective-permute-done.2.rest_3_ = bf16[8,2176]{1,0:T(8,128)(2,1)S(1)} collective-permute-done((bf16[8,2176]{1,0:T(8,128)(2,1)}, bf16[8,2176]{1,0:T(8,128)(2,1)S(1)}, u32[]{:S(2)}, u32[]{:S(2)}) %collective-permute-start.2) | collective-permute-done | bytes 34848 | tf_op jit(solution)/shard_map/ppermute | solution.py:311
  16.8 0.8 %copy-done.5 = bf16[8,2176]{1,0:T(8,128)(2,1)S(1)} copy-done((bf16[8,2176]{1,0:T(8,128)(2,1)S(1)}, bf16[8,2176]{1,0:T(8,128)(2,1)}, u32[]{:S(2)}) %copy-start.5) | copy-done | bytes 34840
  17.6 0.3 shard_map.159.rest_0_
  17.8 0.0 copy-start.3
  17.8 0.1 collective-permute-start.3
  17.9 1.6 %collective-permute-start.4 = (bf16[8,2048]{1,0:T(8,128)(2,1)S(1)}, bf16[8,2048]{1,0:T(8,128)(2,1)S(1)}, u32[]{:S(2)}, u32[]{:S(2)}) collective-permute-start(bf16[8,2048]{1,0:T(8,128)(2,1)S(1)} %shard_map.159.rest_0_), channel_id=1, source_target_pairs={{0,2},{1,3},{2,0},{3,1},{4,6},{5,7},{6,4},{7,5},{8,10},{9,11},{10,... | collective-permute-start | bytes 98312 | tf_op jit(solution)/shard_map/ppermute | solution.py:311
  19.5 0.3 collective-permute-start.5
  19.8 0.0 collective-permute-done.3.rest_1_
  19.8 2.1 %collective-permute-done.4.rest_2_ = bf16[8,2048]{1,0:T(8,128)(2,1)S(1)} collective-permute-done((bf16[8,2048]{1,0:T(8,128)(2,1)S(1)}, bf16[8,2048]{1,0:T(8,128)(2,1)S(1)}, u32[]{:S(2)}, u32[]{:S(2)}) %collective-permute-start.4) | collective-permute-done | bytes 32800 | tf_op jit(solution)/shard_map/ppermute | solution.py:311
  21.9 0.9 %collective-permute-done.5.rest_3_ = bf16[8,2048]{1,0:T(8,128)(2,1)S(1)} collective-permute-done((bf16[8,2048]{1,0:T(8,128)(2,1)S(1)}, bf16[8,2048]{1,0:T(8,128)(2,1)S(1)}, u32[]{:S(2)}, u32[]{:S(2)}) %collective-permute-start.5) | collective-permute-done | bytes 32800 | tf_op jit(solution)/shard_map/ppermute | solution.py:311
  22.8 0.0 copy-done.2
  22.8 0.0 slice-start.3
  22.9 1.6 %shard_map.160 = (f32[8,2048]{1,0:T(8,128)S(1)}, bf16[8,2048]{1,0:T(8,128)(2,1)S(1)}, bf16[8,2048]{1,0:T(8,128)(2,1)S(1)}, bf16[8,2048]{1,0:T(8,128)(2,1)S(1)}) custom-call(bf16[8,2048]{1,0:T(8,128)(2,1)S(1)} %shard_map.159.rest_0_, bf16[8,2048]{1,0:T(8,128)(2,1)S(1)} %collective-permute-done.3.rest_1_, bf16[8,2048]{1,0:T(8,128)(2,1)S(1)} %collective-permute-done.4.rest_2_, ...), custom_call_target="tpu_custom_call" | custom-call | flops 40000000000 | tf_op jit(solution)/shard_map/pallas_call | solution.py:414
  24.4 0.1 collective-permute-start.6
  24.5 1.0 %collective-permute-start.7 = (bf16[8,2048]{1,0:T(8,128)(2,1)S(1)}, bf16[8,2048]{1,0:T(8,128)(2,1)S(1)}, u32[]{:S(2)}, u32[]{:S(2)}) collective-permute-start(bf16[8,2048]{1,0:T(8,128)(2,1)S(1)} %get-tuple-element.22), channel_id=1, source_target_pairs={{0,8},{4,12},{8,0},{12,4},{1,9},{5,13},{9,1},{13,5},{2,10},{6,14},... | collective-permute-start | bytes 98312 | tf_op jit(solution)/shard_map/ppermute | solution.py:311
  25.5 3.4 %collective-permute-start.8 = (bf16[8,2048]{1,0:T(8,128)(2,1)S(1)}, bf16[8,2048]{1,0:T(8,128)(2,1)S(1)}, u32[]{:S(2)}, u32[]{:S(2)}) collective-permute-start(bf16[8,2048]{1,0:T(8,128)(2,1)S(1)} %get-tuple-element.23), channel_id=1, source_target_pairs={{0,12},{4,8},{8,4},{12,0},{1,13},{5,9},{9,5},{13,1},{2,14},{6,10},... | collective-permute-start | bytes 98312 | tf_op jit(solution)/shard_map/ppermute | solution.py:311
  28.9 0.0 collective-permute-done.6.rest_1_
  28.9 0.5 collective-permute-done.7.rest_2_
  29.4 1.8 %collective-permute-done.8.rest_3_ = bf16[8,2048]{1,0:T(8,128)(2,1)S(1)} collective-permute-done((bf16[8,2048]{1,0:T(8,128)(2,1)S(1)}, bf16[8,2048]{1,0:T(8,128)(2,1)S(1)}, u32[]{:S(2)}, u32[]{:S(2)}) %collective-permute-start.8) | collective-permute-done | bytes 32800 | tf_op jit(solution)/shard_map/ppermute | solution.py:311
  31.2 0.0 copy-done.3
  31.2 0.0 copy-start.4
  31.3 0.7 %shard_map.161 = (bf16[4,2,2048]{2,1,0:T(2,128)(2,1)}, bf16[8,2048]{1,0:T(8,128)(2,1)S(1)}) custom-call(bf16[4,2,2048]{2,1,0:T(2,128)(2,1)S(1)} %copy-done.3, f32[8,2048]{1,0:T(8,128)S(1)} %get-tuple-element.20.rest_0_, bf16[8,2048]{1,0:T(8,128)(2,1)S(1)} %collective-permute-done.6.rest_1_, bf16[8,2048]{1,0:T(8,128)(2,1)S(1)} %collective-permute-done.7.rest_2_, ...), custom_call_target="tpu_custom_call" | custom-call | flops 40000000000 | tf_op jit(solution)/shard_map/pallas_call | solution.py:428
  31.9 0.2 collective-permute-start.10
  32.1 3.2 %collective-permute-start.11 = (bf16[8,2048]{1,0:T(8,128)(2,1)S(1)}, bf16[8,2048]{1,0:T(8,128)(2,1)S(1)}, u32[]{:S(2)}, u32[]{:S(2)}) collective-permute-start(bf16[8,2048]{1,0:T(8,128)(2,1)S(1)} %get-tuple-element.25.rest_0_), channel_id=1, source_target_pairs={{0,12},{4,8},{8,4},{12,0},{1,13},{5,9},{9,5},{13,1},{2,14},{6,10},... | collective-permute-start | bytes 98312 | tf_op jit(solution)/shard_map/ppermute | solution.py:311
  35.3 0.6 %collective-permute-start.9 = (bf16[8,2048]{1,0:T(8,128)(2,1)S(1)}, bf16[8,2048]{1,0:T(8,128)(2,1)S(1)}, u32[]{:S(2)}, u32[]{:S(2)}) collective-permute-start(bf16[8,2048]{1,0:T(8,128)(2,1)S(1)} %get-tuple-element.25.rest_0_), channel_id=1, source_target_pairs={{0,4},{4,0},{8,12},{12,8},{1,5},{5,1},{9,13},{13,9},{2,6},{6,2},{1... | collective-permute-start | bytes 98312 | tf_op jit(solution)/shard_map/ppermute | solution.py:311
  35.8 0.9 %collective-permute-done.10.rest_2_ = bf16[8,2048]{1,0:T(8,128)(2,1)S(1)} collective-permute-done((bf16[8,2048]{1,0:T(8,128)(2,1)S(1)}, bf16[8,2048]{1,0:T(8,128)(2,1)S(1)}, u32[]{:S(2)}, u32[]{:S(2)}) %collective-permute-start.10) | collective-permute-done | bytes 32800 | tf_op jit(solution)/shard_map/ppermute | solution.py:311
  36.8 1.2 %collective-permute-done.11.rest_3_ = bf16[8,2048]{1,0:T(8,128)(2,1)S(1)} collective-permute-done((bf16[8,2048]{1,0:T(8,128)(2,1)S(1)}, bf16[8,2048]{1,0:T(8,128)(2,1)S(1)}, u32[]{:S(2)}, u32[]{:S(2)}) %collective-permute-start.11) | collective-permute-done | bytes 32800 | tf_op jit(solution)/shard_map/ppermute | solution.py:311
  37.9 1.3 %collective-permute-done.9.rest_1_ = bf16[8,2048]{1,0:T(8,128)(2,1)S(1)} collective-permute-done((bf16[8,2048]{1,0:T(8,128)(2,1)S(1)}, bf16[8,2048]{1,0:T(8,128)(2,1)S(1)}, u32[]{:S(2)}, u32[]{:S(2)}) %collective-permute-start.9) | collective-permute-done | bytes 32800 | tf_op jit(solution)/shard_map/ppermute | solution.py:311
  39.2 0.0 slice-done
  39.2 0.0 slice-done.1
  39.2 0.0 slice-done.2
  39.2 0.0 slice-done.3
  39.2 0.0 slice-done.4
  39.3 6.2 %shard_map.163 = (f32[8,7296]{1,0:T(8,128)S(1)}, bf16[8,7296]{1,0:T(8,128)(2,1)S(1)}, bf16[8,7296]{1,0:T(8,128)(2,1)S(1)}, bf16[8,7296]{1,0:T(8,128)(2,1)S(1)}) custom-call(bf16[2048]{0:T(1024)(128)(2,1)S(1)} %copy-done.4, bf16[8,2048]{1,0:T(8,128)(2,1)S(1)} %get-tuple-element.25.rest_0_, bf16[8,2048]{1,0:T(8,128)(2,1)S(1)} %collective-permute-done.9.rest_1_, ...), custom_call_target="tpu_custom_call" | custom-call | flops 16000000000 | tf_op jit(solution)/shard_map/pallas_call | solution.py:438
  45.4 0.1 collective-permute-start.12
  45.5 1.0 %collective-permute-start.13 = (bf16[8,7296]{1,0:T(8,128)(2,1)S(1)}, bf16[8,7296]{1,0:T(8,128)(2,1)S(1)}, u32[]{:S(2)}, u32[]{:S(2)}) collective-permute-start(bf16[8,7296]{1,0:T(8,128)(2,1)S(1)} %get-tuple-element.28), channel_id=1, source_target_pairs={{0,2},{1,3},{2,0},{3,1},{4,6},{5,7},{6,4},{7,5},{8,10},{9,11},{10,... | collective-permute-start | bytes 350216 | tf_op jit(solution)/shard_map/ppermute | solution.py:311
  46.5 0.9 %collective-permute-start.14 = (bf16[8,7296]{1,0:T(8,128)(2,1)S(1)}, bf16[8,7296]{1,0:T(8,128)(2,1)S(1)}, u32[]{:S(2)}, u32[]{:S(2)}) collective-permute-start(bf16[8,7296]{1,0:T(8,128)(2,1)S(1)} %get-tuple-element.29), channel_id=1, source_target_pairs={{0,3},{1,2},{2,1},{3,0},{4,7},{5,6},{6,5},{7,4},{8,11},{9,10},{10,... | collective-permute-start | bytes 350216 | tf_op jit(solution)/shard_map/ppermute | solution.py:311
  47.4 0.8 %shard_map.162.scales = f32[8,3584]{1,0:T(8,128)S(1)} custom-call(s32[4]{0:T(128)S(1)} %copy-done.1, bf16[128,3584]{1,0:T(8,128)(2,1)S(1)} %copy-done), custom_call_target="tpu_custom_call" | custom-call | tf_op jit(solution)/shard_map/pallas_call | solution.py:355
  48.1 0.0 collective-permute-done.12.rest_1_
  48.2 3.4 %collective-permute-done.13.rest_2_ = bf16[8,7296]{1,0:T(8,128)(2,1)S(1)} collective-permute-done((bf16[8,7296]{1,0:T(8,128)(2,1)S(1)}, bf16[8,7296]{1,0:T(8,128)(2,1)S(1)}, u32[]{:S(2)}, u32[]{:S(2)}) %collective-permute-start.13) | collective-permute-done | bytes 116768 | tf_op jit(solution)/shard_map/ppermute | solution.py:311
  51.6 1.6 %collective-permute-done.14.rest_3_ = bf16[8,7296]{1,0:T(8,128)(2,1)S(1)} collective-permute-done((bf16[8,7296]{1,0:T(8,128)(2,1)S(1)}, bf16[8,7296]{1,0:T(8,128)(2,1)S(1)}, u32[]{:S(2)}, u32[]{:S(2)}) %collective-permute-start.14) | collective-permute-done | bytes 116768 | tf_op jit(solution)/shard_map/ppermute | solution.py:311
  53.2 0.8 %shard_map.164 = bf16[4,2,3584]{2,1,0:T(2,128)(2,1)} custom-call(f32[8,3584]{1,0:T(8,128)S(1)} %shard_map.162.scales, f32[8,7296]{1,0:T(8,128)S(1)} %get-tuple-element.26.rest_0_, bf16[8,7296]{1,0:T(8,128)(2,1)S(1)} %collective-permute-done.12.rest_1_, bf16[8,7296]{1,0:T(8,128)(2,1)S(1)} %collective-permute-done.13.rest_2_, ...), custom_call_target="tpu_custom_call" | custom-call | tf_op jit(solution)/shard_map/pallas_call | solution.py:453
  (16 shorter events, 0.0 us)
Async XLA Ops:
  5.2 5.7 %collective-permute-start = (bf16[8,2176]{1,0:T(8,128)(2,1)}, bf16[8,2176]{1,0:T(8,128)(2,1)S(1)}, u32[]{:S(2)}, u32[]{:S(2)}) collective-permute-start(bf16[8,2176]{1,0:T(8,128)(2,1)} %get-tuple-element.17), channel_id=1, source_target_pairs={{0,4},{4,0},{8,12},{12,8},{1,5},{5,1},{9,13},{13,9},{2,6},{6,2},{1... | collective-permute-start | bytes 104456 | tf_op jit(solution)/shard_map/ppermute | solution.py:311
  8.3 5.7 %collective-permute-start.1 = (bf16[8,2176]{1,0:T(8,128)(2,1)}, bf16[8,2176]{1,0:T(8,128)(2,1)S(1)}, u32[]{:S(2)}, u32[]{:S(2)}) collective-permute-start(bf16[8,2176]{1,0:T(8,128)(2,1)} %get-tuple-element.18), channel_id=1, source_target_pairs={{0,8},{4,12},{8,0},{12,4},{1,9},{5,13},{9,1},{13,5},{2,10},{6,14},... | collective-permute-start | bytes 104456 | tf_op jit(solution)/shard_map/ppermute | solution.py:311
  10.9 5.9 %collective-permute-start.2 = (bf16[8,2176]{1,0:T(8,128)(2,1)}, bf16[8,2176]{1,0:T(8,128)(2,1)S(1)}, u32[]{:S(2)}, u32[]{:S(2)}) collective-permute-start(bf16[8,2176]{1,0:T(8,128)(2,1)} %get-tuple-element.19), channel_id=1, source_target_pairs={{0,12},{4,8},{8,4},{12,0},{1,13},{5,9},{9,5},{13,1},{2,14},{6,10},... | collective-permute-start | bytes 104456 | tf_op jit(solution)/shard_map/ppermute | solution.py:311
  16.8 0.8 %copy-start.5 = (bf16[8,2176]{1,0:T(8,128)(2,1)S(1)}, bf16[8,2176]{1,0:T(8,128)(2,1)}, u32[]{:S(2)}) copy-start(bf16[8,2176]{1,0:T(8,128)(2,1)} %get-tuple-element.16.rest_0_) | copy-start | bytes 104452
  17.6 5.3 %copy-start.2 = (bf16[2048,2048]{1,0:T(8,128)(2,1)S(1)}, bf16[2048,2048]{1,0:T(8,128)(2,1)}, u32[]{:S(2)}) copy-start(bf16[2048,2048]{1,0:T(8,128)(2,1)} %rest_4_.2) | copy-start | bytes 25165828
  17.8 13.4 %copy-start.3 = (bf16[4,2,2048]{2,1,0:T(2,128)(2,1)S(1)}, bf16[4,2,2048]{2,1,0:T(2,128)(2,1)}, u32[]{:S(2)}) copy-start(bf16[4,2,2048]{2,1,0:T(2,128)(2,1)} %hidden.1) | copy-start | bytes 98308
  17.8 1.9 %collective-permute-start.3 = (bf16[8,2048]{1,0:T(8,128)(2,1)S(1)}, bf16[8,2048]{1,0:T(8,128)(2,1)S(1)}, u32[]{:S(2)}, u32[]{:S(2)}) collective-permute-start(bf16[8,2048]{1,0:T(8,128)(2,1)S(1)} %shard_map.159.rest_0_), channel_id=1, source_target_pairs={{0,1},{1,0},{2,3},{3,2},{4,5},{5,4},{6,7},{7,6},{8,9},{9,8},{10,11... | collective-permute-start | bytes 98312 | tf_op jit(solution)/shard_map/ppermute | solution.py:311
  17.9 4.0 %collective-permute-start.4 = (bf16[8,2048]{1,0:T(8,128)(2,1)S(1)}, bf16[8,2048]{1,0:T(8,128)(2,1)S(1)}, u32[]{:S(2)}, u32[]{:S(2)}) collective-permute-start(bf16[8,2048]{1,0:T(8,128)(2,1)S(1)} %shard_map.159.rest_0_), channel_id=1, source_target_pairs={{0,2},{1,3},{2,0},{3,1},{4,6},{5,7},{6,4},{7,5},{8,10},{9,11},{10,... | collective-permute-start | bytes 98312 | tf_op jit(solution)/shard_map/ppermute | solution.py:311
  19.5 3.3 %collective-permute-start.5 = (bf16[8,2048]{1,0:T(8,128)(2,1)S(1)}, bf16[8,2048]{1,0:T(8,128)(2,1)S(1)}, u32[]{:S(2)}, u32[]{:S(2)}) collective-permute-start(bf16[8,2048]{1,0:T(8,128)(2,1)S(1)} %shard_map.159.rest_0_), channel_id=1, source_target_pairs={{0,3},{1,2},{2,1},{3,0},{4,7},{5,6},{6,5},{7,4},{8,11},{9,10},{10,... | collective-permute-start | bytes 98312 | tf_op jit(solution)/shard_map/ppermute | solution.py:311
  22.8 16.4 %slice-start = ((s8[29360128]{0:T(1024)(128)(4,1)}), s8[4194304]{0:T(1024)(128)(4,1)S(1)}, s32[]{:S(2)}) async-start(s8[29360128]{0:T(1024)(128)(4,1)} %bitcast), calls=%async_computation | async-start | bytes 8388608
  22.8 16.4 %slice-start.1 = ((s8[29360128]{0:T(1024)(128)(4,1)}), s8[4194304]{0:T(1024)(128)(4,1)S(1)}, s32[]{:S(2)}) async-start(s8[29360128]{0:T(1024)(128)(4,1)} %bitcast), calls=%async_computation.1 | async-start | bytes 8388608
  22.8 16.4 %slice-start.2 = ((s8[29360128]{0:T(1024)(128)(4,1)}), s8[4194304]{0:T(1024)(128)(4,1)S(1)}, s32[]{:S(2)}) async-start(s8[29360128]{0:T(1024)(128)(4,1)} %bitcast), calls=%async_computation.2 | async-start | bytes 8388608
  22.8 16.4 %slice-start.3 = ((s8[29360128]{0:T(1024)(128)(4,1)}), s8[4194304]{0:T(1024)(128)(4,1)S(1)}, s32[]{:S(2)}) async-start(s8[29360128]{0:T(1024)(128)(4,1)} %bitcast), calls=%async_computation.3 | async-start | bytes 8388608
  24.4 4.5 %collective-permute-start.6 = (bf16[8,2048]{1,0:T(8,128)(2,1)S(1)}, bf16[8,2048]{1,0:T(8,128)(2,1)S(1)}, u32[]{:S(2)}, u32[]{:S(2)}) collective-permute-start(bf16[8,2048]{1,0:T(8,128)(2,1)S(1)} %get-tuple-element.21), channel_id=1, source_target_pairs={{0,4},{4,0},{8,12},{12,8},{1,5},{5,1},{9,13},{13,9},{2,6},{6,2},{1... | collective-permute-start | bytes 98312 | tf_op jit(solution)/shard_map/ppermute | solution.py:311
  24.5 4.9 %collective-permute-start.7 = (bf16[8,2048]{1,0:T(8,128)(2,1)S(1)}, bf16[8,2048]{1,0:T(8,128)(2,1)S(1)}, u32[]{:S(2)}, u32[]{:S(2)}) collective-permute-start(bf16[8,2048]{1,0:T(8,128)(2,1)S(1)} %get-tuple-element.22), channel_id=1, source_target_pairs={{0,8},{4,12},{8,0},{12,4},{1,9},{5,13},{9,1},{13,5},{2,10},{6,14},... | collective-permute-start | bytes 98312 | tf_op jit(solution)/shard_map/ppermute | solution.py:311
  25.5 5.7 %collective-permute-start.8 = (bf16[8,2048]{1,0:T(8,128)(2,1)S(1)}, bf16[8,2048]{1,0:T(8,128)(2,1)S(1)}, u32[]{:S(2)}, u32[]{:S(2)}) collective-permute-start(bf16[8,2048]{1,0:T(8,128)(2,1)S(1)} %get-tuple-element.23), channel_id=1, source_target_pairs={{0,12},{4,8},{8,4},{12,0},{1,13},{5,9},{9,5},{13,1},{2,14},{6,10},... | collective-permute-start | bytes 98312 | tf_op jit(solution)/shard_map/ppermute | solution.py:311
  31.2 8.0 %slice-start.4 = ((s8[29360128]{0:T(1024)(128)(4,1)}), s8[4194304]{0:T(1024)(128)(4,1)S(1)}, s32[]{:S(2)}) async-start(s8[29360128]{0:T(1024)(128)(4,1)} %bitcast), calls=%async_computation.4 | async-start | bytes 8388608
  31.2 8.0 %slice-start.5 = ((s8[29360128]{0:T(1024)(128)(4,1)}), s8[4194304]{0:T(1024)(128)(4,1)S(1)}, s32[]{:S(2)}) async-start(s8[29360128]{0:T(1024)(128)(4,1)} %bitcast), calls=%async_computation.5 | async-start | bytes 8388608
  31.2 8.0 %slice-start.6 = ((s8[29360128]{0:T(1024)(128)(4,1)}), s8[4194304]{0:T(1024)(128)(4,1)S(1)}, s32[]{:S(2)}) async-start(s8[29360128]{0:T(1024)(128)(4,1)} %bitcast), calls=%async_computation.6 | async-start | bytes 8388608
  31.2 8.0 %copy-start.4 = (bf16[2048]{0:T(1024)(128)(2,1)S(1)}, bf16[2048]{0:T(1024)(128)(2,1)}, u32[]{:S(2)}) copy-start(bf16[2048]{0:T(1024)(128)(2,1)} %gain.1) | copy-start | bytes 12292
  31.9 15.5 %copy-start = (bf16[128,3584]{1,0:T(8,128)(2,1)S(1)}, bf16[128,3584]{1,0:T(8,128)(2,1)}, u32[]{:S(2)}) copy-start(bf16[128,3584]{1,0:T(8,128)(2,1)} %table.1) | copy-start | bytes 2752516
  31.9 15.5 %copy-start.1 = (s32[4]{0:T(128)S(1)}, s32[4]{0:T(128)}, u32[]{:S(2)}) copy-start(s32[4]{0:T(128)} %ids.3) | copy-start | bytes 52
  31.9 4.8 %collective-permute-start.10 = (bf16[8,2048]{1,0:T(8,128)(2,1)S(1)}, bf16[8,2048]{1,0:T(8,128)(2,1)S(1)}, u32[]{:S(2)}, u32[]{:S(2)}) collective-permute-start(bf16[8,2048]{1,0:T(8,128)(2,1)S(1)} %get-tuple-element.25.rest_0_), channel_id=1, source_target_pairs={{0,8},{4,12},{8,0},{12,4},{1,9},{5,13},{9,1},{13,5},{2,10},{6,14},... | collective-permute-start | bytes 98312 | tf_op jit(solution)/shard_map/ppermute | solution.py:311
  32.1 5.8 %collective-permute-start.11 = (bf16[8,2048]{1,0:T(8,128)(2,1)S(1)}, bf16[8,2048]{1,0:T(8,128)(2,1)S(1)}, u32[]{:S(2)}, u32[]{:S(2)}) collective-permute-start(bf16[8,2048]{1,0:T(8,128)(2,1)S(1)} %get-tuple-element.25.rest_0_), channel_id=1, source_target_pairs={{0,12},{4,8},{8,4},{12,0},{1,13},{5,9},{9,5},{13,1},{2,14},{6,10},... | collective-permute-start | bytes 98312 | tf_op jit(solution)/shard_map/ppermute | solution.py:311
  35.3 3.9 %collective-permute-start.9 = (bf16[8,2048]{1,0:T(8,128)(2,1)S(1)}, bf16[8,2048]{1,0:T(8,128)(2,1)S(1)}, u32[]{:S(2)}, u32[]{:S(2)}) collective-permute-start(bf16[8,2048]{1,0:T(8,128)(2,1)S(1)} %get-tuple-element.25.rest_0_), channel_id=1, source_target_pairs={{0,4},{4,0},{8,12},{12,8},{1,5},{5,1},{9,13},{13,9},{2,6},{6,2},{1... | collective-permute-start | bytes 98312 | tf_op jit(solution)/shard_map/ppermute | solution.py:311
  45.4 2.7 %collective-permute-start.12 = (bf16[8,7296]{1,0:T(8,128)(2,1)S(1)}, bf16[8,7296]{1,0:T(8,128)(2,1)S(1)}, u32[]{:S(2)}, u32[]{:S(2)}) collective-permute-start(bf16[8,7296]{1,0:T(8,128)(2,1)S(1)} %get-tuple-element.27), channel_id=1, source_target_pairs={{0,1},{1,0},{2,3},{3,2},{4,5},{5,4},{6,7},{7,6},{8,9},{9,8},{10,11... | collective-permute-start | bytes 350216 | tf_op jit(solution)/shard_map/ppermute | solution.py:311
  45.5 6.1 %collective-permute-start.13 = (bf16[8,7296]{1,0:T(8,128)(2,1)S(1)}, bf16[8,7296]{1,0:T(8,128)(2,1)S(1)}, u32[]{:S(2)}, u32[]{:S(2)}) collective-permute-start(bf16[8,7296]{1,0:T(8,128)(2,1)S(1)} %get-tuple-element.28), channel_id=1, source_target_pairs={{0,2},{1,3},{2,0},{3,1},{4,6},{5,7},{6,4},{7,5},{8,10},{9,11},{10,... | collective-permute-start | bytes 350216 | tf_op jit(solution)/shard_map/ppermute | solution.py:311
  46.5 6.7 %collective-permute-start.14 = (bf16[8,7296]{1,0:T(8,128)(2,1)S(1)}, bf16[8,7296]{1,0:T(8,128)(2,1)S(1)}, u32[]{:S(2)}, u32[]{:S(2)}) collective-permute-start(bf16[8,7296]{1,0:T(8,128)(2,1)S(1)} %get-tuple-element.29), channel_id=1, source_target_pairs={{0,3},{1,2},{2,1},{3,0},{4,7},{5,6},{6,5},{7,4},{8,11},{9,10},{10,... | collective-permute-start | bytes 350216 | tf_op jit(solution)/shard_map/ppermute | solution.py:311

commit v4 on v3

--- a/solution.py
+++ b/solution.py
@@ -244,15 +244,54 @@
     out[...] = value.astype(bf16).reshape(out.shape)
 
 
-def feed_kernel(pre_count, row_count, gain, *rest):
+def column_tile(columns):
+    return next(size for size in (512, 256, 128) if columns % size == 0)
+
+
+def split_columns(wide):
+    unit = 512 if wide >= 1024 else LANES
+    first = -(-(wide // 2) // unit) * unit
+    return first, wide - first
+
+
+def hand_out(row_count, product, columns, extra, keep, sent):
+    rows = product.shape[0] // 2
+    tokens = keep.shape[1]
+    row_at = lax.axis_index("row")
+    for j in range(row_count // 2):
+        for at, out in ((row_at ^ (2 * j), keep), (row_at ^ (2 * j + 1), sent)):
+            start = pl.multiple_of(at * tokens, tokens)
+            own = pl.ds(start, tokens)
+            out[j, :, :columns] = product[own, :columns].astype(out.dtype)
+            out[j, :, columns : 2 * columns] = product[
+                pl.ds(rows + start, tokens), :columns
+            ].astype(out.dtype)
+            if extra:
+                out[j, :, 2 * columns :] = product[own, columns:].astype(out.dtype)
+
+
+def multiply(left, weight, first, columns, product):
+    depth, _, wide = weight.shape
+    flat = weight.reshape(2 * depth, wide)
+    tile = column_tile(columns)
+    for start in range(0, columns, tile):
+        product[:, start : start + tile] = dot(
+            left, flat[:, first + start : first + start + tile]
+        )
+
+
+def placed_parts(value):
+    lane = lax.broadcasted_iota(jnp.int32, (value.shape[0], LANES), 1)
+    pieces = three_parts(value)
+    return sum(jnp.where(lane == place, piece, 0.0) for place, piece in enumerate(pieces))
+
+
+def feed_first_kernel(pre_count, row_count, columns, gain, *rest):
     blocks, weight = rest[:pre_count], rest[pre_count]
-    outs = rest[pre_count + 1 : pre_count + 1 + row_count]
-    stacked, spread, product = rest[pre_count + 1 + row_count :]
+    keep, sent, spread, stacked, product = rest[pre_count + 1 :]
     amount, depth = blocks[0].shape
     rows = pre_count * amount
-    tokens = rows // row_count
-    wide = weight.shape[2]
-    pre_at, row_at = lax.axis_index("pre"), lax.axis_index("row")
+    pre_at = lax.axis_index("pre")
     for s, ref in enumerate(blocks):
         start = pl.multiple_of(source_of(pre_at, s, pre_count) * amount, amount)
         stacked[pl.ds(start, amount), :] = ref[...].astype(f32)
@@ -268,20 +307,26 @@
             spread[half * rows : (half + 1) * rows, 2 * b * HD : 2 * (b + 1) * HD] = dot(
                 piece, selector
             ).astype(bf16)
-    left = spread[...]
-    flat = weight.reshape(2 * depth, wide)
-    tile = next(size for size in (512, 448, 256, 128) if wide % size == 0)
-    for j in range(wide // tile):
-        product[:, j * tile : (j + 1) * tile] = dot(left, flat[:, j * tile : (j + 1) * tile])
-    lane = lax.broadcasted_iota(jnp.int32, (rows, LANES), 1)
-    pieces = three_parts(squares)
-    packed = sum(jnp.where(lane == place, piece, 0.0) for place, piece in enumerate(pieces))
-    product[0:rows, wide:] = packed
-    for s, out in enumerate(outs):
-        start = pl.multiple_of(target_of(row_at, s, row_count) * tokens, tokens)
-        out[:, :wide] = product[pl.ds(start, tokens), :wide].astype(out.dtype)
-        out[:, wide : 2 * wide] = product[pl.ds(rows + start, tokens), :wide].astype(out.dtype)
-        out[:, 2 * wide :] = product[pl.ds(start, tokens), wide:].astype(out.dtype)
+    multiply(spread[...], weight, 0, columns, product)
+    product[0:rows, columns:] = placed_parts(squares)
+    hand_out(row_count, product, columns, True, keep, sent)
+
+
+def feed_second_kernel(row_count, first, columns, spread, weight, keep, sent, product):
+    multiply(spread[...], weight, first, columns, product)
+    hand_out(row_count, product, columns, False, keep, sent)
+
+
+def pair_kernel(extra, keep, received, *outs):
+    for j, out in enumerate(outs):
+        value = keep[j] + received[j].astype(f32)
+        if extra:
+            edge = value.shape[1] - LANES
+            out[:, :edge] = value[:, :edge].astype(out.dtype)
+            total = jnp.sum(value[:, edge:], axis=1, keepdims=True)
+            out[:, edge:] = placed_parts(total).astype(out.dtype)
+        else:
+            out[...] = value.astype(out.dtype)
 
 
 def scale_kernel(ids, table, out):
@@ -293,16 +338,18 @@
     out[...] = dot((chosen == column).astype(bf16), table[...])
 
 
-def activate_kernel(parts, scales, *rest):
-    blocks, out = rest[:parts], rest[parts]
-    tokens, wide = scales.shape
-    squares = sum(ref[:, 2 * wide :].astype(f32) for ref in blocks)
+def activate_kernel(parts, first, scales, *rest):
+    front, back, out = rest[:parts], rest[parts : 2 * parts], rest[2 * parts]
+    wide = scales.shape[1]
+    squares = sum(ref[:, 2 * first :].astype(f32) for ref in front)
     squares = jnp.sum(squares, axis=1, keepdims=True)
     inverse = lax.rsqrt(squares / D + 1e-05)
-    gate = sum(ref[:, :wide].astype(f32) for ref in blocks) * inverse
-    up = sum(ref[:, wide : 2 * wide].astype(f32) for ref in blocks) * inverse
-    value = gate / (1.0 + jnp.exp(-gate)) * up * scales[...]
-    out[...] = value.astype(bf16).reshape(out.shape)
+    for blocks, start, columns in ((front, 0, first), (back, first, wide - first)):
+        gate = sum(ref[:, :columns].astype(f32) for ref in blocks) * inverse
+        up = sum(ref[:, columns : 2 * columns].astype(f32) for ref in blocks) * inverse
+        value = gate / (1.0 + jnp.exp(-gate)) * up * scales[:, start : start + columns]
+        rows, steps, _ = out.shape
+        out[:, :, start : start + columns] = value.astype(bf16).reshape(rows, steps, columns)
 
 
 def shifted(parts, axis):
@@ -435,28 +482,61 @@
     )(hidden, *shifted(products, "pre"))
     stacked = shifted([sent] * pre_count, "pre")
     total_rows = pre_count * amount
-    fed = pl.pallas_call(
-        functools.partial(feed_kernel, pre_count, row_count),
+    half = row_count // 2
+    first, second = split_columns(wide)
+    sizes = (2 * first + LANES, 2 * second)
+    *front, spread = pl.pallas_call(
+        functools.partial(feed_first_kernel, pre_count, row_count, first),
         in_specs=[VMEM] * (pre_count + 2),
-        out_specs=[VMEM] * row_count,
+        out_specs=[VMEM] * 3,
         out_shape=[
-            shape_of((tokens, 2 * wide + LANES), bf16 if s else f32) for s in range(row_count)
+            shape_of((half, tokens, sizes[0]), f32),
+            shape_of((half, tokens, sizes[0])),
+            shape_of((2 * total_rows, 2 * depth)),
         ],
         scratch_shapes=[
             pltpu.VMEM((total_rows, depth), f32),
-            pltpu.VMEM((2 * total_rows, 2 * depth), bf16),
-            pltpu.VMEM((2 * total_rows, wide + LANES), f32),
+            pltpu.VMEM((2 * total_rows, first + LANES), f32),
         ],
         compiler_params=params(8),
         cost_estimate=cost(16),
     )(norm_gain, *stacked, gate_up)
+    back = pl.pallas_call(
+        functools.partial(feed_second_kernel, row_count, first, second),
+        in_specs=[VMEM] * 2,
+        out_specs=[VMEM] * 2,
+        out_shape=[
+            shape_of((half, tokens, sizes[1]), f32),
+            shape_of((half, tokens, sizes[1])),
+        ],
+        scratch_shapes=[pltpu.VMEM((2 * total_rows, second), f32)],
+        compiler_params=pltpu.CompilerParams(
+            vmem_limit_bytes=(8 << 20) + 2 * depth * (total_rows + 1)
+        ),
+        cost_estimate=cost(16),
+    )(spread, gate_up)
+    finals = []
+    for extra, size, (keep, sent) in ((True, sizes[0], front), (False, sizes[1], back)):
+        received = lax.ppermute(sent, "row", [(i, i ^ 1) for i in range(row_count)])
+        sums = pl.pallas_call(
+            functools.partial(pair_kernel, extra),
+            in_specs=[VMEM] * 2,
+            out_specs=[VMEM] * half,
+            out_shape=[shape_of((tokens, size), bf16 if j else f32) for j in range(half)],
+            compiler_params=params(4),
+        )(keep, received)
+        finals.append(sums[0])
+        finals += [
+            lax.ppermute(sums[j], "row", [(i, i ^ (2 * j)) for i in range(row_count)])
+            for j in range(1, half)
+        ]
     activation = pl.pallas_call(
-        functools.partial(activate_kernel, row_count),
-        in_specs=[VMEM] * (row_count + 1),
+        functools.partial(activate_kernel, half, first),
+        in_specs=[VMEM] * (2 * half + 1),
         out_specs=VMEM,
         out_shape=shape_of((rows, STEPS, wide)),
         compiler_params=params(4),
-    )(ffn_rows, *shifted(fed, "row"))
+    )(ffn_rows, *finals)
     return (residual, activation)
 
 

time: 54.2 us -> 52.6 us (0.970)
  waiting for transfers between devices: 19.7 us -> 17.1 us
  starting transfers between devices: 17.9 us -> 18.7 us
    ppermute x15 -> x12, waiting for transfers between devices: 19.7 us -> 14.7 us  [shifted(): lax.ppermute(parts[s], axis, [(i, target_of(i, s, count)) for i in range(...]
    ppermute x0 -> x4, starting transfers between devices: none -> 2.73 us  [the longest x2 2.13 us: per_device(): lax.ppermute(sums[j], 'row', [(i, i ^ 2 * j) for i in range(row_count)])]
    ppermute x0 -> x4, waiting for transfers between devices: none -> 2.47 us  [the longest x2 2.46 us: per_device(): lax.ppermute(sums[j], 'row', [(i, i ^ 2 * j) for i in range(row_count)])]
    ppermute x15 -> x12, starting transfers between devices: 17.9 us -> 16 us  [shifted(): lax.ppermute(parts[s], axis, [(i, target_of(i, s, count)) for i in range(...]
    pallas_call x2 -> x5, Pallas kernels: 6.93 us -> 7.08 us  [the longest x1 3.7 us: per_device(): pl.pallas_call(functools.partial(feed_first_kernel, pre_count, row_count,...]
  transfers between devices with their start and end apart: 15 -> 16, of which waited for: 11 -> 10; matrix products, arithmetic and copies ran while one was open for 0% -> 0% of each run, Pallas kernels for 1% -> 6%
where the time goes in v4:
time: 52.6 us; the launch traced here: 52.4 us
  starting transfers between devices  18.7 us (36%)
  waiting for transfers between devices  17.1 us (33%)
  Pallas kernels  14.9 us (28%)
  local copies, waits for them, and re-layouts  0.82 us (2%)
  between operations  0.82 us (2%)
    ppermute x12, starting transfers between devices, shifted(): lax.ppermute(parts[s], axis, [(i, target_of(i, s, count)) for i in range(...  16 us
    ppermute x12, waiting for transfers between devices, shifted(): lax.ppermute(parts[s], axis, [(i, target_of(i, s, count)) for i in range(...  14.7 us
    pallas_call x1, Pallas kernels, per_device(): pl.pallas_call(functools.partial(attend_kernel, pre_count), in_specs=[HBM...  4.54 us
    pallas_call x1, Pallas kernels, per_device(): pl.pallas_call(functools.partial(feed_first_kernel, pre_count, row_count,...  3.7 us
    pallas_call x1, Pallas kernels, per_device(): pl.pallas_call(functools.partial(feed_second_kernel, row_count, first, se...  2.5 us
    ppermute x2, waiting for transfers between devices, per_device(): lax.ppermute(sums[j], 'row', [(i, i ^ 2 * j) for i in range(row_count)])  2.46 us
    ppermute x2, starting transfers between devices, per_device(): lax.ppermute(sums[j], 'row', [(i, i ^ 2 * j) for i in range(row_count)])  2.13 us
    pallas_call x1, Pallas kernels, per_device(): pl.pallas_call(functools.partial(project_kernel, row_count, pre_count), i...  1.56 us
  transfers between devices with their start and end apart: 16, of which 10 were waited for; matrix products, arithmetic and copies ran while one was open for 0% of the time, Pallas kernels for 6%

profile of v4, /device:TPU:0, one launch (start us, length us, event | category | flops | bytes accessed | tf_op | source)
XLA Modules:
  0.0 52.4 jit_solution(13473925853920332729)
XLA Ops:
  0.6 4.5 %shard_map.158 = (bf16[8,2176]{1,0:T(8,128)(2,1)}, bf16[8,2176]{1,0:T(8,128)(2,1)}, bf16[8,2176]{1,0:T(8,128)(2,1)}, bf16[8,2176]{1,0:T(8,128)(2,1)}) custom-call(s32[4]{0:T(128)} %ids.3, s32[4]{0:T(128)} %lengths.1, bf16[4,2,8192]{2,1,0:T(2,128)(2,1)} %queries.1, bf16[128,1024]{1,0:T(8,128)(2,1)} %prefix_keys.1, bf16[128,1024]{1,0:T(8,128)(2,1)} %prefix_values.1, ...), custom_call_target="tpu_custom_call" | custom-call | flops 20000000000 | tf_op jit(solution)/shard_map/pallas_call | solution.py:410
  5.2 3.1 %collective-permute-start = (bf16[8,2176]{1,0:T(8,128)(2,1)}, bf16[8,2176]{1,0:T(8,128)(2,1)S(1)}, u32[]{:S(2)}, u32[]{:S(2)}) collective-permute-start(bf16[8,2176]{1,0:T(8,128)(2,1)} %get-tuple-element.22), channel_id=1, source_target_pairs={{0,4},{4,0},{8,12},{12,8},{1,5},{5,1},{9,13},{13,9},{2,6},{6,2},{1... | collective-permute-start | bytes 104456 | tf_op jit(solution)/shard_map/ppermute | solution.py:358
  8.3 2.6 %collective-permute-start.1 = (bf16[8,2176]{1,0:T(8,128)(2,1)}, bf16[8,2176]{1,0:T(8,128)(2,1)S(1)}, u32[]{:S(2)}, u32[]{:S(2)}) collective-permute-start(bf16[8,2176]{1,0:T(8,128)(2,1)} %get-tuple-element.23), channel_id=1, source_target_pairs={{0,8},{4,12},{8,0},{12,4},{1,9},{5,13},{9,1},{13,5},{2,10},{6,14},... | collective-permute-start | bytes 104456 | tf_op jit(solution)/shard_map/ppermute | solution.py:358
  10.9 0.0 collective-permute-start.2
  10.9 0.0 collective-permute-done.rest_1_
  10.9 3.1 %collective-permute-done.1.rest_2_ = bf16[8,2176]{1,0:T(8,128)(2,1)S(1)} collective-permute-done((bf16[8,2176]{1,0:T(8,128)(2,1)}, bf16[8,2176]{1,0:T(8,128)(2,1)S(1)}, u32[]{:S(2)}, u32[]{:S(2)}) %collective-permute-start.1) | collective-permute-done | bytes 34848 | tf_op jit(solution)/shard_map/ppermute | solution.py:358
  13.9 2.9 %collective-permute-done.2.rest_3_ = bf16[8,2176]{1,0:T(8,128)(2,1)S(1)} collective-permute-done((bf16[8,2176]{1,0:T(8,128)(2,1)}, bf16[8,2176]{1,0:T(8,128)(2,1)S(1)}, u32[]{:S(2)}, u32[]{:S(2)}) %collective-permute-start.2) | collective-permute-done | bytes 34848 | tf_op jit(solution)/shard_map/ppermute | solution.py:358
  16.8 0.8 %copy-done.5 = bf16[8,2176]{1,0:T(8,128)(2,1)S(1)} copy-done((bf16[8,2176]{1,0:T(8,128)(2,1)S(1)}, bf16[8,2176]{1,0:T(8,128)(2,1)}, u32[]{:S(2)}) %copy-start.5) | copy-done | bytes 34840
  17.6 0.3 shard_map.159.rest_0_
  17.8 0.0 copy-start.3
  17.8 0.1 collective-permute-start.3
  17.9 1.6 %collective-permute-start.4 = (bf16[8,2048]{1,0:T(8,128)(2,1)S(1)}, bf16[8,2048]{1,0:T(8,128)(2,1)S(1)}, u32[]{:S(2)}, u32[]{:S(2)}) collective-permute-start(bf16[8,2048]{1,0:T(8,128)(2,1)S(1)} %shard_map.159.rest_0_), channel_id=1, source_target_pairs={{0,2},{1,3},{2,0},{3,1},{4,6},{5,7},{6,4},{7,5},{8,10},{9,11},{10,... | collective-permute-start | bytes 98312 | tf_op jit(solution)/shard_map/ppermute | solution.py:358
  19.5 0.3 collective-permute-start.5
  19.8 0.0 collective-permute-done.3.rest_1_
  19.8 2.1 %collective-permute-done.4.rest_2_ = bf16[8,2048]{1,0:T(8,128)(2,1)S(1)} collective-permute-done((bf16[8,2048]{1,0:T(8,128)(2,1)S(1)}, bf16[8,2048]{1,0:T(8,128)(2,1)S(1)}, u32[]{:S(2)}, u32[]{:S(2)}) %collective-permute-start.4) | collective-permute-done | bytes 32800 | tf_op jit(solution)/shard_map/ppermute | solution.py:358
  21.9 0.9 %collective-permute-done.5.rest_3_ = bf16[8,2048]{1,0:T(8,128)(2,1)S(1)} collective-permute-done((bf16[8,2048]{1,0:T(8,128)(2,1)S(1)}, bf16[8,2048]{1,0:T(8,128)(2,1)S(1)}, u32[]{:S(2)}, u32[]{:S(2)}) %collective-permute-start.5) | collective-permute-done | bytes 32800 | tf_op jit(solution)/shard_map/ppermute | solution.py:358
  22.8 0.0 slice-start.3
  22.9 1.6 %shard_map.160 = (f32[8,2048]{1,0:T(8,128)S(1)}, bf16[8,2048]{1,0:T(8,128)(2,1)S(1)}, bf16[8,2048]{1,0:T(8,128)(2,1)S(1)}, bf16[8,2048]{1,0:T(8,128)(2,1)S(1)}) custom-call(bf16[8,2048]{1,0:T(8,128)(2,1)S(1)} %shard_map.159.rest_0_, bf16[8,2048]{1,0:T(8,128)(2,1)S(1)} %collective-permute-done.3.rest_1_, bf16[8,2048]{1,0:T(8,128)(2,1)S(1)} %collective-permute-done.4.rest_2_, ...), custom_call_target="tpu_custom_call" | custom-call | flops 40000000000 | tf_op jit(solution)/shard_map/pallas_call | solution.py:461
  24.4 0.1 collective-permute-start.6
  24.5 1.0 %collective-permute-start.7 = (bf16[8,2048]{1,0:T(8,128)(2,1)S(1)}, bf16[8,2048]{1,0:T(8,128)(2,1)S(1)}, u32[]{:S(2)}, u32[]{:S(2)}) collective-permute-start(bf16[8,2048]{1,0:T(8,128)(2,1)S(1)} %get-tuple-element.27), channel_id=1, source_target_pairs={{0,8},{4,12},{8,0},{12,4},{1,9},{5,13},{9,1},{13,5},{2,10},{6,14},... | collective-permute-start | bytes 98312 | tf_op jit(solution)/shard_map/ppermute | solution.py:358
  25.5 3.4 %collective-permute-start.8 = (bf16[8,2048]{1,0:T(8,128)(2,1)S(1)}, bf16[8,2048]{1,0:T(8,128)(2,1)S(1)}, u32[]{:S(2)}, u32[]{:S(2)}) collective-permute-start(bf16[8,2048]{1,0:T(8,128)(2,1)S(1)} %get-tuple-element.28), channel_id=1, source_target_pairs={{0,12},{4,8},{8,4},{12,0},{1,13},{5,9},{9,5},{13,1},{2,14},{6,10},... | collective-permute-start | bytes 98312 | tf_op jit(solution)/shard_map/ppermute | solution.py:358
  28.9 0.0 collective-permute-done.6.rest_1_
  28.9 0.5 collective-permute-done.7.rest_2_
  29.4 1.8 %collective-permute-done.8.rest_3_ = bf16[8,2048]{1,0:T(8,128)(2,1)S(1)} collective-permute-done((bf16[8,2048]{1,0:T(8,128)(2,1)S(1)}, bf16[8,2048]{1,0:T(8,128)(2,1)S(1)}, u32[]{:S(2)}, u32[]{:S(2)}) %collective-permute-start.8) | collective-permute-done | bytes 32800 | tf_op jit(solution)/shard_map/ppermute | solution.py:358
  31.2 0.0 copy-start.4
  31.2 0.7 %shard_map.161 = (bf16[4,2,2048]{2,1,0:T(2,128)(2,1)}, bf16[8,2048]{1,0:T(8,128)(2,1)S(1)}) custom-call(bf16[4,2,2048]{2,1,0:T(2,128)(2,1)S(1)} %copy-done.3, f32[8,2048]{1,0:T(8,128)S(1)} %get-tuple-element.25.rest_0_, bf16[8,2048]{1,0:T(8,128)(2,1)S(1)} %collective-permute-done.6.rest_1_, bf16[8,2048]{1,0:T(8,128)(2,1)S(1)} %collective-permute-done.7.rest_2_, ...), custom_call_target="tpu_custom_call" | custom-call | flops 40000000000 | tf_op jit(solution)/shard_map/pallas_call | solution.py:475
  31.9 0.2 collective-permute-start.10
  32.1 3.2 %collective-permute-start.11 = (bf16[8,2048]{1,0:T(8,128)(2,1)S(1)}, bf16[8,2048]{1,0:T(8,128)(2,1)S(1)}, u32[]{:S(2)}, u32[]{:S(2)}) collective-permute-start(bf16[8,2048]{1,0:T(8,128)(2,1)S(1)} %get-tuple-element.30.rest_0_), channel_id=1, source_target_pairs={{0,12},{4,8},{8,4},{12,0},{1,13},{5,9},{9,5},{13,1},{2,14},{6,10},... | collective-permute-start | bytes 98312 | tf_op jit(solution)/shard_map/ppermute | solution.py:358
  35.3 0.6 %collective-permute-start.9 = (bf16[8,2048]{1,0:T(8,128)(2,1)S(1)}, bf16[8,2048]{1,0:T(8,128)(2,1)S(1)}, u32[]{:S(2)}, u32[]{:S(2)}) collective-permute-start(bf16[8,2048]{1,0:T(8,128)(2,1)S(1)} %get-tuple-element.30.rest_0_), channel_id=1, source_target_pairs={{0,4},{4,0},{8,12},{12,8},{1,5},{5,1},{9,13},{13,9},{2,6},{6,2},{1... | collective-permute-start | bytes 98312 | tf_op jit(solution)/shard_map/ppermute | solution.py:358
  35.8 0.9 %collective-permute-done.10.rest_2_ = bf16[8,2048]{1,0:T(8,128)(2,1)S(1)} collective-permute-done((bf16[8,2048]{1,0:T(8,128)(2,1)S(1)}, bf16[8,2048]{1,0:T(8,128)(2,1)S(1)}, u32[]{:S(2)}, u32[]{:S(2)}) %collective-permute-start.10) | collective-permute-done | bytes 32800 | tf_op jit(solution)/shard_map/ppermute | solution.py:358
  36.7 1.2 %collective-permute-done.11.rest_3_ = bf16[8,2048]{1,0:T(8,128)(2,1)S(1)} collective-permute-done((bf16[8,2048]{1,0:T(8,128)(2,1)S(1)}, bf16[8,2048]{1,0:T(8,128)(2,1)S(1)}, u32[]{:S(2)}, u32[]{:S(2)}) %collective-permute-start.11) | collective-permute-done | bytes 32800 | tf_op jit(solution)/shard_map/ppermute | solution.py:358
  37.9 1.3 %collective-permute-done.9.rest_1_ = bf16[8,2048]{1,0:T(8,128)(2,1)S(1)} collective-permute-done((bf16[8,2048]{1,0:T(8,128)(2,1)S(1)}, bf16[8,2048]{1,0:T(8,128)(2,1)S(1)}, u32[]{:S(2)}, u32[]{:S(2)}) %collective-permute-start.9) | collective-permute-done | bytes 32800 | tf_op jit(solution)/shard_map/ppermute | solution.py:358
  39.2 0.0 slice-done.1
  39.3 3.7 %shard_map.163 = (f32[2,8,4224]{2,1,0:T(8,128)S(1)}, bf16[2,8,4224]{2,1,0:T(8,128)(2,1)S(1)}, bf16[64,4096]{1,0:T(8,128)(2,1)S(1)}) custom-call(bf16[2048]{0:T(1024)(128)(2,1)S(1)} %copy-done.4, bf16[8,2048]{1,0:T(8,128)(2,1)S(1)} %get-tuple-element.30.rest_0_, bf16[8,2048]{1,0:T(8,128)(2,1)S(1)} %collective-permute-done.9.rest_1_, ...), custom_call_target="tpu_custom_call" | custom-call | flops 16000000000 | tf_op jit(solution)/shard_map/pallas_call | solution.py:488
  43.0 0.1 collective-permute-start.12
  43.0 0.0 copy-start
  43.1 0.0 copy-start.1
  43.1 2.5 %shard_map.165 = (f32[2,8,3072]{2,1,0:T(8,128)S(1)}, bf16[2,8,3072]{2,1,0:T(8,128)(2,1)S(1)}) custom-call(bf16[64,4096]{1,0:T(8,128)(2,1)S(1)} %get-tuple-element.35.spread, bf16[2048,2,3584]{2,1,0:T(2,128)(2,1)S(1)} %bitcast.1), custom_call_target="tpu_custom_call" | custom-call | flops 16000000000 | tf_op jit(solution)/shard_map/pallas_call | solution.py:504
  45.6 0.5 %collective-permute-start.14 = (bf16[2,8,3072]{2,1,0:T(8,128)(2,1)S(1)}, bf16[2,8,3072]{2,1,0:T(8,128)(2,1)S(1)}, u32[]{:S(2)}, u32[]{:S(2)}) collective-permute-start(bf16[2,8,3072]{2,1,0:T(8,128)(2,1)S(1)} %get-tuple-element.37), channel_id=1, source_target_pairs={{0,1},{1,0},{2,3},{3,2},{4,5},{5,4},{6,7},{7,6},{8,9},{9,8},{10,11... | collective-permute-start | bytes 294920 | tf_op jit(solution)/shard_map/ppermute | solution.py:520
  46.1 0.0 collective-permute-done.12.received
  46.1 0.1 shard_map.164
  46.2 1.0 %collective-permute-start.13 = (bf16[8,4224]{1,0:T(8,128)(2,1)S(1)}, bf16[8,4224]{1,0:T(8,128)(2,1)S(1)}, u32[]{:S(2)}, u32[]{:S(2)}) collective-permute-start(bf16[8,4224]{1,0:T(8,128)(2,1)S(1)} %get-tuple-element.34), channel_id=1, source_target_pairs={{0,2},{1,3},{2,0},{3,1},{4,6},{5,7},{6,4},{7,5},{8,10},{9,11},{10,... | collective-permute-start | bytes 202760 | tf_op jit(solution)/shard_map/ppermute | solution.py:530
  47.2 0.0 collective-permute-done.14.received
  47.2 1.2 %collective-permute-start.15 = (bf16[8,3072]{1,0:T(8,128)(2,1)S(1)}, bf16[8,3072]{1,0:T(8,128)(2,1)S(1)}, u32[]{:S(2)}, u32[]{:S(2)}) collective-permute-start(bf16[8,3072]{1,0:T(8,128)(2,1)S(1)} %get-tuple-element.39), channel_id=1, source_target_pairs={{0,2},{1,3},{2,0},{3,1},{4,6},{5,7},{6,4},{7,5},{8,10},{9,11},{10,... | collective-permute-start | bytes 147464 | tf_op jit(solution)/shard_map/ppermute | solution.py:530
  48.4 0.8 %shard_map.162.scales = f32[8,3584]{1,0:T(8,128)S(1)} custom-call(s32[4]{0:T(128)S(1)} %copy-done.1, bf16[128,3584]{1,0:T(8,128)(2,1)S(1)} %copy-done), custom_call_target="tpu_custom_call" | custom-call | tf_op jit(solution)/shard_map/pallas_call | solution.py:402
  49.1 2.5 %collective-permute-done.15.rest_3_ = bf16[8,3072]{1,0:T(8,128)(2,1)S(1)} collective-permute-done((bf16[8,3072]{1,0:T(8,128)(2,1)S(1)}, bf16[8,3072]{1,0:T(8,128)(2,1)S(1)}, u32[]{:S(2)}, u32[]{:S(2)}) %collective-permute-start.15) | collective-permute-done | bytes 49184 | tf_op jit(solution)/shard_map/ppermute | solution.py:530
  51.6 0.0 collective-permute-done.13.rest_1_
  51.6 0.8 %shard_map.167 = bf16[4,2,3584]{2,1,0:T(2,128)(2,1)} custom-call(f32[8,3584]{1,0:T(8,128)S(1)} %shard_map.162.scales, f32[8,4224]{1,0:T(8,128)S(1)} %get-tuple-element.33.rest_0_, bf16[8,4224]{1,0:T(8,128)(2,1)S(1)} %collective-permute-done.13.rest_1_, f32[8,3072]{1,0:T(8,128)S(1)} %get-tuple-element.38.rest_2_, ...), custom_call_target="tpu_custom_call" | custom-call | tf_op jit(solution)/shard_map/pallas_call | solution.py:533
  (21 shorter events, 0.1 us)
Async XLA Ops:
  5.2 5.7 %collective-permute-start = (bf16[8,2176]{1,0:T(8,128)(2,1)}, bf16[8,2176]{1,0:T(8,128)(2,1)S(1)}, u32[]{:S(2)}, u32[]{:S(2)}) collective-permute-start(bf16[8,2176]{1,0:T(8,128)(2,1)} %get-tuple-element.22), channel_id=1, source_target_pairs={{0,4},{4,0},{8,12},{12,8},{1,5},{5,1},{9,13},{13,9},{2,6},{6,2},{1... | collective-permute-start | bytes 104456 | tf_op jit(solution)/shard_map/ppermute | solution.py:358
  8.3 5.7 %collective-permute-start.1 = (bf16[8,2176]{1,0:T(8,128)(2,1)}, bf16[8,2176]{1,0:T(8,128)(2,1)S(1)}, u32[]{:S(2)}, u32[]{:S(2)}) collective-permute-start(bf16[8,2176]{1,0:T(8,128)(2,1)} %get-tuple-element.23), channel_id=1, source_target_pairs={{0,8},{4,12},{8,0},{12,4},{1,9},{5,13},{9,1},{13,5},{2,10},{6,14},... | collective-permute-start | bytes 104456 | tf_op jit(solution)/shard_map/ppermute | solution.py:358
  10.9 5.9 %collective-permute-start.2 = (bf16[8,2176]{1,0:T(8,128)(2,1)}, bf16[8,2176]{1,0:T(8,128)(2,1)S(1)}, u32[]{:S(2)}, u32[]{:S(2)}) collective-permute-start(bf16[8,2176]{1,0:T(8,128)(2,1)} %get-tuple-element.24), channel_id=1, source_target_pairs={{0,12},{4,8},{8,4},{12,0},{1,13},{5,9},{9,5},{13,1},{2,14},{6,10},... | collective-permute-start | bytes 104456 | tf_op jit(solution)/shard_map/ppermute | solution.py:358
  16.8 0.8 %copy-start.5 = (bf16[8,2176]{1,0:T(8,128)(2,1)S(1)}, bf16[8,2176]{1,0:T(8,128)(2,1)}, u32[]{:S(2)}) copy-start(bf16[8,2176]{1,0:T(8,128)(2,1)} %get-tuple-element.21.rest_0_) | copy-start | bytes 104452
  17.6 5.3 %copy-start.2 = (bf16[2048,2048]{1,0:T(8,128)(2,1)S(1)}, bf16[2048,2048]{1,0:T(8,128)(2,1)}, u32[]{:S(2)}) copy-start(bf16[2048,2048]{1,0:T(8,128)(2,1)} %rest_4_.2) | copy-start | bytes 25165828
  17.8 13.4 %copy-start.3 = (bf16[4,2,2048]{2,1,0:T(2,128)(2,1)S(1)}, bf16[4,2,2048]{2,1,0:T(2,128)(2,1)}, u32[]{:S(2)}) copy-start(bf16[4,2,2048]{2,1,0:T(2,128)(2,1)} %hidden.1) | copy-start | bytes 98308
  17.8 1.9 %collective-permute-start.3 = (bf16[8,2048]{1,0:T(8,128)(2,1)S(1)}, bf16[8,2048]{1,0:T(8,128)(2,1)S(1)}, u32[]{:S(2)}, u32[]{:S(2)}) collective-permute-start(bf16[8,2048]{1,0:T(8,128)(2,1)S(1)} %shard_map.159.rest_0_), channel_id=1, source_target_pairs={{0,1},{1,0},{2,3},{3,2},{4,5},{5,4},{6,7},{7,6},{8,9},{9,8},{10,11... | collective-permute-start | bytes 98312 | tf_op jit(solution)/shard_map/ppermute | solution.py:358
  17.9 4.0 %collective-permute-start.4 = (bf16[8,2048]{1,0:T(8,128)(2,1)S(1)}, bf16[8,2048]{1,0:T(8,128)(2,1)S(1)}, u32[]{:S(2)}, u32[]{:S(2)}) collective-permute-start(bf16[8,2048]{1,0:T(8,128)(2,1)S(1)} %shard_map.159.rest_0_), channel_id=1, source_target_pairs={{0,2},{1,3},{2,0},{3,1},{4,6},{5,7},{6,4},{7,5},{8,10},{9,11},{10,... | collective-permute-start | bytes 98312 | tf_op jit(solution)/shard_map/ppermute | solution.py:358
  19.5 3.3 %collective-permute-start.5 = (bf16[8,2048]{1,0:T(8,128)(2,1)S(1)}, bf16[8,2048]{1,0:T(8,128)(2,1)S(1)}, u32[]{:S(2)}, u32[]{:S(2)}) collective-permute-start(bf16[8,2048]{1,0:T(8,128)(2,1)S(1)} %shard_map.159.rest_0_), channel_id=1, source_target_pairs={{0,3},{1,2},{2,1},{3,0},{4,7},{5,6},{6,5},{7,4},{8,11},{9,10},{10,... | collective-permute-start | bytes 98312 | tf_op jit(solution)/shard_map/ppermute | solution.py:358
  22.8 16.4 %slice-start = ((s8[29360128]{0:T(1024)(128)(4,1)}), s8[4194304]{0:T(1024)(128)(4,1)S(1)}, s32[]{:S(2)}) async-start(s8[29360128]{0:T(1024)(128)(4,1)} %bitcast), calls=%async_computation | async-start | bytes 8388608
  22.8 16.4 %slice-start.1 = ((s8[29360128]{0:T(1024)(128)(4,1)}), s8[4194304]{0:T(1024)(128)(4,1)S(1)}, s32[]{:S(2)}) async-start(s8[29360128]{0:T(1024)(128)(4,1)} %bitcast), calls=%async_computation.1 | async-start | bytes 8388608
  22.8 16.4 %slice-start.2 = ((s8[29360128]{0:T(1024)(128)(4,1)}), s8[4194304]{0:T(1024)(128)(4,1)S(1)}, s32[]{:S(2)}) async-start(s8[29360128]{0:T(1024)(128)(4,1)} %bitcast), calls=%async_computation.2 | async-start | bytes 8388608
  22.8 16.4 %slice-start.3 = ((s8[29360128]{0:T(1024)(128)(4,1)}), s8[4194304]{0:T(1024)(128)(4,1)S(1)}, s32[]{:S(2)}) async-start(s8[29360128]{0:T(1024)(128)(4,1)} %bitcast), calls=%async_computation.3 | async-start | bytes 8388608
  24.4 4.5 %collective-permute-start.6 = (bf16[8,2048]{1,0:T(8,128)(2,1)S(1)}, bf16[8,2048]{1,0:T(8,128)(2,1)S(1)}, u32[]{:S(2)}, u32[]{:S(2)}) collective-permute-start(bf16[8,2048]{1,0:T(8,128)(2,1)S(1)} %get-tuple-element.26), channel_id=1, source_target_pairs={{0,4},{4,0},{8,12},{12,8},{1,5},{5,1},{9,13},{13,9},{2,6},{6,2},{1... | collective-permute-start | bytes 98312 | tf_op jit(solution)/shard_map/ppermute | solution.py:358
  24.5 4.9 %collective-permute-start.7 = (bf16[8,2048]{1,0:T(8,128)(2,1)S(1)}, bf16[8,2048]{1,0:T(8,128)(2,1)S(1)}, u32[]{:S(2)}, u32[]{:S(2)}) collective-permute-start(bf16[8,2048]{1,0:T(8,128)(2,1)S(1)} %get-tuple-element.27), channel_id=1, source_target_pairs={{0,8},{4,12},{8,0},{12,4},{1,9},{5,13},{9,1},{13,5},{2,10},{6,14},... | collective-permute-start | bytes 98312 | tf_op jit(solution)/shard_map/ppermute | solution.py:358
  25.5 5.7 %collective-permute-start.8 = (bf16[8,2048]{1,0:T(8,128)(2,1)S(1)}, bf16[8,2048]{1,0:T(8,128)(2,1)S(1)}, u32[]{:S(2)}, u32[]{:S(2)}) collective-permute-start(bf16[8,2048]{1,0:T(8,128)(2,1)S(1)} %get-tuple-element.28), channel_id=1, source_target_pairs={{0,12},{4,8},{8,4},{12,0},{1,13},{5,9},{9,5},{13,1},{2,14},{6,10},... | collective-permute-start | bytes 98312 | tf_op jit(solution)/shard_map/ppermute | solution.py:358
  31.2 8.0 %slice-start.4 = ((s8[29360128]{0:T(1024)(128)(4,1)}), s8[4194304]{0:T(1024)(128)(4,1)S(1)}, s32[]{:S(2)}) async-start(s8[29360128]{0:T(1024)(128)(4,1)} %bitcast), calls=%async_computation.4 | async-start | bytes 8388608
  31.2 8.0 %slice-start.5 = ((s8[29360128]{0:T(1024)(128)(4,1)}), s8[4194304]{0:T(1024)(128)(4,1)S(1)}, s32[]{:S(2)}) async-start(s8[29360128]{0:T(1024)(128)(4,1)} %bitcast), calls=%async_computation.5 | async-start | bytes 8388608
  31.2 8.0 %slice-start.6 = ((s8[29360128]{0:T(1024)(128)(4,1)}), s8[4194304]{0:T(1024)(128)(4,1)S(1)}, s32[]{:S(2)}) async-start(s8[29360128]{0:T(1024)(128)(4,1)} %bitcast), calls=%async_computation.6 | async-start | bytes 8388608
  31.2 8.0 %copy-start.4 = (bf16[2048]{0:T(1024)(128)(2,1)S(1)}, bf16[2048]{0:T(1024)(128)(2,1)}, u32[]{:S(2)}) copy-start(bf16[2048]{0:T(1024)(128)(2,1)} %gain.1) | copy-start | bytes 12292
  31.9 4.8 %collective-permute-start.10 = (bf16[8,2048]{1,0:T(8,128)(2,1)S(1)}, bf16[8,2048]{1,0:T(8,128)(2,1)S(1)}, u32[]{:S(2)}, u32[]{:S(2)}) collective-permute-start(bf16[8,2048]{1,0:T(8,128)(2,1)S(1)} %get-tuple-element.30.rest_0_), channel_id=1, source_target_pairs={{0,8},{4,12},{8,0},{12,4},{1,9},{5,13},{9,1},{13,5},{2,10},{6,14},... | collective-permute-start | bytes 98312 | tf_op jit(solution)/shard_map/ppermute | solution.py:358
  32.1 5.8 %collective-permute-start.11 = (bf16[8,2048]{1,0:T(8,128)(2,1)S(1)}, bf16[8,2048]{1,0:T(8,128)(2,1)S(1)}, u32[]{:S(2)}, u32[]{:S(2)}) collective-permute-start(bf16[8,2048]{1,0:T(8,128)(2,1)S(1)} %get-tuple-element.30.rest_0_), channel_id=1, source_target_pairs={{0,12},{4,8},{8,4},{12,0},{1,13},{5,9},{9,5},{13,1},{2,14},{6,10},... | collective-permute-start | bytes 98312 | tf_op jit(solution)/shard_map/ppermute | solution.py:358
  35.3 3.9 %collective-permute-start.9 = (bf16[8,2048]{1,0:T(8,128)(2,1)S(1)}, bf16[8,2048]{1,0:T(8,128)(2,1)S(1)}, u32[]{:S(2)}, u32[]{:S(2)}) collective-permute-start(bf16[8,2048]{1,0:T(8,128)(2,1)S(1)} %get-tuple-element.30.rest_0_), channel_id=1, source_target_pairs={{0,4},{4,0},{8,12},{12,8},{1,5},{5,1},{9,13},{13,9},{2,6},{6,2},{1... | collective-permute-start | bytes 98312 | tf_op jit(solution)/shard_map/ppermute | solution.py:358
  43.0 3.1 %collective-permute-start.12 = (bf16[2,8,4224]{2,1,0:T(8,128)(2,1)S(1)}, bf16[2,8,4224]{2,1,0:T(8,128)(2,1)S(1)}, u32[]{:S(2)}, u32[]{:S(2)}) collective-permute-start(bf16[2,8,4224]{2,1,0:T(8,128)(2,1)S(1)} %get-tuple-element.32), channel_id=1, source_target_pairs={{0,1},{1,0},{2,3},{3,2},{4,5},{5,4},{6,7},{7,6},{8,9},{9,8},{10,11... | collective-permute-start | bytes 405512 | tf_op jit(solution)/shard_map/ppermute | solution.py:520
  43.0 5.3 %copy-start = (bf16[128,3584]{1,0:T(8,128)(2,1)S(1)}, bf16[128,3584]{1,0:T(8,128)(2,1)}, u32[]{:S(2)}) copy-start(bf16[128,3584]{1,0:T(8,128)(2,1)} %table.1) | copy-start | bytes 2752516
  43.1 5.3 %copy-start.1 = (s32[4]{0:T(128)S(1)}, s32[4]{0:T(128)}, u32[]{:S(2)}) copy-start(s32[4]{0:T(128)} %ids.3) | copy-start | bytes 52
  45.6 1.6 %collective-permute-start.14 = (bf16[2,8,3072]{2,1,0:T(8,128)(2,1)S(1)}, bf16[2,8,3072]{2,1,0:T(8,128)(2,1)S(1)}, u32[]{:S(2)}, u32[]{:S(2)}) collective-permute-start(bf16[2,8,3072]{2,1,0:T(8,128)(2,1)S(1)} %get-tuple-element.37), channel_id=1, source_target_pairs={{0,1},{1,0},{2,3},{3,2},{4,5},{5,4},{6,7},{7,6},{8,9},{9,8},{10,11... | collective-permute-start | bytes 294920 | tf_op jit(solution)/shard_map/ppermute | solution.py:520
  46.2 5.4 %collective-permute-start.13 = (bf16[8,4224]{1,0:T(8,128)(2,1)S(1)}, bf16[8,4224]{1,0:T(8,128)(2,1)S(1)}, u32[]{:S(2)}, u32[]{:S(2)}) collective-permute-start(bf16[8,4224]{1,0:T(8,128)(2,1)S(1)} %get-tuple-element.34), channel_id=1, source_target_pairs={{0,2},{1,3},{2,0},{3,1},{4,6},{5,7},{6,4},{7,5},{8,10},{9,11},{10,... | collective-permute-start | bytes 202760 | tf_op jit(solution)/shard_map/ppermute | solution.py:530
  47.2 4.4 %collective-permute-start.15 = (bf16[8,3072]{1,0:T(8,128)(2,1)S(1)}, bf16[8,3072]{1,0:T(8,128)(2,1)S(1)}, u32[]{:S(2)}, u32[]{:S(2)}) collective-permute-start(bf16[8,3072]{1,0:T(8,128)(2,1)S(1)} %get-tuple-element.39), channel_id=1, source_target_pairs={{0,2},{1,3},{2,0},{3,1},{4,6},{5,7},{6,4},{7,5},{8,10},{9,11},{10,... | collective-permute-start | bytes 147464 | tf_op jit(solution)/shard_map/ppermute | solution.py:530

commit v5 on v4

--- a/solution.py
+++ b/solution.py
@@ -19,7 +19,6 @@
 bf16 = jnp.bfloat16
 VMEM = pl.BlockSpec(memory_space=pltpu.VMEM)
 SMEM = pl.BlockSpec(memory_space=pltpu.SMEM)
-HBM = pl.BlockSpec(memory_space=pltpu.HBM)
 
 
 def target_of(index, step, count):
@@ -56,10 +55,36 @@
     return high, middle, rest - middle
 
 
+def mask_kernel(tokens, suffix_local, lengths, out):
+    rows = tokens // STEPS
+    suffix_all = rows * suffix_local
+    me = lax.axis_index("pre")
+    row_at = lax.broadcasted_iota(jnp.int32, out.shape, 0)
+    column = lax.broadcasted_iota(jnp.int32, out.shape, 1)
+    token = lax.rem(row_at, tokens)
+    row_of = token // STEPS
+    step = lax.rem(token, STEPS)
+    limit = pick(row_of, [lengths[r] for r in range(rows)])
+    in_suffix = (
+        (column < suffix_all)
+        & (column // suffix_local == row_of)
+        & (me * suffix_local + lax.rem(column, suffix_local) < limit)
+    )
+    fresh = column - suffix_all
+    in_new = (
+        (fresh >= 0)
+        & (fresh < tokens)
+        & (fresh // STEPS == row_of)
+        & (lax.rem(fresh + LANES * STEPS, STEPS) <= step)
+        & (me == 0)
+    )
+    out[...] = (in_suffix | in_new).astype(jnp.int32)
+
+
 def attend_kernel(
     pre_count,
     ids,
-    lengths,
+    mask,
     queries,
     prefix_keys,
     prefix_values,
@@ -70,28 +95,7 @@
     kv_scales,
     *rest,
 ):
-    outs, (scales, stage, sem) = rest[:pre_count], rest[pre_count : pre_count + 3]
-    held, (id_mem, length_mem, small_sem, held_sem) = rest[pre_count + 3 : -4], rest[-4:]
-    id_copy = pltpu.make_async_copy(ids, id_mem, small_sem.at[0])
-    length_copy = pltpu.make_async_copy(lengths, length_mem, small_sem.at[1])
-    id_copy.start()
-    length_copy.start()
-    sources = (
-        queries,
-        prefix_keys,
-        suffix_keys,
-        new_keys,
-        new_values,
-        suffix_values,
-        prefix_values,
-    )
-    loads = [
-        pltpu.make_async_copy(source, target, held_sem.at[at])
-        for at, (source, target) in enumerate(zip(sources, held))
-    ]
-    for copy in loads:
-        copy.start()
-    queries, prefix_keys, suffix_keys, new_keys, new_values, suffix_values, prefix_values = held
+    outs, (scales, stage) = rest[:pre_count], rest[pre_count:]
     rows = queries.shape[0]
     tokens = rows * STEPS
     suffix_local = suffix_keys.shape[1]
@@ -101,44 +105,13 @@
     block = HEADS * HD // pre_count
     block_heads = block // HD
     me = lax.axis_index("pre")
-    id_copy.wait()
-    copies = [
-        pltpu.make_async_copy(kv_scales.at[id_mem[r]], scales.at[r], sem.at[r])
-        for r in range(rows)
-    ]
-    for copy in copies:
-        copy.start()
-
-    length_copy.wait()
-    count = group * tokens
-    row_at = lax.broadcasted_iota(jnp.int32, (count, LANES), 0)
-    column = lax.broadcasted_iota(jnp.int32, (count, LANES), 1)
-    token = lax.rem(row_at, tokens)
-    row_of = token // STEPS
-    step = lax.rem(token, STEPS)
-    limit = pick(row_of, [length_mem[r] for r in range(rows)])
-    in_suffix = (
-        (column < suffix_all)
-        & (column // suffix_local == row_of)
-        & (me * suffix_local + lax.rem(column, suffix_local) < limit)
-    )
-    fresh = column - suffix_all
-    in_new = (
-        (fresh >= 0)
-        & (fresh < tokens)
-        & (fresh // STEPS == row_of)
-        & (lax.rem(fresh + LANES * STEPS, STEPS) <= step)
-        & (me == 0)
-    )
-    allowed = in_suffix | in_new
-
-    for copy in loads:
-        copy.wait()
+    allowed = mask[...] != 0
+    for r in range(rows):
+        scales[2 * r : 2 * r + 2, :] = kv_scales[ids[r]].astype(f32)
+
     query = queries[...].reshape(tokens, HEADS * HD).astype(f32)
     fill = jnp.zeros((LANES - suffix_all - tokens, width), f32)
-    for copy in copies:
-        copy.wait()
-    scale = scales[...].reshape(tokens, width).astype(f32)
+    scale = scales[...]
     odd = lax.rem(lax.broadcasted_iota(jnp.int32, scale.shape, 0), 2) == 1
     key_scale = jnp.where(odd, pltpu.roll(scale, 1, 0), scale)
     value_scale = jnp.where(odd, scale, pltpu.roll(scale, tokens - 1, 0))
@@ -407,39 +380,29 @@
         compiler_params=params(4),
     )(adapter_ids, ffn_scales)
 
+    suffix_local = suffix_keys.shape[1]
+    mask = pl.pallas_call(
+        functools.partial(mask_kernel, tokens, suffix_local),
+        in_specs=[SMEM],
+        out_specs=VMEM,
+        out_shape=shape_of((HEADS // KV_HEADS * tokens, LANES), jnp.int32),
+        compiler_params=params(1),
+        cost_estimate=cost(20),
+    )(suffix_lengths)
     partials = pl.pallas_call(
         functools.partial(attend_kernel, pre_count),
-        in_specs=[HBM] * 10,
+        in_specs=[SMEM] + [VMEM] * 9,
         out_specs=[VMEM] * pre_count,
         out_shape=[shape_of((tokens, block + LANES))] * pre_count,
         scratch_shapes=[
-            pltpu.VMEM((rows, 2, kv_width), bf16),
+            pltpu.VMEM((tokens, kv_width), f32),
             pltpu.VMEM((pre_count, tokens, block + LANES), bf16),
-            pltpu.SemaphoreType.DMA((rows,)),
-        ]
-        + [
-            pltpu.VMEM(source.shape, source.dtype)
-            for source in (
-                queries,
-                prefix_keys,
-                suffix_keys,
-                new_keys,
-                new_values,
-                suffix_values,
-                prefix_values,
-            )
-        ]
-        + [
-            pltpu.SMEM((rows,), jnp.int32),
-            pltpu.SMEM((rows,), jnp.int32),
-            pltpu.SemaphoreType.DMA((2,)),
-            pltpu.SemaphoreType.DMA((7,)),
-        ],
-        compiler_params=params(60),
+        ],
+        compiler_params=params(8),
         cost_estimate=cost(20),
     )(
         adapter_ids,
-        suffix_lengths,
+        mask,
         queries,
         prefix_keys,
         prefix_values,

time: 52.6 us -> 51.3 us (0.975)
  Pallas kernels: 14.9 us -> 13.6 us
    pallas_call x1 -> x2, Pallas kernels: 4.54 us -> 3.29 us  [the longest x1 2.71 us: per_device(): pl.pallas_call(functools.partial(attend_kernel, pre_count), in_specs=[SME...]
  transfers between devices with their start and end apart: 16 -> 16, of which waited for: 10 -> 10; matrix products, arithmetic and copies ran while one was open for 0% -> 0% of each run, Pallas kernels for 6% -> 7%
where the time goes in v5:
time: 51.3 us; the launch traced here: 51.1 us
  starting transfers between devices  18.7 us (36%)
  waiting for transfers between devices  16.9 us (33%)
  Pallas kernels  13.6 us (27%)
  between operations  1 us (2%)
  local copies, waits for them, and re-layouts  0.85 us (2%)
    ppermute x12, starting transfers between devices, shifted(): lax.ppermute(parts[s], axis, [(i, target_of(i, s, count)) for i in range(...  16 us
    ppermute x12, waiting for transfers between devices, shifted(): lax.ppermute(parts[s], axis, [(i, target_of(i, s, count)) for i in range(...  14.5 us
    pallas_call x1, Pallas kernels, per_device(): pl.pallas_call(functools.partial(feed_first_kernel, pre_count, row_count,...  3.69 us
    pallas_call x1, Pallas kernels, per_device(): pl.pallas_call(functools.partial(attend_kernel, pre_count), in_specs=[SME...  2.71 us
    pallas_call x1, Pallas kernels, per_device(): pl.pallas_call(functools.partial(feed_second_kernel, row_count, first, se...  2.5 us
    ppermute x2, waiting for transfers between devices, per_device(): lax.ppermute(sums[j], 'row', [(i, i ^ 2 * j) for i in range(row_count)])  2.46 us
    ppermute x2, starting transfers between devices, per_device(): lax.ppermute(sums[j], 'row', [(i, i ^ 2 * j) for i in range(row_count)])  2.13 us
    pallas_call x1, Pallas kernels, per_device(): pl.pallas_call(functools.partial(project_kernel, row_count, pre_count), i...  1.56 us
  transfers between devices with their start and end apart: 16, of which 10 were waited for; matrix products, arithmetic and copies ran while one was open for 0% of the time, Pallas kernels for 7%

profile of v5, /device:TPU:0, one launch (start us, length us, event | category | flops | bytes accessed | tf_op | source)
XLA Modules:
  0.0 51.1 jit_solution(11910197877676000785)
XLA Ops:
  0.7 0.0 copy-start.1
  0.7 0.7 %copy-done.13 = s32[4]{0:T(128)S(1)} copy-done((s32[4]{0:T(128)S(1)}, s32[4]{0:T(128)}, u32[]{:S(2)}) %copy-start.13) | copy-done | bytes 40
  1.5 0.6 %shard_map.158.mask = s32[64,128]{1,0:T(8,128)S(1)} custom-call(s32[4]{0:T(128)S(1)} %copy-done.13), custom_call_target="tpu_custom_call" | custom-call | flops 20000000000 | tf_op jit(solution)/shard_map/pallas_call | solution.py:384
  2.2 0.0 slice-start.7
  2.2 2.7 %shard_map.159 = (bf16[8,2176]{1,0:T(8,128)(2,1)S(1)}, bf16[8,2176]{1,0:T(8,128)(2,1)S(1)}, bf16[8,2176]{1,0:T(8,128)(2,1)S(1)}, bf16[8,2176]{1,0:T(8,128)(2,1)S(1)}) custom-call(s32[4]{0:T(128)S(1)} %copy-done.1, s32[64,128]{1,0:T(8,128)S(1)} %shard_map.158.mask, bf16[4,2,8192]{2,1,0:T(2,128)(2,1)S(1)} %copy-done.6, bf16[128,1024]{1,0:T(8,128)(2,1)S(1)} %copy-done.4, ...), custom_call_target="tpu_custom_call" | custom-call | flops 20000000000 | tf_op jit(solution)/shard_map/pallas_call | solution.py:392
  4.9 3.1 %collective-permute-start = (bf16[8,2176]{1,0:T(8,128)(2,1)S(1)}, bf16[8,2176]{1,0:T(8,128)(2,1)S(1)}, u32[]{:S(2)}, u32[]{:S(2)}) collective-permute-start(bf16[8,2176]{1,0:T(8,128)(2,1)S(1)} %get-tuple-element.22), channel_id=1, source_target_pairs={{0,4},{4,0},{8,12},{12,8},{1,5},{5,1},{9,13},{13,9},{2,6},{6,2},{1... | collective-permute-start | bytes 104456 | tf_op jit(solution)/shard_map/ppermute | solution.py:331
  8.0 2.6 %collective-permute-start.1 = (bf16[8,2176]{1,0:T(8,128)(2,1)S(1)}, bf16[8,2176]{1,0:T(8,128)(2,1)S(1)}, u32[]{:S(2)}, u32[]{:S(2)}) collective-permute-start(bf16[8,2176]{1,0:T(8,128)(2,1)S(1)} %get-tuple-element.23), channel_id=1, source_target_pairs={{0,8},{4,12},{8,0},{12,4},{1,9},{5,13},{9,1},{13,5},{2,10},{6,14},... | collective-permute-start | bytes 104456 | tf_op jit(solution)/shard_map/ppermute | solution.py:331
  10.6 0.0 collective-permute-start.2
  10.6 0.0 collective-permute-done.rest_1_
  10.6 2.9 %collective-permute-done.1.rest_2_ = bf16[8,2176]{1,0:T(8,128)(2,1)S(1)} collective-permute-done((bf16[8,2176]{1,0:T(8,128)(2,1)S(1)}, bf16[8,2176]{1,0:T(8,128)(2,1)S(1)}, u32[]{:S(2)}, u32[]{:S(2)}) %collective-permute-start.1) | collective-permute-done | bytes 34848 | tf_op jit(solution)/shard_map/ppermute | solution.py:331
  13.4 2.9 %collective-permute-done.2.rest_3_ = bf16[8,2176]{1,0:T(8,128)(2,1)S(1)} collective-permute-done((bf16[8,2176]{1,0:T(8,128)(2,1)S(1)}, bf16[8,2176]{1,0:T(8,128)(2,1)S(1)}, u32[]{:S(2)}, u32[]{:S(2)}) %collective-permute-start.2) | collective-permute-done | bytes 34848 | tf_op jit(solution)/shard_map/ppermute | solution.py:331
  16.3 0.3 shard_map.160.rest_0_
  16.6 0.0 copy-start.9
  16.6 0.1 collective-permute-start.3
  16.7 1.6 %collective-permute-start.4 = (bf16[8,2048]{1,0:T(8,128)(2,1)S(1)}, bf16[8,2048]{1,0:T(8,128)(2,1)S(1)}, u32[]{:S(2)}, u32[]{:S(2)}) collective-permute-start(bf16[8,2048]{1,0:T(8,128)(2,1)S(1)} %shard_map.160.rest_0_), channel_id=1, source_target_pairs={{0,2},{1,3},{2,0},{3,1},{4,6},{5,7},{6,4},{7,5},{8,10},{9,11},{10,... | collective-permute-start | bytes 98312 | tf_op jit(solution)/shard_map/ppermute | solution.py:331
  18.2 0.3 collective-permute-start.5
  18.5 0.0 collective-permute-done.3.rest_1_
  18.5 2.1 %collective-permute-done.4.rest_2_ = bf16[8,2048]{1,0:T(8,128)(2,1)S(1)} collective-permute-done((bf16[8,2048]{1,0:T(8,128)(2,1)S(1)}, bf16[8,2048]{1,0:T(8,128)(2,1)S(1)}, u32[]{:S(2)}, u32[]{:S(2)}) %collective-permute-start.4) | collective-permute-done | bytes 32800 | tf_op jit(solution)/shard_map/ppermute | solution.py:331
  20.6 0.9 %collective-permute-done.5.rest_3_ = bf16[8,2048]{1,0:T(8,128)(2,1)S(1)} collective-permute-done((bf16[8,2048]{1,0:T(8,128)(2,1)S(1)}, bf16[8,2048]{1,0:T(8,128)(2,1)S(1)}, u32[]{:S(2)}, u32[]{:S(2)}) %collective-permute-start.5) | collective-permute-done | bytes 32800 | tf_op jit(solution)/shard_map/ppermute | solution.py:331
  21.6 0.0 slice-start.1
  21.6 0.0 slice-start.2
  21.6 0.0 slice-start.3
  21.6 1.6 %shard_map.161 = (f32[8,2048]{1,0:T(8,128)S(1)}, bf16[8,2048]{1,0:T(8,128)(2,1)S(1)}, bf16[8,2048]{1,0:T(8,128)(2,1)S(1)}, bf16[8,2048]{1,0:T(8,128)(2,1)S(1)}) custom-call(bf16[8,2048]{1,0:T(8,128)(2,1)S(1)} %shard_map.160.rest_0_, bf16[8,2048]{1,0:T(8,128)(2,1)S(1)} %collective-permute-done.3.rest_1_, bf16[8,2048]{1,0:T(8,128)(2,1)S(1)} %collective-permute-done.4.rest_2_, ...), custom_call_target="tpu_custom_call" | custom-call | flops 40000000000 | tf_op jit(solution)/shard_map/pallas_call | solution.py:424
  23.2 0.1 collective-permute-start.6
  23.3 1.0 %collective-permute-start.7 = (bf16[8,2048]{1,0:T(8,128)(2,1)S(1)}, bf16[8,2048]{1,0:T(8,128)(2,1)S(1)}, u32[]{:S(2)}, u32[]{:S(2)}) collective-permute-start(bf16[8,2048]{1,0:T(8,128)(2,1)S(1)} %get-tuple-element.27), channel_id=1, source_target_pairs={{0,8},{4,12},{8,0},{12,4},{1,9},{5,13},{9,1},{13,5},{2,10},{6,14},... | collective-permute-start | bytes 98312 | tf_op jit(solution)/shard_map/ppermute | solution.py:331
  24.3 3.4 %collective-permute-start.8 = (bf16[8,2048]{1,0:T(8,128)(2,1)S(1)}, bf16[8,2048]{1,0:T(8,128)(2,1)S(1)}, u32[]{:S(2)}, u32[]{:S(2)}) collective-permute-start(bf16[8,2048]{1,0:T(8,128)(2,1)S(1)} %get-tuple-element.28), channel_id=1, source_target_pairs={{0,12},{4,8},{8,4},{12,0},{1,13},{5,9},{9,5},{13,1},{2,14},{6,10},... | collective-permute-start | bytes 98312 | tf_op jit(solution)/shard_map/ppermute | solution.py:331
  27.6 0.5 %collective-permute-done.7.rest_2_ = bf16[8,2048]{1,0:T(8,128)(2,1)S(1)} collective-permute-done((bf16[8,2048]{1,0:T(8,128)(2,1)S(1)}, bf16[8,2048]{1,0:T(8,128)(2,1)S(1)}, u32[]{:S(2)}, u32[]{:S(2)}) %collective-permute-start.7) | collective-permute-done | bytes 32800 | tf_op jit(solution)/shard_map/ppermute | solution.py:331
  28.1 1.8 %collective-permute-done.8.rest_3_ = bf16[8,2048]{1,0:T(8,128)(2,1)S(1)} collective-permute-done((bf16[8,2048]{1,0:T(8,128)(2,1)S(1)}, bf16[8,2048]{1,0:T(8,128)(2,1)S(1)}, u32[]{:S(2)}, u32[]{:S(2)}) %collective-permute-start.8) | collective-permute-done | bytes 32800 | tf_op jit(solution)/shard_map/ppermute | solution.py:331
  30.0 0.0 copy-start.12
  30.0 0.7 %shard_map.162 = (bf16[4,2,2048]{2,1,0:T(2,128)(2,1)}, bf16[8,2048]{1,0:T(8,128)(2,1)S(1)}) custom-call(bf16[4,2,2048]{2,1,0:T(2,128)(2,1)S(1)} %copy-done.9, f32[8,2048]{1,0:T(8,128)S(1)} %get-tuple-element.25.rest_0_, bf16[8,2048]{1,0:T(8,128)(2,1)S(1)} %collective-permute-done.6.rest_1_, bf16[8,2048]{1,0:T(8,128)(2,1)S(1)} %collective-permute-done.7.rest_2_, ...), custom_call_target="tpu_custom_call" | custom-call | flops 40000000000 | tf_op jit(solution)/shard_map/pallas_call | solution.py:438
  30.7 0.2 collective-permute-start.10
  30.8 3.2 %collective-permute-start.11 = (bf16[8,2048]{1,0:T(8,128)(2,1)S(1)}, bf16[8,2048]{1,0:T(8,128)(2,1)S(1)}, u32[]{:S(2)}, u32[]{:S(2)}) collective-permute-start(bf16[8,2048]{1,0:T(8,128)(2,1)S(1)} %get-tuple-element.30.rest_0_), channel_id=1, source_target_pairs={{0,12},{4,8},{8,4},{12,0},{1,13},{5,9},{9,5},{13,1},{2,14},{6,10},... | collective-permute-start | bytes 98312 | tf_op jit(solution)/shard_map/ppermute | solution.py:331
  34.0 0.6 %collective-permute-start.9 = (bf16[8,2048]{1,0:T(8,128)(2,1)S(1)}, bf16[8,2048]{1,0:T(8,128)(2,1)S(1)}, u32[]{:S(2)}, u32[]{:S(2)}) collective-permute-start(bf16[8,2048]{1,0:T(8,128)(2,1)S(1)} %get-tuple-element.30.rest_0_), channel_id=1, source_target_pairs={{0,4},{4,0},{8,12},{12,8},{1,5},{5,1},{9,13},{13,9},{2,6},{6,2},{1... | collective-permute-start | bytes 98312 | tf_op jit(solution)/shard_map/ppermute | solution.py:331
  34.6 0.9 %collective-permute-done.10.rest_2_ = bf16[8,2048]{1,0:T(8,128)(2,1)S(1)} collective-permute-done((bf16[8,2048]{1,0:T(8,128)(2,1)S(1)}, bf16[8,2048]{1,0:T(8,128)(2,1)S(1)}, u32[]{:S(2)}, u32[]{:S(2)}) %collective-permute-start.10) | collective-permute-done | bytes 32800 | tf_op jit(solution)/shard_map/ppermute | solution.py:331
  35.5 1.2 %collective-permute-done.11.rest_3_ = bf16[8,2048]{1,0:T(8,128)(2,1)S(1)} collective-permute-done((bf16[8,2048]{1,0:T(8,128)(2,1)S(1)}, bf16[8,2048]{1,0:T(8,128)(2,1)S(1)}, u32[]{:S(2)}, u32[]{:S(2)}) %collective-permute-start.11) | collective-permute-done | bytes 32800 | tf_op jit(solution)/shard_map/ppermute | solution.py:331
  36.7 1.3 %collective-permute-done.9.rest_1_ = bf16[8,2048]{1,0:T(8,128)(2,1)S(1)} collective-permute-done((bf16[8,2048]{1,0:T(8,128)(2,1)S(1)}, bf16[8,2048]{1,0:T(8,128)(2,1)S(1)}, u32[]{:S(2)}, u32[]{:S(2)}) %collective-permute-start.9) | collective-permute-done | bytes 32800 | tf_op jit(solution)/shard_map/ppermute | solution.py:331
  38.0 3.7 %shard_map.164 = (f32[2,8,4224]{2,1,0:T(8,128)S(1)}, bf16[2,8,4224]{2,1,0:T(8,128)(2,1)S(1)}, bf16[64,4096]{1,0:T(8,128)(2,1)S(1)}) custom-call(bf16[2048]{0:T(1024)(128)(2,1)S(1)} %copy-done.12, bf16[8,2048]{1,0:T(8,128)(2,1)S(1)} %get-tuple-element.30.rest_0_, bf16[8,2048]{1,0:T(8,128)(2,1)S(1)} %collective-permute-done.9.rest_1_, ...), custom_call_target="tpu_custom_call" | custom-call | flops 16000000000 | tf_op jit(solution)/shard_map/pallas_call | solution.py:451
  41.7 0.1 collective-permute-start.12
  41.8 0.0 copy-start
  41.8 0.0 copy-start.2
  41.8 2.5 %shard_map.166 = (f32[2,8,3072]{2,1,0:T(8,128)S(1)}, bf16[2,8,3072]{2,1,0:T(8,128)(2,1)S(1)}) custom-call(bf16[64,4096]{1,0:T(8,128)(2,1)S(1)} %get-tuple-element.35.spread, bf16[2048,2,3584]{2,1,0:T(2,128)(2,1)S(1)} %bitcast.1), custom_call_target="tpu_custom_call" | custom-call | flops 16000000000 | tf_op jit(solution)/shard_map/pallas_call | solution.py:467
  44.3 0.5 %collective-permute-start.14 = (bf16[2,8,3072]{2,1,0:T(8,128)(2,1)S(1)}, bf16[2,8,3072]{2,1,0:T(8,128)(2,1)S(1)}, u32[]{:S(2)}, u32[]{:S(2)}) collective-permute-start(bf16[2,8,3072]{2,1,0:T(8,128)(2,1)S(1)} %get-tuple-element.37), channel_id=1, source_target_pairs={{0,1},{1,0},{2,3},{3,2},{4,5},{5,4},{6,7},{7,6},{8,9},{9,8},{10,11... | collective-permute-start | bytes 294920 | tf_op jit(solution)/shard_map/ppermute | solution.py:483
  44.9 0.1 shard_map.165
  45.0 1.0 %collective-permute-start.13 = (bf16[8,4224]{1,0:T(8,128)(2,1)S(1)}, bf16[8,4224]{1,0:T(8,128)(2,1)S(1)}, u32[]{:S(2)}, u32[]{:S(2)}) collective-permute-start(bf16[8,4224]{1,0:T(8,128)(2,1)S(1)} %get-tuple-element.34), channel_id=1, source_target_pairs={{0,2},{1,3},{2,0},{3,1},{4,6},{5,7},{6,4},{7,5},{8,10},{9,11},{10,... | collective-permute-start | bytes 202760 | tf_op jit(solution)/shard_map/ppermute | solution.py:493
  46.0 1.2 %collective-permute-start.15 = (bf16[8,3072]{1,0:T(8,128)(2,1)S(1)}, bf16[8,3072]{1,0:T(8,128)(2,1)S(1)}, u32[]{:S(2)}, u32[]{:S(2)}) collective-permute-start(bf16[8,3072]{1,0:T(8,128)(2,1)S(1)} %get-tuple-element.39), channel_id=1, source_target_pairs={{0,2},{1,3},{2,0},{3,1},{4,6},{5,7},{6,4},{7,5},{8,10},{9,11},{10,... | collective-permute-start | bytes 147464 | tf_op jit(solution)/shard_map/ppermute | solution.py:493
  47.1 0.8 %shard_map.163.scales = f32[8,3584]{1,0:T(8,128)S(1)} custom-call(s32[4]{0:T(128)S(1)} %copy-done.2, bf16[128,3584]{1,0:T(8,128)(2,1)S(1)} %copy-done), custom_call_target="tpu_custom_call" | custom-call | tf_op jit(solution)/shard_map/pallas_call | solution.py:375
  47.9 2.5 %collective-permute-done.15.rest_3_ = bf16[8,3072]{1,0:T(8,128)(2,1)S(1)} collective-permute-done((bf16[8,3072]{1,0:T(8,128)(2,1)S(1)}, bf16[8,3072]{1,0:T(8,128)(2,1)S(1)}, u32[]{:S(2)}, u32[]{:S(2)}) %collective-permute-start.15) | collective-permute-done | bytes 49184 | tf_op jit(solution)/shard_map/ppermute | solution.py:493
  50.3 0.8 %shard_map.168 = bf16[4,2,3584]{2,1,0:T(2,128)(2,1)} custom-call(f32[8,3584]{1,0:T(8,128)S(1)} %shard_map.163.scales, f32[8,4224]{1,0:T(8,128)S(1)} %get-tuple-element.33.rest_0_, bf16[8,4224]{1,0:T(8,128)(2,1)S(1)} %collective-permute-done.13.rest_1_, f32[8,3072]{1,0:T(8,128)S(1)} %get-tuple-element.38.rest_2_, ...), custom_call_target="tpu_custom_call" | custom-call | tf_op jit(solution)/shard_map/pallas_call | solution.py:496
  (43 shorter events, 0.1 us)
Async XLA Ops:
  0.6 1.4 %copy-start.6 = (bf16[4,2,8192]{2,1,0:T(2,128)(2,1)S(1)}, bf16[4,2,8192]{2,1,0:T(2,128)(2,1)}, u32[]{:S(2)}) copy-start(bf16[4,2,8192]{2,1,0:T(2,128)(2,1)} %queries.1) | copy-start | bytes 393220
  0.6 1.4 %copy-start.4 = (bf16[128,1024]{1,0:T(8,128)(2,1)S(1)}, bf16[128,1024]{1,0:T(8,128)(2,1)}, u32[]{:S(2)}) copy-start(bf16[128,1024]{1,0:T(8,128)(2,1)} %prefix_keys.1) | copy-start | bytes 786436
  0.7 1.4 %copy-start.5 = (bf16[128,1024]{1,0:T(8,128)(2,1)S(1)}, bf16[128,1024]{1,0:T(8,128)(2,1)}, u32[]{:S(2)}) copy-start(bf16[128,1024]{1,0:T(8,128)(2,1)} %prefix_values.1) | copy-start | bytes 786436
  0.7 1.4 %copy-start.7 = (bf16[4,16,1024]{2,1,0:T(8,128)(2,1)S(1)}, bf16[4,16,1024]{2,1,0:T(8,128)(2,1)}, u32[]{:S(2)}) copy-start(bf16[4,16,1024]{2,1,0:T(8,128)(2,1)} %suffix_keys.1) | copy-start | bytes 393220
  0.7 1.4 %copy-start.8 = (bf16[4,16,1024]{2,1,0:T(8,128)(2,1)S(1)}, bf16[4,16,1024]{2,1,0:T(8,128)(2,1)}, u32[]{:S(2)}) copy-start(bf16[4,16,1024]{2,1,0:T(8,128)(2,1)} %suffix_values.1) | copy-start | bytes 393220
  0.7 1.4 %copy-start.10 = (bf16[4,2,1024]{2,1,0:T(2,128)(2,1)S(1)}, bf16[4,2,1024]{2,1,0:T(2,128)(2,1)}, u32[]{:S(2)}) copy-start(bf16[4,2,1024]{2,1,0:T(2,128)(2,1)} %new_keys.1) | copy-start | bytes 49156
  0.7 1.4 %copy-start.11 = (bf16[4,2,1024]{2,1,0:T(2,128)(2,1)S(1)}, bf16[4,2,1024]{2,1,0:T(2,128)(2,1)}, u32[]{:S(2)}) copy-start(bf16[4,2,1024]{2,1,0:T(2,128)(2,1)} %new_values.1) | copy-start | bytes 49156
  0.7 1.4 %copy-start.1 = (s32[4]{0:T(128)S(1)}, s32[4]{0:T(128)}, u32[]{:S(2)}) copy-start(s32[4]{0:T(128)} %ids.3) | copy-start | bytes 52
  0.7 1.4 %copy-start.3 = (bf16[128,2,1024]{2,1,0:T(2,128)(2,1)S(1)}, bf16[128,2,1024]{2,1,0:T(2,128)(2,1)}, u32[]{:S(2)}) copy-start(bf16[128,2,1024]{2,1,0:T(2,128)(2,1)} %kv_scales.1) | copy-start | bytes 1572868
  0.7 0.8 %copy-start.13 = (s32[4]{0:T(128)S(1)}, s32[4]{0:T(128)}, u32[]{:S(2)}) copy-start(s32[4]{0:T(128)} %lengths.1) | copy-start | bytes 52
  2.2 19.4 %slice-start.7 = ((s8[8388608]{0:T(1024)(128)(4,1)}), s8[4194304]{0:T(1024)(128)(4,1)S(1)}, s32[]{:S(2)}) async-start(s8[8388608]{0:T(1024)(128)(4,1)} %bitcast.2), calls=%async_computation.7 | async-start | bytes 8388608
  4.9 5.7 %collective-permute-start = (bf16[8,2176]{1,0:T(8,128)(2,1)S(1)}, bf16[8,2176]{1,0:T(8,128)(2,1)S(1)}, u32[]{:S(2)}, u32[]{:S(2)}) collective-permute-start(bf16[8,2176]{1,0:T(8,128)(2,1)S(1)} %get-tuple-element.22), channel_id=1, source_target_pairs={{0,4},{4,0},{8,12},{12,8},{1,5},{5,1},{9,13},{13,9},{2,6},{6,2},{1... | collective-permute-start | bytes 104456 | tf_op jit(solution)/shard_map/ppermute | solution.py:331
  8.0 5.5 %collective-permute-start.1 = (bf16[8,2176]{1,0:T(8,128)(2,1)S(1)}, bf16[8,2176]{1,0:T(8,128)(2,1)S(1)}, u32[]{:S(2)}, u32[]{:S(2)}) collective-permute-start(bf16[8,2176]{1,0:T(8,128)(2,1)S(1)} %get-tuple-element.23), channel_id=1, source_target_pairs={{0,8},{4,12},{8,0},{12,4},{1,9},{5,13},{9,1},{13,5},{2,10},{6,14},... | collective-permute-start | bytes 104456 | tf_op jit(solution)/shard_map/ppermute | solution.py:331
  10.6 5.7 %collective-permute-start.2 = (bf16[8,2176]{1,0:T(8,128)(2,1)S(1)}, bf16[8,2176]{1,0:T(8,128)(2,1)S(1)}, u32[]{:S(2)}, u32[]{:S(2)}) collective-permute-start(bf16[8,2176]{1,0:T(8,128)(2,1)S(1)} %get-tuple-element.24), channel_id=1, source_target_pairs={{0,12},{4,8},{8,4},{12,0},{1,13},{5,9},{9,5},{13,1},{2,14},{6,10},... | collective-permute-start | bytes 104456 | tf_op jit(solution)/shard_map/ppermute | solution.py:331
  16.3 5.3 %slice-start.8 = ((s8[8388608]{0:T(1024)(128)(4,1)}), s8[4194304]{0:T(1024)(128)(4,1)S(1)}, s32[]{:S(2)}) async-start(s8[8388608]{0:T(1024)(128)(4,1)} %bitcast.2), calls=%async_computation.8 | async-start | bytes 8388608
  16.6 13.4 %copy-start.9 = (bf16[4,2,2048]{2,1,0:T(2,128)(2,1)S(1)}, bf16[4,2,2048]{2,1,0:T(2,128)(2,1)}, u32[]{:S(2)}) copy-start(bf16[4,2,2048]{2,1,0:T(2,128)(2,1)} %hidden.1) | copy-start | bytes 98308
  16.6 1.9 %collective-permute-start.3 = (bf16[8,2048]{1,0:T(8,128)(2,1)S(1)}, bf16[8,2048]{1,0:T(8,128)(2,1)S(1)}, u32[]{:S(2)}, u32[]{:S(2)}) collective-permute-start(bf16[8,2048]{1,0:T(8,128)(2,1)S(1)} %shard_map.160.rest_0_), channel_id=1, source_target_pairs={{0,1},{1,0},{2,3},{3,2},{4,5},{5,4},{6,7},{7,6},{8,9},{9,8},{10,11... | collective-permute-start | bytes 98312 | tf_op jit(solution)/shard_map/ppermute | solution.py:331
  16.7 4.0 %collective-permute-start.4 = (bf16[8,2048]{1,0:T(8,128)(2,1)S(1)}, bf16[8,2048]{1,0:T(8,128)(2,1)S(1)}, u32[]{:S(2)}, u32[]{:S(2)}) collective-permute-start(bf16[8,2048]{1,0:T(8,128)(2,1)S(1)} %shard_map.160.rest_0_), channel_id=1, source_target_pairs={{0,2},{1,3},{2,0},{3,1},{4,6},{5,7},{6,4},{7,5},{8,10},{9,11},{10,... | collective-permute-start | bytes 98312 | tf_op jit(solution)/shard_map/ppermute | solution.py:331
  18.2 3.3 %collective-permute-start.5 = (bf16[8,2048]{1,0:T(8,128)(2,1)S(1)}, bf16[8,2048]{1,0:T(8,128)(2,1)S(1)}, u32[]{:S(2)}, u32[]{:S(2)}) collective-permute-start(bf16[8,2048]{1,0:T(8,128)(2,1)S(1)} %shard_map.160.rest_0_), channel_id=1, source_target_pairs={{0,3},{1,2},{2,1},{3,0},{4,7},{5,6},{6,5},{7,4},{8,11},{9,10},{10,... | collective-permute-start | bytes 98312 | tf_op jit(solution)/shard_map/ppermute | solution.py:331
  21.6 16.4 %slice-start = ((s8[29360128]{0:T(1024)(128)(4,1)}), s8[4194304]{0:T(1024)(128)(4,1)S(1)}, s32[]{:S(2)}) async-start(s8[29360128]{0:T(1024)(128)(4,1)} %bitcast), calls=%async_computation | async-start | bytes 8388608
  21.6 16.4 %slice-start.1 = ((s8[29360128]{0:T(1024)(128)(4,1)}), s8[4194304]{0:T(1024)(128)(4,1)S(1)}, s32[]{:S(2)}) async-start(s8[29360128]{0:T(1024)(128)(4,1)} %bitcast), calls=%async_computation.1 | async-start | bytes 8388608
  21.6 16.4 %slice-start.2 = ((s8[29360128]{0:T(1024)(128)(4,1)}), s8[4194304]{0:T(1024)(128)(4,1)S(1)}, s32[]{:S(2)}) async-start(s8[29360128]{0:T(1024)(128)(4,1)} %bitcast), calls=%async_computation.2 | async-start | bytes 8388608
  21.6 16.4 %slice-start.3 = ((s8[29360128]{0:T(1024)(128)(4,1)}), s8[4194304]{0:T(1024)(128)(4,1)S(1)}, s32[]{:S(2)}) async-start(s8[29360128]{0:T(1024)(128)(4,1)} %bitcast), calls=%async_computation.3 | async-start | bytes 8388608
  23.2 4.5 %collective-permute-start.6 = (bf16[8,2048]{1,0:T(8,128)(2,1)S(1)}, bf16[8,2048]{1,0:T(8,128)(2,1)S(1)}, u32[]{:S(2)}, u32[]{:S(2)}) collective-permute-start(bf16[8,2048]{1,0:T(8,128)(2,1)S(1)} %get-tuple-element.26), channel_id=1, source_target_pairs={{0,4},{4,0},{8,12},{12,8},{1,5},{5,1},{9,13},{13,9},{2,6},{6,2},{1... | collective-permute-start | bytes 98312 | tf_op jit(solution)/shard_map/ppermute | solution.py:331
  23.3 4.9 %collective-permute-start.7 = (bf16[8,2048]{1,0:T(8,128)(2,1)S(1)}, bf16[8,2048]{1,0:T(8,128)(2,1)S(1)}, u32[]{:S(2)}, u32[]{:S(2)}) collective-permute-start(bf16[8,2048]{1,0:T(8,128)(2,1)S(1)} %get-tuple-element.27), channel_id=1, source_target_pairs={{0,8},{4,12},{8,0},{12,4},{1,9},{5,13},{9,1},{13,5},{2,10},{6,14},... | collective-permute-start | bytes 98312 | tf_op jit(solution)/shard_map/ppermute | solution.py:331
  24.3 5.7 %collective-permute-start.8 = (bf16[8,2048]{1,0:T(8,128)(2,1)S(1)}, bf16[8,2048]{1,0:T(8,128)(2,1)S(1)}, u32[]{:S(2)}, u32[]{:S(2)}) collective-permute-start(bf16[8,2048]{1,0:T(8,128)(2,1)S(1)} %get-tuple-element.28), channel_id=1, source_target_pairs={{0,12},{4,8},{8,4},{12,0},{1,13},{5,9},{9,5},{13,1},{2,14},{6,10},... | collective-permute-start | bytes 98312 | tf_op jit(solution)/shard_map/ppermute | solution.py:331
  30.0 8.0 %slice-start.4 = ((s8[29360128]{0:T(1024)(128)(4,1)}), s8[4194304]{0:T(1024)(128)(4,1)S(1)}, s32[]{:S(2)}) async-start(s8[29360128]{0:T(1024)(128)(4,1)} %bitcast), calls=%async_computation.4 | async-start | bytes 8388608
  30.0 8.0 %slice-start.5 = ((s8[29360128]{0:T(1024)(128)(4,1)}), s8[4194304]{0:T(1024)(128)(4,1)S(1)}, s32[]{:S(2)}) async-start(s8[29360128]{0:T(1024)(128)(4,1)} %bitcast), calls=%async_computation.5 | async-start | bytes 8388608
  30.0 8.0 %slice-start.6 = ((s8[29360128]{0:T(1024)(128)(4,1)}), s8[4194304]{0:T(1024)(128)(4,1)S(1)}, s32[]{:S(2)}) async-start(s8[29360128]{0:T(1024)(128)(4,1)} %bitcast), calls=%async_computation.6 | async-start | bytes 8388608
  30.0 8.0 %copy-start.12 = (bf16[2048]{0:T(1024)(128)(2,1)S(1)}, bf16[2048]{0:T(1024)(128)(2,1)}, u32[]{:S(2)}) copy-start(bf16[2048]{0:T(1024)(128)(2,1)} %gain.1) | copy-start | bytes 12292
  30.7 4.8 %collective-permute-start.10 = (bf16[8,2048]{1,0:T(8,128)(2,1)S(1)}, bf16[8,2048]{1,0:T(8,128)(2,1)S(1)}, u32[]{:S(2)}, u32[]{:S(2)}) collective-permute-start(bf16[8,2048]{1,0:T(8,128)(2,1)S(1)} %get-tuple-element.30.rest_0_), channel_id=1, source_target_pairs={{0,8},{4,12},{8,0},{12,4},{1,9},{5,13},{9,1},{13,5},{2,10},{6,14},... | collective-permute-start | bytes 98312 | tf_op jit(solution)/shard_map/ppermute | solution.py:331
  30.8 5.8 %collective-permute-start.11 = (bf16[8,2048]{1,0:T(8,128)(2,1)S(1)}, bf16[8,2048]{1,0:T(8,128)(2,1)S(1)}, u32[]{:S(2)}, u32[]{:S(2)}) collective-permute-start(bf16[8,2048]{1,0:T(8,128)(2,1)S(1)} %get-tuple-element.30.rest_0_), channel_id=1, source_target_pairs={{0,12},{4,8},{8,4},{12,0},{1,13},{5,9},{9,5},{13,1},{2,14},{6,10},... | collective-permute-start | bytes 98312 | tf_op jit(solution)/shard_map/ppermute | solution.py:331
  34.0 3.9 %collective-permute-start.9 = (bf16[8,2048]{1,0:T(8,128)(2,1)S(1)}, bf16[8,2048]{1,0:T(8,128)(2,1)S(1)}, u32[]{:S(2)}, u32[]{:S(2)}) collective-permute-start(bf16[8,2048]{1,0:T(8,128)(2,1)S(1)} %get-tuple-element.30.rest_0_), channel_id=1, source_target_pairs={{0,4},{4,0},{8,12},{12,8},{1,5},{5,1},{9,13},{13,9},{2,6},{6,2},{1... | collective-permute-start | bytes 98312 | tf_op jit(solution)/shard_map/ppermute | solution.py:331
  41.7 3.1 %collective-permute-start.12 = (bf16[2,8,4224]{2,1,0:T(8,128)(2,1)S(1)}, bf16[2,8,4224]{2,1,0:T(8,128)(2,1)S(1)}, u32[]{:S(2)}, u32[]{:S(2)}) collective-permute-start(bf16[2,8,4224]{2,1,0:T(8,128)(2,1)S(1)} %get-tuple-element.32), channel_id=1, source_target_pairs={{0,1},{1,0},{2,3},{3,2},{4,5},{5,4},{6,7},{7,6},{8,9},{9,8},{10,11... | collective-permute-start | bytes 405512 | tf_op jit(solution)/shard_map/ppermute | solution.py:483
  41.8 5.3 %copy-start = (bf16[128,3584]{1,0:T(8,128)(2,1)S(1)}, bf16[128,3584]{1,0:T(8,128)(2,1)}, u32[]{:S(2)}) copy-start(bf16[128,3584]{1,0:T(8,128)(2,1)} %table.1) | copy-start | bytes 2752516
  41.8 5.3 %copy-start.2 = (s32[4]{0:T(128)S(1)}, s32[4]{0:T(128)}, u32[]{:S(2)}) copy-start(s32[4]{0:T(128)} %ids.3) | copy-start | bytes 52
  44.3 1.6 %collective-permute-start.14 = (bf16[2,8,3072]{2,1,0:T(8,128)(2,1)S(1)}, bf16[2,8,3072]{2,1,0:T(8,128)(2,1)S(1)}, u32[]{:S(2)}, u32[]{:S(2)}) collective-permute-start(bf16[2,8,3072]{2,1,0:T(8,128)(2,1)S(1)} %get-tuple-element.37), channel_id=1, source_target_pairs={{0,1},{1,0},{2,3},{3,2},{4,5},{5,4},{6,7},{7,6},{8,9},{9,8},{10,11... | collective-permute-start | bytes 294920 | tf_op jit(solution)/shard_map/ppermute | solution.py:483
  45.0 5.4 %collective-permute-start.13 = (bf16[8,4224]{1,0:T(8,128)(2,1)S(1)}, bf16[8,4224]{1,0:T(8,128)(2,1)S(1)}, u32[]{:S(2)}, u32[]{:S(2)}) collective-permute-start(bf16[8,4224]{1,0:T(8,128)(2,1)S(1)} %get-tuple-element.34), channel_id=1, source_target_pairs={{0,2},{1,3},{2,0},{3,1},{4,6},{5,7},{6,4},{7,5},{8,10},{9,11},{10,... | collective-permute-start | bytes 202760 | tf_op jit(solution)/shard_map/ppermute | solution.py:493
  46.0 4.4 %collective-permute-start.15 = (bf16[8,3072]{1,0:T(8,128)(2,1)S(1)}, bf16[8,3072]{1,0:T(8,128)(2,1)S(1)}, u32[]{:S(2)}, u32[]{:S(2)}) collective-permute-start(bf16[8,3072]{1,0:T(8,128)(2,1)S(1)} %get-tuple-element.39), channel_id=1, source_target_pairs={{0,2},{1,3},{2,0},{3,1},{4,6},{5,7},{6,4},{7,5},{8,10},{9,11},{10,... | collective-permute-start | bytes 147464 | tf_op jit(solution)/shard_map/ppermute | solution.py:493

commit v6 on v5

--- a/solution.py
+++ b/solution.py
@@ -333,6 +333,18 @@
     ]
 
 
+def gathered_pairs(value, axis):
+    count = lax.axis_size(axis)
+    if count & (count - 1) or count < 2:
+        return shifted([value] * count, axis)
+    near = [(i, i ^ 1) for i in range(count)]
+    parts = []
+    for s in range(0, count, 2):
+        far = lax.ppermute(value, axis, [(i, i ^ s) for i in range(count)]) if s else value
+        parts += [far, lax.ppermute(far, axis, near)]
+    return parts
+
+
 def shape_of(dims, dtype=bf16):
     return jax.ShapeDtypeStruct(dims, dtype)
 
@@ -420,7 +432,7 @@
         compiler_params=params(4),
         cost_estimate=cost(40),
     )(*shifted(partials, "pre"))
-    gathered = shifted([mixed] * row_count, "row")
+    gathered = gathered_pairs(mixed, "row")
     products = pl.pallas_call(
         functools.partial(project_kernel, row_count, pre_count),
         in_specs=[VMEM] * (row_count + 1),
@@ -443,7 +455,7 @@
         compiler_params=params(4),
         cost_estimate=cost(40),
     )(hidden, *shifted(products, "pre"))
-    stacked = shifted([sent] * pre_count, "pre")
+    stacked = gathered_pairs(sent, "pre")
     total_rows = pre_count * amount
     half = row_count // 2
     first, second = split_columns(wide)

time: 51.3 us -> 53.3 us (1.039)
  waiting for transfers between devices: 16.9 us -> 18 us
  starting transfers between devices: 18.7 us -> 19.7 us
    ppermute x0 -> x6, waiting for transfers between devices: none -> 7.42 us  [the longest x4 4.11 us: gathered_pairs(): parts += [far, lax.ppermute(far, axis, near)]]
    ppermute x0 -> x6, starting transfers between devices: none -> 6.49 us  [the longest x4 4.75 us: gathered_pairs(): parts += [far, lax.ppermute(far, axis, near)]]
    ppermute x12 -> x6, waiting for transfers between devices: 14.5 us -> 8.08 us  [shifted(): lax.ppermute(parts[s], axis, [(i, target_of(i, s, count)) for i in range(...]
    ppermute x12 -> x6, starting transfers between devices: 16 us -> 10.1 us  [shifted(): lax.ppermute(parts[s], axis, [(i, target_of(i, s, count)) for i in range(...]
  transfers between devices with their start and end apart: 16 -> 16, of which waited for: 10 -> 9; matrix products, arithmetic and copies ran while one was open for 0% -> 0% of each run, Pallas kernels for 7% -> 6%
where the time goes in v6:
time: 53.3 us; the launch traced here: 53.1 us
  starting transfers between devices  19.7 us (37%)
  waiting for transfers between devices  18 us (34%)
  Pallas kernels  13.6 us (26%)
  between operations  0.99 us (2%)
  local copies, waits for them, and re-layouts  0.85 us (2%)
    ppermute x6, starting transfers between devices, shifted(): lax.ppermute(parts[s], axis, [(i, target_of(i, s, count)) for i in range(...  10.1 us
    ppermute x6, waiting for transfers between devices, shifted(): lax.ppermute(parts[s], axis, [(i, target_of(i, s, count)) for i in range(...  8.08 us
    ppermute x4, starting transfers between devices, gathered_pairs(): parts += [far, lax.ppermute(far, axis, near)]  4.75 us
    ppermute x4, waiting for transfers between devices, gathered_pairs(): parts += [far, lax.ppermute(far, axis, near)]  4.11 us
    pallas_call x1, Pallas kernels, per_device(): pl.pallas_call(functools.partial(feed_first_kernel, pre_count, row_count,...  3.7 us
    ppermute x2, waiting for transfers between devices, gathered_pairs(): lax.ppermute(value, axis, [(i, i ^ s) for i in range(count)])  3.31 us
    pallas_call x1, Pallas kernels, per_device(): pl.pallas_call(functools.partial(attend_kernel, pre_count), in_specs=[SME...  2.71 us
    ppermute x2, waiting for transfers between devices, per_device(): lax.ppermute(sums[j], 'row', [(i, i ^ 2 * j) for i in range(row_count)])  2.51 us
  transfers between devices with their start and end apart: 16, of which 9 were waited for; matrix products, arithmetic and copies ran while one was open for 0% of the time, Pallas kernels for 6%

profile of v6, /device:TPU:0, one launch (start us, length us, event | category | flops | bytes accessed | tf_op | source)
XLA Modules:
  0.0 53.1 jit_solution(2657950150533056204)
XLA Ops:
  0.7 0.0 copy-start.1
  0.7 0.7 %copy-done.13 = s32[4]{0:T(128)S(1)} copy-done((s32[4]{0:T(128)S(1)}, s32[4]{0:T(128)}, u32[]{:S(2)}) %copy-start.13) | copy-done | bytes 40
  1.5 0.6 %shard_map.158.mask = s32[64,128]{1,0:T(8,128)S(1)} custom-call(s32[4]{0:T(128)S(1)} %copy-done.13), custom_call_target="tpu_custom_call" | custom-call | flops 20000000000 | tf_op jit(solution)/shard_map/pallas_call | solution.py:396
  2.2 0.0 slice-start.7
  2.2 2.7 %shard_map.159 = (bf16[8,2176]{1,0:T(8,128)(2,1)S(1)}, bf16[8,2176]{1,0:T(8,128)(2,1)S(1)}, bf16[8,2176]{1,0:T(8,128)(2,1)S(1)}, bf16[8,2176]{1,0:T(8,128)(2,1)S(1)}) custom-call(s32[4]{0:T(128)S(1)} %copy-done.1, s32[64,128]{1,0:T(8,128)S(1)} %shard_map.158.mask, bf16[4,2,8192]{2,1,0:T(2,128)(2,1)S(1)} %copy-done.6, bf16[128,1024]{1,0:T(8,128)(2,1)S(1)} %copy-done.4, ...), custom_call_target="tpu_custom_call" | custom-call | flops 20000000000 | tf_op jit(solution)/shard_map/pallas_call | solution.py:404
  4.9 3.1 %collective-permute-start = (bf16[8,2176]{1,0:T(8,128)(2,1)S(1)}, bf16[8,2176]{1,0:T(8,128)(2,1)S(1)}, u32[]{:S(2)}, u32[]{:S(2)}) collective-permute-start(bf16[8,2176]{1,0:T(8,128)(2,1)S(1)} %get-tuple-element.22), channel_id=1, source_target_pairs={{0,4},{4,0},{8,12},{12,8},{1,5},{5,1},{9,13},{13,9},{2,6},{6,2},{1... | collective-permute-start | bytes 104456 | tf_op jit(solution)/shard_map/ppermute | solution.py:331
  8.0 2.6 %collective-permute-start.1 = (bf16[8,2176]{1,0:T(8,128)(2,1)S(1)}, bf16[8,2176]{1,0:T(8,128)(2,1)S(1)}, u32[]{:S(2)}, u32[]{:S(2)}) collective-permute-start(bf16[8,2176]{1,0:T(8,128)(2,1)S(1)} %get-tuple-element.23), channel_id=1, source_target_pairs={{0,8},{4,12},{8,0},{12,4},{1,9},{5,13},{9,1},{13,5},{2,10},{6,14},... | collective-permute-start | bytes 104456 | tf_op jit(solution)/shard_map/ppermute | solution.py:331
  10.6 0.0 collective-permute-start.2
  10.6 0.0 collective-permute-done.rest_1_
  10.6 2.9 %collective-permute-done.1.rest_2_ = bf16[8,2176]{1,0:T(8,128)(2,1)S(1)} collective-permute-done((bf16[8,2176]{1,0:T(8,128)(2,1)S(1)}, bf16[8,2176]{1,0:T(8,128)(2,1)S(1)}, u32[]{:S(2)}, u32[]{:S(2)}) %collective-permute-start.1) | collective-permute-done | bytes 34848 | tf_op jit(solution)/shard_map/ppermute | solution.py:331
  13.4 2.9 %collective-permute-done.2.rest_3_ = bf16[8,2176]{1,0:T(8,128)(2,1)S(1)} collective-permute-done((bf16[8,2176]{1,0:T(8,128)(2,1)S(1)}, bf16[8,2176]{1,0:T(8,128)(2,1)S(1)}, u32[]{:S(2)}, u32[]{:S(2)}) %collective-permute-start.2) | collective-permute-done | bytes 34848 | tf_op jit(solution)/shard_map/ppermute | solution.py:331
  16.3 0.3 shard_map.160.rest_0_
  16.6 0.0 copy-start.9
  16.6 1.6 %collective-permute-start.4 = (bf16[8,2048]{1,0:T(8,128)(2,1)S(1)}, bf16[8,2048]{1,0:T(8,128)(2,1)S(1)}, u32[]{:S(2)}, u32[]{:S(2)}) collective-permute-start(bf16[8,2048]{1,0:T(8,128)(2,1)S(1)} %shard_map.160.rest_0_), channel_id=1, source_target_pairs={{0,2},{1,3},{2,0},{3,1},{4,6},{5,7},{6,4},{7,5},{8,10},{9,11},{10,... | collective-permute-start | bytes 98312 | tf_op jit(solution)/shard_map/ppermute | solution.py:343
  18.1 2.4 %collective-permute-done.4.rest_2_ = bf16[8,2048]{1,0:T(8,128)(2,1)S(1)} collective-permute-done((bf16[8,2048]{1,0:T(8,128)(2,1)S(1)}, bf16[8,2048]{1,0:T(8,128)(2,1)S(1)}, u32[]{:S(2)}, u32[]{:S(2)}) %collective-permute-start.4) | collective-permute-done | bytes 32800 | tf_op jit(solution)/shard_map/ppermute | solution.py:343
  20.6 0.0 collective-permute-start.5
  20.6 0.0 collective-permute-done.3.rest_1_
  20.6 1.2 %collective-permute-done.5.rest_3_ = bf16[8,2048]{1,0:T(8,128)(2,1)S(1)} collective-permute-done((bf16[8,2048]{1,0:T(8,128)(2,1)S(1)}, bf16[8,2048]{1,0:T(8,128)(2,1)S(1)}, u32[]{:S(2)}, u32[]{:S(2)}) %collective-permute-start.5) | collective-permute-done | bytes 32800 | tf_op jit(solution)/shard_map/ppermute | solution.py:344
  21.8 0.0 slice-start.1
  21.8 0.0 slice-start.2
  21.8 0.0 slice-start.3
  21.8 1.6 %shard_map.161 = (f32[8,2048]{1,0:T(8,128)S(1)}, bf16[8,2048]{1,0:T(8,128)(2,1)S(1)}, bf16[8,2048]{1,0:T(8,128)(2,1)S(1)}, bf16[8,2048]{1,0:T(8,128)(2,1)S(1)}) custom-call(bf16[8,2048]{1,0:T(8,128)(2,1)S(1)} %shard_map.160.rest_0_, bf16[8,2048]{1,0:T(8,128)(2,1)S(1)} %collective-permute-done.3.rest_1_, bf16[8,2048]{1,0:T(8,128)(2,1)S(1)} %collective-permute-done.4.rest_2_, ...), custom_call_target="tpu_custom_call" | custom-call | flops 40000000000 | tf_op jit(solution)/shard_map/pallas_call | solution.py:436
  23.4 0.1 collective-permute-start.6
  23.5 1.0 %collective-permute-start.7 = (bf16[8,2048]{1,0:T(8,128)(2,1)S(1)}, bf16[8,2048]{1,0:T(8,128)(2,1)S(1)}, u32[]{:S(2)}, u32[]{:S(2)}) collective-permute-start(bf16[8,2048]{1,0:T(8,128)(2,1)S(1)} %get-tuple-element.27), channel_id=1, source_target_pairs={{0,8},{4,12},{8,0},{12,4},{1,9},{5,13},{9,1},{13,5},{2,10},{6,14},... | collective-permute-start | bytes 98312 | tf_op jit(solution)/shard_map/ppermute | solution.py:331
  24.5 3.4 %collective-permute-start.8 = (bf16[8,2048]{1,0:T(8,128)(2,1)S(1)}, bf16[8,2048]{1,0:T(8,128)(2,1)S(1)}, u32[]{:S(2)}, u32[]{:S(2)}) collective-permute-start(bf16[8,2048]{1,0:T(8,128)(2,1)S(1)} %get-tuple-element.28), channel_id=1, source_target_pairs={{0,12},{4,8},{8,4},{12,0},{1,13},{5,9},{9,5},{13,1},{2,14},{6,10},... | collective-permute-start | bytes 98312 | tf_op jit(solution)/shard_map/ppermute | solution.py:331
  27.8 0.0 collective-permute-done.6.rest_1_
  27.8 0.5 collective-permute-done.7.rest_2_
  28.4 1.8 %collective-permute-done.8.rest_3_ = bf16[8,2048]{1,0:T(8,128)(2,1)S(1)} collective-permute-done((bf16[8,2048]{1,0:T(8,128)(2,1)S(1)}, bf16[8,2048]{1,0:T(8,128)(2,1)S(1)}, u32[]{:S(2)}, u32[]{:S(2)}) %collective-permute-start.8) | collective-permute-done | bytes 32800 | tf_op jit(solution)/shard_map/ppermute | solution.py:331
  30.2 0.0 copy-start.12
  30.2 0.7 %shard_map.162 = (bf16[4,2,2048]{2,1,0:T(2,128)(2,1)}, bf16[8,2048]{1,0:T(8,128)(2,1)S(1)}) custom-call(bf16[4,2,2048]{2,1,0:T(2,128)(2,1)S(1)} %copy-done.9, f32[8,2048]{1,0:T(8,128)S(1)} %get-tuple-element.25.rest_0_, bf16[8,2048]{1,0:T(8,128)(2,1)S(1)} %collective-permute-done.6.rest_1_, bf16[8,2048]{1,0:T(8,128)(2,1)S(1)} %collective-permute-done.7.rest_2_, ...), custom_call_target="tpu_custom_call" | custom-call | flops 40000000000 | tf_op jit(solution)/shard_map/pallas_call | solution.py:450
  30.9 0.2 collective-permute-start.10
  31.1 3.7 %collective-permute-start.9 = (bf16[8,2048]{1,0:T(8,128)(2,1)S(1)}, bf16[8,2048]{1,0:T(8,128)(2,1)S(1)}, u32[]{:S(2)}, u32[]{:S(2)}) collective-permute-start(bf16[8,2048]{1,0:T(8,128)(2,1)S(1)} %get-tuple-element.30.rest_0_), channel_id=1, source_target_pairs={{0,4},{4,0},{8,12},{12,8},{1,5},{5,1},{9,13},{13,9},{2,6},{6,2},{1... | collective-permute-start | bytes 98312 | tf_op jit(solution)/shard_map/ppermute | solution.py:344
  34.8 0.9 %collective-permute-done.10.rest_2_ = bf16[8,2048]{1,0:T(8,128)(2,1)S(1)} collective-permute-done((bf16[8,2048]{1,0:T(8,128)(2,1)S(1)}, bf16[8,2048]{1,0:T(8,128)(2,1)S(1)}, u32[]{:S(2)}, u32[]{:S(2)}) %collective-permute-start.10) | collective-permute-done | bytes 32800 | tf_op jit(solution)/shard_map/ppermute | solution.py:343
  35.7 1.0 %collective-permute-start.11 = (bf16[8,2048]{1,0:T(8,128)(2,1)S(1)}, bf16[8,2048]{1,0:T(8,128)(2,1)S(1)}, u32[]{:S(2)}, u32[]{:S(2)}) collective-permute-start(bf16[8,2048]{1,0:T(8,128)(2,1)S(1)} %collective-permute-done.10.rest_2_), channel_id=1, source_target_pairs={{0,4},{4,0},{8,12},{12,8},{1,5},{5,1},{9,13},{13,9},{2,6},{6,2},{1... | collective-permute-start | bytes 98312 | tf_op jit(solution)/shard_map/ppermute | solution.py:344
  36.7 0.0 collective-permute-done.9.rest_1_
  36.7 2.9 %collective-permute-done.11.rest_3_ = bf16[8,2048]{1,0:T(8,128)(2,1)S(1)} collective-permute-done((bf16[8,2048]{1,0:T(8,128)(2,1)S(1)}, bf16[8,2048]{1,0:T(8,128)(2,1)S(1)}, u32[]{:S(2)}, u32[]{:S(2)}) %collective-permute-start.11) | collective-permute-done | bytes 32800 | tf_op jit(solution)/shard_map/ppermute | solution.py:344
  39.7 3.7 %shard_map.164 = (f32[2,8,4224]{2,1,0:T(8,128)S(1)}, bf16[2,8,4224]{2,1,0:T(8,128)(2,1)S(1)}, bf16[64,4096]{1,0:T(8,128)(2,1)S(1)}) custom-call(bf16[2048]{0:T(1024)(128)(2,1)S(1)} %copy-done.12, bf16[8,2048]{1,0:T(8,128)(2,1)S(1)} %get-tuple-element.30.rest_0_, bf16[8,2048]{1,0:T(8,128)(2,1)S(1)} %collective-permute-done.9.rest_1_, ...), custom_call_target="tpu_custom_call" | custom-call | flops 16000000000 | tf_op jit(solution)/shard_map/pallas_call | solution.py:463
  43.4 0.1 collective-permute-start.12
  43.5 0.0 copy-start
  43.5 0.0 copy-start.2
  43.5 2.5 %shard_map.166 = (f32[2,8,3072]{2,1,0:T(8,128)S(1)}, bf16[2,8,3072]{2,1,0:T(8,128)(2,1)S(1)}) custom-call(bf16[64,4096]{1,0:T(8,128)(2,1)S(1)} %get-tuple-element.35.spread, bf16[2048,2,3584]{2,1,0:T(2,128)(2,1)S(1)} %bitcast.1), custom_call_target="tpu_custom_call" | custom-call | flops 16000000000 | tf_op jit(solution)/shard_map/pallas_call | solution.py:479
  46.0 0.5 %collective-permute-start.14 = (bf16[2,8,3072]{2,1,0:T(8,128)(2,1)S(1)}, bf16[2,8,3072]{2,1,0:T(8,128)(2,1)S(1)}, u32[]{:S(2)}, u32[]{:S(2)}) collective-permute-start(bf16[2,8,3072]{2,1,0:T(8,128)(2,1)S(1)} %get-tuple-element.37), channel_id=1, source_target_pairs={{0,1},{1,0},{2,3},{3,2},{4,5},{5,4},{6,7},{7,6},{8,9},{9,8},{10,11... | collective-permute-start | bytes 294920 | tf_op jit(solution)/shard_map/ppermute | solution.py:495
  46.5 0.1 shard_map.165
  46.6 1.6 %collective-permute-start.13 = (bf16[8,4224]{1,0:T(8,128)(2,1)S(1)}, bf16[8,4224]{1,0:T(8,128)(2,1)S(1)}, u32[]{:S(2)}, u32[]{:S(2)}) collective-permute-start(bf16[8,4224]{1,0:T(8,128)(2,1)S(1)} %get-tuple-element.34), channel_id=1, source_target_pairs={{0,2},{1,3},{2,0},{3,1},{4,6},{5,7},{6,4},{7,5},{8,10},{9,11},{10,... | collective-permute-start | bytes 202760 | tf_op jit(solution)/shard_map/ppermute | solution.py:505
  48.2 0.9 %collective-permute-start.15 = (bf16[8,3072]{1,0:T(8,128)(2,1)S(1)}, bf16[8,3072]{1,0:T(8,128)(2,1)S(1)}, u32[]{:S(2)}, u32[]{:S(2)}) collective-permute-start(bf16[8,3072]{1,0:T(8,128)(2,1)S(1)} %get-tuple-element.39), channel_id=1, source_target_pairs={{0,2},{1,3},{2,0},{3,1},{4,6},{5,7},{6,4},{7,5},{8,10},{9,11},{10,... | collective-permute-start | bytes 147464 | tf_op jit(solution)/shard_map/ppermute | solution.py:505
  49.1 0.8 %shard_map.163.scales = f32[8,3584]{1,0:T(8,128)S(1)} custom-call(s32[4]{0:T(128)S(1)} %copy-done.2, bf16[128,3584]{1,0:T(8,128)(2,1)S(1)} %copy-done), custom_call_target="tpu_custom_call" | custom-call | tf_op jit(solution)/shard_map/pallas_call | solution.py:387
  49.8 2.5 %collective-permute-done.15.rest_3_ = bf16[8,3072]{1,0:T(8,128)(2,1)S(1)} collective-permute-done((bf16[8,3072]{1,0:T(8,128)(2,1)S(1)}, bf16[8,3072]{1,0:T(8,128)(2,1)S(1)}, u32[]{:S(2)}, u32[]{:S(2)}) %collective-permute-start.15) | collective-permute-done | bytes 49184 | tf_op jit(solution)/shard_map/ppermute | solution.py:505
  52.4 0.8 %shard_map.168 = bf16[4,2,3584]{2,1,0:T(2,128)(2,1)} custom-call(f32[8,3584]{1,0:T(8,128)S(1)} %shard_map.163.scales, f32[8,4224]{1,0:T(8,128)S(1)} %get-tuple-element.33.rest_0_, bf16[8,4224]{1,0:T(8,128)(2,1)S(1)} %collective-permute-done.13.rest_1_, f32[8,3072]{1,0:T(8,128)S(1)} %get-tuple-element.38.rest_2_, ...), custom_call_target="tpu_custom_call" | custom-call | tf_op jit(solution)/shard_map/pallas_call | solution.py:508
  (43 shorter events, 0.1 us)
Async XLA Ops:
  0.6 1.4 %copy-start.6 = (bf16[4,2,8192]{2,1,0:T(2,128)(2,1)S(1)}, bf16[4,2,8192]{2,1,0:T(2,128)(2,1)}, u32[]{:S(2)}) copy-start(bf16[4,2,8192]{2,1,0:T(2,128)(2,1)} %queries.1) | copy-start | bytes 393220
  0.6 1.4 %copy-start.4 = (bf16[128,1024]{1,0:T(8,128)(2,1)S(1)}, bf16[128,1024]{1,0:T(8,128)(2,1)}, u32[]{:S(2)}) copy-start(bf16[128,1024]{1,0:T(8,128)(2,1)} %prefix_keys.1) | copy-start | bytes 786436
  0.7 1.4 %copy-start.5 = (bf16[128,1024]{1,0:T(8,128)(2,1)S(1)}, bf16[128,1024]{1,0:T(8,128)(2,1)}, u32[]{:S(2)}) copy-start(bf16[128,1024]{1,0:T(8,128)(2,1)} %prefix_values.1) | copy-start | bytes 786436
  0.7 1.4 %copy-start.7 = (bf16[4,16,1024]{2,1,0:T(8,128)(2,1)S(1)}, bf16[4,16,1024]{2,1,0:T(8,128)(2,1)}, u32[]{:S(2)}) copy-start(bf16[4,16,1024]{2,1,0:T(8,128)(2,1)} %suffix_keys.1) | copy-start | bytes 393220
  0.7 1.4 %copy-start.8 = (bf16[4,16,1024]{2,1,0:T(8,128)(2,1)S(1)}, bf16[4,16,1024]{2,1,0:T(8,128)(2,1)}, u32[]{:S(2)}) copy-start(bf16[4,16,1024]{2,1,0:T(8,128)(2,1)} %suffix_values.1) | copy-start | bytes 393220
  0.7 1.4 %copy-start.10 = (bf16[4,2,1024]{2,1,0:T(2,128)(2,1)S(1)}, bf16[4,2,1024]{2,1,0:T(2,128)(2,1)}, u32[]{:S(2)}) copy-start(bf16[4,2,1024]{2,1,0:T(2,128)(2,1)} %new_keys.1) | copy-start | bytes 49156
  0.7 1.4 %copy-start.11 = (bf16[4,2,1024]{2,1,0:T(2,128)(2,1)S(1)}, bf16[4,2,1024]{2,1,0:T(2,128)(2,1)}, u32[]{:S(2)}) copy-start(bf16[4,2,1024]{2,1,0:T(2,128)(2,1)} %new_values.1) | copy-start | bytes 49156
  0.7 1.4 %copy-start.1 = (s32[4]{0:T(128)S(1)}, s32[4]{0:T(128)}, u32[]{:S(2)}) copy-start(s32[4]{0:T(128)} %ids.3) | copy-start | bytes 52
  0.7 1.4 %copy-start.3 = (bf16[128,2,1024]{2,1,0:T(2,128)(2,1)S(1)}, bf16[128,2,1024]{2,1,0:T(2,128)(2,1)}, u32[]{:S(2)}) copy-start(bf16[128,2,1024]{2,1,0:T(2,128)(2,1)} %kv_scales.1) | copy-start | bytes 1572868
  0.7 0.8 %copy-start.13 = (s32[4]{0:T(128)S(1)}, s32[4]{0:T(128)}, u32[]{:S(2)}) copy-start(s32[4]{0:T(128)} %lengths.1) | copy-start | bytes 52
  2.2 19.6 %slice-start.7 = ((s8[8388608]{0:T(1024)(128)(4,1)}), s8[4194304]{0:T(1024)(128)(4,1)S(1)}, s32[]{:S(2)}) async-start(s8[8388608]{0:T(1024)(128)(4,1)} %bitcast.2), calls=%async_computation.7 | async-start | bytes 8388608
  4.9 5.7 %collective-permute-start = (bf16[8,2176]{1,0:T(8,128)(2,1)S(1)}, bf16[8,2176]{1,0:T(8,128)(2,1)S(1)}, u32[]{:S(2)}, u32[]{:S(2)}) collective-permute-start(bf16[8,2176]{1,0:T(8,128)(2,1)S(1)} %get-tuple-element.22), channel_id=1, source_target_pairs={{0,4},{4,0},{8,12},{12,8},{1,5},{5,1},{9,13},{13,9},{2,6},{6,2},{1... | collective-permute-start | bytes 104456 | tf_op jit(solution)/shard_map/ppermute | solution.py:331
  8.0 5.5 %collective-permute-start.1 = (bf16[8,2176]{1,0:T(8,128)(2,1)S(1)}, bf16[8,2176]{1,0:T(8,128)(2,1)S(1)}, u32[]{:S(2)}, u32[]{:S(2)}) collective-permute-start(bf16[8,2176]{1,0:T(8,128)(2,1)S(1)} %get-tuple-element.23), channel_id=1, source_target_pairs={{0,8},{4,12},{8,0},{12,4},{1,9},{5,13},{9,1},{13,5},{2,10},{6,14},... | collective-permute-start | bytes 104456 | tf_op jit(solution)/shard_map/ppermute | solution.py:331
  10.6 5.7 %collective-permute-start.2 = (bf16[8,2176]{1,0:T(8,128)(2,1)S(1)}, bf16[8,2176]{1,0:T(8,128)(2,1)S(1)}, u32[]{:S(2)}, u32[]{:S(2)}) collective-permute-start(bf16[8,2176]{1,0:T(8,128)(2,1)S(1)} %get-tuple-element.24), channel_id=1, source_target_pairs={{0,12},{4,8},{8,4},{12,0},{1,13},{5,9},{9,5},{13,1},{2,14},{6,10},... | collective-permute-start | bytes 104456 | tf_op jit(solution)/shard_map/ppermute | solution.py:331
  16.3 5.5 %slice-start.8 = ((s8[8388608]{0:T(1024)(128)(4,1)}), s8[4194304]{0:T(1024)(128)(4,1)S(1)}, s32[]{:S(2)}) async-start(s8[8388608]{0:T(1024)(128)(4,1)} %bitcast.2), calls=%async_computation.8 | async-start | bytes 8388608
  16.6 13.6 %copy-start.9 = (bf16[4,2,2048]{2,1,0:T(2,128)(2,1)S(1)}, bf16[4,2,2048]{2,1,0:T(2,128)(2,1)}, u32[]{:S(2)}) copy-start(bf16[4,2,2048]{2,1,0:T(2,128)(2,1)} %hidden.1) | copy-start | bytes 98308
  16.6 4.0 %collective-permute-start.4 = (bf16[8,2048]{1,0:T(8,128)(2,1)S(1)}, bf16[8,2048]{1,0:T(8,128)(2,1)S(1)}, u32[]{:S(2)}, u32[]{:S(2)}) collective-permute-start(bf16[8,2048]{1,0:T(8,128)(2,1)S(1)} %shard_map.160.rest_0_), channel_id=1, source_target_pairs={{0,2},{1,3},{2,0},{3,1},{4,6},{5,7},{6,4},{7,5},{8,10},{9,11},{10,... | collective-permute-start | bytes 98312 | tf_op jit(solution)/shard_map/ppermute | solution.py:343
  18.1 2.4 %collective-permute-start.3 = (bf16[8,2048]{1,0:T(8,128)(2,1)S(1)}, bf16[8,2048]{1,0:T(8,128)(2,1)S(1)}, u32[]{:S(2)}, u32[]{:S(2)}) collective-permute-start(bf16[8,2048]{1,0:T(8,128)(2,1)S(1)} %shard_map.160.rest_0_), channel_id=1, source_target_pairs={{0,1},{1,0},{2,3},{3,2},{4,5},{5,4},{6,7},{7,6},{8,9},{9,8},{10,11... | collective-permute-start | bytes 98312 | tf_op jit(solution)/shard_map/ppermute | solution.py:344
  20.6 1.2 %collective-permute-start.5 = (bf16[8,2048]{1,0:T(8,128)(2,1)S(1)}, bf16[8,2048]{1,0:T(8,128)(2,1)S(1)}, u32[]{:S(2)}, u32[]{:S(2)}) collective-permute-start(bf16[8,2048]{1,0:T(8,128)(2,1)S(1)} %collective-permute-done.4.rest_2_), channel_id=1, source_target_pairs={{0,1},{1,0},{2,3},{3,2},{4,5},{5,4},{6,7},{7,6},{8,9},{9,8},{10,11... | collective-permute-start | bytes 98312 | tf_op jit(solution)/shard_map/ppermute | solution.py:344
  21.8 17.8 %slice-start = ((s8[29360128]{0:T(1024)(128)(4,1)}), s8[4194304]{0:T(1024)(128)(4,1)S(1)}, s32[]{:S(2)}) async-start(s8[29360128]{0:T(1024)(128)(4,1)} %bitcast), calls=%async_computation | async-start | bytes 8388608
  21.8 17.8 %slice-start.1 = ((s8[29360128]{0:T(1024)(128)(4,1)}), s8[4194304]{0:T(1024)(128)(4,1)S(1)}, s32[]{:S(2)}) async-start(s8[29360128]{0:T(1024)(128)(4,1)} %bitcast), calls=%async_computation.1 | async-start | bytes 8388608
  21.8 17.8 %slice-start.2 = ((s8[29360128]{0:T(1024)(128)(4,1)}), s8[4194304]{0:T(1024)(128)(4,1)S(1)}, s32[]{:S(2)}) async-start(s8[29360128]{0:T(1024)(128)(4,1)} %bitcast), calls=%async_computation.2 | async-start | bytes 8388608
  21.8 17.8 %slice-start.3 = ((s8[29360128]{0:T(1024)(128)(4,1)}), s8[4194304]{0:T(1024)(128)(4,1)S(1)}, s32[]{:S(2)}) async-start(s8[29360128]{0:T(1024)(128)(4,1)} %bitcast), calls=%async_computation.3 | async-start | bytes 8388608
  23.4 4.5 %collective-permute-start.6 = (bf16[8,2048]{1,0:T(8,128)(2,1)S(1)}, bf16[8,2048]{1,0:T(8,128)(2,1)S(1)}, u32[]{:S(2)}, u32[]{:S(2)}) collective-permute-start(bf16[8,2048]{1,0:T(8,128)(2,1)S(1)} %get-tuple-element.26), channel_id=1, source_target_pairs={{0,4},{4,0},{8,12},{12,8},{1,5},{5,1},{9,13},{13,9},{2,6},{6,2},{1... | collective-permute-start | bytes 98312 | tf_op jit(solution)/shard_map/ppermute | solution.py:331
  23.5 4.9 %collective-permute-start.7 = (bf16[8,2048]{1,0:T(8,128)(2,1)S(1)}, bf16[8,2048]{1,0:T(8,128)(2,1)S(1)}, u32[]{:S(2)}, u32[]{:S(2)}) collective-permute-start(bf16[8,2048]{1,0:T(8,128)(2,1)S(1)} %get-tuple-element.27), channel_id=1, source_target_pairs={{0,8},{4,12},{8,0},{12,4},{1,9},{5,13},{9,1},{13,5},{2,10},{6,14},... | collective-permute-start | bytes 98312 | tf_op jit(solution)/shard_map/ppermute | solution.py:331
  24.5 5.7 %collective-permute-start.8 = (bf16[8,2048]{1,0:T(8,128)(2,1)S(1)}, bf16[8,2048]{1,0:T(8,128)(2,1)S(1)}, u32[]{:S(2)}, u32[]{:S(2)}) collective-permute-start(bf16[8,2048]{1,0:T(8,128)(2,1)S(1)} %get-tuple-element.28), channel_id=1, source_target_pairs={{0,12},{4,8},{8,4},{12,0},{1,13},{5,9},{9,5},{13,1},{2,14},{6,10},... | collective-permute-start | bytes 98312 | tf_op jit(solution)/shard_map/ppermute | solution.py:331
  30.2 9.4 %slice-start.4 = ((s8[29360128]{0:T(1024)(128)(4,1)}), s8[4194304]{0:T(1024)(128)(4,1)S(1)}, s32[]{:S(2)}) async-start(s8[29360128]{0:T(1024)(128)(4,1)} %bitcast), calls=%async_computation.4 | async-start | bytes 8388608
  30.2 9.4 %slice-start.5 = ((s8[29360128]{0:T(1024)(128)(4,1)}), s8[4194304]{0:T(1024)(128)(4,1)S(1)}, s32[]{:S(2)}) async-start(s8[29360128]{0:T(1024)(128)(4,1)} %bitcast), calls=%async_computation.5 | async-start | bytes 8388608
  30.2 9.4 %slice-start.6 = ((s8[29360128]{0:T(1024)(128)(4,1)}), s8[4194304]{0:T(1024)(128)(4,1)S(1)}, s32[]{:S(2)}) async-start(s8[29360128]{0:T(1024)(128)(4,1)} %bitcast), calls=%async_computation.6 | async-start | bytes 8388608
  30.2 9.5 %copy-start.12 = (bf16[2048]{0:T(1024)(128)(2,1)S(1)}, bf16[2048]{0:T(1024)(128)(2,1)}, u32[]{:S(2)}) copy-start(bf16[2048]{0:T(1024)(128)(2,1)} %gain.1) | copy-start | bytes 12292
  30.9 4.8 %collective-permute-start.10 = (bf16[8,2048]{1,0:T(8,128)(2,1)S(1)}, bf16[8,2048]{1,0:T(8,128)(2,1)S(1)}, u32[]{:S(2)}, u32[]{:S(2)}) collective-permute-start(bf16[8,2048]{1,0:T(8,128)(2,1)S(1)} %get-tuple-element.30.rest_0_), channel_id=1, source_target_pairs={{0,8},{4,12},{8,0},{12,4},{1,9},{5,13},{9,1},{13,5},{2,10},{6,14},... | collective-permute-start | bytes 98312 | tf_op jit(solution)/shard_map/ppermute | solution.py:343
  31.1 5.6 %collective-permute-start.9 = (bf16[8,2048]{1,0:T(8,128)(2,1)S(1)}, bf16[8,2048]{1,0:T(8,128)(2,1)S(1)}, u32[]{:S(2)}, u32[]{:S(2)}) collective-permute-start(bf16[8,2048]{1,0:T(8,128)(2,1)S(1)} %get-tuple-element.30.rest_0_), channel_id=1, source_target_pairs={{0,4},{4,0},{8,12},{12,8},{1,5},{5,1},{9,13},{13,9},{2,6},{6,2},{1... | collective-permute-start | bytes 98312 | tf_op jit(solution)/shard_map/ppermute | solution.py:344
  35.7 3.9 %collective-permute-start.11 = (bf16[8,2048]{1,0:T(8,128)(2,1)S(1)}, bf16[8,2048]{1,0:T(8,128)(2,1)S(1)}, u32[]{:S(2)}, u32[]{:S(2)}) collective-permute-start(bf16[8,2048]{1,0:T(8,128)(2,1)S(1)} %collective-permute-done.10.rest_2_), channel_id=1, source_target_pairs={{0,4},{4,0},{8,12},{12,8},{1,5},{5,1},{9,13},{13,9},{2,6},{6,2},{1... | collective-permute-start | bytes 98312 | tf_op jit(solution)/shard_map/ppermute | solution.py:344
  43.4 3.1 %collective-permute-start.12 = (bf16[2,8,4224]{2,1,0:T(8,128)(2,1)S(1)}, bf16[2,8,4224]{2,1,0:T(8,128)(2,1)S(1)}, u32[]{:S(2)}, u32[]{:S(2)}) collective-permute-start(bf16[2,8,4224]{2,1,0:T(8,128)(2,1)S(1)} %get-tuple-element.32), channel_id=1, source_target_pairs={{0,1},{1,0},{2,3},{3,2},{4,5},{5,4},{6,7},{7,6},{8,9},{9,8},{10,11... | collective-permute-start | bytes 405512 | tf_op jit(solution)/shard_map/ppermute | solution.py:495
  43.5 5.6 %copy-start = (bf16[128,3584]{1,0:T(8,128)(2,1)S(1)}, bf16[128,3584]{1,0:T(8,128)(2,1)}, u32[]{:S(2)}) copy-start(bf16[128,3584]{1,0:T(8,128)(2,1)} %table.1) | copy-start | bytes 2752516
  43.5 5.6 %copy-start.2 = (s32[4]{0:T(128)S(1)}, s32[4]{0:T(128)}, u32[]{:S(2)}) copy-start(s32[4]{0:T(128)} %ids.3) | copy-start | bytes 52
  46.0 2.2 %collective-permute-start.14 = (bf16[2,8,3072]{2,1,0:T(8,128)(2,1)S(1)}, bf16[2,8,3072]{2,1,0:T(8,128)(2,1)S(1)}, u32[]{:S(2)}, u32[]{:S(2)}) collective-permute-start(bf16[2,8,3072]{2,1,0:T(8,128)(2,1)S(1)} %get-tuple-element.37), channel_id=1, source_target_pairs={{0,1},{1,0},{2,3},{3,2},{4,5},{5,4},{6,7},{7,6},{8,9},{9,8},{10,11... | collective-permute-start | bytes 294920 | tf_op jit(solution)/shard_map/ppermute | solution.py:495
  46.6 5.7 %collective-permute-start.13 = (bf16[8,4224]{1,0:T(8,128)(2,1)S(1)}, bf16[8,4224]{1,0:T(8,128)(2,1)S(1)}, u32[]{:S(2)}, u32[]{:S(2)}) collective-permute-start(bf16[8,4224]{1,0:T(8,128)(2,1)S(1)} %get-tuple-element.34), channel_id=1, source_target_pairs={{0,2},{1,3},{2,0},{3,1},{4,6},{5,7},{6,4},{7,5},{8,10},{9,11},{10,... | collective-permute-start | bytes 202760 | tf_op jit(solution)/shard_map/ppermute | solution.py:505
  48.2 4.2 %collective-permute-start.15 = (bf16[8,3072]{1,0:T(8,128)(2,1)S(1)}, bf16[8,3072]{1,0:T(8,128)(2,1)S(1)}, u32[]{:S(2)}, u32[]{:S(2)}) collective-permute-start(bf16[8,3072]{1,0:T(8,128)(2,1)S(1)} %get-tuple-element.39), channel_id=1, source_target_pairs={{0,2},{1,3},{2,0},{3,1},{4,6},{5,7},{6,4},{7,5},{8,10},{9,11},{10,... | collective-permute-start | bytes 147464 | tf_op jit(solution)/shard_map/ppermute | solution.py:505

commit v7 on v5

--- a/solution.py
+++ b/solution.py
@@ -59,25 +59,15 @@
     rows = tokens // STEPS
     suffix_all = rows * suffix_local
     me = lax.axis_index("pre")
-    row_at = lax.broadcasted_iota(jnp.int32, out.shape, 0)
+    token = lax.broadcasted_iota(jnp.int32, out.shape, 0)
     column = lax.broadcasted_iota(jnp.int32, out.shape, 1)
-    token = lax.rem(row_at, tokens)
     row_of = token // STEPS
-    step = lax.rem(token, STEPS)
+    step = token - row_of * STEPS
     limit = pick(row_of, [lengths[r] for r in range(rows)])
-    in_suffix = (
-        (column < suffix_all)
-        & (column // suffix_local == row_of)
-        & (me * suffix_local + lax.rem(column, suffix_local) < limit)
-    )
-    fresh = column - suffix_all
-    in_new = (
-        (fresh >= 0)
-        & (fresh < tokens)
-        & (fresh // STEPS == row_of)
-        & (lax.rem(fresh + LANES * STEPS, STEPS) <= step)
-        & (me == 0)
-    )
+    at = column - row_of * suffix_local
+    in_suffix = (at >= 0) & (at < suffix_local) & (me * suffix_local + at < limit)
+    fresh = column - suffix_all - row_of * STEPS
+    in_new = (fresh >= 0) & (fresh <= step) & (me == 0)
     out[...] = (in_suffix | in_new).astype(jnp.int32)
 
 
@@ -105,7 +95,7 @@
     block = HEADS * HD // pre_count
     block_heads = block // HD
     me = lax.axis_index("pre")
-    allowed = mask[...] != 0
+    allowed = jnp.concatenate([mask[...]] * group, axis=0) != 0
     for r in range(rows):
         scales[2 * r : 2 * r + 2, :] = kv_scales[ids[r]].astype(f32)
 
@@ -212,9 +202,9 @@
     blocks, (out, sent) = rest[:parts], rest[parts:]
     amount, width = sent.shape
     value = sum(ref[...].astype(f32) for ref in blocks)
-    value = hidden[...].reshape(amount, width).astype(f32) + value
+    value = hidden.reshape(amount, width)[...].astype(f32) + value
     sent[...] = value.astype(bf16)
-    out[...] = value.astype(bf16).reshape(out.shape)
+    out.reshape(amount, width)[...] = value.astype(bf16)
 
 
 def column_tile(columns):
@@ -273,13 +263,16 @@
     normed = (value * gain[...].astype(f32).reshape(1, depth)).astype(bf16)
     source = lax.broadcasted_iota(jnp.int32, (HD, 2 * HD), 0)
     target = lax.broadcasted_iota(jnp.int32, (HD, 2 * HD), 1)
-    for b in range(depth // HD):
-        piece = normed[:, b * HD : (b + 1) * HD]
-        for half in range(2):
-            selector = (target == 2 * source + half).astype(bf16)
-            spread[half * rows : (half + 1) * rows, 2 * b * HD : 2 * (b + 1) * HD] = dot(
-                piece, selector
-            ).astype(bf16)
+    pieces = jnp.concatenate(
+        [normed[:, b * HD : (b + 1) * HD] for b in range(depth // HD)], axis=0
+    )
+    for half in range(2):
+        selector = (target == 2 * source + half).astype(bf16)
+        wider = dot(pieces, selector).astype(bf16)
+        for b in range(depth // HD):
+            spread[half * rows : (half + 1) * rows, 2 * b * HD : 2 * (b + 1) * HD] = wider[
+                b * rows : (b + 1) * rows
+            ]
     multiply(spread[...], weight, 0, columns, product)
     product[0:rows, columns:] = placed_parts(squares)
     hand_out(row_count, product, columns, True, keep, sent)
@@ -313,7 +306,8 @@
 
 def activate_kernel(parts, first, scales, *rest):
     front, back, out = rest[:parts], rest[parts : 2 * parts], rest[2 * parts]
-    wide = scales.shape[1]
+    tokens, wide = scales.shape
+    flat = out.reshape(tokens, wide)
     squares = sum(ref[:, 2 * first :].astype(f32) for ref in front)
     squares = jnp.sum(squares, axis=1, keepdims=True)
     inverse = lax.rsqrt(squares / D + 1e-05)
@@ -321,8 +315,7 @@
         gate = sum(ref[:, :columns].astype(f32) for ref in blocks) * inverse
         up = sum(ref[:, columns : 2 * columns].astype(f32) for ref in blocks) * inverse
         value = gate / (1.0 + jnp.exp(-gate)) * up * scales[:, start : start + columns]
-        rows, steps, _ = out.shape
-        out[:, :, start : start + columns] = value.astype(bf16).reshape(rows, steps, columns)
+        flat[:, start : start + columns] = value.astype(bf16)
 
 
 def shifted(parts, axis):
@@ -385,7 +378,7 @@
         functools.partial(mask_kernel, tokens, suffix_local),
         in_specs=[SMEM],
         out_specs=VMEM,
-        out_shape=shape_of((HEADS // KV_HEADS * tokens, LANES), jnp.int32),
+        out_shape=shape_of((tokens, LANES), jnp.int32),
         compiler_params=params(1),
         cost_estimate=cost(20),
     )(suffix_lengths)

time: 51.3 us -> 51.1 us (level)
  no operation moved by 1% of the time
where the time goes in v7:
time: 51.1 us; the launch traced here: 51 us
  starting transfers between devices  18.7 us (37%)
  waiting for transfers between devices  16.9 us (33%)
  Pallas kernels  13.4 us (26%)
  between operations  1 us (2%)
  local copies, waits for them, and re-layouts  0.85 us (2%)
    ppermute x12, starting transfers between devices, shifted(): lax.ppermute(parts[s], axis, [(i, target_of(i, s, count)) for i in range(...  16 us
    ppermute x12, waiting for transfers between devices, shifted(): lax.ppermute(parts[s], axis, [(i, target_of(i, s, count)) for i in range(...  14.5 us
    pallas_call x1, Pallas kernels, per_device(): pl.pallas_call(functools.partial(feed_first_kernel, pre_count, row_count,...  3.56 us
    pallas_call x1, Pallas kernels, per_device(): pl.pallas_call(functools.partial(attend_kernel, pre_count), in_specs=[SME...  2.71 us
    pallas_call x1, Pallas kernels, per_device(): pl.pallas_call(functools.partial(feed_second_kernel, row_count, first, se...  2.48 us
    ppermute x2, waiting for transfers between devices, per_device(): lax.ppermute(sums[j], 'row', [(i, i ^ 2 * j) for i in range(row_count)])  2.46 us
    ppermute x2, starting transfers between devices, per_device(): lax.ppermute(sums[j], 'row', [(i, i ^ 2 * j) for i in range(row_count)])  2.13 us
    pallas_call x1, Pallas kernels, per_device(): pl.pallas_call(functools.partial(project_kernel, row_count, pre_count), i...  1.56 us
  transfers between devices with their start and end apart: 16, of which 10 were waited for; matrix products, arithmetic and copies ran while one was open for 0% of the time, Pallas kernels for 7%

profile of v7, /device:TPU:0, one launch (start us, length us, event | category | flops | bytes accessed | tf_op | source)
XLA Modules:
  0.0 51.0 jit_solution(2061128968590089700)
XLA Ops:
  0.7 0.0 copy-start.1
  0.7 0.7 %copy-done.13 = s32[4]{0:T(128)S(1)} copy-done((s32[4]{0:T(128)S(1)}, s32[4]{0:T(128)}, u32[]{:S(2)}) %copy-start.13) | copy-done | bytes 40
  1.5 0.6 %shard_map.158.mask = s32[8,128]{1,0:T(8,128)S(1)} custom-call(s32[4]{0:T(128)S(1)} %copy-done.13), custom_call_target="tpu_custom_call" | custom-call | flops 20000000000 | tf_op jit(solution)/shard_map/pallas_call | solution.py:377
  2.1 0.0 slice-start.7
  2.1 2.7 %shard_map.159 = (bf16[8,2176]{1,0:T(8,128)(2,1)S(1)}, bf16[8,2176]{1,0:T(8,128)(2,1)S(1)}, bf16[8,2176]{1,0:T(8,128)(2,1)S(1)}, bf16[8,2176]{1,0:T(8,128)(2,1)S(1)}) custom-call(s32[4]{0:T(128)S(1)} %copy-done.1, s32[8,128]{1,0:T(8,128)S(1)} %shard_map.158.mask, bf16[4,2,8192]{2,1,0:T(2,128)(2,1)S(1)} %copy-done.6, bf16[128,1024]{1,0:T(8,128)(2,1)S(1)} %copy-done.4, ...), custom_call_target="tpu_custom_call" | custom-call | flops 20000000000 | tf_op jit(solution)/shard_map/pallas_call | solution.py:385
  4.9 3.1 %collective-permute-start = (bf16[8,2176]{1,0:T(8,128)(2,1)S(1)}, bf16[8,2176]{1,0:T(8,128)(2,1)S(1)}, u32[]{:S(2)}, u32[]{:S(2)}) collective-permute-start(bf16[8,2176]{1,0:T(8,128)(2,1)S(1)} %get-tuple-element.22), channel_id=1, source_target_pairs={{0,4},{4,0},{8,12},{12,8},{1,5},{5,1},{9,13},{13,9},{2,6},{6,2},{1... | collective-permute-start | bytes 104456 | tf_op jit(solution)/shard_map/ppermute | solution.py:324
  7.9 2.6 %collective-permute-start.1 = (bf16[8,2176]{1,0:T(8,128)(2,1)S(1)}, bf16[8,2176]{1,0:T(8,128)(2,1)S(1)}, u32[]{:S(2)}, u32[]{:S(2)}) collective-permute-start(bf16[8,2176]{1,0:T(8,128)(2,1)S(1)} %get-tuple-element.23), channel_id=1, source_target_pairs={{0,8},{4,12},{8,0},{12,4},{1,9},{5,13},{9,1},{13,5},{2,10},{6,14},... | collective-permute-start | bytes 104456 | tf_op jit(solution)/shard_map/ppermute | solution.py:324
  10.5 0.0 collective-permute-start.2
  10.5 0.0 collective-permute-done.rest_1_
  10.5 2.9 %collective-permute-done.1.rest_2_ = bf16[8,2176]{1,0:T(8,128)(2,1)S(1)} collective-permute-done((bf16[8,2176]{1,0:T(8,128)(2,1)S(1)}, bf16[8,2176]{1,0:T(8,128)(2,1)S(1)}, u32[]{:S(2)}, u32[]{:S(2)}) %collective-permute-start.1) | collective-permute-done | bytes 34848 | tf_op jit(solution)/shard_map/ppermute | solution.py:324
  13.4 2.9 %collective-permute-done.2.rest_3_ = bf16[8,2176]{1,0:T(8,128)(2,1)S(1)} collective-permute-done((bf16[8,2176]{1,0:T(8,128)(2,1)S(1)}, bf16[8,2176]{1,0:T(8,128)(2,1)S(1)}, u32[]{:S(2)}, u32[]{:S(2)}) %collective-permute-start.2) | collective-permute-done | bytes 34848 | tf_op jit(solution)/shard_map/ppermute | solution.py:324
  16.3 0.3 shard_map.160.rest_0_
  16.5 0.0 copy-start.9
  16.6 0.1 collective-permute-start.3
  16.6 1.6 %collective-permute-start.4 = (bf16[8,2048]{1,0:T(8,128)(2,1)S(1)}, bf16[8,2048]{1,0:T(8,128)(2,1)S(1)}, u32[]{:S(2)}, u32[]{:S(2)}) collective-permute-start(bf16[8,2048]{1,0:T(8,128)(2,1)S(1)} %shard_map.160.rest_0_), channel_id=1, source_target_pairs={{0,2},{1,3},{2,0},{3,1},{4,6},{5,7},{6,4},{7,5},{8,10},{9,11},{10,... | collective-permute-start | bytes 98312 | tf_op jit(solution)/shard_map/ppermute | solution.py:324
  18.2 0.3 collective-permute-start.5
  18.5 2.1 %collective-permute-done.4.rest_2_ = bf16[8,2048]{1,0:T(8,128)(2,1)S(1)} collective-permute-done((bf16[8,2048]{1,0:T(8,128)(2,1)S(1)}, bf16[8,2048]{1,0:T(8,128)(2,1)S(1)}, u32[]{:S(2)}, u32[]{:S(2)}) %collective-permute-start.4) | collective-permute-done | bytes 32800 | tf_op jit(solution)/shard_map/ppermute | solution.py:324
  20.6 0.9 %collective-permute-done.5.rest_3_ = bf16[8,2048]{1,0:T(8,128)(2,1)S(1)} collective-permute-done((bf16[8,2048]{1,0:T(8,128)(2,1)S(1)}, bf16[8,2048]{1,0:T(8,128)(2,1)S(1)}, u32[]{:S(2)}, u32[]{:S(2)}) %collective-permute-start.5) | collective-permute-done | bytes 32800 | tf_op jit(solution)/shard_map/ppermute | solution.py:324
  21.5 0.0 slice-start.1
  21.6 0.0 slice-start.2
  21.6 0.0 slice-start.3
  21.6 1.6 %shard_map.161 = (f32[8,2048]{1,0:T(8,128)S(1)}, bf16[8,2048]{1,0:T(8,128)(2,1)S(1)}, bf16[8,2048]{1,0:T(8,128)(2,1)S(1)}, bf16[8,2048]{1,0:T(8,128)(2,1)S(1)}) custom-call(bf16[8,2048]{1,0:T(8,128)(2,1)S(1)} %shard_map.160.rest_0_, bf16[8,2048]{1,0:T(8,128)(2,1)S(1)} %collective-permute-done.3.rest_1_, bf16[8,2048]{1,0:T(8,128)(2,1)S(1)} %collective-permute-done.4.rest_2_, ...), custom_call_target="tpu_custom_call" | custom-call | flops 40000000000 | tf_op jit(solution)/shard_map/pallas_call | solution.py:417
  23.2 0.1 collective-permute-start.6
  23.2 1.0 %collective-permute-start.7 = (bf16[8,2048]{1,0:T(8,128)(2,1)S(1)}, bf16[8,2048]{1,0:T(8,128)(2,1)S(1)}, u32[]{:S(2)}, u32[]{:S(2)}) collective-permute-start(bf16[8,2048]{1,0:T(8,128)(2,1)S(1)} %get-tuple-element.27), channel_id=1, source_target_pairs={{0,8},{4,12},{8,0},{12,4},{1,9},{5,13},{9,1},{13,5},{2,10},{6,14},... | collective-permute-start | bytes 98312 | tf_op jit(solution)/shard_map/ppermute | solution.py:324
  24.2 3.4 %collective-permute-start.8 = (bf16[8,2048]{1,0:T(8,128)(2,1)S(1)}, bf16[8,2048]{1,0:T(8,128)(2,1)S(1)}, u32[]{:S(2)}, u32[]{:S(2)}) collective-permute-start(bf16[8,2048]{1,0:T(8,128)(2,1)S(1)} %get-tuple-element.28), channel_id=1, source_target_pairs={{0,12},{4,8},{8,4},{12,0},{1,13},{5,9},{9,5},{13,1},{2,14},{6,10},... | collective-permute-start | bytes 98312 | tf_op jit(solution)/shard_map/ppermute | solution.py:324
  27.6 0.5 %collective-permute-done.7.rest_2_ = bf16[8,2048]{1,0:T(8,128)(2,1)S(1)} collective-permute-done((bf16[8,2048]{1,0:T(8,128)(2,1)S(1)}, bf16[8,2048]{1,0:T(8,128)(2,1)S(1)}, u32[]{:S(2)}, u32[]{:S(2)}) %collective-permute-start.7) | collective-permute-done | bytes 32800 | tf_op jit(solution)/shard_map/ppermute | solution.py:324
  28.1 1.8 %collective-permute-done.8.rest_3_ = bf16[8,2048]{1,0:T(8,128)(2,1)S(1)} collective-permute-done((bf16[8,2048]{1,0:T(8,128)(2,1)S(1)}, bf16[8,2048]{1,0:T(8,128)(2,1)S(1)}, u32[]{:S(2)}, u32[]{:S(2)}) %collective-permute-start.8) | collective-permute-done | bytes 32800 | tf_op jit(solution)/shard_map/ppermute | solution.py:324
  30.0 0.0 copy-start.12
  30.0 0.7 %shard_map.162 = (bf16[4,2,2048]{2,1,0:T(2,128)(2,1)}, bf16[8,2048]{1,0:T(8,128)(2,1)S(1)}) custom-call(bf16[4,2,2048]{2,1,0:T(2,128)(2,1)S(1)} %copy-done.9, f32[8,2048]{1,0:T(8,128)S(1)} %get-tuple-element.25.rest_0_, bf16[8,2048]{1,0:T(8,128)(2,1)S(1)} %collective-permute-done.6.rest_1_, bf16[8,2048]{1,0:T(8,128)(2,1)S(1)} %collective-permute-done.7.rest_2_, ...), custom_call_target="tpu_custom_call" | custom-call | flops 40000000000 | tf_op jit(solution)/shard_map/pallas_call | solution.py:431
  30.6 0.2 collective-permute-start.10
  30.8 3.2 %collective-permute-start.11 = (bf16[8,2048]{1,0:T(8,128)(2,1)S(1)}, bf16[8,2048]{1,0:T(8,128)(2,1)S(1)}, u32[]{:S(2)}, u32[]{:S(2)}) collective-permute-start(bf16[8,2048]{1,0:T(8,128)(2,1)S(1)} %get-tuple-element.30.rest_0_), channel_id=1, source_target_pairs={{0,12},{4,8},{8,4},{12,0},{1,13},{5,9},{9,5},{13,1},{2,14},{6,10},... | collective-permute-start | bytes 98312 | tf_op jit(solution)/shard_map/ppermute | solution.py:324
  34.0 0.6 %collective-permute-start.9 = (bf16[8,2048]{1,0:T(8,128)(2,1)S(1)}, bf16[8,2048]{1,0:T(8,128)(2,1)S(1)}, u32[]{:S(2)}, u32[]{:S(2)}) collective-permute-start(bf16[8,2048]{1,0:T(8,128)(2,1)S(1)} %get-tuple-element.30.rest_0_), channel_id=1, source_target_pairs={{0,4},{4,0},{8,12},{12,8},{1,5},{5,1},{9,13},{13,9},{2,6},{6,2},{1... | collective-permute-start | bytes 98312 | tf_op jit(solution)/shard_map/ppermute | solution.py:324
  34.6 0.9 %collective-permute-done.10.rest_2_ = bf16[8,2048]{1,0:T(8,128)(2,1)S(1)} collective-permute-done((bf16[8,2048]{1,0:T(8,128)(2,1)S(1)}, bf16[8,2048]{1,0:T(8,128)(2,1)S(1)}, u32[]{:S(2)}, u32[]{:S(2)}) %collective-permute-start.10) | collective-permute-done | bytes 32800 | tf_op jit(solution)/shard_map/ppermute | solution.py:324
  35.5 1.2 %collective-permute-done.11.rest_3_ = bf16[8,2048]{1,0:T(8,128)(2,1)S(1)} collective-permute-done((bf16[8,2048]{1,0:T(8,128)(2,1)S(1)}, bf16[8,2048]{1,0:T(8,128)(2,1)S(1)}, u32[]{:S(2)}, u32[]{:S(2)}) %collective-permute-start.11) | collective-permute-done | bytes 32800 | tf_op jit(solution)/shard_map/ppermute | solution.py:324
  36.7 1.3 %collective-permute-done.9.rest_1_ = bf16[8,2048]{1,0:T(8,128)(2,1)S(1)} collective-permute-done((bf16[8,2048]{1,0:T(8,128)(2,1)S(1)}, bf16[8,2048]{1,0:T(8,128)(2,1)S(1)}, u32[]{:S(2)}, u32[]{:S(2)}) %collective-permute-start.9) | collective-permute-done | bytes 32800 | tf_op jit(solution)/shard_map/ppermute | solution.py:324
  38.0 3.6 %shard_map.164 = (f32[2,8,4224]{2,1,0:T(8,128)S(1)}, bf16[2,8,4224]{2,1,0:T(8,128)(2,1)S(1)}, bf16[64,4096]{1,0:T(8,128)(2,1)S(1)}) custom-call(bf16[2048]{0:T(1024)(128)(2,1)S(1)} %copy-done.12, bf16[8,2048]{1,0:T(8,128)(2,1)S(1)} %get-tuple-element.30.rest_0_, bf16[8,2048]{1,0:T(8,128)(2,1)S(1)} %collective-permute-done.9.rest_1_, ...), custom_call_target="tpu_custom_call" | custom-call | flops 16000000000 | tf_op jit(solution)/shard_map/pallas_call | solution.py:444
  41.6 0.1 collective-permute-start.12
  41.6 0.0 copy-start
  41.6 0.0 copy-start.2
  41.7 2.5 %shard_map.166 = (f32[2,8,3072]{2,1,0:T(8,128)S(1)}, bf16[2,8,3072]{2,1,0:T(8,128)(2,1)S(1)}) custom-call(bf16[64,4096]{1,0:T(8,128)(2,1)S(1)} %get-tuple-element.35.spread, bf16[2048,2,3584]{2,1,0:T(2,128)(2,1)S(1)} %bitcast.1), custom_call_target="tpu_custom_call" | custom-call | flops 16000000000 | tf_op jit(solution)/shard_map/pallas_call | solution.py:460
  44.2 0.6 %collective-permute-start.14 = (bf16[2,8,3072]{2,1,0:T(8,128)(2,1)S(1)}, bf16[2,8,3072]{2,1,0:T(8,128)(2,1)S(1)}, u32[]{:S(2)}, u32[]{:S(2)}) collective-permute-start(bf16[2,8,3072]{2,1,0:T(8,128)(2,1)S(1)} %get-tuple-element.37), channel_id=1, source_target_pairs={{0,1},{1,0},{2,3},{3,2},{4,5},{5,4},{6,7},{7,6},{8,9},{9,8},{10,11... | collective-permute-start | bytes 294920 | tf_op jit(solution)/shard_map/ppermute | solution.py:476
  44.7 0.1 shard_map.165
  44.8 1.0 %collective-permute-start.13 = (bf16[8,4224]{1,0:T(8,128)(2,1)S(1)}, bf16[8,4224]{1,0:T(8,128)(2,1)S(1)}, u32[]{:S(2)}, u32[]{:S(2)}) collective-permute-start(bf16[8,4224]{1,0:T(8,128)(2,1)S(1)} %get-tuple-element.34), channel_id=1, source_target_pairs={{0,2},{1,3},{2,0},{3,1},{4,6},{5,7},{6,4},{7,5},{8,10},{9,11},{10,... | collective-permute-start | bytes 202760 | tf_op jit(solution)/shard_map/ppermute | solution.py:486
  45.8 1.2 %collective-permute-start.15 = (bf16[8,3072]{1,0:T(8,128)(2,1)S(1)}, bf16[8,3072]{1,0:T(8,128)(2,1)S(1)}, u32[]{:S(2)}, u32[]{:S(2)}) collective-permute-start(bf16[8,3072]{1,0:T(8,128)(2,1)S(1)} %get-tuple-element.39), channel_id=1, source_target_pairs={{0,2},{1,3},{2,0},{3,1},{4,6},{5,7},{6,4},{7,5},{8,10},{9,11},{10,... | collective-permute-start | bytes 147464 | tf_op jit(solution)/shard_map/ppermute | solution.py:486
  47.0 0.8 %shard_map.163.scales = f32[8,3584]{1,0:T(8,128)S(1)} custom-call(s32[4]{0:T(128)S(1)} %copy-done.2, bf16[128,3584]{1,0:T(8,128)(2,1)S(1)} %copy-done), custom_call_target="tpu_custom_call" | custom-call | tf_op jit(solution)/shard_map/pallas_call | solution.py:368
  47.7 2.5 %collective-permute-done.15.rest_3_ = bf16[8,3072]{1,0:T(8,128)(2,1)S(1)} collective-permute-done((bf16[8,3072]{1,0:T(8,128)(2,1)S(1)}, bf16[8,3072]{1,0:T(8,128)(2,1)S(1)}, u32[]{:S(2)}, u32[]{:S(2)}) %collective-permute-start.15) | collective-permute-done | bytes 49184 | tf_op jit(solution)/shard_map/ppermute | solution.py:486
  50.2 0.0 collective-permute-done.13.rest_1_
  50.2 0.8 %shard_map.168 = bf16[4,2,3584]{2,1,0:T(2,128)(2,1)} custom-call(f32[8,3584]{1,0:T(8,128)S(1)} %shard_map.163.scales, f32[8,4224]{1,0:T(8,128)S(1)} %get-tuple-element.33.rest_0_, bf16[8,4224]{1,0:T(8,128)(2,1)S(1)} %collective-permute-done.13.rest_1_, f32[8,3072]{1,0:T(8,128)S(1)} %get-tuple-element.38.rest_2_, ...), custom_call_target="tpu_custom_call" | custom-call | tf_op jit(solution)/shard_map/pallas_call | solution.py:489
  (43 shorter events, 0.1 us)
Async XLA Ops:
  0.6 1.4 %copy-start.6 = (bf16[4,2,8192]{2,1,0:T(2,128)(2,1)S(1)}, bf16[4,2,8192]{2,1,0:T(2,128)(2,1)}, u32[]{:S(2)}) copy-start(bf16[4,2,8192]{2,1,0:T(2,128)(2,1)} %queries.1) | copy-start | bytes 393220
  0.6 1.4 %copy-start.4 = (bf16[128,1024]{1,0:T(8,128)(2,1)S(1)}, bf16[128,1024]{1,0:T(8,128)(2,1)}, u32[]{:S(2)}) copy-start(bf16[128,1024]{1,0:T(8,128)(2,1)} %prefix_keys.1) | copy-start | bytes 786436
  0.7 1.4 %copy-start.5 = (bf16[128,1024]{1,0:T(8,128)(2,1)S(1)}, bf16[128,1024]{1,0:T(8,128)(2,1)}, u32[]{:S(2)}) copy-start(bf16[128,1024]{1,0:T(8,128)(2,1)} %prefix_values.1) | copy-start | bytes 786436
  0.7 1.4 %copy-start.7 = (bf16[4,16,1024]{2,1,0:T(8,128)(2,1)S(1)}, bf16[4,16,1024]{2,1,0:T(8,128)(2,1)}, u32[]{:S(2)}) copy-start(bf16[4,16,1024]{2,1,0:T(8,128)(2,1)} %suffix_keys.1) | copy-start | bytes 393220
  0.7 1.4 %copy-start.8 = (bf16[4,16,1024]{2,1,0:T(8,128)(2,1)S(1)}, bf16[4,16,1024]{2,1,0:T(8,128)(2,1)}, u32[]{:S(2)}) copy-start(bf16[4,16,1024]{2,1,0:T(8,128)(2,1)} %suffix_values.1) | copy-start | bytes 393220
  0.7 1.4 %copy-start.10 = (bf16[4,2,1024]{2,1,0:T(2,128)(2,1)S(1)}, bf16[4,2,1024]{2,1,0:T(2,128)(2,1)}, u32[]{:S(2)}) copy-start(bf16[4,2,1024]{2,1,0:T(2,128)(2,1)} %new_keys.1) | copy-start | bytes 49156
  0.7 1.4 %copy-start.11 = (bf16[4,2,1024]{2,1,0:T(2,128)(2,1)S(1)}, bf16[4,2,1024]{2,1,0:T(2,128)(2,1)}, u32[]{:S(2)}) copy-start(bf16[4,2,1024]{2,1,0:T(2,128)(2,1)} %new_values.1) | copy-start | bytes 49156
  0.7 1.4 %copy-start.1 = (s32[4]{0:T(128)S(1)}, s32[4]{0:T(128)}, u32[]{:S(2)}) copy-start(s32[4]{0:T(128)} %ids.3) | copy-start | bytes 52
  0.7 1.4 %copy-start.3 = (bf16[128,2,1024]{2,1,0:T(2,128)(2,1)S(1)}, bf16[128,2,1024]{2,1,0:T(2,128)(2,1)}, u32[]{:S(2)}) copy-start(bf16[128,2,1024]{2,1,0:T(2,128)(2,1)} %kv_scales.1) | copy-start | bytes 1572868
  0.7 0.8 %copy-start.13 = (s32[4]{0:T(128)S(1)}, s32[4]{0:T(128)}, u32[]{:S(2)}) copy-start(s32[4]{0:T(128)} %lengths.1) | copy-start | bytes 52
  2.1 19.4 %slice-start.7 = ((s8[8388608]{0:T(1024)(128)(4,1)}), s8[4194304]{0:T(1024)(128)(4,1)S(1)}, s32[]{:S(2)}) async-start(s8[8388608]{0:T(1024)(128)(4,1)} %bitcast.2), calls=%async_computation.7 | async-start | bytes 8388608
  4.9 5.7 %collective-permute-start = (bf16[8,2176]{1,0:T(8,128)(2,1)S(1)}, bf16[8,2176]{1,0:T(8,128)(2,1)S(1)}, u32[]{:S(2)}, u32[]{:S(2)}) collective-permute-start(bf16[8,2176]{1,0:T(8,128)(2,1)S(1)} %get-tuple-element.22), channel_id=1, source_target_pairs={{0,4},{4,0},{8,12},{12,8},{1,5},{5,1},{9,13},{13,9},{2,6},{6,2},{1... | collective-permute-start | bytes 104456 | tf_op jit(solution)/shard_map/ppermute | solution.py:324
  7.9 5.5 %collective-permute-start.1 = (bf16[8,2176]{1,0:T(8,128)(2,1)S(1)}, bf16[8,2176]{1,0:T(8,128)(2,1)S(1)}, u32[]{:S(2)}, u32[]{:S(2)}) collective-permute-start(bf16[8,2176]{1,0:T(8,128)(2,1)S(1)} %get-tuple-element.23), channel_id=1, source_target_pairs={{0,8},{4,12},{8,0},{12,4},{1,9},{5,13},{9,1},{13,5},{2,10},{6,14},... | collective-permute-start | bytes 104456 | tf_op jit(solution)/shard_map/ppermute | solution.py:324
  10.5 5.7 %collective-permute-start.2 = (bf16[8,2176]{1,0:T(8,128)(2,1)S(1)}, bf16[8,2176]{1,0:T(8,128)(2,1)S(1)}, u32[]{:S(2)}, u32[]{:S(2)}) collective-permute-start(bf16[8,2176]{1,0:T(8,128)(2,1)S(1)} %get-tuple-element.24), channel_id=1, source_target_pairs={{0,12},{4,8},{8,4},{12,0},{1,13},{5,9},{9,5},{13,1},{2,14},{6,10},... | collective-permute-start | bytes 104456 | tf_op jit(solution)/shard_map/ppermute | solution.py:324
  16.3 5.3 %slice-start.8 = ((s8[8388608]{0:T(1024)(128)(4,1)}), s8[4194304]{0:T(1024)(128)(4,1)S(1)}, s32[]{:S(2)}) async-start(s8[8388608]{0:T(1024)(128)(4,1)} %bitcast.2), calls=%async_computation.8 | async-start | bytes 8388608
  16.5 13.4 %copy-start.9 = (bf16[4,2,2048]{2,1,0:T(2,128)(2,1)S(1)}, bf16[4,2,2048]{2,1,0:T(2,128)(2,1)}, u32[]{:S(2)}) copy-start(bf16[4,2,2048]{2,1,0:T(2,128)(2,1)} %hidden.1) | copy-start | bytes 98308
  16.6 1.9 %collective-permute-start.3 = (bf16[8,2048]{1,0:T(8,128)(2,1)S(1)}, bf16[8,2048]{1,0:T(8,128)(2,1)S(1)}, u32[]{:S(2)}, u32[]{:S(2)}) collective-permute-start(bf16[8,2048]{1,0:T(8,128)(2,1)S(1)} %shard_map.160.rest_0_), channel_id=1, source_target_pairs={{0,1},{1,0},{2,3},{3,2},{4,5},{5,4},{6,7},{7,6},{8,9},{9,8},{10,11... | collective-permute-start | bytes 98312 | tf_op jit(solution)/shard_map/ppermute | solution.py:324
  16.6 4.0 %collective-permute-start.4 = (bf16[8,2048]{1,0:T(8,128)(2,1)S(1)}, bf16[8,2048]{1,0:T(8,128)(2,1)S(1)}, u32[]{:S(2)}, u32[]{:S(2)}) collective-permute-start(bf16[8,2048]{1,0:T(8,128)(2,1)S(1)} %shard_map.160.rest_0_), channel_id=1, source_target_pairs={{0,2},{1,3},{2,0},{3,1},{4,6},{5,7},{6,4},{7,5},{8,10},{9,11},{10,... | collective-permute-start | bytes 98312 | tf_op jit(solution)/shard_map/ppermute | solution.py:324
  18.2 3.3 %collective-permute-start.5 = (bf16[8,2048]{1,0:T(8,128)(2,1)S(1)}, bf16[8,2048]{1,0:T(8,128)(2,1)S(1)}, u32[]{:S(2)}, u32[]{:S(2)}) collective-permute-start(bf16[8,2048]{1,0:T(8,128)(2,1)S(1)} %shard_map.160.rest_0_), channel_id=1, source_target_pairs={{0,3},{1,2},{2,1},{3,0},{4,7},{5,6},{6,5},{7,4},{8,11},{9,10},{10,... | collective-permute-start | bytes 98312 | tf_op jit(solution)/shard_map/ppermute | solution.py:324
  21.5 16.4 %slice-start = ((s8[29360128]{0:T(1024)(128)(4,1)}), s8[4194304]{0:T(1024)(128)(4,1)S(1)}, s32[]{:S(2)}) async-start(s8[29360128]{0:T(1024)(128)(4,1)} %bitcast), calls=%async_computation | async-start | bytes 8388608
  21.5 16.4 %slice-start.1 = ((s8[29360128]{0:T(1024)(128)(4,1)}), s8[4194304]{0:T(1024)(128)(4,1)S(1)}, s32[]{:S(2)}) async-start(s8[29360128]{0:T(1024)(128)(4,1)} %bitcast), calls=%async_computation.1 | async-start | bytes 8388608
  21.6 16.4 %slice-start.2 = ((s8[29360128]{0:T(1024)(128)(4,1)}), s8[4194304]{0:T(1024)(128)(4,1)S(1)}, s32[]{:S(2)}) async-start(s8[29360128]{0:T(1024)(128)(4,1)} %bitcast), calls=%async_computation.2 | async-start | bytes 8388608
  21.6 16.4 %slice-start.3 = ((s8[29360128]{0:T(1024)(128)(4,1)}), s8[4194304]{0:T(1024)(128)(4,1)S(1)}, s32[]{:S(2)}) async-start(s8[29360128]{0:T(1024)(128)(4,1)} %bitcast), calls=%async_computation.3 | async-start | bytes 8388608
  23.2 4.5 %collective-permute-start.6 = (bf16[8,2048]{1,0:T(8,128)(2,1)S(1)}, bf16[8,2048]{1,0:T(8,128)(2,1)S(1)}, u32[]{:S(2)}, u32[]{:S(2)}) collective-permute-start(bf16[8,2048]{1,0:T(8,128)(2,1)S(1)} %get-tuple-element.26), channel_id=1, source_target_pairs={{0,4},{4,0},{8,12},{12,8},{1,5},{5,1},{9,13},{13,9},{2,6},{6,2},{1... | collective-permute-start | bytes 98312 | tf_op jit(solution)/shard_map/ppermute | solution.py:324
  23.2 4.9 %collective-permute-start.7 = (bf16[8,2048]{1,0:T(8,128)(2,1)S(1)}, bf16[8,2048]{1,0:T(8,128)(2,1)S(1)}, u32[]{:S(2)}, u32[]{:S(2)}) collective-permute-start(bf16[8,2048]{1,0:T(8,128)(2,1)S(1)} %get-tuple-element.27), channel_id=1, source_target_pairs={{0,8},{4,12},{8,0},{12,4},{1,9},{5,13},{9,1},{13,5},{2,10},{6,14},... | collective-permute-start | bytes 98312 | tf_op jit(solution)/shard_map/ppermute | solution.py:324
  24.2 5.7 %collective-permute-start.8 = (bf16[8,2048]{1,0:T(8,128)(2,1)S(1)}, bf16[8,2048]{1,0:T(8,128)(2,1)S(1)}, u32[]{:S(2)}, u32[]{:S(2)}) collective-permute-start(bf16[8,2048]{1,0:T(8,128)(2,1)S(1)} %get-tuple-element.28), channel_id=1, source_target_pairs={{0,12},{4,8},{8,4},{12,0},{1,13},{5,9},{9,5},{13,1},{2,14},{6,10},... | collective-permute-start | bytes 98312 | tf_op jit(solution)/shard_map/ppermute | solution.py:324
  30.0 8.0 %slice-start.4 = ((s8[29360128]{0:T(1024)(128)(4,1)}), s8[4194304]{0:T(1024)(128)(4,1)S(1)}, s32[]{:S(2)}) async-start(s8[29360128]{0:T(1024)(128)(4,1)} %bitcast), calls=%async_computation.4 | async-start | bytes 8388608
  30.0 8.0 %slice-start.5 = ((s8[29360128]{0:T(1024)(128)(4,1)}), s8[4194304]{0:T(1024)(128)(4,1)S(1)}, s32[]{:S(2)}) async-start(s8[29360128]{0:T(1024)(128)(4,1)} %bitcast), calls=%async_computation.5 | async-start | bytes 8388608
  30.0 8.0 %slice-start.6 = ((s8[29360128]{0:T(1024)(128)(4,1)}), s8[4194304]{0:T(1024)(128)(4,1)S(1)}, s32[]{:S(2)}) async-start(s8[29360128]{0:T(1024)(128)(4,1)} %bitcast), calls=%async_computation.6 | async-start | bytes 8388608
  30.0 8.0 %copy-start.12 = (bf16[2048]{0:T(1024)(128)(2,1)S(1)}, bf16[2048]{0:T(1024)(128)(2,1)}, u32[]{:S(2)}) copy-start(bf16[2048]{0:T(1024)(128)(2,1)} %gain.1) | copy-start | bytes 12292
  30.6 4.8 %collective-permute-start.10 = (bf16[8,2048]{1,0:T(8,128)(2,1)S(1)}, bf16[8,2048]{1,0:T(8,128)(2,1)S(1)}, u32[]{:S(2)}, u32[]{:S(2)}) collective-permute-start(bf16[8,2048]{1,0:T(8,128)(2,1)S(1)} %get-tuple-element.30.rest_0_), channel_id=1, source_target_pairs={{0,8},{4,12},{8,0},{12,4},{1,9},{5,13},{9,1},{13,5},{2,10},{6,14},... | collective-permute-start | bytes 98312 | tf_op jit(solution)/shard_map/ppermute | solution.py:324
  30.8 5.8 %collective-permute-start.11 = (bf16[8,2048]{1,0:T(8,128)(2,1)S(1)}, bf16[8,2048]{1,0:T(8,128)(2,1)S(1)}, u32[]{:S(2)}, u32[]{:S(2)}) collective-permute-start(bf16[8,2048]{1,0:T(8,128)(2,1)S(1)} %get-tuple-element.30.rest_0_), channel_id=1, source_target_pairs={{0,12},{4,8},{8,4},{12,0},{1,13},{5,9},{9,5},{13,1},{2,14},{6,10},... | collective-permute-start | bytes 98312 | tf_op jit(solution)/shard_map/ppermute | solution.py:324
  34.0 3.9 %collective-permute-start.9 = (bf16[8,2048]{1,0:T(8,128)(2,1)S(1)}, bf16[8,2048]{1,0:T(8,128)(2,1)S(1)}, u32[]{:S(2)}, u32[]{:S(2)}) collective-permute-start(bf16[8,2048]{1,0:T(8,128)(2,1)S(1)} %get-tuple-element.30.rest_0_), channel_id=1, source_target_pairs={{0,4},{4,0},{8,12},{12,8},{1,5},{5,1},{9,13},{13,9},{2,6},{6,2},{1... | collective-permute-start | bytes 98312 | tf_op jit(solution)/shard_map/ppermute | solution.py:324
  41.6 3.2 %collective-permute-start.12 = (bf16[2,8,4224]{2,1,0:T(8,128)(2,1)S(1)}, bf16[2,8,4224]{2,1,0:T(8,128)(2,1)S(1)}, u32[]{:S(2)}, u32[]{:S(2)}) collective-permute-start(bf16[2,8,4224]{2,1,0:T(8,128)(2,1)S(1)} %get-tuple-element.32), channel_id=1, source_target_pairs={{0,1},{1,0},{2,3},{3,2},{4,5},{5,4},{6,7},{7,6},{8,9},{9,8},{10,11... | collective-permute-start | bytes 405512 | tf_op jit(solution)/shard_map/ppermute | solution.py:476
  41.6 5.3 %copy-start = (bf16[128,3584]{1,0:T(8,128)(2,1)S(1)}, bf16[128,3584]{1,0:T(8,128)(2,1)}, u32[]{:S(2)}) copy-start(bf16[128,3584]{1,0:T(8,128)(2,1)} %table.1) | copy-start | bytes 2752516
  41.6 5.3 %copy-start.2 = (s32[4]{0:T(128)S(1)}, s32[4]{0:T(128)}, u32[]{:S(2)}) copy-start(s32[4]{0:T(128)} %ids.3) | copy-start | bytes 52
  44.2 1.6 %collective-permute-start.14 = (bf16[2,8,3072]{2,1,0:T(8,128)(2,1)S(1)}, bf16[2,8,3072]{2,1,0:T(8,128)(2,1)S(1)}, u32[]{:S(2)}, u32[]{:S(2)}) collective-permute-start(bf16[2,8,3072]{2,1,0:T(8,128)(2,1)S(1)} %get-tuple-element.37), channel_id=1, source_target_pairs={{0,1},{1,0},{2,3},{3,2},{4,5},{5,4},{6,7},{7,6},{8,9},{9,8},{10,11... | collective-permute-start | bytes 294920 | tf_op jit(solution)/shard_map/ppermute | solution.py:476
  44.8 5.4 %collective-permute-start.13 = (bf16[8,4224]{1,0:T(8,128)(2,1)S(1)}, bf16[8,4224]{1,0:T(8,128)(2,1)S(1)}, u32[]{:S(2)}, u32[]{:S(2)}) collective-permute-start(bf16[8,4224]{1,0:T(8,128)(2,1)S(1)} %get-tuple-element.34), channel_id=1, source_target_pairs={{0,2},{1,3},{2,0},{3,1},{4,6},{5,7},{6,4},{7,5},{8,10},{9,11},{10,... | collective-permute-start | bytes 202760 | tf_op jit(solution)/shard_map/ppermute | solution.py:486
  45.8 4.4 %collective-permute-start.15 = (bf16[8,3072]{1,0:T(8,128)(2,1)S(1)}, bf16[8,3072]{1,0:T(8,128)(2,1)S(1)}, u32[]{:S(2)}, u32[]{:S(2)}) collective-permute-start(bf16[8,3072]{1,0:T(8,128)(2,1)S(1)} %get-tuple-element.39), channel_id=1, source_target_pairs={{0,2},{1,3},{2,0},{3,1},{4,6},{5,7},{6,4},{7,5},{8,10},{9,11},{10,... | collective-permute-start | bytes 147464 | tf_op jit(solution)/shard_map/ppermute | solution.py:486

commit v8 on v7

--- a/solution.py
+++ b/solution.py
@@ -182,17 +182,11 @@
         out[:, span] = value.astype(bf16)
 
 
-def project_kernel(row_count, pre_count, *rest):
-    blocks, weight = rest[:row_count], rest[row_count]
-    outs = rest[row_count + 1 : row_count + 1 + pre_count]
-    stacked, product = rest[row_count + 1 + pre_count :]
-    tokens = blocks[0].shape[0]
+def project_kernel(pre_count, stacked, weight, *rest):
+    outs, product = rest[:pre_count], rest[pre_count]
     amount = outs[0].shape[0]
-    pre_at, row_at = lax.axis_index("pre"), lax.axis_index("row")
-    for s, ref in enumerate(blocks):
-        start = pl.multiple_of(source_of(row_at, s, row_count) * tokens, tokens)
-        stacked[pl.ds(start, tokens), :] = ref[...].astype(f32)
-    product[...] = dot(stacked[...].astype(bf16), weight[...])
+    pre_at = lax.axis_index("pre")
+    product[...] = dot(stacked[...], weight[...])
     for s, out in enumerate(outs):
         start = pl.multiple_of(target_of(pre_at, s, pre_count) * amount, amount)
         out[...] = product[pl.ds(start, amount), :].astype(out.dtype)
@@ -413,21 +407,20 @@
         compiler_params=params(4),
         cost_estimate=cost(40),
     )(*shifted(partials, "pre"))
-    gathered = shifted([mixed] * row_count, "row")
+    gathered = lax.all_gather(mixed, "row", axis=0, tiled=True)
     products = pl.pallas_call(
-        functools.partial(project_kernel, row_count, pre_count),
-        in_specs=[VMEM] * (row_count + 1),
+        functools.partial(project_kernel, pre_count),
+        in_specs=[VMEM] * 2,
         out_specs=[VMEM] * pre_count,
         out_shape=[
             shape_of((amount, out_cols), bf16 if s else f32) for s in range(pre_count)
         ],
         scratch_shapes=[
-            pltpu.VMEM((row_count * tokens, block), f32),
             pltpu.VMEM((row_count * tokens, out_cols), f32),
         ],
         compiler_params=params(8),
         cost_estimate=cost(40),
-    )(*gathered, out_weight)
+    )(gathered, out_weight)
     residual, sent = pl.pallas_call(
         functools.partial(residual_kernel, pre_count),
         in_specs=[VMEM] * (pre_count + 1),

time: 51.1 us -> 54.4 us (1.065)
  blocking collectives: 0 us -> 5.56 us
  starting transfers between devices: 18.7 us -> 17.6 us
  waiting for transfers between devices: 16.9 us -> 15.8 us
    all_gather x0 -> x1, blocking collectives: none -> 5.56 us  [per_device(): gathered = lax.all_gather(mixed, 'row', axis=0, tiled=True)]
    ppermute x12 -> x9, starting transfers between devices: 16 us -> 14.5 us  [shifted(): lax.ppermute(parts[s], axis, [(i, target_of(i, s, count)) for i in range(...]
    ppermute x12 -> x9, waiting for transfers between devices: 14.5 us -> 13.3 us  [shifted(): lax.ppermute(parts[s], axis, [(i, target_of(i, s, count)) for i in range(...]
  transfers between devices with their start and end apart: 16 -> 13, of which waited for: 10 -> 7; matrix products, arithmetic and copies ran while one was open for 0% -> 0% of each run, Pallas kernels for 7% -> 6%
where the time goes in v8:
time: 54.4 us; the launch traced here: 54.2 us
  starting transfers between devices  17.6 us (32%)
  waiting for transfers between devices  15.8 us (29%)
  Pallas kernels  13.4 us (25%)
  blocking collectives  5.56 us (10%)
  between operations  0.98 us (2%)
  local copies, waits for them, and re-layouts  0.85 us (2%)
    ppermute x9, starting transfers between devices, shifted(): lax.ppermute(parts[s], axis, [(i, target_of(i, s, count)) for i in range(...  14.5 us
    ppermute x9, waiting for transfers between devices, shifted(): lax.ppermute(parts[s], axis, [(i, target_of(i, s, count)) for i in range(...  13.3 us
    all_gather x1, blocking collectives, per_device(): gathered = lax.all_gather(mixed, 'row', axis=0, tiled=True)  5.56 us
    pallas_call x1, Pallas kernels, per_device(): pl.pallas_call(functools.partial(feed_first_kernel, pre_count, row_count,...  3.56 us
    pallas_call x1, Pallas kernels, per_device(): pl.pallas_call(functools.partial(attend_kernel, pre_count), in_specs=[SME...  2.71 us
    ppermute x2, waiting for transfers between devices, per_device(): lax.ppermute(sums[j], 'row', [(i, i ^ 2 * j) for i in range(row_count)])  2.51 us
    pallas_call x1, Pallas kernels, per_device(): pl.pallas_call(functools.partial(feed_second_kernel, row_count, first, se...  2.49 us
    ppermute x2, starting transfers between devices, per_device(): lax.ppermute(sums[j], 'row', [(i, i ^ 2 * j) for i in range(row_count)])  2.45 us
  transfers between devices with their start and end apart: 13, of which 7 were waited for; matrix products, arithmetic and copies ran while one was open for 0% of the time, Pallas kernels for 6%

profile of v8, /device:TPU:0, one launch (start us, length us, event | category | flops | bytes accessed | tf_op | source)
XLA Modules:
  0.0 54.2 jit_solution(15774288469986405292)
XLA Ops:
  0.7 0.0 copy-start.1
  0.7 0.0 copy-start.3
  0.7 0.0 copy-start.13
  0.7 0.7 %copy-done.13 = s32[4]{0:T(128)S(1)} copy-done((s32[4]{0:T(128)S(1)}, s32[4]{0:T(128)}, u32[]{:S(2)}) %copy-start.13) | copy-done | bytes 40
  1.5 0.6 %shard_map.158.mask = s32[8,128]{1,0:T(8,128)S(1)} custom-call(s32[4]{0:T(128)S(1)} %copy-done.13), custom_call_target="tpu_custom_call" | custom-call | flops 20000000000 | tf_op jit(solution)/shard_map/pallas_call | solution.py:371
  2.1 0.0 slice-start.7
  2.1 2.7 %shard_map.159 = (bf16[8,2176]{1,0:T(8,128)(2,1)S(1)}, bf16[8,2176]{1,0:T(8,128)(2,1)S(1)}, bf16[8,2176]{1,0:T(8,128)(2,1)S(1)}, bf16[8,2176]{1,0:T(8,128)(2,1)S(1)}) custom-call(s32[4]{0:T(128)S(1)} %copy-done.1, s32[8,128]{1,0:T(8,128)S(1)} %shard_map.158.mask, bf16[4,2,8192]{2,1,0:T(2,128)(2,1)S(1)} %copy-done.6, bf16[128,1024]{1,0:T(8,128)(2,1)S(1)} %copy-done.4, ...), custom_call_target="tpu_custom_call" | custom-call | flops 20000000000 | tf_op jit(solution)/shard_map/pallas_call | solution.py:379
  4.9 3.1 %collective-permute-start = (bf16[8,2176]{1,0:T(8,128)(2,1)S(1)}, bf16[8,2176]{1,0:T(8,128)(2,1)S(1)}, u32[]{:S(2)}, u32[]{:S(2)}) collective-permute-start(bf16[8,2176]{1,0:T(8,128)(2,1)S(1)} %get-tuple-element.22), channel_id=1, source_target_pairs={{0,4},{4,0},{8,12},{12,8},{1,5},{5,1},{9,13},{13,9},{2,6},{6,2},{1... | collective-permute-start | bytes 104456 | tf_op jit(solution)/shard_map/ppermute | solution.py:318
  7.9 2.6 %collective-permute-start.1 = (bf16[8,2176]{1,0:T(8,128)(2,1)S(1)}, bf16[8,2176]{1,0:T(8,128)(2,1)S(1)}, u32[]{:S(2)}, u32[]{:S(2)}) collective-permute-start(bf16[8,2176]{1,0:T(8,128)(2,1)S(1)} %get-tuple-element.23), channel_id=1, source_target_pairs={{0,8},{4,12},{8,0},{12,4},{1,9},{5,13},{9,1},{13,5},{2,10},{6,14},... | collective-permute-start | bytes 104456 | tf_op jit(solution)/shard_map/ppermute | solution.py:318
  10.5 0.0 collective-permute-start.2
  10.5 0.0 collective-permute-done.rest_1_
  10.5 2.9 %collective-permute-done.1.rest_2_ = bf16[8,2176]{1,0:T(8,128)(2,1)S(1)} collective-permute-done((bf16[8,2176]{1,0:T(8,128)(2,1)S(1)}, bf16[8,2176]{1,0:T(8,128)(2,1)S(1)}, u32[]{:S(2)}, u32[]{:S(2)}) %collective-permute-start.1) | collective-permute-done | bytes 34848 | tf_op jit(solution)/shard_map/ppermute | solution.py:318
  13.4 2.9 %collective-permute-done.2.rest_3_ = bf16[8,2176]{1,0:T(8,128)(2,1)S(1)} collective-permute-done((bf16[8,2176]{1,0:T(8,128)(2,1)S(1)}, bf16[8,2176]{1,0:T(8,128)(2,1)S(1)}, u32[]{:S(2)}, u32[]{:S(2)}) %collective-permute-start.2) | collective-permute-done | bytes 34848 | tf_op jit(solution)/shard_map/ppermute | solution.py:318
  16.3 0.3 shard_map.160
  16.5 5.6 %all_gather.3.stacked = bf16[32,2048]{1,0:T(8,128)(2,1)S(1)} all-gather(bf16[8,2048]{1,0:T(8,128)(2,1)S(1)} %shard_map.160), channel_id=1, replica_groups=mesh['grp'=2,'pre'=4,'row'=4] {'row'}, dimensions={0}, use_global_device_ids=true | all-gather | bytes 163840 | tf_op jit(solution)/shard_map/all_gather | solution.py:410
  22.1 0.0 slice-start.1
  22.1 0.0 slice-start.2
  22.1 0.0 slice-start.3
  22.2 1.6 %shard_map.161 = (f32[8,2048]{1,0:T(8,128)S(1)}, bf16[8,2048]{1,0:T(8,128)(2,1)S(1)}, bf16[8,2048]{1,0:T(8,128)(2,1)S(1)}, bf16[8,2048]{1,0:T(8,128)(2,1)S(1)}) custom-call(bf16[32,2048]{1,0:T(8,128)(2,1)S(1)} %all_gather.3.stacked, bf16[2048,2048]{1,0:T(8,128)(2,1)S(1)} %bitcast.3), custom_call_target="tpu_custom_call" | custom-call | flops 40000000000 | tf_op jit(solution)/shard_map/pallas_call | solution.py:411
  23.7 0.1 collective-permute-start.3
  23.8 1.0 %collective-permute-start.4 = (bf16[8,2048]{1,0:T(8,128)(2,1)S(1)}, bf16[8,2048]{1,0:T(8,128)(2,1)S(1)}, u32[]{:S(2)}, u32[]{:S(2)}) collective-permute-start(bf16[8,2048]{1,0:T(8,128)(2,1)S(1)} %get-tuple-element.27), channel_id=1, source_target_pairs={{0,8},{4,12},{8,0},{12,4},{1,9},{5,13},{9,1},{13,5},{2,10},{6,14},... | collective-permute-start | bytes 98312 | tf_op jit(solution)/shard_map/ppermute | solution.py:318
  24.8 3.4 %collective-permute-start.5 = (bf16[8,2048]{1,0:T(8,128)(2,1)S(1)}, bf16[8,2048]{1,0:T(8,128)(2,1)S(1)}, u32[]{:S(2)}, u32[]{:S(2)}) collective-permute-start(bf16[8,2048]{1,0:T(8,128)(2,1)S(1)} %get-tuple-element.28), channel_id=1, source_target_pairs={{0,12},{4,8},{8,4},{12,0},{1,13},{5,9},{9,5},{13,1},{2,14},{6,10},... | collective-permute-start | bytes 98312 | tf_op jit(solution)/shard_map/ppermute | solution.py:318
  28.2 0.0 collective-permute-done.3.rest_1_
  28.2 0.6 %collective-permute-done.4.rest_2_ = bf16[8,2048]{1,0:T(8,128)(2,1)S(1)} collective-permute-done((bf16[8,2048]{1,0:T(8,128)(2,1)S(1)}, bf16[8,2048]{1,0:T(8,128)(2,1)S(1)}, u32[]{:S(2)}, u32[]{:S(2)}) %collective-permute-start.4) | collective-permute-done | bytes 32800 | tf_op jit(solution)/shard_map/ppermute | solution.py:318
  28.8 1.8 %collective-permute-done.5.rest_3_ = bf16[8,2048]{1,0:T(8,128)(2,1)S(1)} collective-permute-done((bf16[8,2048]{1,0:T(8,128)(2,1)S(1)}, bf16[8,2048]{1,0:T(8,128)(2,1)S(1)}, u32[]{:S(2)}, u32[]{:S(2)}) %collective-permute-start.5) | collective-permute-done | bytes 32800 | tf_op jit(solution)/shard_map/ppermute | solution.py:318
  30.6 0.0 copy-start.12
  30.6 0.7 %shard_map.162 = (bf16[4,2,2048]{2,1,0:T(2,128)(2,1)}, bf16[8,2048]{1,0:T(8,128)(2,1)S(1)}) custom-call(bf16[4,2,2048]{2,1,0:T(2,128)(2,1)S(1)} %copy-done.9, f32[8,2048]{1,0:T(8,128)S(1)} %get-tuple-element.25.rest_0_, bf16[8,2048]{1,0:T(8,128)(2,1)S(1)} %collective-permute-done.3.rest_1_, bf16[8,2048]{1,0:T(8,128)(2,1)S(1)} %collective-permute-done.4.rest_2_, ...), custom_call_target="tpu_custom_call" | custom-call | flops 40000000000 | tf_op jit(solution)/shard_map/pallas_call | solution.py:424
  31.2 0.6 %collective-permute-start.6 = (bf16[8,2048]{1,0:T(8,128)(2,1)S(1)}, bf16[8,2048]{1,0:T(8,128)(2,1)S(1)}, u32[]{:S(2)}, u32[]{:S(2)}) collective-permute-start(bf16[8,2048]{1,0:T(8,128)(2,1)S(1)} %get-tuple-element.30.rest_0_), channel_id=1, source_target_pairs={{0,4},{4,0},{8,12},{12,8},{1,5},{5,1},{9,13},{13,9},{2,6},{6,2},{1... | collective-permute-start | bytes 98312 | tf_op jit(solution)/shard_map/ppermute | solution.py:318
  31.8 3.3 %collective-permute-start.7 = (bf16[8,2048]{1,0:T(8,128)(2,1)S(1)}, bf16[8,2048]{1,0:T(8,128)(2,1)S(1)}, u32[]{:S(2)}, u32[]{:S(2)}) collective-permute-start(bf16[8,2048]{1,0:T(8,128)(2,1)S(1)} %get-tuple-element.30.rest_0_), channel_id=1, source_target_pairs={{0,8},{4,12},{8,0},{12,4},{1,9},{5,13},{9,1},{13,5},{2,10},{6,14},... | collective-permute-start | bytes 98312 | tf_op jit(solution)/shard_map/ppermute | solution.py:318
  35.1 0.5 collective-permute-start.8
  35.6 0.0 collective-permute-done.6.rest_1_
  35.6 1.4 %collective-permute-done.7.rest_2_ = bf16[8,2048]{1,0:T(8,128)(2,1)S(1)} collective-permute-done((bf16[8,2048]{1,0:T(8,128)(2,1)S(1)}, bf16[8,2048]{1,0:T(8,128)(2,1)S(1)}, u32[]{:S(2)}, u32[]{:S(2)}) %collective-permute-start.7) | collective-permute-done | bytes 32800 | tf_op jit(solution)/shard_map/ppermute | solution.py:318
  37.0 3.8 %collective-permute-done.8.rest_3_ = bf16[8,2048]{1,0:T(8,128)(2,1)S(1)} collective-permute-done((bf16[8,2048]{1,0:T(8,128)(2,1)S(1)}, bf16[8,2048]{1,0:T(8,128)(2,1)S(1)}, u32[]{:S(2)}, u32[]{:S(2)}) %collective-permute-start.8) | collective-permute-done | bytes 32800 | tf_op jit(solution)/shard_map/ppermute | solution.py:318
  40.9 3.6 %shard_map.164 = (f32[2,8,4224]{2,1,0:T(8,128)S(1)}, bf16[2,8,4224]{2,1,0:T(8,128)(2,1)S(1)}, bf16[64,4096]{1,0:T(8,128)(2,1)S(1)}) custom-call(bf16[2048]{0:T(1024)(128)(2,1)S(1)} %copy-done.12, bf16[8,2048]{1,0:T(8,128)(2,1)S(1)} %get-tuple-element.30.rest_0_, bf16[8,2048]{1,0:T(8,128)(2,1)S(1)} %collective-permute-done.6.rest_1_, ...), custom_call_target="tpu_custom_call" | custom-call | flops 16000000000 | tf_op jit(solution)/shard_map/pallas_call | solution.py:437
  44.5 0.1 collective-permute-start.9
  44.6 0.0 copy-start
  44.6 0.0 copy-start.2
  44.6 2.5 %shard_map.166 = (f32[2,8,3072]{2,1,0:T(8,128)S(1)}, bf16[2,8,3072]{2,1,0:T(8,128)(2,1)S(1)}) custom-call(bf16[64,4096]{1,0:T(8,128)(2,1)S(1)} %get-tuple-element.35.spread, bf16[2048,2,3584]{2,1,0:T(2,128)(2,1)S(1)} %bitcast.1), custom_call_target="tpu_custom_call" | custom-call | flops 16000000000 | tf_op jit(solution)/shard_map/pallas_call | solution.py:453
  47.1 0.5 collective-permute-start.11
  47.6 0.0 collective-permute-done.9.received
  47.6 0.1 shard_map.165
  47.7 1.6 %collective-permute-start.10 = (bf16[8,4224]{1,0:T(8,128)(2,1)S(1)}, bf16[8,4224]{1,0:T(8,128)(2,1)S(1)}, u32[]{:S(2)}, u32[]{:S(2)}) collective-permute-start(bf16[8,4224]{1,0:T(8,128)(2,1)S(1)} %get-tuple-element.34), channel_id=1, source_target_pairs={{0,2},{1,3},{2,0},{3,1},{4,6},{5,7},{6,4},{7,5},{8,10},{9,11},{10,... | collective-permute-start | bytes 202760 | tf_op jit(solution)/shard_map/ppermute | solution.py:479
  49.3 0.0 collective-permute-done.11.received
  49.3 0.9 %collective-permute-start.12 = (bf16[8,3072]{1,0:T(8,128)(2,1)S(1)}, bf16[8,3072]{1,0:T(8,128)(2,1)S(1)}, u32[]{:S(2)}, u32[]{:S(2)}) collective-permute-start(bf16[8,3072]{1,0:T(8,128)(2,1)S(1)} %get-tuple-element.39), channel_id=1, source_target_pairs={{0,2},{1,3},{2,0},{3,1},{4,6},{5,7},{6,4},{7,5},{8,10},{9,11},{10,... | collective-permute-start | bytes 147464 | tf_op jit(solution)/shard_map/ppermute | solution.py:479
  50.2 0.8 %shard_map.163.scales = f32[8,3584]{1,0:T(8,128)S(1)} custom-call(s32[4]{0:T(128)S(1)} %copy-done.2, bf16[128,3584]{1,0:T(8,128)(2,1)S(1)} %copy-done), custom_call_target="tpu_custom_call" | custom-call | tf_op jit(solution)/shard_map/pallas_call | solution.py:362
  51.0 2.5 %collective-permute-done.12.rest_3_ = bf16[8,3072]{1,0:T(8,128)(2,1)S(1)} collective-permute-done((bf16[8,3072]{1,0:T(8,128)(2,1)S(1)}, bf16[8,3072]{1,0:T(8,128)(2,1)S(1)}, u32[]{:S(2)}, u32[]{:S(2)}) %collective-permute-start.12) | collective-permute-done | bytes 49184 | tf_op jit(solution)/shard_map/ppermute | solution.py:479
  53.5 0.0 collective-permute-done.10.rest_1_
  53.5 0.8 %shard_map.168 = bf16[4,2,3584]{2,1,0:T(2,128)(2,1)} custom-call(f32[8,3584]{1,0:T(8,128)S(1)} %shard_map.163.scales, f32[8,4224]{1,0:T(8,128)S(1)} %get-tuple-element.33.rest_0_, bf16[8,4224]{1,0:T(8,128)(2,1)S(1)} %collective-permute-done.10.rest_1_, f32[8,3072]{1,0:T(8,128)S(1)} %get-tuple-element.38.rest_2_, ...), custom_call_target="tpu_custom_call" | custom-call | tf_op jit(solution)/shard_map/pallas_call | solution.py:482
  (38 shorter events, 0.1 us)
Async XLA Ops:
  0.6 1.4 %copy-start.6 = (bf16[4,2,8192]{2,1,0:T(2,128)(2,1)S(1)}, bf16[4,2,8192]{2,1,0:T(2,128)(2,1)}, u32[]{:S(2)}) copy-start(bf16[4,2,8192]{2,1,0:T(2,128)(2,1)} %queries.1) | copy-start | bytes 393220
  0.6 1.4 %copy-start.4 = (bf16[128,1024]{1,0:T(8,128)(2,1)S(1)}, bf16[128,1024]{1,0:T(8,128)(2,1)}, u32[]{:S(2)}) copy-start(bf16[128,1024]{1,0:T(8,128)(2,1)} %prefix_keys.1) | copy-start | bytes 786436
  0.7 1.4 %copy-start.5 = (bf16[128,1024]{1,0:T(8,128)(2,1)S(1)}, bf16[128,1024]{1,0:T(8,128)(2,1)}, u32[]{:S(2)}) copy-start(bf16[128,1024]{1,0:T(8,128)(2,1)} %prefix_values.1) | copy-start | bytes 786436
  0.7 1.4 %copy-start.7 = (bf16[4,16,1024]{2,1,0:T(8,128)(2,1)S(1)}, bf16[4,16,1024]{2,1,0:T(8,128)(2,1)}, u32[]{:S(2)}) copy-start(bf16[4,16,1024]{2,1,0:T(8,128)(2,1)} %suffix_keys.1) | copy-start | bytes 393220
  0.7 1.4 %copy-start.8 = (bf16[4,16,1024]{2,1,0:T(8,128)(2,1)S(1)}, bf16[4,16,1024]{2,1,0:T(8,128)(2,1)}, u32[]{:S(2)}) copy-start(bf16[4,16,1024]{2,1,0:T(8,128)(2,1)} %suffix_values.1) | copy-start | bytes 393220
  0.7 1.4 %copy-start.10 = (bf16[4,2,1024]{2,1,0:T(2,128)(2,1)S(1)}, bf16[4,2,1024]{2,1,0:T(2,128)(2,1)}, u32[]{:S(2)}) copy-start(bf16[4,2,1024]{2,1,0:T(2,128)(2,1)} %new_keys.1) | copy-start | bytes 49156
  0.7 1.4 %copy-start.11 = (bf16[4,2,1024]{2,1,0:T(2,128)(2,1)S(1)}, bf16[4,2,1024]{2,1,0:T(2,128)(2,1)}, u32[]{:S(2)}) copy-start(bf16[4,2,1024]{2,1,0:T(2,128)(2,1)} %new_values.1) | copy-start | bytes 49156
  0.7 1.4 %copy-start.1 = (s32[4]{0:T(128)S(1)}, s32[4]{0:T(128)}, u32[]{:S(2)}) copy-start(s32[4]{0:T(128)} %ids.3) | copy-start | bytes 52
  0.7 1.4 %copy-start.3 = (bf16[128,2,1024]{2,1,0:T(2,128)(2,1)S(1)}, bf16[128,2,1024]{2,1,0:T(2,128)(2,1)}, u32[]{:S(2)}) copy-start(bf16[128,2,1024]{2,1,0:T(2,128)(2,1)} %kv_scales.1) | copy-start | bytes 1572868
  0.7 0.8 %copy-start.13 = (s32[4]{0:T(128)S(1)}, s32[4]{0:T(128)}, u32[]{:S(2)}) copy-start(s32[4]{0:T(128)} %lengths.1) | copy-start | bytes 52
  2.1 20.0 %slice-start.7 = ((s8[8388608]{0:T(1024)(128)(4,1)}), s8[4194304]{0:T(1024)(128)(4,1)S(1)}, s32[]{:S(2)}) async-start(s8[8388608]{0:T(1024)(128)(4,1)} %bitcast.2), calls=%async_computation.7 | async-start | bytes 8388608
  4.9 5.7 %collective-permute-start = (bf16[8,2176]{1,0:T(8,128)(2,1)S(1)}, bf16[8,2176]{1,0:T(8,128)(2,1)S(1)}, u32[]{:S(2)}, u32[]{:S(2)}) collective-permute-start(bf16[8,2176]{1,0:T(8,128)(2,1)S(1)} %get-tuple-element.22), channel_id=1, source_target_pairs={{0,4},{4,0},{8,12},{12,8},{1,5},{5,1},{9,13},{13,9},{2,6},{6,2},{1... | collective-permute-start | bytes 104456 | tf_op jit(solution)/shard_map/ppermute | solution.py:318
  7.9 5.5 %collective-permute-start.1 = (bf16[8,2176]{1,0:T(8,128)(2,1)S(1)}, bf16[8,2176]{1,0:T(8,128)(2,1)S(1)}, u32[]{:S(2)}, u32[]{:S(2)}) collective-permute-start(bf16[8,2176]{1,0:T(8,128)(2,1)S(1)} %get-tuple-element.23), channel_id=1, source_target_pairs={{0,8},{4,12},{8,0},{12,4},{1,9},{5,13},{9,1},{13,5},{2,10},{6,14},... | collective-permute-start | bytes 104456 | tf_op jit(solution)/shard_map/ppermute | solution.py:318
  10.5 5.7 %collective-permute-start.2 = (bf16[8,2176]{1,0:T(8,128)(2,1)S(1)}, bf16[8,2176]{1,0:T(8,128)(2,1)S(1)}, u32[]{:S(2)}, u32[]{:S(2)}) collective-permute-start(bf16[8,2176]{1,0:T(8,128)(2,1)S(1)} %get-tuple-element.24), channel_id=1, source_target_pairs={{0,12},{4,8},{8,4},{12,0},{1,13},{5,9},{9,5},{13,1},{2,14},{6,10},... | collective-permute-start | bytes 104456 | tf_op jit(solution)/shard_map/ppermute | solution.py:318
  16.3 5.8 %slice-start.8 = ((s8[8388608]{0:T(1024)(128)(4,1)}), s8[4194304]{0:T(1024)(128)(4,1)S(1)}, s32[]{:S(2)}) async-start(s8[8388608]{0:T(1024)(128)(4,1)} %bitcast.2), calls=%async_computation.8 | async-start | bytes 8388608
  22.1 8.5 %copy-start.9 = (bf16[4,2,2048]{2,1,0:T(2,128)(2,1)S(1)}, bf16[4,2,2048]{2,1,0:T(2,128)(2,1)}, u32[]{:S(2)}) copy-start(bf16[4,2,2048]{2,1,0:T(2,128)(2,1)} %hidden.1) | copy-start | bytes 98308
  22.1 18.7 %slice-start = ((s8[29360128]{0:T(1024)(128)(4,1)}), s8[4194304]{0:T(1024)(128)(4,1)S(1)}, s32[]{:S(2)}) async-start(s8[29360128]{0:T(1024)(128)(4,1)} %bitcast), calls=%async_computation | async-start | bytes 8388608
  22.1 18.7 %slice-start.1 = ((s8[29360128]{0:T(1024)(128)(4,1)}), s8[4194304]{0:T(1024)(128)(4,1)S(1)}, s32[]{:S(2)}) async-start(s8[29360128]{0:T(1024)(128)(4,1)} %bitcast), calls=%async_computation.1 | async-start | bytes 8388608
  22.1 18.7 %slice-start.2 = ((s8[29360128]{0:T(1024)(128)(4,1)}), s8[4194304]{0:T(1024)(128)(4,1)S(1)}, s32[]{:S(2)}) async-start(s8[29360128]{0:T(1024)(128)(4,1)} %bitcast), calls=%async_computation.2 | async-start | bytes 8388608
  22.1 18.7 %slice-start.3 = ((s8[29360128]{0:T(1024)(128)(4,1)}), s8[4194304]{0:T(1024)(128)(4,1)S(1)}, s32[]{:S(2)}) async-start(s8[29360128]{0:T(1024)(128)(4,1)} %bitcast), calls=%async_computation.3 | async-start | bytes 8388608
  23.7 4.5 %collective-permute-start.3 = (bf16[8,2048]{1,0:T(8,128)(2,1)S(1)}, bf16[8,2048]{1,0:T(8,128)(2,1)S(1)}, u32[]{:S(2)}, u32[]{:S(2)}) collective-permute-start(bf16[8,2048]{1,0:T(8,128)(2,1)S(1)} %get-tuple-element.26), channel_id=1, source_target_pairs={{0,4},{4,0},{8,12},{12,8},{1,5},{5,1},{9,13},{13,9},{2,6},{6,2},{1... | collective-permute-start | bytes 98312 | tf_op jit(solution)/shard_map/ppermute | solution.py:318
  23.8 5.0 %collective-permute-start.4 = (bf16[8,2048]{1,0:T(8,128)(2,1)S(1)}, bf16[8,2048]{1,0:T(8,128)(2,1)S(1)}, u32[]{:S(2)}, u32[]{:S(2)}) collective-permute-start(bf16[8,2048]{1,0:T(8,128)(2,1)S(1)} %get-tuple-element.27), channel_id=1, source_target_pairs={{0,8},{4,12},{8,0},{12,4},{1,9},{5,13},{9,1},{13,5},{2,10},{6,14},... | collective-permute-start | bytes 98312 | tf_op jit(solution)/shard_map/ppermute | solution.py:318
  24.8 5.8 %collective-permute-start.5 = (bf16[8,2048]{1,0:T(8,128)(2,1)S(1)}, bf16[8,2048]{1,0:T(8,128)(2,1)S(1)}, u32[]{:S(2)}, u32[]{:S(2)}) collective-permute-start(bf16[8,2048]{1,0:T(8,128)(2,1)S(1)} %get-tuple-element.28), channel_id=1, source_target_pairs={{0,12},{4,8},{8,4},{12,0},{1,13},{5,9},{9,5},{13,1},{2,14},{6,10},... | collective-permute-start | bytes 98312 | tf_op jit(solution)/shard_map/ppermute | solution.py:318
  30.6 10.3 %slice-start.4 = ((s8[29360128]{0:T(1024)(128)(4,1)}), s8[4194304]{0:T(1024)(128)(4,1)S(1)}, s32[]{:S(2)}) async-start(s8[29360128]{0:T(1024)(128)(4,1)} %bitcast), calls=%async_computation.4 | async-start | bytes 8388608
  30.6 10.3 %slice-start.5 = ((s8[29360128]{0:T(1024)(128)(4,1)}), s8[4194304]{0:T(1024)(128)(4,1)S(1)}, s32[]{:S(2)}) async-start(s8[29360128]{0:T(1024)(128)(4,1)} %bitcast), calls=%async_computation.5 | async-start | bytes 8388608
  30.6 10.3 %slice-start.6 = ((s8[29360128]{0:T(1024)(128)(4,1)}), s8[4194304]{0:T(1024)(128)(4,1)S(1)}, s32[]{:S(2)}) async-start(s8[29360128]{0:T(1024)(128)(4,1)} %bitcast), calls=%async_computation.6 | async-start | bytes 8388608
  30.6 10.3 %copy-start.12 = (bf16[2048]{0:T(1024)(128)(2,1)S(1)}, bf16[2048]{0:T(1024)(128)(2,1)}, u32[]{:S(2)}) copy-start(bf16[2048]{0:T(1024)(128)(2,1)} %gain.1) | copy-start | bytes 12292
  31.2 4.4 %collective-permute-start.6 = (bf16[8,2048]{1,0:T(8,128)(2,1)S(1)}, bf16[8,2048]{1,0:T(8,128)(2,1)S(1)}, u32[]{:S(2)}, u32[]{:S(2)}) collective-permute-start(bf16[8,2048]{1,0:T(8,128)(2,1)S(1)} %get-tuple-element.30.rest_0_), channel_id=1, source_target_pairs={{0,4},{4,0},{8,12},{12,8},{1,5},{5,1},{9,13},{13,9},{2,6},{6,2},{1... | collective-permute-start | bytes 98312 | tf_op jit(solution)/shard_map/ppermute | solution.py:318
  31.8 5.2 %collective-permute-start.7 = (bf16[8,2048]{1,0:T(8,128)(2,1)S(1)}, bf16[8,2048]{1,0:T(8,128)(2,1)S(1)}, u32[]{:S(2)}, u32[]{:S(2)}) collective-permute-start(bf16[8,2048]{1,0:T(8,128)(2,1)S(1)} %get-tuple-element.30.rest_0_), channel_id=1, source_target_pairs={{0,8},{4,12},{8,0},{12,4},{1,9},{5,13},{9,1},{13,5},{2,10},{6,14},... | collective-permute-start | bytes 98312 | tf_op jit(solution)/shard_map/ppermute | solution.py:318
  35.1 5.7 %collective-permute-start.8 = (bf16[8,2048]{1,0:T(8,128)(2,1)S(1)}, bf16[8,2048]{1,0:T(8,128)(2,1)S(1)}, u32[]{:S(2)}, u32[]{:S(2)}) collective-permute-start(bf16[8,2048]{1,0:T(8,128)(2,1)S(1)} %get-tuple-element.30.rest_0_), channel_id=1, source_target_pairs={{0,12},{4,8},{8,4},{12,0},{1,13},{5,9},{9,5},{13,1},{2,14},{6,10},... | collective-permute-start | bytes 98312 | tf_op jit(solution)/shard_map/ppermute | solution.py:318
  44.5 3.1 %collective-permute-start.9 = (bf16[2,8,4224]{2,1,0:T(8,128)(2,1)S(1)}, bf16[2,8,4224]{2,1,0:T(8,128)(2,1)S(1)}, u32[]{:S(2)}, u32[]{:S(2)}) collective-permute-start(bf16[2,8,4224]{2,1,0:T(8,128)(2,1)S(1)} %get-tuple-element.32), channel_id=1, source_target_pairs={{0,1},{1,0},{2,3},{3,2},{4,5},{5,4},{6,7},{7,6},{8,9},{9,8},{10,11... | collective-permute-start | bytes 405512 | tf_op jit(solution)/shard_map/ppermute | solution.py:469
  44.6 5.6 %copy-start = (bf16[128,3584]{1,0:T(8,128)(2,1)S(1)}, bf16[128,3584]{1,0:T(8,128)(2,1)}, u32[]{:S(2)}) copy-start(bf16[128,3584]{1,0:T(8,128)(2,1)} %table.1) | copy-start | bytes 2752516
  44.6 5.6 %copy-start.2 = (s32[4]{0:T(128)S(1)}, s32[4]{0:T(128)}, u32[]{:S(2)}) copy-start(s32[4]{0:T(128)} %ids.3) | copy-start | bytes 52
  47.1 2.2 %collective-permute-start.11 = (bf16[2,8,3072]{2,1,0:T(8,128)(2,1)S(1)}, bf16[2,8,3072]{2,1,0:T(8,128)(2,1)S(1)}, u32[]{:S(2)}, u32[]{:S(2)}) collective-permute-start(bf16[2,8,3072]{2,1,0:T(8,128)(2,1)S(1)} %get-tuple-element.37), channel_id=1, source_target_pairs={{0,1},{1,0},{2,3},{3,2},{4,5},{5,4},{6,7},{7,6},{8,9},{9,8},{10,11... | collective-permute-start | bytes 294920 | tf_op jit(solution)/shard_map/ppermute | solution.py:469
  47.7 5.8 %collective-permute-start.10 = (bf16[8,4224]{1,0:T(8,128)(2,1)S(1)}, bf16[8,4224]{1,0:T(8,128)(2,1)S(1)}, u32[]{:S(2)}, u32[]{:S(2)}) collective-permute-start(bf16[8,4224]{1,0:T(8,128)(2,1)S(1)} %get-tuple-element.34), channel_id=1, source_target_pairs={{0,2},{1,3},{2,0},{3,1},{4,6},{5,7},{6,4},{7,5},{8,10},{9,11},{10,... | collective-permute-start | bytes 202760 | tf_op jit(solution)/shard_map/ppermute | solution.py:479
  49.3 4.2 %collective-permute-start.12 = (bf16[8,3072]{1,0:T(8,128)(2,1)S(1)}, bf16[8,3072]{1,0:T(8,128)(2,1)S(1)}, u32[]{:S(2)}, u32[]{:S(2)}) collective-permute-start(bf16[8,3072]{1,0:T(8,128)(2,1)S(1)} %get-tuple-element.39), channel_id=1, source_target_pairs={{0,2},{1,3},{2,0},{3,1},{4,6},{5,7},{6,4},{7,5},{8,10},{9,11},{10,... | collective-permute-start | bytes 147464 | tf_op jit(solution)/shard_map/ppermute | solution.py:479

commit v9 on v7

--- a/solution.py
+++ b/solution.py
@@ -151,7 +151,7 @@
             packed = packed + (pltpu.roll(piece, place * block_heads, 1) if place else piece)
         stage[at, :, block:] = packed.astype(bf16)
     for s in range(pre_count):
-        outs[s][...] = stage[target_of(me, s, pre_count)]
+        outs[s][...] = stage[lax.rem(me + s, pre_count)]
 
 
 def merge_kernel(parts, *rest):
@@ -405,6 +405,10 @@
         new_values,
         kv_scales,
     )
+    ring = [partials[0]] + [
+        lax.ppermute(partials[s], "pre", [(i, (i + s) % pre_count) for i in range(pre_count)])
+        for s in range(1, pre_count)
+    ]
     mixed = pl.pallas_call(
         functools.partial(merge_kernel, pre_count),
         in_specs=[VMEM] * pre_count,
@@ -412,7 +416,7 @@
         out_shape=shape_of((tokens, block)),
         compiler_params=params(4),
         cost_estimate=cost(40),
-    )(*shifted(partials, "pre"))
+    )(*ring)
     gathered = shifted([mixed] * row_count, "row")
     products = pl.pallas_call(
         functools.partial(project_kernel, row_count, pre_count),

time: 51.1 us -> 50.4 us (0.986)
  waiting for transfers between devices: 16.9 us -> 15.4 us
  starting transfers between devices: 18.7 us -> 19.6 us
    ppermute x0 -> x3, starting transfers between devices: none -> 7 us  [per_device(): lax.ppermute(partials[s], 'pre', [(i, (i + s) % pre_count) for i in range...]
    ppermute x12 -> x9, starting transfers between devices: 16 us -> 9.87 us  [shifted(): lax.ppermute(parts[s], axis, [(i, target_of(i, s, count)) for i in range(...]
    ppermute x12 -> x9, waiting for transfers between devices: 14.5 us -> 10.3 us  [shifted(): lax.ppermute(parts[s], axis, [(i, target_of(i, s, count)) for i in range(...]
    ppermute x0 -> x3, waiting for transfers between devices: none -> 2.59 us  [per_device(): lax.ppermute(partials[s], 'pre', [(i, (i + s) % pre_count) for i in range...]
  transfers between devices with their start and end apart: 16 -> 16, of which waited for: 10 -> 9; matrix products, arithmetic and copies ran while one was open for 0% -> 0% of each run, Pallas kernels for 7% -> 7%
where the time goes in v9:
time: 50.4 us; the launch traced here: 50.3 us
  starting transfers between devices  19.6 us (39%)
  waiting for transfers between devices  15.4 us (31%)
  Pallas kernels  13.4 us (27%)
  between operations  0.99 us (2%)
  local copies, waits for them, and re-layouts  0.85 us (2%)
    ppermute x9, waiting for transfers between devices, shifted(): lax.ppermute(parts[s], axis, [(i, target_of(i, s, count)) for i in range(...  10.3 us
    ppermute x9, starting transfers between devices, shifted(): lax.ppermute(parts[s], axis, [(i, target_of(i, s, count)) for i in range(...  9.87 us
    ppermute x3, starting transfers between devices, per_device(): lax.ppermute(partials[s], 'pre', [(i, (i + s) % pre_count) for i in range...  7 us
    pallas_call x1, Pallas kernels, per_device(): pl.pallas_call(functools.partial(feed_first_kernel, pre_count, row_count,...  3.56 us
    pallas_call x1, Pallas kernels, per_device(): pl.pallas_call(functools.partial(attend_kernel, pre_count), in_specs=[SME...  2.7 us
    ppermute x3, waiting for transfers between devices, per_device(): lax.ppermute(partials[s], 'pre', [(i, (i + s) % pre_count) for i in range...  2.59 us
    pallas_call x1, Pallas kernels, per_device(): pl.pallas_call(functools.partial(feed_second_kernel, row_count, first, se...  2.48 us
    ppermute x2, waiting for transfers between devices, per_device(): lax.ppermute(sums[j], 'row', [(i, i ^ 2 * j) for i in range(row_count)])  2.46 us
  transfers between devices with their start and end apart: 16, of which 9 were waited for; matrix products, arithmetic and copies ran while one was open for 0% of the time, Pallas kernels for 7%

profile of v9, /device:TPU:0, one launch (start us, length us, event | category | flops | bytes accessed | tf_op | source)
XLA Modules:
  0.0 50.3 jit_solution(18219694809355804073)
XLA Ops:
  0.7 0.0 copy-start.1
  0.7 0.7 %copy-done.13 = s32[4]{0:T(128)S(1)} copy-done((s32[4]{0:T(128)S(1)}, s32[4]{0:T(128)}, u32[]{:S(2)}) %copy-start.13) | copy-done | bytes 40
  1.5 0.6 %shard_map.158.mask = s32[8,128]{1,0:T(8,128)S(1)} custom-call(s32[4]{0:T(128)S(1)} %copy-done.13), custom_call_target="tpu_custom_call" | custom-call | flops 20000000000 | tf_op jit(solution)/shard_map/pallas_call | solution.py:377
  2.1 0.0 slice-start.7
  2.1 2.7 %shard_map.159 = (bf16[8,2176]{1,0:T(8,128)(2,1)S(1)}, bf16[8,2176]{1,0:T(8,128)(2,1)S(1)}, bf16[8,2176]{1,0:T(8,128)(2,1)S(1)}, bf16[8,2176]{1,0:T(8,128)(2,1)S(1)}) custom-call(s32[4]{0:T(128)S(1)} %copy-done.1, s32[8,128]{1,0:T(8,128)S(1)} %shard_map.158.mask, bf16[4,2,8192]{2,1,0:T(2,128)(2,1)S(1)} %copy-done.6, bf16[128,1024]{1,0:T(8,128)(2,1)S(1)} %copy-done.4, ...), custom_call_target="tpu_custom_call" | custom-call | flops 20000000000 | tf_op jit(solution)/shard_map/pallas_call | solution.py:385
  4.8 3.1 %collective-permute-start = (bf16[8,2176]{1,0:T(8,128)(2,1)S(1)}, bf16[8,2176]{1,0:T(8,128)(2,1)S(1)}, u32[]{:S(2)}, u32[]{:S(2)}) collective-permute-start(bf16[8,2176]{1,0:T(8,128)(2,1)S(1)} %get-tuple-element.22), channel_id=1, source_target_pairs={{0,4},{4,8},{8,12},{12,0},{1,5},{5,9},{9,13},{13,1},{2,6},{6,10},{... | collective-permute-start | bytes 104456 | tf_op jit(solution)/shard_map/ppermute | solution.py:409
  7.9 2.6 %collective-permute-start.1 = (bf16[8,2176]{1,0:T(8,128)(2,1)S(1)}, bf16[8,2176]{1,0:T(8,128)(2,1)S(1)}, u32[]{:S(2)}, u32[]{:S(2)}) collective-permute-start(bf16[8,2176]{1,0:T(8,128)(2,1)S(1)} %get-tuple-element.23), channel_id=1, source_target_pairs={{0,8},{4,12},{8,0},{12,4},{1,9},{5,13},{9,1},{13,5},{2,10},{6,14},... | collective-permute-start | bytes 104456 | tf_op jit(solution)/shard_map/ppermute | solution.py:409
  10.5 1.3 %collective-permute-start.2 = (bf16[8,2176]{1,0:T(8,128)(2,1)S(1)}, bf16[8,2176]{1,0:T(8,128)(2,1)S(1)}, u32[]{:S(2)}, u32[]{:S(2)}) collective-permute-start(bf16[8,2176]{1,0:T(8,128)(2,1)S(1)} %get-tuple-element.24), channel_id=1, source_target_pairs={{0,12},{4,0},{8,4},{12,8},{1,13},{5,1},{9,5},{13,9},{2,14},{6,2},{... | collective-permute-start | bytes 104456 | tf_op jit(solution)/shard_map/ppermute | solution.py:409
  11.9 1.3 %collective-permute-done.1.rest_2_ = bf16[8,2176]{1,0:T(8,128)(2,1)S(1)} collective-permute-done((bf16[8,2176]{1,0:T(8,128)(2,1)S(1)}, bf16[8,2176]{1,0:T(8,128)(2,1)S(1)}, u32[]{:S(2)}, u32[]{:S(2)}) %collective-permute-start.1) | collective-permute-done | bytes 34848 | tf_op jit(solution)/shard_map/ppermute | solution.py:409
  13.1 1.3 %collective-permute-done.2.rest_3_ = bf16[8,2176]{1,0:T(8,128)(2,1)S(1)} collective-permute-done((bf16[8,2176]{1,0:T(8,128)(2,1)S(1)}, bf16[8,2176]{1,0:T(8,128)(2,1)S(1)}, u32[]{:S(2)}, u32[]{:S(2)}) %collective-permute-start.2) | collective-permute-done | bytes 34848 | tf_op jit(solution)/shard_map/ppermute | solution.py:409
  14.4 0.3 shard_map.160.rest_0_
  14.7 0.0 copy-start.9
  14.7 0.1 collective-permute-start.3
  14.8 1.6 %collective-permute-start.4 = (bf16[8,2048]{1,0:T(8,128)(2,1)S(1)}, bf16[8,2048]{1,0:T(8,128)(2,1)S(1)}, u32[]{:S(2)}, u32[]{:S(2)}) collective-permute-start(bf16[8,2048]{1,0:T(8,128)(2,1)S(1)} %shard_map.160.rest_0_), channel_id=1, source_target_pairs={{0,2},{1,3},{2,0},{3,1},{4,6},{5,7},{6,4},{7,5},{8,10},{9,11},{10,... | collective-permute-start | bytes 98312 | tf_op jit(solution)/shard_map/ppermute | solution.py:324
  16.4 0.3 collective-permute-start.5
  16.7 0.0 collective-permute-done.3.rest_1_
  16.7 2.1 %collective-permute-done.4.rest_2_ = bf16[8,2048]{1,0:T(8,128)(2,1)S(1)} collective-permute-done((bf16[8,2048]{1,0:T(8,128)(2,1)S(1)}, bf16[8,2048]{1,0:T(8,128)(2,1)S(1)}, u32[]{:S(2)}, u32[]{:S(2)}) %collective-permute-start.4) | collective-permute-done | bytes 32800 | tf_op jit(solution)/shard_map/ppermute | solution.py:324
  18.8 0.9 %collective-permute-done.5.rest_3_ = bf16[8,2048]{1,0:T(8,128)(2,1)S(1)} collective-permute-done((bf16[8,2048]{1,0:T(8,128)(2,1)S(1)}, bf16[8,2048]{1,0:T(8,128)(2,1)S(1)}, u32[]{:S(2)}, u32[]{:S(2)}) %collective-permute-start.5) | collective-permute-done | bytes 32800 | tf_op jit(solution)/shard_map/ppermute | solution.py:324
  19.7 0.0 slice-start.1
  19.7 0.0 slice-start.2
  19.7 0.0 slice-start.3
  19.7 1.6 %shard_map.161 = (f32[8,2048]{1,0:T(8,128)S(1)}, bf16[8,2048]{1,0:T(8,128)(2,1)S(1)}, bf16[8,2048]{1,0:T(8,128)(2,1)S(1)}, bf16[8,2048]{1,0:T(8,128)(2,1)S(1)}) custom-call(bf16[8,2048]{1,0:T(8,128)(2,1)S(1)} %shard_map.160.rest_0_, bf16[8,2048]{1,0:T(8,128)(2,1)S(1)} %collective-permute-done.3.rest_1_, bf16[8,2048]{1,0:T(8,128)(2,1)S(1)} %collective-permute-done.4.rest_2_, ...), custom_call_target="tpu_custom_call" | custom-call | flops 40000000000 | tf_op jit(solution)/shard_map/pallas_call | solution.py:421
  21.3 0.3 collective-permute-start.6
  21.6 3.5 %collective-permute-start.7 = (bf16[8,2048]{1,0:T(8,128)(2,1)S(1)}, bf16[8,2048]{1,0:T(8,128)(2,1)S(1)}, u32[]{:S(2)}, u32[]{:S(2)}) collective-permute-start(bf16[8,2048]{1,0:T(8,128)(2,1)S(1)} %get-tuple-element.27), channel_id=1, source_target_pairs={{0,8},{4,12},{8,0},{12,4},{1,9},{5,13},{9,1},{13,5},{2,10},{6,14},... | collective-permute-start | bytes 98312 | tf_op jit(solution)/shard_map/ppermute | solution.py:324
  25.1 0.7 %collective-permute-start.8 = (bf16[8,2048]{1,0:T(8,128)(2,1)S(1)}, bf16[8,2048]{1,0:T(8,128)(2,1)S(1)}, u32[]{:S(2)}, u32[]{:S(2)}) collective-permute-start(bf16[8,2048]{1,0:T(8,128)(2,1)S(1)} %get-tuple-element.28), channel_id=1, source_target_pairs={{0,12},{4,8},{8,4},{12,0},{1,13},{5,9},{9,5},{13,1},{2,14},{6,10},... | collective-permute-start | bytes 98312 | tf_op jit(solution)/shard_map/ppermute | solution.py:324
  25.8 1.4 %collective-permute-done.7.rest_2_ = bf16[8,2048]{1,0:T(8,128)(2,1)S(1)} collective-permute-done((bf16[8,2048]{1,0:T(8,128)(2,1)S(1)}, bf16[8,2048]{1,0:T(8,128)(2,1)S(1)}, u32[]{:S(2)}, u32[]{:S(2)}) %collective-permute-start.7) | collective-permute-done | bytes 32800 | tf_op jit(solution)/shard_map/ppermute | solution.py:324
  27.2 3.6 %collective-permute-done.8.rest_3_ = bf16[8,2048]{1,0:T(8,128)(2,1)S(1)} collective-permute-done((bf16[8,2048]{1,0:T(8,128)(2,1)S(1)}, bf16[8,2048]{1,0:T(8,128)(2,1)S(1)}, u32[]{:S(2)}, u32[]{:S(2)}) %collective-permute-start.8) | collective-permute-done | bytes 32800 | tf_op jit(solution)/shard_map/ppermute | solution.py:324
  30.8 0.0 copy-start.12
  30.8 0.7 %shard_map.162 = (bf16[4,2,2048]{2,1,0:T(2,128)(2,1)}, bf16[8,2048]{1,0:T(8,128)(2,1)S(1)}) custom-call(bf16[4,2,2048]{2,1,0:T(2,128)(2,1)S(1)} %copy-done.9, f32[8,2048]{1,0:T(8,128)S(1)} %get-tuple-element.25.rest_0_, bf16[8,2048]{1,0:T(8,128)(2,1)S(1)} %collective-permute-done.6.rest_1_, bf16[8,2048]{1,0:T(8,128)(2,1)S(1)} %collective-permute-done.7.rest_2_, ...), custom_call_target="tpu_custom_call" | custom-call | flops 40000000000 | tf_op jit(solution)/shard_map/pallas_call | solution.py:435
  31.5 0.7 %collective-permute-start.11 = (bf16[8,2048]{1,0:T(8,128)(2,1)S(1)}, bf16[8,2048]{1,0:T(8,128)(2,1)S(1)}, u32[]{:S(2)}, u32[]{:S(2)}) collective-permute-start(bf16[8,2048]{1,0:T(8,128)(2,1)S(1)} %get-tuple-element.30.rest_0_), channel_id=1, source_target_pairs={{0,12},{4,8},{8,4},{12,0},{1,13},{5,9},{9,5},{13,1},{2,14},{6,10},... | collective-permute-start | bytes 98312 | tf_op jit(solution)/shard_map/ppermute | solution.py:324
  32.2 2.8 %collective-permute-start.9 = (bf16[8,2048]{1,0:T(8,128)(2,1)S(1)}, bf16[8,2048]{1,0:T(8,128)(2,1)S(1)}, u32[]{:S(2)}, u32[]{:S(2)}) collective-permute-start(bf16[8,2048]{1,0:T(8,128)(2,1)S(1)} %get-tuple-element.30.rest_0_), channel_id=1, source_target_pairs={{0,4},{4,0},{8,12},{12,8},{1,5},{5,1},{9,13},{13,9},{2,6},{6,2},{1... | collective-permute-start | bytes 98312 | tf_op jit(solution)/shard_map/ppermute | solution.py:324
  35.0 1.3 %collective-permute-done.10.rest_2_ = bf16[8,2048]{1,0:T(8,128)(2,1)S(1)} collective-permute-done((bf16[8,2048]{1,0:T(8,128)(2,1)S(1)}, bf16[8,2048]{1,0:T(8,128)(2,1)S(1)}, u32[]{:S(2)}, u32[]{:S(2)}) %collective-permute-start.10) | collective-permute-done | bytes 32800 | tf_op jit(solution)/shard_map/ppermute | solution.py:324
  36.3 0.9 %collective-permute-done.11.rest_3_ = bf16[8,2048]{1,0:T(8,128)(2,1)S(1)} collective-permute-done((bf16[8,2048]{1,0:T(8,128)(2,1)S(1)}, bf16[8,2048]{1,0:T(8,128)(2,1)S(1)}, u32[]{:S(2)}, u32[]{:S(2)}) %collective-permute-start.11) | collective-permute-done | bytes 32800 | tf_op jit(solution)/shard_map/ppermute | solution.py:324
  37.2 0.0 collective-permute-done.9.rest_1_
  37.3 3.6 %shard_map.164 = (f32[2,8,4224]{2,1,0:T(8,128)S(1)}, bf16[2,8,4224]{2,1,0:T(8,128)(2,1)S(1)}, bf16[64,4096]{1,0:T(8,128)(2,1)S(1)}) custom-call(bf16[2048]{0:T(1024)(128)(2,1)S(1)} %copy-done.12, bf16[8,2048]{1,0:T(8,128)(2,1)S(1)} %get-tuple-element.30.rest_0_, bf16[8,2048]{1,0:T(8,128)(2,1)S(1)} %collective-permute-done.9.rest_1_, ...), custom_call_target="tpu_custom_call" | custom-call | flops 16000000000 | tf_op jit(solution)/shard_map/pallas_call | solution.py:448
  40.9 0.1 collective-permute-start.12
  41.0 0.0 copy-start
  41.0 0.0 copy-start.2
  41.0 2.5 %shard_map.166 = (f32[2,8,3072]{2,1,0:T(8,128)S(1)}, bf16[2,8,3072]{2,1,0:T(8,128)(2,1)S(1)}) custom-call(bf16[64,4096]{1,0:T(8,128)(2,1)S(1)} %get-tuple-element.35.spread, bf16[2048,2,3584]{2,1,0:T(2,128)(2,1)S(1)} %bitcast.1), custom_call_target="tpu_custom_call" | custom-call | flops 16000000000 | tf_op jit(solution)/shard_map/pallas_call | solution.py:464
  43.5 0.6 %collective-permute-start.14 = (bf16[2,8,3072]{2,1,0:T(8,128)(2,1)S(1)}, bf16[2,8,3072]{2,1,0:T(8,128)(2,1)S(1)}, u32[]{:S(2)}, u32[]{:S(2)}) collective-permute-start(bf16[2,8,3072]{2,1,0:T(8,128)(2,1)S(1)} %get-tuple-element.37), channel_id=1, source_target_pairs={{0,1},{1,0},{2,3},{3,2},{4,5},{5,4},{6,7},{7,6},{8,9},{9,8},{10,11... | collective-permute-start | bytes 294920 | tf_op jit(solution)/shard_map/ppermute | solution.py:480
  44.0 0.0 collective-permute-done.12.received
  44.0 0.1 shard_map.165
  44.1 0.9 %collective-permute-start.13 = (bf16[8,4224]{1,0:T(8,128)(2,1)S(1)}, bf16[8,4224]{1,0:T(8,128)(2,1)S(1)}, u32[]{:S(2)}, u32[]{:S(2)}) collective-permute-start(bf16[8,4224]{1,0:T(8,128)(2,1)S(1)} %get-tuple-element.34), channel_id=1, source_target_pairs={{0,2},{1,3},{2,0},{3,1},{4,6},{5,7},{6,4},{7,5},{8,10},{9,11},{10,... | collective-permute-start | bytes 202760 | tf_op jit(solution)/shard_map/ppermute | solution.py:490
  45.1 0.0 collective-permute-done.14.received
  45.1 1.2 %collective-permute-start.15 = (bf16[8,3072]{1,0:T(8,128)(2,1)S(1)}, bf16[8,3072]{1,0:T(8,128)(2,1)S(1)}, u32[]{:S(2)}, u32[]{:S(2)}) collective-permute-start(bf16[8,3072]{1,0:T(8,128)(2,1)S(1)} %get-tuple-element.39), channel_id=1, source_target_pairs={{0,2},{1,3},{2,0},{3,1},{4,6},{5,7},{6,4},{7,5},{8,10},{9,11},{10,... | collective-permute-start | bytes 147464 | tf_op jit(solution)/shard_map/ppermute | solution.py:490
  46.3 0.8 %shard_map.163.scales = f32[8,3584]{1,0:T(8,128)S(1)} custom-call(s32[4]{0:T(128)S(1)} %copy-done.2, bf16[128,3584]{1,0:T(8,128)(2,1)S(1)} %copy-done), custom_call_target="tpu_custom_call" | custom-call | tf_op jit(solution)/shard_map/pallas_call | solution.py:368
  47.0 2.5 %collective-permute-done.15.rest_3_ = bf16[8,3072]{1,0:T(8,128)(2,1)S(1)} collective-permute-done((bf16[8,3072]{1,0:T(8,128)(2,1)S(1)}, bf16[8,3072]{1,0:T(8,128)(2,1)S(1)}, u32[]{:S(2)}, u32[]{:S(2)}) %collective-permute-start.15) | collective-permute-done | bytes 49184 | tf_op jit(solution)/shard_map/ppermute | solution.py:490
  49.5 0.8 %shard_map.168 = bf16[4,2,3584]{2,1,0:T(2,128)(2,1)} custom-call(f32[8,3584]{1,0:T(8,128)S(1)} %shard_map.163.scales, f32[8,4224]{1,0:T(8,128)S(1)} %get-tuple-element.33.rest_0_, bf16[8,4224]{1,0:T(8,128)(2,1)S(1)} %collective-permute-done.13.rest_1_, f32[8,3072]{1,0:T(8,128)S(1)} %get-tuple-element.38.rest_2_, ...), custom_call_target="tpu_custom_call" | custom-call | tf_op jit(solution)/shard_map/pallas_call | solution.py:493
  (43 shorter events, 0.1 us)
Async XLA Ops:
  0.6 1.4 %copy-start.6 = (bf16[4,2,8192]{2,1,0:T(2,128)(2,1)S(1)}, bf16[4,2,8192]{2,1,0:T(2,128)(2,1)}, u32[]{:S(2)}) copy-start(bf16[4,2,8192]{2,1,0:T(2,128)(2,1)} %queries.1) | copy-start | bytes 393220
  0.6 1.4 %copy-start.4 = (bf16[128,1024]{1,0:T(8,128)(2,1)S(1)}, bf16[128,1024]{1,0:T(8,128)(2,1)}, u32[]{:S(2)}) copy-start(bf16[128,1024]{1,0:T(8,128)(2,1)} %prefix_keys.1) | copy-start | bytes 786436
  0.7 1.4 %copy-start.5 = (bf16[128,1024]{1,0:T(8,128)(2,1)S(1)}, bf16[128,1024]{1,0:T(8,128)(2,1)}, u32[]{:S(2)}) copy-start(bf16[128,1024]{1,0:T(8,128)(2,1)} %prefix_values.1) | copy-start | bytes 786436
  0.7 1.4 %copy-start.7 = (bf16[4,16,1024]{2,1,0:T(8,128)(2,1)S(1)}, bf16[4,16,1024]{2,1,0:T(8,128)(2,1)}, u32[]{:S(2)}) copy-start(bf16[4,16,1024]{2,1,0:T(8,128)(2,1)} %suffix_keys.1) | copy-start | bytes 393220
  0.7 1.4 %copy-start.8 = (bf16[4,16,1024]{2,1,0:T(8,128)(2,1)S(1)}, bf16[4,16,1024]{2,1,0:T(8,128)(2,1)}, u32[]{:S(2)}) copy-start(bf16[4,16,1024]{2,1,0:T(8,128)(2,1)} %suffix_values.1) | copy-start | bytes 393220
  0.7 1.4 %copy-start.10 = (bf16[4,2,1024]{2,1,0:T(2,128)(2,1)S(1)}, bf16[4,2,1024]{2,1,0:T(2,128)(2,1)}, u32[]{:S(2)}) copy-start(bf16[4,2,1024]{2,1,0:T(2,128)(2,1)} %new_keys.1) | copy-start | bytes 49156
  0.7 1.4 %copy-start.11 = (bf16[4,2,1024]{2,1,0:T(2,128)(2,1)S(1)}, bf16[4,2,1024]{2,1,0:T(2,128)(2,1)}, u32[]{:S(2)}) copy-start(bf16[4,2,1024]{2,1,0:T(2,128)(2,1)} %new_values.1) | copy-start | bytes 49156
  0.7 1.4 %copy-start.1 = (s32[4]{0:T(128)S(1)}, s32[4]{0:T(128)}, u32[]{:S(2)}) copy-start(s32[4]{0:T(128)} %ids.3) | copy-start | bytes 52
  0.7 1.4 %copy-start.3 = (bf16[128,2,1024]{2,1,0:T(2,128)(2,1)S(1)}, bf16[128,2,1024]{2,1,0:T(2,128)(2,1)}, u32[]{:S(2)}) copy-start(bf16[128,2,1024]{2,1,0:T(2,128)(2,1)} %kv_scales.1) | copy-start | bytes 1572868
  0.7 0.8 %copy-start.13 = (s32[4]{0:T(128)S(1)}, s32[4]{0:T(128)}, u32[]{:S(2)}) copy-start(s32[4]{0:T(128)} %lengths.1) | copy-start | bytes 52
  2.1 17.6 %slice-start.7 = ((s8[8388608]{0:T(1024)(128)(4,1)}), s8[4194304]{0:T(1024)(128)(4,1)S(1)}, s32[]{:S(2)}) async-start(s8[8388608]{0:T(1024)(128)(4,1)} %bitcast.2), calls=%async_computation.7 | async-start | bytes 8388608
  4.8 7.0 %collective-permute-start = (bf16[8,2176]{1,0:T(8,128)(2,1)S(1)}, bf16[8,2176]{1,0:T(8,128)(2,1)S(1)}, u32[]{:S(2)}, u32[]{:S(2)}) collective-permute-start(bf16[8,2176]{1,0:T(8,128)(2,1)S(1)} %get-tuple-element.22), channel_id=1, source_target_pairs={{0,4},{4,8},{8,12},{12,0},{1,5},{5,9},{9,13},{13,1},{2,6},{6,10},{... | collective-permute-start | bytes 104456 | tf_op jit(solution)/shard_map/ppermute | solution.py:409
  7.9 5.2 %collective-permute-start.1 = (bf16[8,2176]{1,0:T(8,128)(2,1)S(1)}, bf16[8,2176]{1,0:T(8,128)(2,1)S(1)}, u32[]{:S(2)}, u32[]{:S(2)}) collective-permute-start(bf16[8,2176]{1,0:T(8,128)(2,1)S(1)} %get-tuple-element.23), channel_id=1, source_target_pairs={{0,8},{4,12},{8,0},{12,4},{1,9},{5,13},{9,1},{13,5},{2,10},{6,14},... | collective-permute-start | bytes 104456 | tf_op jit(solution)/shard_map/ppermute | solution.py:409
  10.5 3.9 %collective-permute-start.2 = (bf16[8,2176]{1,0:T(8,128)(2,1)S(1)}, bf16[8,2176]{1,0:T(8,128)(2,1)S(1)}, u32[]{:S(2)}, u32[]{:S(2)}) collective-permute-start(bf16[8,2176]{1,0:T(8,128)(2,1)S(1)} %get-tuple-element.24), channel_id=1, source_target_pairs={{0,12},{4,0},{8,4},{12,8},{1,13},{5,1},{9,5},{13,9},{2,14},{6,2},{... | collective-permute-start | bytes 104456 | tf_op jit(solution)/shard_map/ppermute | solution.py:409
  14.4 5.3 %slice-start.8 = ((s8[8388608]{0:T(1024)(128)(4,1)}), s8[4194304]{0:T(1024)(128)(4,1)S(1)}, s32[]{:S(2)}) async-start(s8[8388608]{0:T(1024)(128)(4,1)} %bitcast.2), calls=%async_computation.8 | async-start | bytes 8388608
  14.7 16.1 %copy-start.9 = (bf16[4,2,2048]{2,1,0:T(2,128)(2,1)S(1)}, bf16[4,2,2048]{2,1,0:T(2,128)(2,1)}, u32[]{:S(2)}) copy-start(bf16[4,2,2048]{2,1,0:T(2,128)(2,1)} %hidden.1) | copy-start | bytes 98308
  14.7 1.9 %collective-permute-start.3 = (bf16[8,2048]{1,0:T(8,128)(2,1)S(1)}, bf16[8,2048]{1,0:T(8,128)(2,1)S(1)}, u32[]{:S(2)}, u32[]{:S(2)}) collective-permute-start(bf16[8,2048]{1,0:T(8,128)(2,1)S(1)} %shard_map.160.rest_0_), channel_id=1, source_target_pairs={{0,1},{1,0},{2,3},{3,2},{4,5},{5,4},{6,7},{7,6},{8,9},{9,8},{10,11... | collective-permute-start | bytes 98312 | tf_op jit(solution)/shard_map/ppermute | solution.py:324
  14.8 4.0 %collective-permute-start.4 = (bf16[8,2048]{1,0:T(8,128)(2,1)S(1)}, bf16[8,2048]{1,0:T(8,128)(2,1)S(1)}, u32[]{:S(2)}, u32[]{:S(2)}) collective-permute-start(bf16[8,2048]{1,0:T(8,128)(2,1)S(1)} %shard_map.160.rest_0_), channel_id=1, source_target_pairs={{0,2},{1,3},{2,0},{3,1},{4,6},{5,7},{6,4},{7,5},{8,10},{9,11},{10,... | collective-permute-start | bytes 98312 | tf_op jit(solution)/shard_map/ppermute | solution.py:324
  16.4 3.3 %collective-permute-start.5 = (bf16[8,2048]{1,0:T(8,128)(2,1)S(1)}, bf16[8,2048]{1,0:T(8,128)(2,1)S(1)}, u32[]{:S(2)}, u32[]{:S(2)}) collective-permute-start(bf16[8,2048]{1,0:T(8,128)(2,1)S(1)} %shard_map.160.rest_0_), channel_id=1, source_target_pairs={{0,3},{1,2},{2,1},{3,0},{4,7},{5,6},{6,5},{7,4},{8,11},{9,10},{10,... | collective-permute-start | bytes 98312 | tf_op jit(solution)/shard_map/ppermute | solution.py:324
  19.7 17.5 %slice-start = ((s8[29360128]{0:T(1024)(128)(4,1)}), s8[4194304]{0:T(1024)(128)(4,1)S(1)}, s32[]{:S(2)}) async-start(s8[29360128]{0:T(1024)(128)(4,1)} %bitcast), calls=%async_computation | async-start | bytes 8388608
  19.7 17.5 %slice-start.1 = ((s8[29360128]{0:T(1024)(128)(4,1)}), s8[4194304]{0:T(1024)(128)(4,1)S(1)}, s32[]{:S(2)}) async-start(s8[29360128]{0:T(1024)(128)(4,1)} %bitcast), calls=%async_computation.1 | async-start | bytes 8388608
  19.7 17.5 %slice-start.2 = ((s8[29360128]{0:T(1024)(128)(4,1)}), s8[4194304]{0:T(1024)(128)(4,1)S(1)}, s32[]{:S(2)}) async-start(s8[29360128]{0:T(1024)(128)(4,1)} %bitcast), calls=%async_computation.2 | async-start | bytes 8388608
  19.7 17.5 %slice-start.3 = ((s8[29360128]{0:T(1024)(128)(4,1)}), s8[4194304]{0:T(1024)(128)(4,1)S(1)}, s32[]{:S(2)}) async-start(s8[29360128]{0:T(1024)(128)(4,1)} %bitcast), calls=%async_computation.3 | async-start | bytes 8388608
  21.3 4.5 %collective-permute-start.6 = (bf16[8,2048]{1,0:T(8,128)(2,1)S(1)}, bf16[8,2048]{1,0:T(8,128)(2,1)S(1)}, u32[]{:S(2)}, u32[]{:S(2)}) collective-permute-start(bf16[8,2048]{1,0:T(8,128)(2,1)S(1)} %get-tuple-element.26), channel_id=1, source_target_pairs={{0,4},{4,0},{8,12},{12,8},{1,5},{5,1},{9,13},{13,9},{2,6},{6,2},{1... | collective-permute-start | bytes 98312 | tf_op jit(solution)/shard_map/ppermute | solution.py:324
  21.6 5.5 %collective-permute-start.7 = (bf16[8,2048]{1,0:T(8,128)(2,1)S(1)}, bf16[8,2048]{1,0:T(8,128)(2,1)S(1)}, u32[]{:S(2)}, u32[]{:S(2)}) collective-permute-start(bf16[8,2048]{1,0:T(8,128)(2,1)S(1)} %get-tuple-element.27), channel_id=1, source_target_pairs={{0,8},{4,12},{8,0},{12,4},{1,9},{5,13},{9,1},{13,5},{2,10},{6,14},... | collective-permute-start | bytes 98312 | tf_op jit(solution)/shard_map/ppermute | solution.py:324
  25.1 5.7 %collective-permute-start.8 = (bf16[8,2048]{1,0:T(8,128)(2,1)S(1)}, bf16[8,2048]{1,0:T(8,128)(2,1)S(1)}, u32[]{:S(2)}, u32[]{:S(2)}) collective-permute-start(bf16[8,2048]{1,0:T(8,128)(2,1)S(1)} %get-tuple-element.28), channel_id=1, source_target_pairs={{0,12},{4,8},{8,4},{12,0},{1,13},{5,9},{9,5},{13,1},{2,14},{6,10},... | collective-permute-start | bytes 98312 | tf_op jit(solution)/shard_map/ppermute | solution.py:324
  30.8 6.4 %slice-start.4 = ((s8[29360128]{0:T(1024)(128)(4,1)}), s8[4194304]{0:T(1024)(128)(4,1)S(1)}, s32[]{:S(2)}) async-start(s8[29360128]{0:T(1024)(128)(4,1)} %bitcast), calls=%async_computation.4 | async-start | bytes 8388608
  30.8 6.5 %slice-start.5 = ((s8[29360128]{0:T(1024)(128)(4,1)}), s8[4194304]{0:T(1024)(128)(4,1)S(1)}, s32[]{:S(2)}) async-start(s8[29360128]{0:T(1024)(128)(4,1)} %bitcast), calls=%async_computation.5 | async-start | bytes 8388608
  30.8 6.5 %slice-start.6 = ((s8[29360128]{0:T(1024)(128)(4,1)}), s8[4194304]{0:T(1024)(128)(4,1)S(1)}, s32[]{:S(2)}) async-start(s8[29360128]{0:T(1024)(128)(4,1)} %bitcast), calls=%async_computation.6 | async-start | bytes 8388608
  30.8 6.5 %copy-start.12 = (bf16[2048]{0:T(1024)(128)(2,1)S(1)}, bf16[2048]{0:T(1024)(128)(2,1)}, u32[]{:S(2)}) copy-start(bf16[2048]{0:T(1024)(128)(2,1)} %gain.1) | copy-start | bytes 12292
  31.5 4.8 %collective-permute-start.10 = (bf16[8,2048]{1,0:T(8,128)(2,1)S(1)}, bf16[8,2048]{1,0:T(8,128)(2,1)S(1)}, u32[]{:S(2)}, u32[]{:S(2)}) collective-permute-start(bf16[8,2048]{1,0:T(8,128)(2,1)S(1)} %get-tuple-element.30.rest_0_), channel_id=1, source_target_pairs={{0,8},{4,12},{8,0},{12,4},{1,9},{5,13},{9,1},{13,5},{2,10},{6,14},... | collective-permute-start | bytes 98312 | tf_op jit(solution)/shard_map/ppermute | solution.py:324
  31.5 5.7 %collective-permute-start.11 = (bf16[8,2048]{1,0:T(8,128)(2,1)S(1)}, bf16[8,2048]{1,0:T(8,128)(2,1)S(1)}, u32[]{:S(2)}, u32[]{:S(2)}) collective-permute-start(bf16[8,2048]{1,0:T(8,128)(2,1)S(1)} %get-tuple-element.30.rest_0_), channel_id=1, source_target_pairs={{0,12},{4,8},{8,4},{12,0},{1,13},{5,9},{9,5},{13,1},{2,14},{6,10},... | collective-permute-start | bytes 98312 | tf_op jit(solution)/shard_map/ppermute | solution.py:324
  32.2 5.1 %collective-permute-start.9 = (bf16[8,2048]{1,0:T(8,128)(2,1)S(1)}, bf16[8,2048]{1,0:T(8,128)(2,1)S(1)}, u32[]{:S(2)}, u32[]{:S(2)}) collective-permute-start(bf16[8,2048]{1,0:T(8,128)(2,1)S(1)} %get-tuple-element.30.rest_0_), channel_id=1, source_target_pairs={{0,4},{4,0},{8,12},{12,8},{1,5},{5,1},{9,13},{13,9},{2,6},{6,2},{1... | collective-permute-start | bytes 98312 | tf_op jit(solution)/shard_map/ppermute | solution.py:324
  40.9 3.2 %collective-permute-start.12 = (bf16[2,8,4224]{2,1,0:T(8,128)(2,1)S(1)}, bf16[2,8,4224]{2,1,0:T(8,128)(2,1)S(1)}, u32[]{:S(2)}, u32[]{:S(2)}) collective-permute-start(bf16[2,8,4224]{2,1,0:T(8,128)(2,1)S(1)} %get-tuple-element.32), channel_id=1, source_target_pairs={{0,1},{1,0},{2,3},{3,2},{4,5},{5,4},{6,7},{7,6},{8,9},{9,8},{10,11... | collective-permute-start | bytes 405512 | tf_op jit(solution)/shard_map/ppermute | solution.py:480
  41.0 5.3 %copy-start = (bf16[128,3584]{1,0:T(8,128)(2,1)S(1)}, bf16[128,3584]{1,0:T(8,128)(2,1)}, u32[]{:S(2)}) copy-start(bf16[128,3584]{1,0:T(8,128)(2,1)} %table.1) | copy-start | bytes 2752516
  41.0 5.3 %copy-start.2 = (s32[4]{0:T(128)S(1)}, s32[4]{0:T(128)}, u32[]{:S(2)}) copy-start(s32[4]{0:T(128)} %ids.3) | copy-start | bytes 52
  43.5 1.6 %collective-permute-start.14 = (bf16[2,8,3072]{2,1,0:T(8,128)(2,1)S(1)}, bf16[2,8,3072]{2,1,0:T(8,128)(2,1)S(1)}, u32[]{:S(2)}, u32[]{:S(2)}) collective-permute-start(bf16[2,8,3072]{2,1,0:T(8,128)(2,1)S(1)} %get-tuple-element.37), channel_id=1, source_target_pairs={{0,1},{1,0},{2,3},{3,2},{4,5},{5,4},{6,7},{7,6},{8,9},{9,8},{10,11... | collective-permute-start | bytes 294920 | tf_op jit(solution)/shard_map/ppermute | solution.py:480
  44.1 5.4 %collective-permute-start.13 = (bf16[8,4224]{1,0:T(8,128)(2,1)S(1)}, bf16[8,4224]{1,0:T(8,128)(2,1)S(1)}, u32[]{:S(2)}, u32[]{:S(2)}) collective-permute-start(bf16[8,4224]{1,0:T(8,128)(2,1)S(1)} %get-tuple-element.34), channel_id=1, source_target_pairs={{0,2},{1,3},{2,0},{3,1},{4,6},{5,7},{6,4},{7,5},{8,10},{9,11},{10,... | collective-permute-start | bytes 202760 | tf_op jit(solution)/shard_map/ppermute | solution.py:490
  45.1 4.4 %collective-permute-start.15 = (bf16[8,3072]{1,0:T(8,128)(2,1)S(1)}, bf16[8,3072]{1,0:T(8,128)(2,1)S(1)}, u32[]{:S(2)}, u32[]{:S(2)}) collective-permute-start(bf16[8,3072]{1,0:T(8,128)(2,1)S(1)} %get-tuple-element.39), channel_id=1, source_target_pairs={{0,2},{1,3},{2,0},{3,1},{4,6},{5,7},{6,4},{7,5},{8,10},{9,11},{10,... | collective-permute-start | bytes 147464 | tf_op jit(solution)/shard_map/ppermute | solution.py:490

commit v10 on v9

--- a/solution.py
+++ b/solution.py
@@ -190,7 +190,7 @@
     amount = outs[0].shape[0]
     pre_at, row_at = lax.axis_index("pre"), lax.axis_index("row")
     for s, ref in enumerate(blocks):
-        start = pl.multiple_of(source_of(row_at, s, row_count) * tokens, tokens)
+        start = pl.multiple_of(lax.rem(row_at + row_count - s, row_count) * tokens, tokens)
         stacked[pl.ds(start, tokens), :] = ref[...].astype(f32)
     product[...] = dot(stacked[...].astype(bf16), weight[...])
     for s, out in enumerate(outs):
@@ -417,7 +417,10 @@
         compiler_params=params(4),
         cost_estimate=cost(40),
     )(*ring)
-    gathered = shifted([mixed] * row_count, "row")
+    gathered = [mixed] + [
+        lax.ppermute(mixed, "row", [(i, (i + s) % row_count) for i in range(row_count)])
+        for s in range(1, row_count)
+    ]
     products = pl.pallas_call(
         functools.partial(project_kernel, row_count, pre_count),
         in_specs=[VMEM] * (row_count + 1),

time: 50.4 us -> 50 us (level)
  waiting for transfers between devices: 15.4 us -> 13.9 us
  starting transfers between devices: 19.6 us -> 20.7 us
    ppermute x9 -> x6, waiting for transfers between devices: 10.3 us -> 7.29 us  [shifted(): lax.ppermute(parts[s], axis, [(i, target_of(i, s, count)) for i in range(...]
    ppermute x0 -> x3, starting transfers between devices: none -> 3 us  [per_device(): lax.ppermute(mixed, 'row', [(i, (i + s) % row_count) for i in range(row_c...]
    ppermute x9 -> x6, starting transfers between devices: 9.87 us -> 7.95 us  [shifted(): lax.ppermute(parts[s], axis, [(i, target_of(i, s, count)) for i in range(...]
    ppermute x0 -> x3, waiting for transfers between devices: none -> 1.6 us  [per_device(): lax.ppermute(mixed, 'row', [(i, (i + s) % row_count) for i in range(row_c...]
  transfers between devices with their start and end apart: 16 -> 16, of which waited for: 9 -> 10; matrix products, arithmetic and copies ran while one was open for 0% -> 0% of each run, Pallas kernels for 7% -> 7%
where the time goes in v10:
time: 50 us; the launch traced here: 49.9 us
  starting transfers between devices  20.7 us (41%)
  waiting for transfers between devices  13.9 us (28%)
  Pallas kernels  13.4 us (27%)
  between operations  0.99 us (2%)
  local copies, waits for them, and re-layouts  0.85 us (2%)
    ppermute x6, starting transfers between devices, shifted(): lax.ppermute(parts[s], axis, [(i, target_of(i, s, count)) for i in range(...  7.95 us
    ppermute x6, waiting for transfers between devices, shifted(): lax.ppermute(parts[s], axis, [(i, target_of(i, s, count)) for i in range(...  7.29 us
    ppermute x3, starting transfers between devices, per_device(): lax.ppermute(partials[s], 'pre', [(i, (i + s) % pre_count) for i in range...  7 us
    pallas_call x1, Pallas kernels, per_device(): pl.pallas_call(functools.partial(feed_first_kernel, pre_count, row_count,...  3.55 us
    ppermute x3, starting transfers between devices, per_device(): lax.ppermute(mixed, 'row', [(i, (i + s) % row_count) for i in range(row_c...  3 us
    pallas_call x1, Pallas kernels, per_device(): pl.pallas_call(functools.partial(attend_kernel, pre_count), in_specs=[SME...  2.7 us
    ppermute x3, waiting for transfers between devices, per_device(): lax.ppermute(partials[s], 'pre', [(i, (i + s) % pre_count) for i in range...  2.59 us
    pallas_call x1, Pallas kernels, per_device(): pl.pallas_call(functools.partial(feed_second_kernel, row_count, first, se...  2.49 us
  transfers between devices with their start and end apart: 16, of which 10 were waited for; matrix products, arithmetic and copies ran while one was open for 0% of the time, Pallas kernels for 7%

profile of v10, /device:TPU:0, one launch (start us, length us, event | category | flops | bytes accessed | tf_op | source)
XLA Modules:
  0.0 49.9 jit_solution(14144153024324446064)
XLA Ops:
  0.7 0.0 copy-start.1
  0.7 0.7 %copy-done.13 = s32[4]{0:T(128)S(1)} copy-done((s32[4]{0:T(128)S(1)}, s32[4]{0:T(128)}, u32[]{:S(2)}) %copy-start.13) | copy-done | bytes 40
  1.5 0.6 %shard_map.158.mask = s32[8,128]{1,0:T(8,128)S(1)} custom-call(s32[4]{0:T(128)S(1)} %copy-done.13), custom_call_target="tpu_custom_call" | custom-call | flops 20000000000 | tf_op jit(solution)/shard_map/pallas_call | solution.py:377
  2.1 0.0 slice-start.7
  2.1 2.7 %shard_map.159 = (bf16[8,2176]{1,0:T(8,128)(2,1)S(1)}, bf16[8,2176]{1,0:T(8,128)(2,1)S(1)}, bf16[8,2176]{1,0:T(8,128)(2,1)S(1)}, bf16[8,2176]{1,0:T(8,128)(2,1)S(1)}) custom-call(s32[4]{0:T(128)S(1)} %copy-done.1, s32[8,128]{1,0:T(8,128)S(1)} %shard_map.158.mask, bf16[4,2,8192]{2,1,0:T(2,128)(2,1)S(1)} %copy-done.6, bf16[128,1024]{1,0:T(8,128)(2,1)S(1)} %copy-done.4, ...), custom_call_target="tpu_custom_call" | custom-call | flops 20000000000 | tf_op jit(solution)/shard_map/pallas_call | solution.py:385
  4.8 3.1 %collective-permute-start = (bf16[8,2176]{1,0:T(8,128)(2,1)S(1)}, bf16[8,2176]{1,0:T(8,128)(2,1)S(1)}, u32[]{:S(2)}, u32[]{:S(2)}) collective-permute-start(bf16[8,2176]{1,0:T(8,128)(2,1)S(1)} %get-tuple-element.22), channel_id=1, source_target_pairs={{0,4},{4,8},{8,12},{12,0},{1,5},{5,9},{9,13},{13,1},{2,6},{6,10},{... | collective-permute-start | bytes 104456 | tf_op jit(solution)/shard_map/ppermute | solution.py:409
  7.9 2.6 %collective-permute-start.1 = (bf16[8,2176]{1,0:T(8,128)(2,1)S(1)}, bf16[8,2176]{1,0:T(8,128)(2,1)S(1)}, u32[]{:S(2)}, u32[]{:S(2)}) collective-permute-start(bf16[8,2176]{1,0:T(8,128)(2,1)S(1)} %get-tuple-element.23), channel_id=1, source_target_pairs={{0,8},{4,12},{8,0},{12,4},{1,9},{5,13},{9,1},{13,5},{2,10},{6,14},... | collective-permute-start | bytes 104456 | tf_op jit(solution)/shard_map/ppermute | solution.py:409
  10.5 1.3 %collective-permute-start.2 = (bf16[8,2176]{1,0:T(8,128)(2,1)S(1)}, bf16[8,2176]{1,0:T(8,128)(2,1)S(1)}, u32[]{:S(2)}, u32[]{:S(2)}) collective-permute-start(bf16[8,2176]{1,0:T(8,128)(2,1)S(1)} %get-tuple-element.24), channel_id=1, source_target_pairs={{0,12},{4,0},{8,4},{12,8},{1,13},{5,1},{9,5},{13,9},{2,14},{6,2},{... | collective-permute-start | bytes 104456 | tf_op jit(solution)/shard_map/ppermute | solution.py:409
  11.9 1.3 %collective-permute-done.1.rest_2_ = bf16[8,2176]{1,0:T(8,128)(2,1)S(1)} collective-permute-done((bf16[8,2176]{1,0:T(8,128)(2,1)S(1)}, bf16[8,2176]{1,0:T(8,128)(2,1)S(1)}, u32[]{:S(2)}, u32[]{:S(2)}) %collective-permute-start.1) | collective-permute-done | bytes 34848 | tf_op jit(solution)/shard_map/ppermute | solution.py:409
  13.1 1.3 %collective-permute-done.2.rest_3_ = bf16[8,2176]{1,0:T(8,128)(2,1)S(1)} collective-permute-done((bf16[8,2176]{1,0:T(8,128)(2,1)S(1)}, bf16[8,2176]{1,0:T(8,128)(2,1)S(1)}, u32[]{:S(2)}, u32[]{:S(2)}) %collective-permute-start.2) | collective-permute-done | bytes 34848 | tf_op jit(solution)/shard_map/ppermute | solution.py:409
  14.4 0.3 shard_map.160.rest_0_
  14.7 0.0 copy-start.9
  14.7 0.1 collective-permute-start.3
  14.8 1.6 %collective-permute-start.4 = (bf16[8,2048]{1,0:T(8,128)(2,1)S(1)}, bf16[8,2048]{1,0:T(8,128)(2,1)S(1)}, u32[]{:S(2)}, u32[]{:S(2)}) collective-permute-start(bf16[8,2048]{1,0:T(8,128)(2,1)S(1)} %shard_map.160.rest_0_), channel_id=1, source_target_pairs={{0,2},{1,3},{2,0},{3,1},{4,6},{5,7},{6,4},{7,5},{8,10},{9,11},{10,... | collective-permute-start | bytes 98312 | tf_op jit(solution)/shard_map/ppermute | solution.py:421
  16.3 1.4 %collective-permute-start.5 = (bf16[8,2048]{1,0:T(8,128)(2,1)S(1)}, bf16[8,2048]{1,0:T(8,128)(2,1)S(1)}, u32[]{:S(2)}, u32[]{:S(2)}) collective-permute-start(bf16[8,2048]{1,0:T(8,128)(2,1)S(1)} %shard_map.160.rest_0_), channel_id=1, source_target_pairs={{0,3},{1,0},{2,1},{3,2},{4,7},{5,4},{6,5},{7,6},{8,11},{9,8},{10,9... | collective-permute-start | bytes 98312 | tf_op jit(solution)/shard_map/ppermute | solution.py:421
  17.7 0.4 collective-permute-done.3.rest_1_
  18.1 0.7 %collective-permute-done.4.rest_2_ = bf16[8,2048]{1,0:T(8,128)(2,1)S(1)} collective-permute-done((bf16[8,2048]{1,0:T(8,128)(2,1)S(1)}, bf16[8,2048]{1,0:T(8,128)(2,1)S(1)}, u32[]{:S(2)}, u32[]{:S(2)}) %collective-permute-start.4) | collective-permute-done | bytes 32800 | tf_op jit(solution)/shard_map/ppermute | solution.py:421
  18.8 0.6 %collective-permute-done.5.rest_3_ = bf16[8,2048]{1,0:T(8,128)(2,1)S(1)} collective-permute-done((bf16[8,2048]{1,0:T(8,128)(2,1)S(1)}, bf16[8,2048]{1,0:T(8,128)(2,1)S(1)}, u32[]{:S(2)}, u32[]{:S(2)}) %collective-permute-start.5) | collective-permute-done | bytes 32800 | tf_op jit(solution)/shard_map/ppermute | solution.py:421
  19.3 0.0 slice-start.2
  19.4 0.0 slice-start.3
  19.4 1.6 %shard_map.161 = (f32[8,2048]{1,0:T(8,128)S(1)}, bf16[8,2048]{1,0:T(8,128)(2,1)S(1)}, bf16[8,2048]{1,0:T(8,128)(2,1)S(1)}, bf16[8,2048]{1,0:T(8,128)(2,1)S(1)}) custom-call(bf16[8,2048]{1,0:T(8,128)(2,1)S(1)} %shard_map.160.rest_0_, bf16[8,2048]{1,0:T(8,128)(2,1)S(1)} %collective-permute-done.3.rest_1_, bf16[8,2048]{1,0:T(8,128)(2,1)S(1)} %collective-permute-done.4.rest_2_, ...), custom_call_target="tpu_custom_call" | custom-call | flops 40000000000 | tf_op jit(solution)/shard_map/pallas_call | solution.py:424
  20.9 0.3 collective-permute-start.6
  21.3 3.5 %collective-permute-start.7 = (bf16[8,2048]{1,0:T(8,128)(2,1)S(1)}, bf16[8,2048]{1,0:T(8,128)(2,1)S(1)}, u32[]{:S(2)}, u32[]{:S(2)}) collective-permute-start(bf16[8,2048]{1,0:T(8,128)(2,1)S(1)} %get-tuple-element.27), channel_id=1, source_target_pairs={{0,8},{4,12},{8,0},{12,4},{1,9},{5,13},{9,1},{13,5},{2,10},{6,14},... | collective-permute-start | bytes 98312 | tf_op jit(solution)/shard_map/ppermute | solution.py:324
  24.7 0.7 %collective-permute-start.8 = (bf16[8,2048]{1,0:T(8,128)(2,1)S(1)}, bf16[8,2048]{1,0:T(8,128)(2,1)S(1)}, u32[]{:S(2)}, u32[]{:S(2)}) collective-permute-start(bf16[8,2048]{1,0:T(8,128)(2,1)S(1)} %get-tuple-element.28), channel_id=1, source_target_pairs={{0,12},{4,8},{8,4},{12,0},{1,13},{5,9},{9,5},{13,1},{2,14},{6,10},... | collective-permute-start | bytes 98312 | tf_op jit(solution)/shard_map/ppermute | solution.py:324
  25.4 2.0 %collective-permute-done.7.rest_2_ = bf16[8,2048]{1,0:T(8,128)(2,1)S(1)} collective-permute-done((bf16[8,2048]{1,0:T(8,128)(2,1)S(1)}, bf16[8,2048]{1,0:T(8,128)(2,1)S(1)}, u32[]{:S(2)}, u32[]{:S(2)}) %collective-permute-start.7) | collective-permute-done | bytes 32800 | tf_op jit(solution)/shard_map/ppermute | solution.py:324
  27.4 3.0 %collective-permute-done.8.rest_3_ = bf16[8,2048]{1,0:T(8,128)(2,1)S(1)} collective-permute-done((bf16[8,2048]{1,0:T(8,128)(2,1)S(1)}, bf16[8,2048]{1,0:T(8,128)(2,1)S(1)}, u32[]{:S(2)}, u32[]{:S(2)}) %collective-permute-start.8) | collective-permute-done | bytes 32800 | tf_op jit(solution)/shard_map/ppermute | solution.py:324
  30.5 0.0 copy-start.12
  30.5 0.7 %shard_map.162 = (bf16[4,2,2048]{2,1,0:T(2,128)(2,1)}, bf16[8,2048]{1,0:T(8,128)(2,1)S(1)}) custom-call(bf16[4,2,2048]{2,1,0:T(2,128)(2,1)S(1)} %copy-done.9, f32[8,2048]{1,0:T(8,128)S(1)} %get-tuple-element.25.rest_0_, bf16[8,2048]{1,0:T(8,128)(2,1)S(1)} %collective-permute-done.6.rest_1_, bf16[8,2048]{1,0:T(8,128)(2,1)S(1)} %collective-permute-done.7.rest_2_, ...), custom_call_target="tpu_custom_call" | custom-call | flops 40000000000 | tf_op jit(solution)/shard_map/pallas_call | solution.py:438
  31.1 0.0 collective-permute-start.10
  31.1 0.7 %collective-permute-start.11 = (bf16[8,2048]{1,0:T(8,128)(2,1)S(1)}, bf16[8,2048]{1,0:T(8,128)(2,1)S(1)}, u32[]{:S(2)}, u32[]{:S(2)}) collective-permute-start(bf16[8,2048]{1,0:T(8,128)(2,1)S(1)} %get-tuple-element.30.rest_0_), channel_id=1, source_target_pairs={{0,12},{4,8},{8,4},{12,0},{1,13},{5,9},{9,5},{13,1},{2,14},{6,10},... | collective-permute-start | bytes 98312 | tf_op jit(solution)/shard_map/ppermute | solution.py:324
  31.8 2.8 %collective-permute-start.9 = (bf16[8,2048]{1,0:T(8,128)(2,1)S(1)}, bf16[8,2048]{1,0:T(8,128)(2,1)S(1)}, u32[]{:S(2)}, u32[]{:S(2)}) collective-permute-start(bf16[8,2048]{1,0:T(8,128)(2,1)S(1)} %get-tuple-element.30.rest_0_), channel_id=1, source_target_pairs={{0,4},{4,0},{8,12},{12,8},{1,5},{5,1},{9,13},{13,9},{2,6},{6,2},{1... | collective-permute-start | bytes 98312 | tf_op jit(solution)/shard_map/ppermute | solution.py:324
  34.6 1.3 %collective-permute-done.10.rest_2_ = bf16[8,2048]{1,0:T(8,128)(2,1)S(1)} collective-permute-done((bf16[8,2048]{1,0:T(8,128)(2,1)S(1)}, bf16[8,2048]{1,0:T(8,128)(2,1)S(1)}, u32[]{:S(2)}, u32[]{:S(2)}) %collective-permute-start.10) | collective-permute-done | bytes 32800 | tf_op jit(solution)/shard_map/ppermute | solution.py:324
  35.9 0.9 %collective-permute-done.11.rest_3_ = bf16[8,2048]{1,0:T(8,128)(2,1)S(1)} collective-permute-done((bf16[8,2048]{1,0:T(8,128)(2,1)S(1)}, bf16[8,2048]{1,0:T(8,128)(2,1)S(1)}, u32[]{:S(2)}, u32[]{:S(2)}) %collective-permute-start.11) | collective-permute-done | bytes 32800 | tf_op jit(solution)/shard_map/ppermute | solution.py:324
  36.9 0.0 collective-permute-done.9.rest_1_
  36.9 3.6 %shard_map.164 = (f32[2,8,4224]{2,1,0:T(8,128)S(1)}, bf16[2,8,4224]{2,1,0:T(8,128)(2,1)S(1)}, bf16[64,4096]{1,0:T(8,128)(2,1)S(1)}) custom-call(bf16[2048]{0:T(1024)(128)(2,1)S(1)} %copy-done.12, bf16[8,2048]{1,0:T(8,128)(2,1)S(1)} %get-tuple-element.30.rest_0_, bf16[8,2048]{1,0:T(8,128)(2,1)S(1)} %collective-permute-done.9.rest_1_, ...), custom_call_target="tpu_custom_call" | custom-call | flops 16000000000 | tf_op jit(solution)/shard_map/pallas_call | solution.py:451
  40.5 0.1 collective-permute-start.12
  40.6 0.0 copy-start
  40.6 0.0 copy-start.2
  40.6 2.5 %shard_map.166 = (f32[2,8,3072]{2,1,0:T(8,128)S(1)}, bf16[2,8,3072]{2,1,0:T(8,128)(2,1)S(1)}) custom-call(bf16[64,4096]{1,0:T(8,128)(2,1)S(1)} %get-tuple-element.35.spread, bf16[2048,2,3584]{2,1,0:T(2,128)(2,1)S(1)} %bitcast.1), custom_call_target="tpu_custom_call" | custom-call | flops 16000000000 | tf_op jit(solution)/shard_map/pallas_call | solution.py:467
  43.1 0.5 %collective-permute-start.14 = (bf16[2,8,3072]{2,1,0:T(8,128)(2,1)S(1)}, bf16[2,8,3072]{2,1,0:T(8,128)(2,1)S(1)}, u32[]{:S(2)}, u32[]{:S(2)}) collective-permute-start(bf16[2,8,3072]{2,1,0:T(8,128)(2,1)S(1)} %get-tuple-element.37), channel_id=1, source_target_pairs={{0,1},{1,0},{2,3},{3,2},{4,5},{5,4},{6,7},{7,6},{8,9},{9,8},{10,11... | collective-permute-start | bytes 294920 | tf_op jit(solution)/shard_map/ppermute | solution.py:483
  43.6 0.1 shard_map.165
  43.7 1.0 %collective-permute-start.13 = (bf16[8,4224]{1,0:T(8,128)(2,1)S(1)}, bf16[8,4224]{1,0:T(8,128)(2,1)S(1)}, u32[]{:S(2)}, u32[]{:S(2)}) collective-permute-start(bf16[8,4224]{1,0:T(8,128)(2,1)S(1)} %get-tuple-element.34), channel_id=1, source_target_pairs={{0,2},{1,3},{2,0},{3,1},{4,6},{5,7},{6,4},{7,5},{8,10},{9,11},{10,... | collective-permute-start | bytes 202760 | tf_op jit(solution)/shard_map/ppermute | solution.py:493
  44.8 0.0 collective-permute-done.14.received
  44.8 1.1 %collective-permute-start.15 = (bf16[8,3072]{1,0:T(8,128)(2,1)S(1)}, bf16[8,3072]{1,0:T(8,128)(2,1)S(1)}, u32[]{:S(2)}, u32[]{:S(2)}) collective-permute-start(bf16[8,3072]{1,0:T(8,128)(2,1)S(1)} %get-tuple-element.39), channel_id=1, source_target_pairs={{0,2},{1,3},{2,0},{3,1},{4,6},{5,7},{6,4},{7,5},{8,10},{9,11},{10,... | collective-permute-start | bytes 147464 | tf_op jit(solution)/shard_map/ppermute | solution.py:493
  45.9 0.8 %shard_map.163.scales = f32[8,3584]{1,0:T(8,128)S(1)} custom-call(s32[4]{0:T(128)S(1)} %copy-done.2, bf16[128,3584]{1,0:T(8,128)(2,1)S(1)} %copy-done), custom_call_target="tpu_custom_call" | custom-call | tf_op jit(solution)/shard_map/pallas_call | solution.py:368
  46.7 2.5 %collective-permute-done.15.rest_3_ = bf16[8,3072]{1,0:T(8,128)(2,1)S(1)} collective-permute-done((bf16[8,3072]{1,0:T(8,128)(2,1)S(1)}, bf16[8,3072]{1,0:T(8,128)(2,1)S(1)}, u32[]{:S(2)}, u32[]{:S(2)}) %collective-permute-start.15) | collective-permute-done | bytes 49184 | tf_op jit(solution)/shard_map/ppermute | solution.py:493
  49.1 0.0 collective-permute-done.13.rest_1_
  49.1 0.8 %shard_map.168 = bf16[4,2,3584]{2,1,0:T(2,128)(2,1)} custom-call(f32[8,3584]{1,0:T(8,128)S(1)} %shard_map.163.scales, f32[8,4224]{1,0:T(8,128)S(1)} %get-tuple-element.33.rest_0_, bf16[8,4224]{1,0:T(8,128)(2,1)S(1)} %collective-permute-done.13.rest_1_, f32[8,3072]{1,0:T(8,128)S(1)} %get-tuple-element.38.rest_2_, ...), custom_call_target="tpu_custom_call" | custom-call | tf_op jit(solution)/shard_map/pallas_call | solution.py:496
  (43 shorter events, 0.1 us)
Async XLA Ops:
  0.6 1.4 %copy-start.6 = (bf16[4,2,8192]{2,1,0:T(2,128)(2,1)S(1)}, bf16[4,2,8192]{2,1,0:T(2,128)(2,1)}, u32[]{:S(2)}) copy-start(bf16[4,2,8192]{2,1,0:T(2,128)(2,1)} %queries.1) | copy-start | bytes 393220
  0.6 1.4 %copy-start.4 = (bf16[128,1024]{1,0:T(8,128)(2,1)S(1)}, bf16[128,1024]{1,0:T(8,128)(2,1)}, u32[]{:S(2)}) copy-start(bf16[128,1024]{1,0:T(8,128)(2,1)} %prefix_keys.1) | copy-start | bytes 786436
  0.7 1.4 %copy-start.5 = (bf16[128,1024]{1,0:T(8,128)(2,1)S(1)}, bf16[128,1024]{1,0:T(8,128)(2,1)}, u32[]{:S(2)}) copy-start(bf16[128,1024]{1,0:T(8,128)(2,1)} %prefix_values.1) | copy-start | bytes 786436
  0.7 1.4 %copy-start.7 = (bf16[4,16,1024]{2,1,0:T(8,128)(2,1)S(1)}, bf16[4,16,1024]{2,1,0:T(8,128)(2,1)}, u32[]{:S(2)}) copy-start(bf16[4,16,1024]{2,1,0:T(8,128)(2,1)} %suffix_keys.1) | copy-start | bytes 393220
  0.7 1.4 %copy-start.8 = (bf16[4,16,1024]{2,1,0:T(8,128)(2,1)S(1)}, bf16[4,16,1024]{2,1,0:T(8,128)(2,1)}, u32[]{:S(2)}) copy-start(bf16[4,16,1024]{2,1,0:T(8,128)(2,1)} %suffix_values.1) | copy-start | bytes 393220
  0.7 1.4 %copy-start.10 = (bf16[4,2,1024]{2,1,0:T(2,128)(2,1)S(1)}, bf16[4,2,1024]{2,1,0:T(2,128)(2,1)}, u32[]{:S(2)}) copy-start(bf16[4,2,1024]{2,1,0:T(2,128)(2,1)} %new_keys.1) | copy-start | bytes 49156
  0.7 1.4 %copy-start.11 = (bf16[4,2,1024]{2,1,0:T(2,128)(2,1)S(1)}, bf16[4,2,1024]{2,1,0:T(2,128)(2,1)}, u32[]{:S(2)}) copy-start(bf16[4,2,1024]{2,1,0:T(2,128)(2,1)} %new_values.1) | copy-start | bytes 49156
  0.7 1.4 %copy-start.1 = (s32[4]{0:T(128)S(1)}, s32[4]{0:T(128)}, u32[]{:S(2)}) copy-start(s32[4]{0:T(128)} %ids.3) | copy-start | bytes 52
  0.7 1.4 %copy-start.3 = (bf16[128,2,1024]{2,1,0:T(2,128)(2,1)S(1)}, bf16[128,2,1024]{2,1,0:T(2,128)(2,1)}, u32[]{:S(2)}) copy-start(bf16[128,2,1024]{2,1,0:T(2,128)(2,1)} %kv_scales.1) | copy-start | bytes 1572868
  0.7 0.8 %copy-start.13 = (s32[4]{0:T(128)S(1)}, s32[4]{0:T(128)}, u32[]{:S(2)}) copy-start(s32[4]{0:T(128)} %lengths.1) | copy-start | bytes 52
  2.1 17.2 %slice-start.7 = ((s8[8388608]{0:T(1024)(128)(4,1)}), s8[4194304]{0:T(1024)(128)(4,1)S(1)}, s32[]{:S(2)}) async-start(s8[8388608]{0:T(1024)(128)(4,1)} %bitcast.2), calls=%async_computation.7 | async-start | bytes 8388608
  4.8 7.0 %collective-permute-start = (bf16[8,2176]{1,0:T(8,128)(2,1)S(1)}, bf16[8,2176]{1,0:T(8,128)(2,1)S(1)}, u32[]{:S(2)}, u32[]{:S(2)}) collective-permute-start(bf16[8,2176]{1,0:T(8,128)(2,1)S(1)} %get-tuple-element.22), channel_id=1, source_target_pairs={{0,4},{4,8},{8,12},{12,0},{1,5},{5,9},{9,13},{13,1},{2,6},{6,10},{... | collective-permute-start | bytes 104456 | tf_op jit(solution)/shard_map/ppermute | solution.py:409
  7.9 5.2 %collective-permute-start.1 = (bf16[8,2176]{1,0:T(8,128)(2,1)S(1)}, bf16[8,2176]{1,0:T(8,128)(2,1)S(1)}, u32[]{:S(2)}, u32[]{:S(2)}) collective-permute-start(bf16[8,2176]{1,0:T(8,128)(2,1)S(1)} %get-tuple-element.23), channel_id=1, source_target_pairs={{0,8},{4,12},{8,0},{12,4},{1,9},{5,13},{9,1},{13,5},{2,10},{6,14},... | collective-permute-start | bytes 104456 | tf_op jit(solution)/shard_map/ppermute | solution.py:409
  10.5 3.9 %collective-permute-start.2 = (bf16[8,2176]{1,0:T(8,128)(2,1)S(1)}, bf16[8,2176]{1,0:T(8,128)(2,1)S(1)}, u32[]{:S(2)}, u32[]{:S(2)}) collective-permute-start(bf16[8,2176]{1,0:T(8,128)(2,1)S(1)} %get-tuple-element.24), channel_id=1, source_target_pairs={{0,12},{4,0},{8,4},{12,8},{1,13},{5,1},{9,5},{13,9},{2,14},{6,2},{... | collective-permute-start | bytes 104456 | tf_op jit(solution)/shard_map/ppermute | solution.py:409
  14.4 4.9 %slice-start.8 = ((s8[8388608]{0:T(1024)(128)(4,1)}), s8[4194304]{0:T(1024)(128)(4,1)S(1)}, s32[]{:S(2)}) async-start(s8[8388608]{0:T(1024)(128)(4,1)} %bitcast.2), calls=%async_computation.8 | async-start | bytes 8388608
  14.7 15.7 %copy-start.9 = (bf16[4,2,2048]{2,1,0:T(2,128)(2,1)S(1)}, bf16[4,2,2048]{2,1,0:T(2,128)(2,1)}, u32[]{:S(2)}) copy-start(bf16[4,2,2048]{2,1,0:T(2,128)(2,1)} %hidden.1) | copy-start | bytes 98308
  14.7 3.4 %collective-permute-start.3 = (bf16[8,2048]{1,0:T(8,128)(2,1)S(1)}, bf16[8,2048]{1,0:T(8,128)(2,1)S(1)}, u32[]{:S(2)}, u32[]{:S(2)}) collective-permute-start(bf16[8,2048]{1,0:T(8,128)(2,1)S(1)} %shard_map.160.rest_0_), channel_id=1, source_target_pairs={{0,1},{1,2},{2,3},{3,0},{4,5},{5,6},{6,7},{7,4},{8,9},{9,10},{10,1... | collective-permute-start | bytes 98312 | tf_op jit(solution)/shard_map/ppermute | solution.py:421
  14.8 4.0 %collective-permute-start.4 = (bf16[8,2048]{1,0:T(8,128)(2,1)S(1)}, bf16[8,2048]{1,0:T(8,128)(2,1)S(1)}, u32[]{:S(2)}, u32[]{:S(2)}) collective-permute-start(bf16[8,2048]{1,0:T(8,128)(2,1)S(1)} %shard_map.160.rest_0_), channel_id=1, source_target_pairs={{0,2},{1,3},{2,0},{3,1},{4,6},{5,7},{6,4},{7,5},{8,10},{9,11},{10,... | collective-permute-start | bytes 98312 | tf_op jit(solution)/shard_map/ppermute | solution.py:421
  16.3 3.0 %collective-permute-start.5 = (bf16[8,2048]{1,0:T(8,128)(2,1)S(1)}, bf16[8,2048]{1,0:T(8,128)(2,1)S(1)}, u32[]{:S(2)}, u32[]{:S(2)}) collective-permute-start(bf16[8,2048]{1,0:T(8,128)(2,1)S(1)} %shard_map.160.rest_0_), channel_id=1, source_target_pairs={{0,3},{1,0},{2,1},{3,2},{4,7},{5,4},{6,5},{7,6},{8,11},{9,8},{10,9... | collective-permute-start | bytes 98312 | tf_op jit(solution)/shard_map/ppermute | solution.py:421
  19.3 17.5 %slice-start = ((s8[29360128]{0:T(1024)(128)(4,1)}), s8[4194304]{0:T(1024)(128)(4,1)S(1)}, s32[]{:S(2)}) async-start(s8[29360128]{0:T(1024)(128)(4,1)} %bitcast), calls=%async_computation | async-start | bytes 8388608
  19.3 17.5 %slice-start.1 = ((s8[29360128]{0:T(1024)(128)(4,1)}), s8[4194304]{0:T(1024)(128)(4,1)S(1)}, s32[]{:S(2)}) async-start(s8[29360128]{0:T(1024)(128)(4,1)} %bitcast), calls=%async_computation.1 | async-start | bytes 8388608
  19.3 17.5 %slice-start.2 = ((s8[29360128]{0:T(1024)(128)(4,1)}), s8[4194304]{0:T(1024)(128)(4,1)S(1)}, s32[]{:S(2)}) async-start(s8[29360128]{0:T(1024)(128)(4,1)} %bitcast), calls=%async_computation.2 | async-start | bytes 8388608
  19.4 17.5 %slice-start.3 = ((s8[29360128]{0:T(1024)(128)(4,1)}), s8[4194304]{0:T(1024)(128)(4,1)S(1)}, s32[]{:S(2)}) async-start(s8[29360128]{0:T(1024)(128)(4,1)} %bitcast), calls=%async_computation.3 | async-start | bytes 8388608
  20.9 4.5 %collective-permute-start.6 = (bf16[8,2048]{1,0:T(8,128)(2,1)S(1)}, bf16[8,2048]{1,0:T(8,128)(2,1)S(1)}, u32[]{:S(2)}, u32[]{:S(2)}) collective-permute-start(bf16[8,2048]{1,0:T(8,128)(2,1)S(1)} %get-tuple-element.26), channel_id=1, source_target_pairs={{0,4},{4,0},{8,12},{12,8},{1,5},{5,1},{9,13},{13,9},{2,6},{6,2},{1... | collective-permute-start | bytes 98312 | tf_op jit(solution)/shard_map/ppermute | solution.py:324
  21.3 6.1 %collective-permute-start.7 = (bf16[8,2048]{1,0:T(8,128)(2,1)S(1)}, bf16[8,2048]{1,0:T(8,128)(2,1)S(1)}, u32[]{:S(2)}, u32[]{:S(2)}) collective-permute-start(bf16[8,2048]{1,0:T(8,128)(2,1)S(1)} %get-tuple-element.27), channel_id=1, source_target_pairs={{0,8},{4,12},{8,0},{12,4},{1,9},{5,13},{9,1},{13,5},{2,10},{6,14},... | collective-permute-start | bytes 98312 | tf_op jit(solution)/shard_map/ppermute | solution.py:324
  24.7 5.7 %collective-permute-start.8 = (bf16[8,2048]{1,0:T(8,128)(2,1)S(1)}, bf16[8,2048]{1,0:T(8,128)(2,1)S(1)}, u32[]{:S(2)}, u32[]{:S(2)}) collective-permute-start(bf16[8,2048]{1,0:T(8,128)(2,1)S(1)} %get-tuple-element.28), channel_id=1, source_target_pairs={{0,12},{4,8},{8,4},{12,0},{1,13},{5,9},{9,5},{13,1},{2,14},{6,10},... | collective-permute-start | bytes 98312 | tf_op jit(solution)/shard_map/ppermute | solution.py:324
  30.4 6.4 %slice-start.4 = ((s8[29360128]{0:T(1024)(128)(4,1)}), s8[4194304]{0:T(1024)(128)(4,1)S(1)}, s32[]{:S(2)}) async-start(s8[29360128]{0:T(1024)(128)(4,1)} %bitcast), calls=%async_computation.4 | async-start | bytes 8388608
  30.5 6.5 %slice-start.5 = ((s8[29360128]{0:T(1024)(128)(4,1)}), s8[4194304]{0:T(1024)(128)(4,1)S(1)}, s32[]{:S(2)}) async-start(s8[29360128]{0:T(1024)(128)(4,1)} %bitcast), calls=%async_computation.5 | async-start | bytes 8388608
  30.5 6.5 %slice-start.6 = ((s8[29360128]{0:T(1024)(128)(4,1)}), s8[4194304]{0:T(1024)(128)(4,1)S(1)}, s32[]{:S(2)}) async-start(s8[29360128]{0:T(1024)(128)(4,1)} %bitcast), calls=%async_computation.6 | async-start | bytes 8388608
  30.5 6.5 %copy-start.12 = (bf16[2048]{0:T(1024)(128)(2,1)S(1)}, bf16[2048]{0:T(1024)(128)(2,1)}, u32[]{:S(2)}) copy-start(bf16[2048]{0:T(1024)(128)(2,1)} %gain.1) | copy-start | bytes 12292
  31.1 4.8 %collective-permute-start.10 = (bf16[8,2048]{1,0:T(8,128)(2,1)S(1)}, bf16[8,2048]{1,0:T(8,128)(2,1)S(1)}, u32[]{:S(2)}, u32[]{:S(2)}) collective-permute-start(bf16[8,2048]{1,0:T(8,128)(2,1)S(1)} %get-tuple-element.30.rest_0_), channel_id=1, source_target_pairs={{0,8},{4,12},{8,0},{12,4},{1,9},{5,13},{9,1},{13,5},{2,10},{6,14},... | collective-permute-start | bytes 98312 | tf_op jit(solution)/shard_map/ppermute | solution.py:324
  31.1 5.7 %collective-permute-start.11 = (bf16[8,2048]{1,0:T(8,128)(2,1)S(1)}, bf16[8,2048]{1,0:T(8,128)(2,1)S(1)}, u32[]{:S(2)}, u32[]{:S(2)}) collective-permute-start(bf16[8,2048]{1,0:T(8,128)(2,1)S(1)} %get-tuple-element.30.rest_0_), channel_id=1, source_target_pairs={{0,12},{4,8},{8,4},{12,0},{1,13},{5,9},{9,5},{13,1},{2,14},{6,10},... | collective-permute-start | bytes 98312 | tf_op jit(solution)/shard_map/ppermute | solution.py:324
  31.8 5.0 %collective-permute-start.9 = (bf16[8,2048]{1,0:T(8,128)(2,1)S(1)}, bf16[8,2048]{1,0:T(8,128)(2,1)S(1)}, u32[]{:S(2)}, u32[]{:S(2)}) collective-permute-start(bf16[8,2048]{1,0:T(8,128)(2,1)S(1)} %get-tuple-element.30.rest_0_), channel_id=1, source_target_pairs={{0,4},{4,0},{8,12},{12,8},{1,5},{5,1},{9,13},{13,9},{2,6},{6,2},{1... | collective-permute-start | bytes 98312 | tf_op jit(solution)/shard_map/ppermute | solution.py:324
  40.5 3.1 %collective-permute-start.12 = (bf16[2,8,4224]{2,1,0:T(8,128)(2,1)S(1)}, bf16[2,8,4224]{2,1,0:T(8,128)(2,1)S(1)}, u32[]{:S(2)}, u32[]{:S(2)}) collective-permute-start(bf16[2,8,4224]{2,1,0:T(8,128)(2,1)S(1)} %get-tuple-element.32), channel_id=1, source_target_pairs={{0,1},{1,0},{2,3},{3,2},{4,5},{5,4},{6,7},{7,6},{8,9},{9,8},{10,11... | collective-permute-start | bytes 405512 | tf_op jit(solution)/shard_map/ppermute | solution.py:483
  40.6 5.3 %copy-start = (bf16[128,3584]{1,0:T(8,128)(2,1)S(1)}, bf16[128,3584]{1,0:T(8,128)(2,1)}, u32[]{:S(2)}) copy-start(bf16[128,3584]{1,0:T(8,128)(2,1)} %table.1) | copy-start | bytes 2752516
  40.6 5.3 %copy-start.2 = (s32[4]{0:T(128)S(1)}, s32[4]{0:T(128)}, u32[]{:S(2)}) copy-start(s32[4]{0:T(128)} %ids.3) | copy-start | bytes 52
  43.1 1.7 %collective-permute-start.14 = (bf16[2,8,3072]{2,1,0:T(8,128)(2,1)S(1)}, bf16[2,8,3072]{2,1,0:T(8,128)(2,1)S(1)}, u32[]{:S(2)}, u32[]{:S(2)}) collective-permute-start(bf16[2,8,3072]{2,1,0:T(8,128)(2,1)S(1)} %get-tuple-element.37), channel_id=1, source_target_pairs={{0,1},{1,0},{2,3},{3,2},{4,5},{5,4},{6,7},{7,6},{8,9},{9,8},{10,11... | collective-permute-start | bytes 294920 | tf_op jit(solution)/shard_map/ppermute | solution.py:483
  43.7 5.4 %collective-permute-start.13 = (bf16[8,4224]{1,0:T(8,128)(2,1)S(1)}, bf16[8,4224]{1,0:T(8,128)(2,1)S(1)}, u32[]{:S(2)}, u32[]{:S(2)}) collective-permute-start(bf16[8,4224]{1,0:T(8,128)(2,1)S(1)} %get-tuple-element.34), channel_id=1, source_target_pairs={{0,2},{1,3},{2,0},{3,1},{4,6},{5,7},{6,4},{7,5},{8,10},{9,11},{10,... | collective-permute-start | bytes 202760 | tf_op jit(solution)/shard_map/ppermute | solution.py:493
  44.8 4.3 %collective-permute-start.15 = (bf16[8,3072]{1,0:T(8,128)(2,1)S(1)}, bf16[8,3072]{1,0:T(8,128)(2,1)S(1)}, u32[]{:S(2)}, u32[]{:S(2)}) collective-permute-start(bf16[8,3072]{1,0:T(8,128)(2,1)S(1)} %get-tuple-element.39), channel_id=1, source_target_pairs={{0,2},{1,3},{2,0},{3,1},{4,6},{5,7},{6,4},{7,5},{8,10},{9,11},{10,... | collective-permute-start | bytes 147464 | tf_op jit(solution)/shard_map/ppermute | solution.py:493
